TPU v7x, 32 devices: a whole 2x2x4 slice. The times are simulated.
32 devices in a mesh: ctx: 8 (over z, x), head: 4 (over y, core).
Axes of the slice: x: 2, y: 2, z: 4, core: 2. Of those that a mesh axis runs over, the one named last changes fastest.
Arguments:
- layer_in: bfloat16 [2048, 2048], P(('ctx', 'head')), may hold values from -6 to 6
- in_proj: bfloat16 [2048, 8, 768], P(None, 'head'), may hold values from -0.125 to 0.125
- conv_weight: float32 [4, 8, 512], P(None, 'head'), may hold values from -2 to 2
- gate_logits: float32 [2, 16, 2048], P(None, 'head', 'ctx'), may hold values from -16 to 4
- norm_gain: float32 [128], replicated, may hold values from 0.1 to 1.9
- out_proj: bfloat16 [2048, 2048], P('head'), may hold values from -0.125 to 0.125
Outputs:
- layer_out: bfloat16 [2048, 2048], P(('ctx', 'head'))
All inputs are finite; a program needn't handle non-finite values.
Results may differ from a plain program's by a relative error of at most 0.0065.
Values may be sent and summed in bfloat16 or wider, within the bound.
No kernel may reach another device: no remote copies, remote signals or barrier semaphores. Data moves between devices by JAX's collectives and lax.ppermute only.
A program may use at most 128 MiB of HBM per device.

v0:
```python
import jax
import jax.numpy as jnp
from jax import lax
from jax.sharding import PartitionSpec as P

HK = 8
VALUE_HEADS = 16
DK = 128
DV = 128
KERNEL = 4
SPAN = 64


EPSILON = 1e-06
HIGHEST_PREC = lax.Precision.HIGHEST


def passed_along(value, axis, steps):
    count = lax.axis_size(axis)
    first, last = (max(0, -steps), min(count, count - steps))
    return lax.ppermute(value, axis, [(source, source + steps) for source in range(first, last)])


def entering(shard, axis, combine, identity):
    peers, place = (lax.axis_size(axis), lax.axis_index(axis))
    everything = jax.tree.map(lambda part: lax.all_gather(part, axis), shard)
    start = jax.tree.map(
        lambda part, zero: jnp.broadcast_to(jnp.asarray(zero, part.dtype), part.shape),
        shard,
        identity,
    )

    def lap(k, before):
        reached = k < place
        new = combine(before, jax.tree.map(lambda part: part[k], everything))
        return jax.tree.map(lambda a, b: jnp.where(reached, a, b), new, before)

    return lax.fori_loop(0, peers, lap, start)


def product(pattern, first, second):
    return jnp.einsum(pattern, first, second, precision=HIGHEST_PREC)


def causal_conv(padded, weight, length):
    taps_count = weight.shape[0]
    running = padded[0:length] * weight[0]
    for offset in range(1, taps_count):
        running = running + padded[offset : offset + length] * weight[offset]
    return running


def l2_normed(values):
    return values * lax.rsqrt(jnp.sum(values * values, axis=-1, keepdims=True) + EPSILON)


def unit_inverse(lower_mat):
    size_now = lower_mat.shape[-1]
    levels = max((size_now - 1).bit_length(), 1)
    identity = jnp.eye(size_now, dtype=lower_mat.dtype)
    power = -lower_mat
    result = identity + power
    for level_index in range(1, levels):
        power = product("...ij,...jk->...ik", power, power)
        result = product("...ij,...jk->...ik", result, identity + power)
    return result


def span_terms(queries, key_rows, values, log_decay, beta_gate):
    cum_decay = jnp.cumsum(log_decay, axis=-1)
    row_ids = jnp.arange(log_decay.shape[-1])
    strict_below = row_ids[:, None] > row_ids[None, :]
    on_or_below = row_ids[:, None] >= row_ids[None, :]
    log_gap = cum_decay[..., :, None] - cum_decay[..., None, :]
    decay_mat = jnp.where(on_or_below, jnp.exp(jnp.where(on_or_below, log_gap, 0.0)), 0.0)
    key_gram = product("...id,...jd->...ij", key_rows, key_rows)
    lower_mat = jnp.where(strict_below, beta_gate[..., :, None] * key_gram * decay_mat, 0.0)
    solver = unit_inverse(lower_mat)
    scaled_k = key_rows * (beta_gate * jnp.exp(cum_decay))[..., None]
    scaled_v = values * beta_gate[..., None]
    w_rows = product("...ij,...jd->...id", solver, scaled_k)
    u_rows = product("...ij,...jd->...id", solver, scaled_v)
    qk_mat = product("...id,...jd->...ij", queries, key_rows) * decay_mat
    q_dec = queries * jnp.exp(cum_decay)[..., None]
    k_dec = key_rows * jnp.exp(cum_decay[..., -1:] - cum_decay)[..., None]
    span_decay = jnp.exp(cum_decay[..., -1])
    return (w_rows, u_rows, qk_mat, q_dec, k_dec, span_decay)


def local(layer_in, in_proj, conv_weight, gate_logits, norm_gain, out_proj):
    model_width, key_heads, group_width = in_proj.shape
    group_ratio = VALUE_HEADS // HK
    head_count = key_heads * group_ratio
    conv_width = 2 * DK + group_ratio * DV
    weight_flat = in_proj.reshape(model_width, key_heads * group_width)
    projected = jnp.dot(
        lax.all_gather(layer_in, "head", axis=0, tiled=True),
        weight_flat,
        preferred_element_type=jnp.float32,
    ).astype(jnp.bfloat16)
    tok_rows = projected.shape[0]
    projected = projected.reshape(tok_rows, key_heads, group_width)
    conv_in = projected[:, :, :conv_width]
    rim_rows = passed_along(conv_in[tok_rows - (KERNEL - 1) :], "ctx", 1)
    padded = jnp.concatenate([rim_rows, conv_in], axis=0).astype(jnp.float32)
    conv_out = jax.nn.silu(causal_conv(padded, conv_weight, tok_rows))
    queries = l2_normed(conv_out[:, :, :DK]) * DK ** (-0.5)
    key_rows = l2_normed(conv_out[:, :, DK : 2 * DK])
    values = conv_out[:, :, 2 * DK :].reshape(tok_rows, head_count, DV)
    gate_z = projected[:, :, conv_width:].reshape(tok_rows, head_count, DV).astype(jnp.float32)
    queries = jnp.repeat(queries, group_ratio, axis=1)
    key_rows = jnp.repeat(key_rows, group_ratio, axis=1)
    spans = tok_rows // SPAN

    def by_span(array_in):
        return array_in.reshape(spans, SPAN, head_count, -1).transpose(0, 2, 1, 3)

    log_decay = (
        (-jax.nn.softplus(gate_logits[0])).reshape(head_count, spans, SPAN).transpose(1, 0, 2)
    )
    beta_gate = jax.nn.sigmoid(gate_logits[1]).reshape(head_count, spans, SPAN).transpose(1, 0, 2)
    w_rows, u_rows, qk_mat, q_dec, k_dec, span_decay = span_terms(
        by_span(queries), by_span(key_rows), by_span(values), log_decay, beta_gate
    )
    eye_key = jnp.eye(DK, dtype=jnp.float32)
    transit = span_decay[..., None, None] * eye_key - product("...cd,...ce->...de", k_dec, w_rows)
    inject = product("...cd,...ce->...de", k_dec, u_rows)

    def fold_step(carry_pair, step_pair):
        prod_now, base_now = carry_pair
        next_prod = product("hij,hjk->hik", step_pair[0], prod_now)
        next_base = product("hij,hjk->hik", step_pair[0], base_now) + step_pair[1]
        return ((next_prod, next_base), (prod_now, base_now))

    start_pair = (
        jnp.broadcast_to(eye_key, (head_count, DK, DK)),
        jnp.zeros((head_count, DK, DV), jnp.float32),
    )
    (dev_prod, dev_base), (prefix_prod, prefix_base) = lax.scan(
        fold_step, start_pair, (transit, inject)
    )

    def combine(earlier_pair, later_pair):
        joined_prod = product("hij,hjk->hik", later_pair[0], earlier_pair[0])
        joined_base = product("hij,hjk->hik", later_pair[0], earlier_pair[1]) + later_pair[1]
        return (joined_prod, joined_base)

    incoming = entering((dev_prod, dev_base), "ctx", combine, start_pair)[1]

    def emit_block(carried, pieces):
        w_part, u_part, qk_part, qd_part, kd_part, decay_part = pieces
        fresh_values = u_part - product("hcd,hde->hce", w_part, carried)
        result = product("hcd,hde->hce", qd_part, carried) + product(
            "hij,hje->hie", qk_part, fresh_values
        )
        carried = decay_part[:, None, None] * carried + product(
            "hcd,hce->hde", kd_part, fresh_values
        )
        return (carried, result)

    final_state, attended = lax.scan(
        emit_block, incoming, (w_rows, u_rows, qk_mat, q_dec, k_dec, span_decay)
    )
    attended = attended.transpose(0, 2, 1, 3).reshape(tok_rows, head_count, DV)
    mean_square = jnp.mean(attended * attended, axis=-1, keepdims=True)
    normed = (attended * lax.rsqrt(mean_square + EPSILON) * norm_gain * jax.nn.silu(gate_z)).astype(
        jnp.bfloat16
    )
    normed = normed.reshape(tok_rows, head_count * DV)
    return lax.psum_scatter(
        jnp.dot(normed, out_proj, preferred_element_type=jnp.float32),
        "head",
        scatter_dimension=0,
        tiled=True,
    ).astype(jnp.bfloat16)


def solution(mesh):
    in_specs = (
        P(("ctx", "head"), None),
        P(None, "head", None),
        P(None, "head", None),
        P(None, "head", "ctx"),
        P(),
        P("head", None),
    )
    out_specs = P(("ctx", "head"), None)
    return jax.shard_map(local, mesh=mesh, in_specs=in_specs, out_specs=out_specs, check_vma=False)
```

profile of v0, /device:TPU:0, one launch (start us, length us, event | category | flops | bytes accessed | tf_op | source)
XLA Modules:
  0.0 257.3 jit_solution(17519052000510728661)
XLA Ops:
  7.3 6.8 %copy.142 = bf16[256,8,2,768]{3,1,2,0:T(8,128)(2,1)} copy(bf16[256,8,2,768]{3,2,1,0:T(2,128)(2,1)} %bitcast.147) | data formatting | bytes 12582912
  16.2 12.2 %all-gather.6.cloned.1.call-done = bf16[256,2048]{1,0:T(8,128)(2,1)} async-done(((bf16[64,2048]{1,0:T(8,128)(2,1)}), bf16[256,2048]{1,0:T(8,128)(2,1)}) %all-gather.6.cloned.1.call-update) | async-done | bytes 1048592 | tf_op jit(solution)/shard_map/all_gather | solution.py:97
  28.4 5.8 %convolution_convert_fusion = bf16[256,1536]{1,0:T(8,128)(2,1)} fusion(bf16[256,2048]{1,0:T(8,128)(2,1)} %all-gather.6.cloned.1.call-done, bf16[2048,1536]{1,0:T(8,128)(2,1)} %bitcast.148), kind=kOutput, calls=%fused_computation.41 | convolution fusion | flops 1611005952 | bytes 8126464 | tf_op jit(solution)/shard_map/dot_general | solution.py:96
  36.5 4.0 %collective-permute-start = (bf16[3,2,512]{2,0,1:T(4,128)(2,1)}, bf16[3,2,512]{2,0,1:T(4,128)(2,1)}, u32[]{:S(2)}, u32[]{:S(2)}) collective-permute-start(bf16[3,2,512]{2,0,1:T(4,128)(2,1)} %copy.140), channel_id=1, source_target_pairs={{0,4},{4,8},{8,12},{12,16},{16,20},{20,24},{24,28},{1,5},{5,9},{9,... | collective-permute-start | bytes 18440 | tf_op jit(solution)/shard_map/ppermute | solution.py:21
  57.5 2.3 reshape_reshape.10
  59.9 1.7 fusion.82
  64.9 2.8 %fusion.74 = f32[4,4,128,128]{3,2,1,0:T(8,128)} fusion(f32[4,4,64,128]{3,2,1,0:T(8,128)S(1)} %fusion.45, f32[4,4,64,128]{3,2,0,1:T(8,128)S(1)} %get-tuple-element.301), kind=kOutput, calls=%fused_computation.119 | convolution fusion | flops 201326592 | bytes 2097152 | tf_op jit(solution)/shard_map/...cd,...ce->...de/dot_general | solution.py:42
  67.7 1.9 convolution_subtract_fusion.1
  69.7 13.8 %while.40 = (s32[]{:T(128)}, f32[4,128,128]{2,1,0:T(8,128)S(1)}, f32[4,128,128]{2,1,0:T(8,128)}, f32[4,4,128,128]{3,2,1,0:T(8,128)S(1)}, f32[4,4,128,128]{3,2,1,0:T(8,128)}, /*index=5*/s32[]{:T(128)}, s32[]{:T(128)}) while((s32[]{:T(128)}, f32[4,128,128]{2,1,0:T(8,128)S(1)}, f32[4,128,128]{2,1,0:T(8,128)}, ...), condition=%wide.region_3.4_spmd.clone, body=%wide.region_2.3_spmd.clone.sunk | while | flops 201457664 | bytes 2884699 | solution.py:139
  70.7 2.0 convolution_add_fusion.8
  74.1 2.0 convolution_add_fusion.8
  77.5 2.0 convolution_add_fusion.8
  81.0 2.0 convolution_add_fusion.8
  86.9 2.1 copy.135
  91.8 1.8 convolution_multiply_fusion
  93.6 38.8 %all-gather.8.cloned.1.call-done = f32[32,128,128]{2,1,0:T(8,128)} async-done(((f32[4,128,128]{2,1,0:T(8,128)}), f32[32,128,128]{2,1,0:T(8,128)}) %all-gather.8.cloned.1.call-update) | async-done | bytes 2097168 | tf_op jit(solution)/shard_map/all_gather | solution.py:26
  132.4 49.9 %all-gather.10.cloned.1.call-done = f32[32,128,128]{2,1,0:T(8,128)} async-done(((f32[4,128,128]{2,1,0:T(8,128)}), f32[32,128,128]{2,1,0:T(8,128)}) %all-gather.10.cloned.1.call-update) | async-done | bytes 2097168 | tf_op jit(solution)/shard_map/all_gather | solution.py:26
  182.4 11.9 %while.41 = (s32[]{:T(128)}, f32[4,128,128]{2,1,0:T(8,128)S(1)}, s32[]{:T(128)}, f32[8,4,128,128]{3,2,1,0:T(8,128)}, f32[8,4,128,128]{3,2,1,0:T(8,128)}, /*index=5*/s32[]{:T(128)}, s32[]{:T(128)}) while((s32[]{:T(128)}, f32[4,128,128]{2,1,0:T(8,128)S(1)}, s32[]{:T(128)}, f32[8,4,128,128]{3,2,1,0:T(8,128)}, ...), condition=%wide.region_5.6_spmd.clone, body=%wide.region_4.5_spmd.clone.sunk | while | flops 100925440 | bytes 1837663 | solution.py:38
  194.3 21.4 %while.39 = (s32[]{:T(128)}, f32[4,128,128]{2,1,0:T(8,128)S(1)}, f32[4,4,64,128]{3,2,1,0:T(8,128)S(1)}, f32[4,4]{1,0:T(4,128)S(1)}, f32[4,4,64,128]{3,2,1,0:T(8,...) while((s32[]{:T(128)}, f32[4,128,128]{2,1,0:T(8,128)S(1)}, ...), condition=%wide.region_8.9_spmd, body=%wide.region_7.8_spmd.sunk | while | flops 176357376 | bytes 2493593 | solution.py:161
  198.1 1.5 convolution_add_fusion.7
  208.8 1.5 convolution_add_fusion.7
  216.8 2.1 fusion.60
  218.9 30.1 %reduce-scatter.2.cloned.1.call-done = f32[64,2048]{1,0:T(8,128)} async-done(((f32[256,2048]{1,0:T(8,128)}), f32[64,2048]{1,0:T(8,128)}) %reduce-scatter.2.cloned.1.call-update) | async-done | bytes 524304 | tf_op jit(solution)/shard_map/reduce_scatter | solution.py:170
  249.0 1.8 convert_element_type.53
  (153 shorter events, 67.7 us)
Async XLA Ops:
  6.5 210.3 %copy-start = (bf16[512,2048]{1,0:T(8,128)(2,1)S(1)}, bf16[512,2048]{1,0:T(8,128)(2,1)}, u32[]{:S(2)}) copy-start(bf16[512,2048]{1,0:T(8,128)(2,1)} %param.17) | copy-start | bytes 6291460
  6.5 21.8 %all-gather.6.cloned.1.call-start = ((), (), s32[]{:S(2)}) async-start(), calls=%async_computation.1 | async-start | bytes 1310720 | tf_op jit(solution)/shard_map/all_gather | solution.py:97
  7.3 125.2 %all-gather.8.cloned.1.call-start = ((), (), s32[]{:S(2)}) async-start(), calls=%async_computation.3 | async-start | bytes 2359296 | tf_op jit(solution)/shard_map/all_gather | solution.py:26
  7.3 6.8 %copy-start.15 = (f32[2,4,256]{2,1,0:T(4,128)S(1)}, f32[2,4,256]{2,1,0:T(4,128)}, u32[]{:S(2)}) copy-start(f32[2,4,256]{2,1,0:T(4,128)} %param.15) | copy-start | bytes 24580
  7.3 8.2 %copy-start.13 = (f32[4,2,512]{2,1,0:T(2,128)S(1)}, f32[4,2,512]{2,1,0:T(2,128)}, u32[]{:S(2)}) copy-start(f32[4,2,512]{2,1,0:T(2,128)} %param.14) | copy-start | bytes 49156
  35.6 10.4 %copy-start.9 = (bf16[256,1536]{0,1:T(8,128)(2,1)}, bf16[256,1536]{0,1:T(8,128)(2,1)S(1)}, u32[]{:S(2)}) copy-start(bf16[256,1536]{0,1:T(8,128)(2,1)S(1)} %copy.112) | copy-start | bytes 2359300
  36.5 8.6 %collective-permute-start = (bf16[3,2,512]{2,0,1:T(4,128)(2,1)}, bf16[3,2,512]{2,0,1:T(4,128)(2,1)}, u32[]{:S(2)}, u32[]{:S(2)}) collective-permute-start(bf16[3,2,512]{2,0,1:T(4,128)(2,1)} %copy.140), channel_id=1, source_target_pairs={{0,4},{4,8},{8,12},{12,16},{16,20},{20,24},{24,28},{1,5},{5,9},{9,... | collective-permute-start | bytes 18440 | tf_op jit(solution)/shard_map/ppermute | solution.py:21
  47.3 2.2 copy-start.4
  47.3 1.2 copy-start.16
  47.4 1.2 copy-start.17
  48.5 15.1 %copy-start.7 = (f32[256,2,2,128]{3,0,2,1:T(8,128)}, f32[256,2,2,128]{3,0,2,1:T(8,128)S(1)}, u32[]{:S(2)}) copy-start(f32[256,2,2,128]{3,0,2,1:T(8,128)S(1)} %broadcast_in_dim.31) | copy-start | bytes 1572868
  53.5 2.8 %slice-start = ((f32[256,2,512]{2,0,1:T(8,128)}), f32[256,2,256]{2,0,1:T(8,128)S(1)}, s32[]{:S(2)}) async-start(f32[256,2,512]{2,0,1:T(8,128)} %copy-done.4), calls=%async_computation.5 | async-start | bytes 1048576 | tf_op jit(solution)/shard_map/slice | solution.py:109
  56.3 5.2 %copy-start.12 = (f32[4,4,64]{1,2,0:T(8,128)S(1)}, f32[4,4,64]{1,2,0:T(8,128)}, u32[]{:S(2)}) copy-start(f32[4,4,64]{1,2,0:T(8,128)} %copy.123) | copy-start | bytes 12292
  63.6 4.1 %copy-start.6 = (f32[4,4,64,128]{3,2,1,0:T(8,128)}, f32[4,4,64,128]{3,2,1,0:T(8,128)S(1)}, u32[]{:S(2)}) copy-start(f32[4,4,64,128]{3,2,1,0:T(8,128)S(1)} %fusion.45) | copy-start | bytes 1572868
  64.0 5.7 %copy-start.2 = (f32[4,4,64,128]{3,2,0,1:T(8,128)}, f32[4,4,64,128]{3,2,0,1:T(8,128)S(1)}, u32[]{:S(2)}) copy-start(f32[4,4,64,128]{3,2,0,1:T(8,128)S(1)} %get-tuple-element.301) | copy-start | bytes 1572868
  64.0 3.8 %copy-start.14 = (f32[4,4]{1,0:T(4,128)S(1)}, f32[4,4]{1,0:T(4,128)}, u32[]{:S(2)}) copy-start(f32[4,4]{1,0:T(4,128)} %exp.45) | copy-start | bytes 196
  64.9 4.8 %copy-start.5 = (f32[4,4,64,128]{3,2,1,0:T(8,128)}, f32[4,4,64,128]{3,2,1,0:T(8,128)S(1)}, u32[]{:S(2)}) copy-start(f32[4,4,64,128]{3,2,1,0:T(8,128)S(1)} %fusion.47) | copy-start | bytes 1572868
  69.7 15.4 %copy-start.18 = (f32[128]{0:T(128)S(1)}, f32[128]{0:T(128)}, u32[]{:S(2)}) copy-start(f32[128]{0:T(128)} %param.16) | copy-start | bytes 1540
  83.5 5.5 %copy-start.3 = (f32[4,4,64,128]{3,2,0,1:T(8,128)S(1)}, f32[4,4,64,128]{3,2,0,1:T(8,128)}, u32[]{:S(2)}) copy-start(f32[4,4,64,128]{3,2,0,1:T(8,128)} %copy-done.2) | copy-start | bytes 1572868
  84.2 98.2 %all-gather.10.cloned.1.call-start = ((), (), s32[]{:S(2)}) async-start(), calls=%async_computation.4 | async-start | bytes 2359296 | tf_op jit(solution)/shard_map/all_gather | solution.py:26
  84.9 164.1 %reduce-scatter.2.cloned.1.call-start = ((), (), s32[]{:S(2)}) async-start(), calls=%async_computation.2 | async-start | bytes 2621440 | tf_op jit(solution)/shard_map/reduce_scatter | solution.py:170
  86.9 4.9 %copy-start.8 = (f32[256,2,2,128]{3,0,2,1:T(8,128)S(1)}, f32[256,2,2,128]{3,0,2,1:T(8,128)}, u32[]{:S(2)}) copy-start(f32[256,2,2,128]{3,0,2,1:T(8,128)} %copy-done.7) | copy-start | bytes 1572868
  182.4 11.9 %copy-start.11 = (f32[4,4,64,128]{3,2,1,0:T(8,128)S(1)}, f32[4,4,64,128]{3,2,1,0:T(8,128)}, u32[]{:S(2)}) copy-start(f32[4,4,64,128]{3,2,1,0:T(8,128)} %custom-call.2) | copy-start | bytes 1572868
  215.7 1.1 copy-start.10
  (1 other events, 0.7 us)
Sparse Core Ops, SparseCore 0:
  8.9 19.4 all-gather.5
  84.3 48.0 all-gather.7
  134.6 47.7 all-gather.9
  219.1 29.8 reduce-scatter.1
where the time goes:
time: 259 us; the launch traced here: 257 us
  waiting for transfers between devices  132 us (51%)
  matrix products  67.7 us (26%)
  local copies, waits for them, and re-layouts  28.2 us (11%)
  between operations  13.6 us (5%)
  other arithmetic  10.5 us (4%)
  starting transfers between devices  4.08 us (2%)
    all_gather x2, waiting for transfers between devices, entering(): everything = jax.tree.map(lambda part: lax.all_gather(part, axis), shard)  88.8 us
    dot_general x48, matrix products, product(): return jnp.einsum(pattern, first, second, precision=HIGHEST_PREC)  59.8 us
    reduce_scatter x1, waiting for transfers between devices, local(): lax.psum_scatter(jnp.dot(normed, out_proj, preferred_element_type=jnp.flo...  30.1 us
    all_gather x1, waiting for transfers between devices, local(): lax.all_gather(layer_in, 'head', axis=0, tiled=True)  12.2 us
    unnamed x41, local copies, waits for them, and re-layouts  9.57 us
    dot_general x1, matrix products, local(): jnp.dot(lax.all_gather(layer_in, 'head', axis=0, tiled=True), weight_flat...  5.85 us
  transfers between devices with their start and end apart: 5, of which 4 were waited for; matrix products, arithmetic and copies ran while one was open for 9% of the time, Pallas kernels for 0%

commit v1 on v0

v1 whole, which is shorter than its diff:
```python
import functools

import jax
import jax.numpy as jnp
from jax import lax
from jax.experimental import pallas as pl
from jax.experimental.pallas import tpu as pltpu
from jax.sharding import PartitionSpec as P

DK = 128
DV = 128
KERNEL = 4
HALO = 16
HALF = 128
EPSILON = 1e-06
F32 = jnp.float32
BF16 = jnp.bfloat16
VMEM_BYTES = 40 * 1024 * 1024


def dot(a, b):
    return jnp.dot(a, b, preferred_element_type=F32)


def dot_t(a, b):
    return lax.dot_general(a, b, (((1,), (1,)), ((), ())), preferred_element_type=F32)


def silu(x):
    return x / (1.0 + jnp.exp(-x))


def l2_normed(x):
    return x * lax.rsqrt(jnp.sum(x * x, axis=-1, keepdims=True) + EPSILON)


def conv_silu(padded, slot, weight, lanes, rows):
    acc = padded[slot, HALO - KERNEL + 1 : HALO - KERNEL + 1 + rows, :] * weight[0:1, lanes]
    for i in range(1, KERNEL):
        lo = HALO - KERNEL + 1 + i
        acc = acc + padded[slot, lo : lo + rows, :] * weight[i : i + 1, lanes]
    return silu(acc)


def block_decay(ccol, crow, a, b):
    gap = ccol[a * HALF : (a + 1) * HALF] - crow[:, b * HALF : (b + 1) * HALF]
    return jnp.exp(jnp.minimum(gap, 0.0))


def keys_kernel(*refs, n_head, key_heads, ratio):
    pieces = refs[:n_head]
    halo, w, cw, cols, rows, s_out, y_out, k_out, x_out, padded = refs[n_head:]
    me = lax.axis_index("head")
    part = pieces[0].shape[0]
    toks = part * n_head
    blocks = toks // HALF
    heads = key_heads * ratio
    x_out[0:HALO, :] = halo[...]
    for s in range(n_head):
        at = pl.multiple_of(HALO + (me ^ s) * part, 16)
        x_out[pl.ds(at, part), :] = pieces[s][...]
    width = DK + ratio * DV
    for g in range(key_heads):
        proj = dot(x_out[...], w[:, g * width : (g + 1) * width])
        proj = proj.astype(BF16).astype(F32)
        for t in range(1 + ratio):
            padded[g * (1 + ratio) + t] = proj[:, t * 128 : (t + 1) * 128]
    ri = lax.broadcasted_iota(jnp.int32, (HALF, HALF), 0)
    ci = lax.broadcasted_iota(jnp.int32, (HALF, HALF), 1)
    below = ri > ci
    level = jnp.where(below, ri ^ ci, 0)
    eye = jnp.where(ri == ci, 1.0, 0.0).astype(F32)
    kts, rhs, lowers, offs = [], [], [], []
    for g in range(key_heads):
        base = g * (1 + ratio)
        k = l2_normed(conv_silu(padded, base, cw, slice(base * 128, base * 128 + 128), toks))
        kb = k.astype(BF16)
        k_out[g] = kb
        kf = kb.astype(F32)
        kts.append(kf.T)
        ks = [kb[b * HALF : (b + 1) * HALF] for b in range(blocks)]
        grams = {(a, b): dot_t(ks[a], ks[b]) for a in range(blocks) for b in range(a + 1)}
        for r in range(ratio):
            j = g * ratio + r
            lanes = slice((base + 1 + r) * 128, (base + 2 + r) * 128)
            v = conv_silu(padded, base + 1 + r, cw, lanes, toks)
            ccol = cols[:, j : j + 1]
            bcol = cols[:, heads + j : heads + j + 1]
            crow = rows[j : j + 1, :]
            rk = (kf * (bcol * jnp.exp(ccol))).astype(BF16)
            rv = (v * bcol).astype(BF16)
            rhs.append(jnp.concatenate([rk, rv], axis=1))
            low, off = [], {}
            for a in range(blocks):
                ba = bcol[a * HALF : (a + 1) * HALF]
                for b in range(a + 1):
                    m = ba * grams[(a, b)] * block_decay(ccol, crow, a, b)
                    if a == b:
                        low.append(jnp.where(below, m, 0.0))
                    else:
                        off[(a, b)] = m.astype(BF16)
            lowers += low
            offs.append(off)
    inv = [eye - jnp.where(level == 1, m, 0.0) for m in lowers]
    size = 2
    while size < HALF:
        here = (level >= size) & (level < 2 * size)
        inv_b = [m.astype(BF16) for m in inv]
        cx = [dot(jnp.where(here, m, 0.0).astype(BF16), x).astype(BF16) for m, x in zip(lowers, inv_b)]
        inv = [x - dot(xb, c) for x, xb, c in zip(inv, inv_b, cx)]
        size *= 2
    inv_b = [m.astype(BF16) for m in inv]
    for j in range(heads):
        ys = []
        for a in range(blocks):
            r = rhs[j][a * HALF : (a + 1) * HALF]
            if a:
                acc = r.astype(F32)
                for b in range(a):
                    acc = acc - dot(offs[j][(a, b)], ys[b])
                r = acc.astype(BF16)
            ys.append(dot(inv_b[j * blocks + a], r).astype(BF16))
        y = jnp.concatenate(ys, axis=0)
        y_out[j] = y
        crow = rows[j : j + 1, :]
        last = crow[:, toks - 1 : toks]
        kd = (kts[j // ratio] * jnp.exp(last - crow)).astype(BF16)
        s = dot(kd, y)
        s_out[j, :, 0:DK] = (eye * jnp.exp(last) - s[:, 0:DK]).astype(BF16)
        s_out[j, :, DK:] = s[:, DK:].astype(BF16)


def queries_kernel(x, w, cw, cols, rows, keys, ys, gain, q_out, o_out, g_out, padded, *, key_heads, ratio):
    toks = x.shape[0] - HALO
    blocks = toks // HALF
    width = DK + ratio * DV
    ri = lax.broadcasted_iota(jnp.int32, (HALF, HALF), 0)
    ci = lax.broadcasted_iota(jnp.int32, (HALF, HALF), 1)
    upto = ri >= ci
    for g in range(key_heads):
        proj = dot(x[...], w[:, g * width : (g + 1) * width]).astype(BF16).astype(F32)
        padded[g] = proj[:, 0:DK]
        for r in range(ratio):
            z = proj[HALO:, DK + r * DV : DK + (r + 1) * DV]
            g_out[g * ratio + r] = gain[...] * silu(z)
    for g in range(key_heads):
        q = l2_normed(conv_silu(padded, g, cw, slice(g * 128, g * 128 + 128), toks)) * DK ** (-0.5)
        qb = q.astype(BF16)
        kb = keys[g]
        grams = {
            (a, b): dot_t(qb[a * HALF : (a + 1) * HALF], kb[b * HALF : (b + 1) * HALF])
            for a in range(blocks)
            for b in range(a + 1)
        }
        for r in range(ratio):
            j = g * ratio + r
            ccol = cols[:, j : j + 1]
            crow = rows[j : j + 1, :]
            for a in range(blocks):
                at = slice(a * HALF, (a + 1) * HALF)
                acc = None
                for b in range(a + 1):
                    m = grams[(a, b)] * block_decay(ccol, crow, a, b)
                    if a == b:
                        m = jnp.where(upto, m, 0.0)
                    term = dot(m.astype(BF16), ys[j, b * HALF : (b + 1) * HALF, :])
                    acc = term if acc is None else acc + term
                q_out[j, at, :] = (q[at] * jnp.exp(ccol[at]) - acc[:, 0:DK]).astype(BF16)
                o_out[j, at, :] = acc[:, DK:]


def pair_kernel(own, got, b_out, t_out):
    odd = lax.axis_index("ctx") % 2 == 1
    for j in range(own.shape[0]):
        mine, other = own[j], got[j]
        later = jnp.where(odd, mine, other)
        earlier = jnp.where(odd, other, mine)
        prod = dot(later[:, 0:DK], earlier)
        t_out[j] = prod[:, 0:DK].astype(BF16)
        b_out[j] = (prod[:, DK:] + later[:, DK:].astype(F32)).astype(BF16)


def pair_absorb_kernel(q, o, got, q_out, o_out):
    odd = lax.axis_index("ctx") % 2 == 1
    for j in range(q.shape[0]):
        prod = dot(q[j], got[j])
        q_out[j] = jnp.where(odd, prod[:, 0:DK], q[j].astype(F32)).astype(BF16)
        o_out[j] = o[j] + jnp.where(odd, prod[:, DK:], 0.0)


def absorb_kernel(q, o, jb, jt, q_out, o_out):
    for j in range(q.shape[0]):
        o_out[j] = o[j] + dot(q[j], jb[j])
        q_out[j] = dot(q[j], jt[j]).astype(BF16)


def join_b_kernel(t, b, jb, b_out):
    for j in range(t.shape[0]):
        b_out[j] = (dot(t[j], jb[j]) + b[j].astype(F32)).astype(BF16)


def join_t_kernel(t, jt, t_out):
    for j in range(t.shape[0]):
        t_out[j] = dot(t[j], jt[j]).astype(BF16)


def normed_kernel(q, o, jb, gate, keep, send, scratch, *, n_head):
    me = lax.axis_index("head")
    for j in range(q.shape[0]):
        att = o[j] + dot(q[j], jb[j])
        scale = lax.rsqrt(jnp.mean(att * att, axis=-1, keepdims=True) + EPSILON)
        scratch[:, j * DV : (j + 1) * DV] = (att * scale * gate[j]).astype(BF16)
    part = scratch.shape[0] // n_head
    for i in range(n_head // 2):
        at = pl.multiple_of((me ^ (2 * i)) * part, 16)
        keep[i * part : (i + 1) * part, :] = scratch[pl.ds(at, part), :]
        at = pl.multiple_of((me ^ (2 * i + 1)) * part, 16)
        send[i * part : (i + 1) * part, :] = scratch[pl.ds(at, part), :]


def out_kernel(own, got, w_own, w_got, out, *, first, part):
    rows = slice(first * part, (first + 1) * part)
    a, b = own[rows, :], got[rows, :]
    out[...] = (dot(a, w_own[...]) + dot(b, w_got[...])).astype(out.dtype)


def call(body, out_shape, args, scratch=(), flops=0, **static):
    nbytes = sum(a.size * a.dtype.itemsize for a in args)
    vmem = pl.BlockSpec(memory_space=pltpu.VMEM)
    return pl.pallas_call(
        functools.partial(body, **static),
        out_shape=out_shape,
        in_specs=[vmem] * len(args),
        out_specs=jax.tree.map(lambda _: vmem, out_shape),
        scratch_shapes=list(scratch),
        compiler_params=pltpu.CompilerParams(vmem_limit_bytes=VMEM_BYTES),
        cost_estimate=pl.CostEstimate(flops=flops, bytes_accessed=nbytes, transcendentals=0),
    )(*args)


def shaped(shape, dtype):
    return jax.ShapeDtypeStruct(shape, dtype)


def xor_sent(value, axis, step):
    count = lax.axis_size(axis)
    return lax.ppermute(value, axis, [(i, i ^ step) for i in range(count)])


def passed_along(value, axis, steps):
    count = lax.axis_size(axis)
    return lax.ppermute(value, axis, [(i, i + steps) for i in range(count - steps)])


def local(layer_in, in_proj, conv_weight, gate_logits, norm_gain, out_proj):
    n_head, n_ctx = lax.axis_size("head"), lax.axis_size("ctx")
    width, key_heads, group = in_proj.shape
    heads = gate_logits.shape[1]
    ratio = heads // key_heads
    part = layer_in.shape[0]
    toks = part * n_head
    ctx_head = ("ctx", "head")

    pieces = [layer_in] + [None] * (n_head - 1)
    step = n_head // 2
    while step:
        for s in range(0, n_head, 2 * step):
            pieces[s + step] = xor_sent(pieces[s], "head", step)
        step //= 2
    tail = layer_in[part - HALO :]
    halo = None
    for h in range(n_head):
        perm = [((c - 1) * n_head + n_head - 1, c * n_head + h) for c in range(1, n_ctx)]
        got = lax.ppermute(tail, ctx_head, perm)
        halo = got if halo is None else halo + got

    def columns(w, spans):
        return jnp.concatenate([w[:, g, a:b] for g in range(key_heads) for a, b in spans], axis=1)

    kv_span = [(DK, 2 * DK + ratio * DV)]
    qz_span = [(0, DK), (2 * DK + ratio * DV, 2 * DK + 2 * ratio * DV)]
    w_kv = columns(in_proj, kv_span)
    w_qz = columns(in_proj, qz_span)
    c_kv = columns(conv_weight, kv_span)
    c_q = columns(conv_weight, [(0, DK)])
    cum = jnp.cumsum(-jax.nn.softplus(gate_logits[0]), axis=-1)
    beta = jax.nn.sigmoid(gate_logits[1])
    rows = cum
    cols = jnp.concatenate([cum, beta], axis=0).T
    w_other = xor_sent(out_proj, "head", 1)

    state = shaped((heads, DK, DV), BF16)
    s_own, ys, keys, x_full = call(
        keys_kernel,
        (
            shaped((heads, DK, DK + DV), BF16),
            shaped((heads, toks, DK + DV), BF16),
            shaped((key_heads, toks, DK), BF16),
            shaped((HALO + toks, width), BF16),
        ),
        [*pieces, halo, w_kv, c_kv, cols, rows],
        [pltpu.VMEM((key_heads * (1 + ratio), HALO + toks, 128), F32)],
        flops=2 * toks * width * group,
        n_head=n_head,
        key_heads=key_heads,
        ratio=ratio,
    )
    got = xor_sent(s_own, "ctx", 1)
    q_shape = shaped((heads, toks, DK), BF16)
    o_shape = shaped((heads, toks, DV), F32)
    q, o, gate = call(
        queries_kernel,
        (q_shape, o_shape, o_shape),
        [x_full, w_qz, c_q, cols, rows, keys, ys, norm_gain[None, :]],
        [pltpu.VMEM((key_heads, HALO + toks, 128), F32)],
        flops=2 * toks * width * group,
        key_heads=key_heads,
        ratio=ratio,
    )
    b, t = call(pair_kernel, (state, state), [s_own, got], flops=heads * 2**23)
    step = 2
    jb = passed_along(b, "ctx", step)
    jt = passed_along(t, "ctx", step)
    q, o = call(pair_absorb_kernel, (q_shape, o_shape), [q, o, got], flops=heads * 2**24)
    while 2 * step < n_ctx:
        b = call(join_b_kernel, state, [t, b, jb], flops=heads * 2**22)
        step *= 2
        more = 2 * step < n_ctx
        if more:
            t = call(join_t_kernel, state, [t, jt], flops=heads * 2**22)
        nb = passed_along(b, "ctx", step)
        nt = passed_along(t, "ctx", step) if more else None
        q, o = call(absorb_kernel, (q_shape, o_shape), [q, o, jb, jt], flops=heads * 2**24)
        jb, jt = nb, nt
    half = shaped((toks // 2, heads * DV), BF16)
    keep, send = call(
        normed_kernel,
        (half, half),
        [q, o, jb, gate],
        [pltpu.VMEM((toks, heads * DV), BF16)],
        flops=heads * 2**23,
        n_head=n_head,
    )
    other = xor_sent(send, "head", 1)
    out_args = [keep, other, out_proj, w_other]
    out = None
    partial = {}
    for i in reversed(range(n_head // 2)):
        dtype = F32 if i == 0 else BF16
        partial[i] = call(
            out_kernel, shaped((part, width), dtype), out_args, flops=part * width * 2**12, first=i, part=part
        )
        if i:
            partial[i] = xor_sent(partial[i], "head", 2 * i)
    for i in range(n_head // 2):
        out = partial[i].astype(F32) if out is None else out + partial[i].astype(F32)
    return out.astype(BF16)


def solution(mesh):
    in_specs = (
        P(("ctx", "head"), None),
        P(None, "head", None),
        P(None, "head", None),
        P(None, "head", "ctx"),
        P(),
        P("head", None),
    )
    out_specs = P(("ctx", "head"), None)
    return jax.shard_map(local, mesh=mesh, in_specs=in_specs, out_specs=out_specs, check_vma=False)
```

time: 259 us -> 88.2 us (0.34)
  waiting for transfers between devices: 132 us -> 12.6 us
  matrix products: 67.7 us -> 0 us
  starting transfers between devices: 4.08 us -> 28.2 us
  Pallas kernels: 0 us -> 14.1 us
  between operations: 13.6 us -> 0.31 us
  other arithmetic: 10.5 us -> 4.45 us
    all_gather x3 -> x0, waiting for transfers between devices: 101 us -> none  [the longest x2 88.8 us: entering(): everything = jax.tree.map(lambda part: lax.all_gather(part, axis), shard)]
    dot_general x50 -> x0, matrix products: 67.7 us -> none  [the longest x48 59.8 us: product(): return jnp.einsum(pattern, first, second, precision=HIGHEST_PREC)]
    reduce_scatter x1 -> x0, waiting for transfers between devices: 30.1 us -> none  [local(): lax.psum_scatter(jnp.dot(normed, out_proj, preferred_element_type=jnp.flo...]
    ppermute x1 -> x14, starting transfers between devices: 3.96 us -> 28.2 us  [the longest x7 12.6 us: xor_sent(): return lax.ppermute(value, axis, [(i, i ^ step) for i in range(count)])]
    slice x7 -> x8, local copies, waits for them, and re-layouts: 3.34 us -> 18.5 us  [the longest x5 16.7 us: columns(): w[:, g, a:b]]
    pallas_call x0 -> x9, Pallas kernels: none -> 14.1 us  [call(): pl.pallas_call(functools.partial(body, **static), out_shape=out_shape, in...]
    ppermute x1 -> x14, waiting for transfers between devices: 0.01 us -> 12.6 us  [the longest x7 12.6 us: xor_sent(): return lax.ppermute(value, axis, [(i, i ^ step) for i in range(count)])]
    unnamed x41 -> x33, local copies, waits for them, and re-layouts: 9.57 us -> 2.23 us
  transfers between devices with their start and end apart: 5 -> 14, of which waited for: 4 -> 5; matrix products, arithmetic and copies ran while one was open for 9% -> 31% of each run, Pallas kernels for 0% -> 14%
where the time goes in v1:
time: 88.2 us; the launch traced here: 86.7 us
  starting transfers between devices  28.2 us (32%)
  local copies, waits for them, and re-layouts  27 us (31%)
  Pallas kernels  14.1 us (16%)
  waiting for transfers between devices  12.6 us (14%)
  other arithmetic  4.45 us (5%)
    slice x5, local copies, waits for them, and re-layouts, columns(): w[:, g, a:b]  16.7 us
    pallas_call x9, Pallas kernels, call(): pl.pallas_call(functools.partial(body, **static), out_shape=out_shape, in...  14.1 us
    ppermute x7, starting transfers between devices, xor_sent(): return lax.ppermute(value, axis, [(i, i ^ step) for i in range(count)])  12.6 us
    ppermute x7, waiting for transfers between devices, xor_sent(): return lax.ppermute(value, axis, [(i, i ^ step) for i in range(count)])  12.6 us
    ppermute x3, starting transfers between devices, passed_along(): lax.ppermute(value, axis, [(i, i + steps) for i in range(count - steps)])  10.7 us
    squeeze x4, local copies, waits for them, and re-layouts, columns(): w[:, g, a:b]  6.03 us
    ppermute x4, starting transfers between devices, local(): got = lax.ppermute(tail, ctx_head, perm)  4.79 us
    unnamed x33, local copies, waits for them, and re-layouts  2.23 us
  transfers between devices with their start and end apart: 14, of which 5 were waited for; matrix products, arithmetic and copies ran while one was open for 31% of the time, Pallas kernels for 14%

profile of v1, /device:TPU:0, one launch (start us, length us, event | category | flops | bytes accessed | tf_op | source)
XLA Modules:
  0.0 86.7 jit_solution(15493876382627868137)
XLA Ops:
  0.0 1.6 %slice.45 = bf16[16,2048]{1,0:T(8,128)(2,1)} slice(bf16[64,2048]{1,0:T(8,128)(2,1)} %refs_0_.1), slice={[48:64], [0:2048]} | slice | bytes 131072 | tf_op jit(solution)/shard_map/slice | solution.py:270
  1.6 1.4 %collective-permute-start.3 = (bf16[16,2048]{1,0:T(8,128)(2,1)}, bf16[16,2048]{1,0:T(8,128)(2,1)}, u32[]{:S(2)}, u32[]{:S(2)}) collective-permute-start(bf16[16,2048]{1,0:T(8,128)(2,1)} %slice.45), channel_id=1, source_target_pairs={{3,4},{7,8},{11,12},{15,16},{19,20},{23,24},{27,28}} | collective-permute-start | bytes 196616 | tf_op jit(solution)/shard_map/ppermute | solution.py:274
  3.0 1.3 %collective-permute-start.4 = (bf16[16,2048]{1,0:T(8,128)(2,1)}, bf16[16,2048]{1,0:T(8,128)(2,1)}, u32[]{:S(2)}, u32[]{:S(2)}) collective-permute-start(bf16[16,2048]{1,0:T(8,128)(2,1)} %slice.45), channel_id=1, source_target_pairs={{3,5},{7,9},{11,13},{15,17},{19,21},{23,25},{27,29}} | collective-permute-start | bytes 196616 | tf_op jit(solution)/shard_map/ppermute | solution.py:274
  4.3 1.3 %collective-permute-start.5 = (bf16[16,2048]{1,0:T(8,128)(2,1)}, bf16[16,2048]{1,0:T(8,128)(2,1)}, u32[]{:S(2)}, u32[]{:S(2)}) collective-permute-start(bf16[16,2048]{1,0:T(8,128)(2,1)} %slice.45), channel_id=1, source_target_pairs={{3,6},{7,10},{11,14},{15,18},{19,22},{23,26},{27,30}} | collective-permute-start | bytes 196616 | tf_op jit(solution)/shard_map/ppermute | solution.py:274
  5.6 3.0 %collective-permute-start.1 = (bf16[64,2048]{1,0:T(8,128)(2,1)}, bf16[64,2048]{1,0:T(8,128)(2,1)}, u32[]{:S(2)}, u32[]{:S(2)}) collective-permute-start(bf16[64,2048]{1,0:T(8,128)(2,1)} %refs_0_.1), channel_id=1, source_target_pairs={{0,2},{1,3},{2,0},{3,1},{4,6},{5,7},{6,4},{7,5},{8,10},{9,11},{10,... | collective-permute-start | bytes 786440 | tf_op jit(solution)/shard_map/ppermute | solution.py:247
  8.6 3.8 %collective-permute-start.12 = (bf16[512,2048]{1,0:T(8,128)(2,1)}, bf16[512,2048]{1,0:T(8,128)(2,1)}, u32[]{:S(2)}, u32[]{:S(2)}) collective-permute-start(bf16[512,2048]{1,0:T(8,128)(2,1)} %w_own.3), channel_id=1, source_target_pairs={{0,1},{1,0},{2,3},{3,2},{4,5},{5,4},{6,7},{7,6},{8,9},{9,8},{10,11... | collective-permute-start | bytes 6291464 | tf_op jit(solution)/shard_map/ppermute | solution.py:247
  12.4 8.7 %fusion.3 = (bf16[2048,1,384]{2,1,0:T(2,128)(2,1)S(1)}, bf16[2048,1,384]{2,1,0:T(2,128)(2,1)}) fusion(bf16[2048,2,768]{2,1,0:T(2,128)(2,1)} %param.7), kind=kLoop, calls=%fused_computation.22 | loop fusion | bytes 6291456 | tf_op jit(solution)/shard_map/slice | solution.py:278
  21.0 4.2 %fusion.2 = (bf16[2048,1,256]{2,1,0:T(2,128)(2,1)}, bf16[2048,1,256]{2,1,0:T(2,128)(2,1)}) fusion(bf16[2048,2,768]{2,1,0:T(2,128)(2,1)S(1)} %bitcast.38), kind=kLoop, calls=%fused_computation.21 | loop fusion | bytes 4194304 | tf_op jit(solution)/shard_map/slice | solution.py:278
  25.3 2.5 %fusion.1 = (bf16[2048,1,128]{2,1,0:T(2,128)(2,1)}, bf16[2048,1,128]{2,1,0:T(2,128)(2,1)}) fusion(bf16[2048,2,768]{2,1,0:T(2,128)(2,1)S(1)} %bitcast.38), kind=kLoop, calls=%fused_computation.20 | loop fusion | bytes 2097152 | tf_op jit(solution)/shard_map/slice | solution.py:278
  28.4 2.5 %copy_bitcast_fusion = (bf16[2048,384]{1,0:T(8,128)(2,1)S(1)}, bf16[2048,384]{1,0:T(8,128)(2,1)S(1)}) fusion(bf16[2048,1,384]{2,1,0:T(2,128)(2,1)} %get-tuple-element.40, bf16[2048,1,384]{2,1,0:T(2,128)(2,1)S(1)} %get-tuple-element.39), kind=kLoop, calls=%fused_computation.2 | loop fusion | bytes 6291456 | tf_op jit(solution)/shard_map/squeeze | solution.py:278
  31.1 1.3 %copy-done.3 = bf16[2048,1,256]{2,1,0:T(2,128)(2,1)S(1)} copy-done((bf16[2048,1,256]{2,1,0:T(2,128)(2,1)S(1)}, bf16[2048,1,256]{2,1,0:T(2,128)(2,1)}, u32[]{:S(2)}) %copy-start.3) | copy-done | bytes 1048600
  33.1 1.8 %copy_bitcast_fusion.2 = (bf16[2048,256]{1,0:T(8,128)(2,1)}, bf16[2048,256]{1,0:T(8,128)(2,1)}) fusion(bf16[2048,1,256]{2,1,0:T(2,128)(2,1)S(1)} %copy-done.4, bf16[2048,1,256]{2,1,0:T(2,128)(2,1)S(1)} %copy-done.3), kind=kLoop, calls=%fused_computation.4 | loop fusion | bytes 4194304 | tf_op jit(solution)/shard_map/squeeze | solution.py:278
  42.5 6.0 %shard_map.64 = (bf16[4,128,256]{2,1,0:T(8,128)(2,1)S(1)}, bf16[4,256,256]{2,1,0:T(8,128)(2,1)S(1)}, bf16[2,256,128]{2,1,0:T(8,128)(2,1)S(1)}, bf16[272,2048]{1,0:T(8,128)(2,1)S(1)}) custom-call(bf16[64,2048]{1,0:T(8,128)(2,1)S(1)} %copy-done.1, bf16[64,2048]{1,0:T(8,128)(2,1)S(1)} %collective-permute-done.refs_1_, ...), custom_call_target="tpu_custom_call" | custom-call | flops 805306368 | bytes 4284416 | tf_op jit(solution)/shard_map/pallas_call | solution.py:230
  48.5 1.6 %collective-permute-start.7 = (bf16[4,128,256]{2,1,0:T(8,128)(2,1)S(1)}, bf16[4,128,256]{2,1,0:T(8,128)(2,1)S(1)}, u32[]{:S(2)}, u32[]{:S(2)}) collective-permute-start(bf16[4,128,256]{2,1,0:T(8,128)(2,1)S(1)} %get-tuple-element.25.own), channel_id=1, source_target_pairs={{0,4},{4,0},{8,12},{12,8},{16,20},{20,16},{24,28},{28,24},{1,5},{5... | collective-permute-start | bytes 786440 | tf_op jit(solution)/shard_map/ppermute | solution.py:247
  50.5 6.4 %collective-permute-done.7.got = bf16[4,128,256]{2,1,0:T(8,128)(2,1)S(1)} collective-permute-done((bf16[4,128,256]{2,1,0:T(8,128)(2,1)S(1)}, bf16[4,128,256]{2,1,0:T(8,128)(2,1)S(1)}, u32[]{:S(2)}, u32[]{:S(2)}) %collective-permute-start.7) | collective-permute-done | bytes 262176 | tf_op jit(solution)/shard_map/ppermute | solution.py:247
  57.1 3.5 %collective-permute-start.8 = (bf16[4,128,128]{2,1,0:T(8,128)(2,1)S(1)}, bf16[4,128,128]{2,1,0:T(8,128)(2,1)S(1)}, u32[]{:S(2)}, u32[]{:S(2)}) collective-permute-start(bf16[4,128,128]{2,1,0:T(8,128)(2,1)S(1)} %get-tuple-element.28.b), channel_id=1, source_target_pairs={{0,8},{4,12},{8,16},{12,20},{16,24},{20,28},{1,9},{5,13},{9,17},{1... | collective-permute-start | bytes 393224 | tf_op jit(solution)/shard_map/ppermute | solution.py:252
  61.4 3.5 %collective-permute-start.9 = (bf16[4,128,128]{2,1,0:T(8,128)(2,1)S(1)}, bf16[4,128,128]{2,1,0:T(8,128)(2,1)S(1)}, u32[]{:S(2)}, u32[]{:S(2)}) collective-permute-start(bf16[4,128,128]{2,1,0:T(8,128)(2,1)S(1)} %get-tuple-element.29.t), channel_id=1, source_target_pairs={{0,8},{4,12},{8,16},{12,20},{16,24},{20,28},{1,9},{5,13},{9,17},{1... | collective-permute-start | bytes 393224 | tf_op jit(solution)/shard_map/ppermute | solution.py:252
  65.1 3.8 %collective-permute-start.10 = (bf16[4,128,128]{2,1,0:T(8,128)(2,1)S(1)}, bf16[4,128,128]{2,1,0:T(8,128)(2,1)S(1)}, u32[]{:S(2)}, u32[]{:S(2)}) collective-permute-start(bf16[4,128,128]{2,1,0:T(8,128)(2,1)S(1)} %shard_map.69), channel_id=1, source_target_pairs={{0,16},{4,20},{8,24},{12,28},{1,17},{5,21},{9,25},{13,29},{2,18},{... | collective-permute-start | bytes 393224 | tf_op jit(solution)/shard_map/ppermute | solution.py:252
  68.9 1.9 %shard_map.65 = (bf16[4,256,128]{2,1,0:T(8,128)(2,1)S(1)}, f32[4,256,128]{2,1,0:T(8,128)S(1)}, f32[4,256,128]{2,1,0:T(8,128)S(1)}) custom-call(bf16[272,2048]{1,0:T(8,128)(2,1)S(1)} %get-tuple-element.20.x, bf16[2048,768]{1,0:T(8,128)(2,1)S(1)} %pad_maximum_fusion.1.w, f32[4,256]{1,0:T(4,128)S(1)} %pad_maximum_fusion.3.cw, f32[256,8]{1,0:T(8,128)S(1)} %copy.13.refs_7_.cols, ...), custom_call_target="tpu_custom_call" | custom-call | flops 805306368 | bytes 4932096 | tf_op jit(solution)/shard_map/pallas_call | solution.py:230
  72.0 1.3 %collective-permute-done.11.got = bf16[128,512]{1,0:T(8,128)(2,1)S(1)} collective-permute-done((bf16[128,512]{1,0:T(8,128)(2,1)S(1)}, bf16[128,512]{1,0:T(8,128)(2,1)S(1)}, u32[]{:S(2)}, u32[]{:S(2)}) %collective-permute-start.11) | collective-permute-done | bytes 131104 | tf_op jit(solution)/shard_map/ppermute | solution.py:247
  73.3 2.4 %shard_map.72 = bf16[64,2048]{1,0:T(8,128)(2,1)S(1)} custom-call(bf16[128,512]{1,0:T(8,128)(2,1)S(1)} %get-tuple-element.33.own, bf16[128,512]{1,0:T(8,128)(2,1)S(1)} %collective-permute-done.11.got, bf16[512,2048]{1,0:T(8,128)(2,1)S(1)} %copy-done, bf16[512,2048]{1,0:T(8,128)(2,1)} %collective-permute-done.12.w_got), custom_call_target="tpu_custom_call" | custom-call | flops 536870912 | bytes 4456448 | tf_op jit(solution)/shard_map/pallas_call | solution.py:230
  75.7 3.6 %collective-permute-start.13 = (bf16[64,2048]{1,0:T(8,128)(2,1)S(1)}, bf16[64,2048]{1,0:T(8,128)(2,1)S(1)}, u32[]{:S(2)}, u32[]{:S(2)}) collective-permute-start(bf16[64,2048]{1,0:T(8,128)(2,1)S(1)} %shard_map.72), channel_id=1, source_target_pairs={{0,2},{1,3},{2,0},{3,1},{4,6},{5,7},{6,4},{7,5},{8,10},{9,11},{10,... | collective-permute-start | bytes 786440 | tf_op jit(solution)/shard_map/ppermute | solution.py:247
  79.4 2.4 %shard_map.71 = f32[64,2048]{1,0:T(8,128)S(1)} custom-call(bf16[128,512]{1,0:T(8,128)(2,1)S(1)} %get-tuple-element.33.own, bf16[128,512]{1,0:T(8,128)(2,1)S(1)} %collective-permute-done.11.got, bf16[512,2048]{1,0:T(8,128)(2,1)S(1)} %copy-done, bf16[512,2048]{1,0:T(8,128)(2,1)} %collective-permute-done.12.w_got), custom_call_target="tpu_custom_call" | custom-call | flops 536870912 | bytes 4456448 | tf_op jit(solution)/shard_map/pallas_call | solution.py:230
  81.8 4.2 %collective-permute-done.13 = bf16[64,2048]{1,0:T(8,128)(2,1)S(1)} collective-permute-done((bf16[64,2048]{1,0:T(8,128)(2,1)S(1)}, bf16[64,2048]{1,0:T(8,128)(2,1)S(1)}, u32[]{:S(2)}, u32[]{:S(2)}) %collective-permute-start.13) | collective-permute-done | bytes 262176 | tf_op jit(solution)/shard_map/ppermute | solution.py:247
  (75 shorter events, 12.4 us)
Async XLA Ops:
  0.0 21.0 %slice-start = ((s8[6291456]{0:T(1024)(128)(4,1)}), s8[4194304]{0:T(1024)(128)(4,1)S(1)}, s32[]{:S(2)}) async-start(s8[6291456]{0:T(1024)(128)(4,1)} %bitcast.37), calls=%async_computation | async-start | bytes 8388608
  1.6 19.4 %slice-start.1 = ((s8[6291456]{0:T(1024)(128)(4,1)}), s8[2097152]{0:T(1024)(128)(4,1)S(1)}, s32[]{:S(2)}) async-start(s8[6291456]{0:T(1024)(128)(4,1)} %bitcast.37), calls=%async_computation.1 | async-start | bytes 4194304
  1.6 37.1 %collective-permute-start.3 = (bf16[16,2048]{1,0:T(8,128)(2,1)}, bf16[16,2048]{1,0:T(8,128)(2,1)}, u32[]{:S(2)}, u32[]{:S(2)}) collective-permute-start(bf16[16,2048]{1,0:T(8,128)(2,1)} %slice.45), channel_id=1, source_target_pairs={{3,4},{7,8},{11,12},{15,16},{19,20},{23,24},{27,28}} | collective-permute-start | bytes 196616 | tf_op jit(solution)/shard_map/ppermute | solution.py:274
  3.0 37.3 %collective-permute-start.4 = (bf16[16,2048]{1,0:T(8,128)(2,1)}, bf16[16,2048]{1,0:T(8,128)(2,1)}, u32[]{:S(2)}, u32[]{:S(2)}) collective-permute-start(bf16[16,2048]{1,0:T(8,128)(2,1)} %slice.45), channel_id=1, source_target_pairs={{3,5},{7,9},{11,13},{15,17},{19,21},{23,25},{27,29}} | collective-permute-start | bytes 196616 | tf_op jit(solution)/shard_map/ppermute | solution.py:274
  4.3 36.6 %collective-permute-start.5 = (bf16[16,2048]{1,0:T(8,128)(2,1)}, bf16[16,2048]{1,0:T(8,128)(2,1)}, u32[]{:S(2)}, u32[]{:S(2)}) collective-permute-start(bf16[16,2048]{1,0:T(8,128)(2,1)} %slice.45), channel_id=1, source_target_pairs={{3,6},{7,10},{11,14},{15,18},{19,22},{23,26},{27,30}} | collective-permute-start | bytes 196616 | tf_op jit(solution)/shard_map/ppermute | solution.py:274
  5.6 34.8 %collective-permute-start.1 = (bf16[64,2048]{1,0:T(8,128)(2,1)}, bf16[64,2048]{1,0:T(8,128)(2,1)}, u32[]{:S(2)}, u32[]{:S(2)}) collective-permute-start(bf16[64,2048]{1,0:T(8,128)(2,1)} %refs_0_.1), channel_id=1, source_target_pairs={{0,2},{1,3},{2,0},{3,1},{4,6},{5,7},{6,4},{7,5},{8,10},{9,11},{10,... | collective-permute-start | bytes 786440 | tf_op jit(solution)/shard_map/ppermute | solution.py:247
  8.6 64.7 %collective-permute-start.12 = (bf16[512,2048]{1,0:T(8,128)(2,1)}, bf16[512,2048]{1,0:T(8,128)(2,1)}, u32[]{:S(2)}, u32[]{:S(2)}) collective-permute-start(bf16[512,2048]{1,0:T(8,128)(2,1)} %w_own.3), channel_id=1, source_target_pairs={{0,1},{1,0},{2,3},{3,2},{4,5},{5,4},{6,7},{7,6},{8,9},{9,8},{10,11... | collective-permute-start | bytes 6291464 | tf_op jit(solution)/shard_map/ppermute | solution.py:247
  34.9 2.9 %copy-start.11 = (f32[4,1,384]{2,1,0:T(1,128)S(1)}, f32[4,1,384]{2,1,0:T(1,128)}, u32[]{:S(2)}) copy-start(f32[4,1,384]{2,1,0:T(1,128)} %get-tuple-element.44) | copy-start | bytes 18436
  34.9 5.4 %copy-start.1 = (bf16[64,2048]{1,0:T(8,128)(2,1)S(1)}, bf16[64,2048]{1,0:T(8,128)(2,1)}, u32[]{:S(2)}) copy-start(bf16[64,2048]{1,0:T(8,128)(2,1)} %refs_0_.1) | copy-start | bytes 786436
  38.6 11.5 %copy-start.7 = (bf16[2048,256]{1,0:T(8,128)(2,1)S(1)}, bf16[2048,256]{1,0:T(8,128)(2,1)}, u32[]{:S(2)}) copy-start(bf16[2048,256]{1,0:T(8,128)(2,1)} %get-tuple-element.51) | copy-start | bytes 3145732
  38.7 11.5 %copy-start.8 = (bf16[2048,256]{1,0:T(8,128)(2,1)S(1)}, bf16[2048,256]{1,0:T(8,128)(2,1)}, u32[]{:S(2)}) copy-start(bf16[2048,256]{1,0:T(8,128)(2,1)} %get-tuple-element.52) | copy-start | bytes 3145732
  38.7 11.5 %copy-start.9 = (bf16[2048,128]{1,0:T(8,128)(2,1)S(1)}, bf16[2048,128]{1,0:T(8,128)(2,1)}, u32[]{:S(2)}) copy-start(bf16[2048,128]{1,0:T(8,128)(2,1)} %get-tuple-element.53) | copy-start | bytes 1572868
  38.7 11.4 %copy-start.10 = (bf16[2048,128]{1,0:T(8,128)(2,1)S(1)}, bf16[2048,128]{1,0:T(8,128)(2,1)}, u32[]{:S(2)}) copy-start(bf16[2048,128]{1,0:T(8,128)(2,1)} %get-tuple-element.54) | copy-start | bytes 1572868
  38.7 2.2 %collective-permute-start.6 = (bf16[16,2048]{1,0:T(8,128)(2,1)}, bf16[16,2048]{1,0:T(8,128)(2,1)S(1)}, u32[]{:S(2)}, u32[]{:S(2)}) collective-permute-start(bf16[16,2048]{1,0:T(8,128)(2,1)} %slice.45), channel_id=1, source_target_pairs={{3,7},{7,11},{11,15},{15,19},{19,23},{23,27},{27,31}} | collective-permute-start | bytes 196616 | tf_op jit(solution)/shard_map/ppermute | solution.py:274
  40.3 1.6 %collective-permute-start = (bf16[64,2048]{1,0:T(8,128)(2,1)S(1)}, bf16[64,2048]{1,0:T(8,128)(2,1)S(1)}, u32[]{:S(2)}, u32[]{:S(2)}) collective-permute-start(bf16[64,2048]{1,0:T(8,128)(2,1)S(1)} %copy-done.1), channel_id=1, source_target_pairs={{0,1},{1,0},{2,3},{3,2},{4,5},{5,4},{6,7},{7,6},{8,9},{9,8},{10,11... | collective-permute-start | bytes 786440 | tf_op jit(solution)/shard_map/ppermute | solution.py:247
  40.4 2.1 %collective-permute-start.2 = (bf16[64,2048]{1,0:T(8,128)(2,1)}, bf16[64,2048]{1,0:T(8,128)(2,1)S(1)}, u32[]{:S(2)}, u32[]{:S(2)}) collective-permute-start(bf16[64,2048]{1,0:T(8,128)(2,1)} %collective-permute-done.1.refs_2_), channel_id=1, source_target_pairs={{0,1},{1,0},{2,3},{3,2},{4,5},{5,4},{6,7},{7,6},{8,9},{9,8},{10,11... | collective-permute-start | bytes 786440 | tf_op jit(solution)/shard_map/ppermute | solution.py:247
  48.5 8.4 %collective-permute-start.7 = (bf16[4,128,256]{2,1,0:T(8,128)(2,1)S(1)}, bf16[4,128,256]{2,1,0:T(8,128)(2,1)S(1)}, u32[]{:S(2)}, u32[]{:S(2)}) collective-permute-start(bf16[4,128,256]{2,1,0:T(8,128)(2,1)S(1)} %get-tuple-element.25.own), channel_id=1, source_target_pairs={{0,4},{4,0},{8,12},{12,8},{16,20},{20,16},{24,28},{28,24},{1,5},{5... | collective-permute-start | bytes 786440 | tf_op jit(solution)/shard_map/ppermute | solution.py:247
  50.1 18.8 %copy-start.2 = (f32[128]{0:T(128)S(1)}, f32[128]{0:T(128)}, u32[]{:S(2)}) copy-start(f32[128]{0:T(128)} %param.10) | copy-start | bytes 1540
  57.1 7.7 %collective-permute-start.8 = (bf16[4,128,128]{2,1,0:T(8,128)(2,1)S(1)}, bf16[4,128,128]{2,1,0:T(8,128)(2,1)S(1)}, u32[]{:S(2)}, u32[]{:S(2)}) collective-permute-start(bf16[4,128,128]{2,1,0:T(8,128)(2,1)S(1)} %get-tuple-element.28.b), channel_id=1, source_target_pairs={{0,8},{4,12},{8,16},{12,20},{16,24},{20,28},{1,9},{5,13},{9,17},{1... | collective-permute-start | bytes 393224 | tf_op jit(solution)/shard_map/ppermute | solution.py:252
  61.4 9.7 %collective-permute-start.9 = (bf16[4,128,128]{2,1,0:T(8,128)(2,1)S(1)}, bf16[4,128,128]{2,1,0:T(8,128)(2,1)S(1)}, u32[]{:S(2)}, u32[]{:S(2)}) collective-permute-start(bf16[4,128,128]{2,1,0:T(8,128)(2,1)S(1)} %get-tuple-element.29.t), channel_id=1, source_target_pairs={{0,8},{4,12},{8,16},{12,20},{16,24},{20,28},{1,9},{5,13},{9,17},{1... | collective-permute-start | bytes 393224 | tf_op jit(solution)/shard_map/ppermute | solution.py:252
  65.1 6.4 %collective-permute-start.10 = (bf16[4,128,128]{2,1,0:T(8,128)(2,1)S(1)}, bf16[4,128,128]{2,1,0:T(8,128)(2,1)S(1)}, u32[]{:S(2)}, u32[]{:S(2)}) collective-permute-start(bf16[4,128,128]{2,1,0:T(8,128)(2,1)S(1)} %shard_map.69), channel_id=1, source_target_pairs={{0,16},{4,20},{8,24},{12,28},{1,17},{5,21},{9,25},{13,29},{2,18},{... | collective-permute-start | bytes 393224 | tf_op jit(solution)/shard_map/ppermute | solution.py:252
  68.9 4.4 %copy-start = (bf16[512,2048]{1,0:T(8,128)(2,1)S(1)}, bf16[512,2048]{1,0:T(8,128)(2,1)}, u32[]{:S(2)}) copy-start(bf16[512,2048]{1,0:T(8,128)(2,1)} %w_own.3) | copy-start | bytes 6291460
  71.9 1.4 %collective-permute-start.11 = (bf16[128,512]{1,0:T(8,128)(2,1)S(1)}, bf16[128,512]{1,0:T(8,128)(2,1)S(1)}, u32[]{:S(2)}, u32[]{:S(2)}) collective-permute-start(bf16[128,512]{1,0:T(8,128)(2,1)S(1)} %get-tuple-element.34), channel_id=1, source_target_pairs={{0,1},{1,0},{2,3},{3,2},{4,5},{5,4},{6,7},{7,6},{8,9},{9,8},{10,11... | collective-permute-start | bytes 393224 | tf_op jit(solution)/shard_map/ppermute | solution.py:247
  75.7 10.3 %collective-permute-start.13 = (bf16[64,2048]{1,0:T(8,128)(2,1)S(1)}, bf16[64,2048]{1,0:T(8,128)(2,1)S(1)}, u32[]{:S(2)}, u32[]{:S(2)}) collective-permute-start(bf16[64,2048]{1,0:T(8,128)(2,1)S(1)} %shard_map.72), channel_id=1, source_target_pairs={{0,2},{1,3},{2,0},{3,1},{4,6},{5,7},{6,4},{7,5},{8,10},{9,11},{10,... | collective-permute-start | bytes 786440 | tf_op jit(solution)/shard_map/ppermute | solution.py:247
  (6 other events, 12.6 us)

commit v2 on v1

--- a/solution.py
+++ b/solution.py
@@ -34,11 +34,11 @@
     return x * lax.rsqrt(jnp.sum(x * x, axis=-1, keepdims=True) + EPSILON)
 
 
-def conv_silu(padded, slot, weight, lanes, rows):
-    acc = padded[slot, HALO - KERNEL + 1 : HALO - KERNEL + 1 + rows, :] * weight[0:1, lanes]
+def conv_silu(padded, slot, weight, g, lanes, rows):
+    acc = padded[slot, HALO - KERNEL + 1 : HALO - KERNEL + 1 + rows, :] * weight[0, g : g + 1, lanes]
     for i in range(1, KERNEL):
         lo = HALO - KERNEL + 1 + i
-        acc = acc + padded[slot, lo : lo + rows, :] * weight[i : i + 1, lanes]
+        acc = acc + padded[slot, lo : lo + rows, :] * weight[i, g : g + 1, lanes]
     return silu(acc)
 
 
@@ -47,21 +47,48 @@
     return jnp.exp(jnp.minimum(gap, 0.0))
 
 
+def gates_kernel(logits, rows, cols, decays):
+    toks = logits.shape[2]
+    blocks = toks // HALF
+    x = logits[0]
+    log_decay = -(jnp.maximum(x, 0.0) + jnp.log1p(jnp.exp(-jnp.abs(x))))
+    beta = 1.0 / (1.0 + jnp.exp(-logits[1]))
+    heads = x.shape[0]
+    ri = lax.broadcasted_iota(jnp.int32, (toks, toks), 0)
+    ci = lax.broadcasted_iota(jnp.int32, (toks, toks), 1)
+    exact = lax.Precision.HIGHEST
+    rows[...] = jnp.dot(log_decay, (ri <= ci).astype(F32), precision=exact, preferred_element_type=F32)
+    last_dims = (((1,), (1,)), ((), ()))
+    ccols = lax.dot_general((ri >= ci).astype(F32), log_decay, last_dims, precision=exact, preferred_element_type=F32)
+    bcols = lax.dot_general((ri == ci).astype(F32), beta, last_dims, precision=exact, preferred_element_type=F32)
+    cols[:, 0:heads] = ccols
+    cols[:, heads : 2 * heads] = bcols
+    below = ri[:HALF, :HALF] > ci[:HALF, :HALF]
+    for j in range(heads):
+        i = 0
+        for a in range(blocks):
+            for b in range(a + 1):
+                m = block_decay(ccols[:, j : j + 1], rows[j : j + 1, :], a, b)
+                m = m * bcols[a * HALF : (a + 1) * HALF, j : j + 1]
+                decays[j, i] = jnp.where(below, m, 0.0) if a == b else m
+                i += 1
+
+
 def keys_kernel(*refs, n_head, key_heads, ratio):
     pieces = refs[:n_head]
-    halo, w, cw, cols, rows, s_out, y_out, k_out, x_out, padded = refs[n_head:]
+    halo, halo_core, w, cw, cols, rows, decays, s_out, y_out, k_out, x_out, padded = refs[n_head:]
     me = lax.axis_index("head")
     part = pieces[0].shape[0]
     toks = part * n_head
     blocks = toks // HALF
     heads = key_heads * ratio
-    x_out[0:HALO, :] = halo[...]
+    x_out[0:HALO, :] = jnp.where(me % 2 == 1, halo[part - HALO :, :], halo_core[part - HALO :, :])
     for s in range(n_head):
         at = pl.multiple_of(HALO + (me ^ s) * part, 16)
         x_out[pl.ds(at, part), :] = pieces[s][...]
-    width = DK + ratio * DV
+    group = 2 * DK + 2 * ratio * DV
     for g in range(key_heads):
-        proj = dot(x_out[...], w[:, g * width : (g + 1) * width])
+        proj = dot(x_out[...], w[:, g * group + DK : g * group + 2 * DK + ratio * DV])
         proj = proj.astype(BF16).astype(F32)
         for t in range(1 + ratio):
             padded[g * (1 + ratio) + t] = proj[:, t * 128 : (t + 1) * 128]
@@ -73,7 +100,7 @@
     kts, rhs, lowers, offs = [], [], [], []
     for g in range(key_heads):
         base = g * (1 + ratio)
-        k = l2_normed(conv_silu(padded, base, cw, slice(base * 128, base * 128 + 128), toks))
+        k = l2_normed(conv_silu(padded, base, cw, g, slice(DK, 2 * DK), toks))
         kb = k.astype(BF16)
         k_out[g] = kb
         kf = kb.astype(F32)
@@ -82,21 +109,20 @@
         grams = {(a, b): dot_t(ks[a], ks[b]) for a in range(blocks) for b in range(a + 1)}
         for r in range(ratio):
             j = g * ratio + r
-            lanes = slice((base + 1 + r) * 128, (base + 2 + r) * 128)
-            v = conv_silu(padded, base + 1 + r, cw, lanes, toks)
+            lanes = slice(2 * DK + r * DV, 2 * DK + (r + 1) * DV)
+            v = conv_silu(padded, base + 1 + r, cw, g, lanes, toks)
             ccol = cols[:, j : j + 1]
             bcol = cols[:, heads + j : heads + j + 1]
-            crow = rows[j : j + 1, :]
             rk = (kf * (bcol * jnp.exp(ccol))).astype(BF16)
             rv = (v * bcol).astype(BF16)
             rhs.append(jnp.concatenate([rk, rv], axis=1))
-            low, off = [], {}
+            low, off, i = [], {}, 0
             for a in range(blocks):
-                ba = bcol[a * HALF : (a + 1) * HALF]
                 for b in range(a + 1):
-                    m = ba * grams[(a, b)] * block_decay(ccol, crow, a, b)
+                    m = grams[(a, b)] * decays[j, i]
+                    i += 1
                     if a == b:
-                        low.append(jnp.where(below, m, 0.0))
+                        low.append(m)
                     else:
                         off[(a, b)] = m.astype(BF16)
             lowers += low
@@ -133,18 +159,18 @@
 def queries_kernel(x, w, cw, cols, rows, keys, ys, gain, q_out, o_out, g_out, padded, *, key_heads, ratio):
     toks = x.shape[0] - HALO
     blocks = toks // HALF
-    width = DK + ratio * DV
+    group = 2 * DK + 2 * ratio * DV
     ri = lax.broadcasted_iota(jnp.int32, (HALF, HALF), 0)
     ci = lax.broadcasted_iota(jnp.int32, (HALF, HALF), 1)
     upto = ri >= ci
     for g in range(key_heads):
-        proj = dot(x[...], w[:, g * width : (g + 1) * width]).astype(BF16).astype(F32)
-        padded[g] = proj[:, 0:DK]
+        padded[g] = dot(x[...], w[:, g * group : g * group + DK]).astype(BF16).astype(F32)
+        proj = dot(x[HALO:, :], w[:, g * group + 2 * DK + ratio * DV : (g + 1) * group]).astype(BF16).astype(F32)
         for r in range(ratio):
-            z = proj[HALO:, DK + r * DV : DK + (r + 1) * DV]
+            z = proj[:, r * DV : (r + 1) * DV]
             g_out[g * ratio + r] = gain[...] * silu(z)
     for g in range(key_heads):
-        q = l2_normed(conv_silu(padded, g, cw, slice(g * 128, g * 128 + 128), toks)) * DK ** (-0.5)
+        q = l2_normed(conv_silu(padded, g, cw, g, slice(0, DK), toks)) * DK ** (-0.5)
         qb = q.astype(BF16)
         kb = keys[g]
         grams = {
@@ -204,10 +230,11 @@
         t_out[j] = dot(t[j], jt[j]).astype(BF16)
 
 
-def normed_kernel(q, o, jb, gate, keep, send, scratch, *, n_head):
+def normed_kernel(q, o, jb, gate, keep, send, scratch, *, n_head, last_step):
     me = lax.axis_index("head")
+    upper = lax.axis_index("ctx") // last_step % 2 == 1
     for j in range(q.shape[0]):
-        att = o[j] + dot(q[j], jb[j])
+        att = o[j] + jnp.where(upper, dot(q[j], jb[j]), 0.0)
         scale = lax.rsqrt(jnp.mean(att * att, axis=-1, keepdims=True) + EPSILON)
         scratch[:, j * DV : (j + 1) * DV] = (att * scale * gate[j]).astype(BF16)
     part = scratch.shape[0] // n_head
@@ -267,26 +294,23 @@
         for s in range(0, n_head, 2 * step):
             pieces[s + step] = xor_sent(pieces[s], "head", step)
         step //= 2
-    tail = layer_in[part - HALO :]
     halo = None
-    for h in range(n_head):
+    for h in range(1, n_head, 2):
         perm = [((c - 1) * n_head + n_head - 1, c * n_head + h) for c in range(1, n_ctx)]
-        got = lax.ppermute(tail, ctx_head, perm)
+        got = lax.ppermute(layer_in, ctx_head, perm)
         halo = got if halo is None else halo + got
-
-    def columns(w, spans):
-        return jnp.concatenate([w[:, g, a:b] for g in range(key_heads) for a, b in spans], axis=1)
-
-    kv_span = [(DK, 2 * DK + ratio * DV)]
-    qz_span = [(0, DK), (2 * DK + ratio * DV, 2 * DK + 2 * ratio * DV)]
-    w_kv = columns(in_proj, kv_span)
-    w_qz = columns(in_proj, qz_span)
-    c_kv = columns(conv_weight, kv_span)
-    c_q = columns(conv_weight, [(0, DK)])
-    cum = jnp.cumsum(-jax.nn.softplus(gate_logits[0]), axis=-1)
-    beta = jax.nn.sigmoid(gate_logits[1])
-    rows = cum
-    cols = jnp.concatenate([cum, beta], axis=0).T
+    halo_core = xor_sent(halo, "head", 1)
+    w_in = in_proj.reshape(width, key_heads * group)
+    blocks = toks // HALF
+    rows, cols, decays = call(
+        gates_kernel,
+        (
+            shaped((heads, toks), F32),
+            shaped((toks, 2 * heads), F32),
+            shaped((heads, blocks * (blocks + 1) // 2, HALF, HALF), F32),
+        ),
+        [gate_logits],
+    )
     w_other = xor_sent(out_proj, "head", 1)
 
     state = shaped((heads, DK, DV), BF16)
@@ -298,7 +322,7 @@
             shaped((key_heads, toks, DK), BF16),
             shaped((HALO + toks, width), BF16),
         ),
-        [*pieces, halo, w_kv, c_kv, cols, rows],
+        [*pieces, halo, halo_core, w_in, conv_weight, cols, rows, decays],
         [pltpu.VMEM((key_heads * (1 + ratio), HALO + toks, 128), F32)],
         flops=2 * toks * width * group,
         n_head=n_head,
@@ -311,7 +335,7 @@
     q, o, gate = call(
         queries_kernel,
         (q_shape, o_shape, o_shape),
-        [x_full, w_qz, c_q, cols, rows, keys, ys, norm_gain[None, :]],
+        [x_full, w_in, conv_weight, cols, rows, keys, ys, norm_gain[None, :]],
         [pltpu.VMEM((key_heads, HALO + toks, 128), F32)],
         flops=2 * toks * width * group,
         key_heads=key_heads,
@@ -328,7 +352,7 @@
         more = 2 * step < n_ctx
         if more:
             t = call(join_t_kernel, state, [t, jt], flops=heads * 2**22)
-        nb = passed_along(b, "ctx", step)
+        nb = passed_along(b, "ctx", step) if more else xor_sent(b, "ctx", step)
         nt = passed_along(t, "ctx", step) if more else None
         q, o = call(absorb_kernel, (q_shape, o_shape), [q, o, jb, jt], flops=heads * 2**24)
         jb, jt = nb, nt
@@ -340,6 +364,7 @@
         [pltpu.VMEM((toks, heads * DV), BF16)],
         flops=heads * 2**23,
         n_head=n_head,
+        last_step=step,
     )
     other = xor_sent(send, "head", 1)
     out_args = [keep, other, out_proj, w_other]

time: 88.2 us -> 61.7 us (0.70); the launches traced: 86.7 us -> 61.4 us
  local copies, waits for them, and re-layouts: 27 us -> 4.9 us
  waiting for transfers between devices: 12.6 us -> 17.3 us
  other arithmetic: 4.45 us -> 0.82 us
  Pallas kernels: 14.1 us -> 11 us
  starting transfers between devices: 28.2 us -> 27.2 us
    slice x8 -> x0, local copies, waits for them, and re-layouts: 18.5 us -> none  [the longest x5 16.7 us: columns(): w[:, g, a:b]]
    squeeze x5 -> x0, local copies, waits for them, and re-layouts: 6.04 us -> none  [the longest x4 6.03 us: columns(): w[:, g, a:b]]
    ppermute x7 -> x9, starting transfers between devices: 12.6 us -> 18.6 us  [xor_sent(): return lax.ppermute(value, axis, [(i, i ^ step) for i in range(count)])]
    ppermute x7 -> x9, waiting for transfers between devices: 12.6 us -> 17.3 us  [xor_sent(): return lax.ppermute(value, axis, [(i, i ^ step) for i in range(count)])]
    ppermute x3 -> x2, starting transfers between devices: 10.7 us -> 7.22 us  [passed_along(): lax.ppermute(value, axis, [(i, i + steps) for i in range(count - steps)])]
    ppermute x4 -> x2, starting transfers between devices: 4.79 us -> 1.34 us  [local(): got = lax.ppermute(layer_in, ctx_head, perm)]
    pallas_call x9 -> x10, Pallas kernels: 14.1 us -> 11 us  [call(): pl.pallas_call(functools.partial(body, **static), out_shape=out_shape, in...]
    unnamed x33 -> x11, local copies, waits for them, and re-layouts: 2.23 us -> 4.9 us
  transfers between devices with their start and end apart: 14 -> 13, of which waited for: 5 -> 4; matrix products, arithmetic and copies ran while one was open for 31% -> 7% of each run, Pallas kernels for 14% -> 17%
where the time goes in v2:
time: 61.7 us; the launch traced here: 61.4 us
  starting transfers between devices  27.2 us (44%)
  waiting for transfers between devices  17.3 us (28%)
  Pallas kernels  11 us (18%)
  local copies, waits for them, and re-layouts  4.9 us (8%)
  other arithmetic  0.82 us (1%)
    ppermute x9, starting transfers between devices, xor_sent(): return lax.ppermute(value, axis, [(i, i ^ step) for i in range(count)])  18.6 us
    ppermute x9, waiting for transfers between devices, xor_sent(): return lax.ppermute(value, axis, [(i, i ^ step) for i in range(count)])  17.3 us
    pallas_call x10, Pallas kernels, call(): pl.pallas_call(functools.partial(body, **static), out_shape=out_shape, in...  11 us
    ppermute x2, starting transfers between devices, passed_along(): lax.ppermute(value, axis, [(i, i + steps) for i in range(count - steps)])  7.22 us
    unnamed x11, local copies, waits for them, and re-layouts  4.9 us
    ppermute x2, starting transfers between devices, local(): got = lax.ppermute(layer_in, ctx_head, perm)  1.34 us
  transfers between devices with their start and end apart: 13, of which 4 were waited for; matrix products, arithmetic and copies ran while one was open for 7% of the time, Pallas kernels for 17%

profile of v2, /device:TPU:0, one launch (start us, length us, event | category | flops | bytes accessed | tf_op | source)
XLA Modules:
  0.0 61.4 jit_solution(13967002516080437363)
XLA Ops:
  0.0 0.5 collective-permute-start.11
  0.5 0.7 %collective-permute-start.3 = (bf16[64,2048]{1,0:T(8,128)(2,1)}, bf16[64,2048]{1,0:T(8,128)(2,1)S(1)}, u32[]{:S(2)}, u32[]{:S(2)}) collective-permute-start(bf16[64,2048]{1,0:T(8,128)(2,1)} %refs_0_.1), channel_id=1, source_target_pairs={{3,5},{7,9},{11,13},{15,17},{19,21},{23,25},{27,29}} | collective-permute-start | bytes 786440 | tf_op jit(solution)/shard_map/ppermute | solution.py:300
  1.1 0.7 %collective-permute-start.4 = (bf16[64,2048]{1,0:T(8,128)(2,1)}, bf16[64,2048]{1,0:T(8,128)(2,1)S(1)}, u32[]{:S(2)}, u32[]{:S(2)}) collective-permute-start(bf16[64,2048]{1,0:T(8,128)(2,1)} %refs_0_.1), channel_id=1, source_target_pairs={{3,7},{7,11},{11,15},{15,19},{19,23},{23,27},{27,31}} | collective-permute-start | bytes 786440 | tf_op jit(solution)/shard_map/ppermute | solution.py:300
  1.8 2.6 %collective-permute-start.1 = (bf16[64,2048]{1,0:T(8,128)(2,1)}, bf16[64,2048]{1,0:T(8,128)(2,1)S(1)}, u32[]{:S(2)}, u32[]{:S(2)}) collective-permute-start(bf16[64,2048]{1,0:T(8,128)(2,1)} %refs_0_.1), channel_id=1, source_target_pairs={{0,2},{1,3},{2,0},{3,1},{4,6},{5,7},{6,4},{7,5},{8,10},{9,11},{10,... | collective-permute-start | bytes 786440 | tf_op jit(solution)/shard_map/ppermute | solution.py:274
  4.4 5.1 %collective-permute-start = (bf16[64,2048]{1,0:T(8,128)(2,1)}, bf16[64,2048]{1,0:T(8,128)(2,1)S(1)}, u32[]{:S(2)}, u32[]{:S(2)}) collective-permute-start(bf16[64,2048]{1,0:T(8,128)(2,1)} %refs_0_.1), channel_id=1, source_target_pairs={{0,1},{1,0},{2,3},{3,2},{4,5},{5,4},{6,7},{7,6},{8,9},{9,8},{10,11... | collective-permute-start | bytes 786440 | tf_op jit(solution)/shard_map/ppermute | solution.py:274
  9.7 3.8 %collective-permute-start.2 = (bf16[64,2048]{1,0:T(8,128)(2,1)S(1)}, bf16[64,2048]{1,0:T(8,128)(2,1)S(1)}, u32[]{:S(2)}, u32[]{:S(2)}) collective-permute-start(bf16[64,2048]{1,0:T(8,128)(2,1)S(1)} %collective-permute-done.1.refs_2_), channel_id=1, source_target_pairs={{0,1},{1,0},{2,3},{3,2},{4,5},{5,4},{6,7},{7,6},{8,9},{9,8},{10,11... | collective-permute-start | bytes 786440 | tf_op jit(solution)/shard_map/ppermute | solution.py:274
  13.5 0.7 %copy-done.3 = f32[2,4,256]{2,1,0:T(4,128)S(1)} copy-done((f32[2,4,256]{2,1,0:T(4,128)S(1)}, f32[2,4,256]{2,1,0:T(4,128)}, u32[]{:S(2)}) %copy-start.3) | copy-done | bytes 8216
  14.2 1.0 %shard_map.64 = (f32[4,256]{1,0:T(4,128)S(1)}, f32[256,8]{1,0:T(8,128)S(1)}, f32[4,3,128,128]{3,2,1,0:T(8,128)S(1)}) custom-call(f32[2,4,256]{2,1,0:T(4,128)S(1)} %copy-done.3), custom_call_target="tpu_custom_call" | custom-call | bytes 8192 | tf_op jit(solution)/shard_map/pallas_call | solution.py:257
  15.2 4.2 %copy.7 = bf16[256,8,2,768]{3,1,2,0:T(8,128)(2,1)S(1)} copy(bf16[256,8,2,768]{3,2,1,0:T(2,128)(2,1)} %bitcast.6) | data formatting | bytes 12582912
  19.5 5.0 %shard_map.65 = (bf16[4,128,256]{2,1,0:T(8,128)(2,1)S(1)}, bf16[4,256,256]{2,1,0:T(8,128)(2,1)S(1)}, bf16[2,256,128]{2,1,0:T(8,128)(2,1)S(1)}, bf16[272,2048]{1,0:T(8,128)(2,1)S(1)}) custom-call(bf16[64,2048]{1,0:T(8,128)(2,1)S(1)} %copy-done.1, bf16[64,2048]{1,0:T(8,128)(2,1)S(1)} %collective-permute-done.refs_1_, ...), custom_call_target="tpu_custom_call" | custom-call | flops 805306368 | bytes 8679424 | tf_op jit(solution)/shard_map/pallas_call | solution.py:257
  24.5 2.9 %collective-permute-start.6 = (bf16[4,128,256]{2,1,0:T(8,128)(2,1)S(1)}, bf16[4,128,256]{2,1,0:T(8,128)(2,1)S(1)}, u32[]{:S(2)}, u32[]{:S(2)}) collective-permute-start(bf16[4,128,256]{2,1,0:T(8,128)(2,1)S(1)} %get-tuple-element.31.own), channel_id=1, source_target_pairs={{0,4},{4,0},{8,12},{12,8},{16,20},{20,16},{24,28},{28,24},{1,5},{5... | collective-permute-start | bytes 786440 | tf_op jit(solution)/shard_map/ppermute | solution.py:274
  27.5 6.5 %collective-permute-done.6.got = bf16[4,128,256]{2,1,0:T(8,128)(2,1)S(1)} collective-permute-done((bf16[4,128,256]{2,1,0:T(8,128)(2,1)S(1)}, bf16[4,128,256]{2,1,0:T(8,128)(2,1)S(1)}, u32[]{:S(2)}, u32[]{:S(2)}) %collective-permute-start.6) | collective-permute-done | bytes 262176 | tf_op jit(solution)/shard_map/ppermute | solution.py:274
  34.2 3.7 %collective-permute-start.7 = (bf16[4,128,128]{2,1,0:T(8,128)(2,1)S(1)}, bf16[4,128,128]{2,1,0:T(8,128)(2,1)S(1)}, u32[]{:S(2)}, u32[]{:S(2)}) collective-permute-start(bf16[4,128,128]{2,1,0:T(8,128)(2,1)S(1)} %get-tuple-element.34.b), channel_id=1, source_target_pairs={{0,8},{4,12},{8,16},{12,20},{16,24},{20,28},{1,9},{5,13},{9,17},{1... | collective-permute-start | bytes 393224 | tf_op jit(solution)/shard_map/ppermute | solution.py:279
  37.9 3.5 %collective-permute-start.8 = (bf16[4,128,128]{2,1,0:T(8,128)(2,1)S(1)}, bf16[4,128,128]{2,1,0:T(8,128)(2,1)S(1)}, u32[]{:S(2)}, u32[]{:S(2)}) collective-permute-start(bf16[4,128,128]{2,1,0:T(8,128)(2,1)S(1)} %get-tuple-element.35.t), channel_id=1, source_target_pairs={{0,8},{4,12},{8,16},{12,20},{16,24},{20,28},{1,9},{5,13},{9,17},{1... | collective-permute-start | bytes 393224 | tf_op jit(solution)/shard_map/ppermute | solution.py:279
  41.6 3.0 %collective-permute-start.9 = (bf16[4,128,128]{2,1,0:T(8,128)(2,1)S(1)}, bf16[4,128,128]{2,1,0:T(8,128)(2,1)S(1)}, u32[]{:S(2)}, u32[]{:S(2)}) collective-permute-start(bf16[4,128,128]{2,1,0:T(8,128)(2,1)S(1)} %shard_map.70), channel_id=1, source_target_pairs={{0,16},{4,20},{8,24},{12,28},{16,0},{20,4},{24,8},{28,12},{1,17},{... | collective-permute-start | bytes 393224 | tf_op jit(solution)/shard_map/ppermute | solution.py:274
  44.6 1.9 %shard_map.66 = (bf16[4,256,128]{2,1,0:T(8,128)(2,1)S(1)}, f32[4,256,128]{2,1,0:T(8,128)S(1)}, f32[4,256,128]{2,1,0:T(8,128)S(1)}) custom-call(bf16[272,2048]{1,0:T(8,128)(2,1)S(1)} %get-tuple-element.26.x, bf16[2048,1536]{1,0:T(8,128)(2,1)S(1)} %bitcast.4, f32[4,2,512]{2,1,0:T(2,128)S(1)} %copy-done.2, f32[256,8]{1,0:T(8,128)S(1)} %get-tuple-element.23.refs_8_.cols, ...), custom_call_target="tpu_custom_call" | custom-call | flops 805306368 | bytes 8090112 | tf_op jit(solution)/shard_map/pallas_call | solution.py:257
  47.1 2.5 %collective-permute-done.9.jb = bf16[4,128,128]{2,1,0:T(8,128)(2,1)S(1)} collective-permute-done((bf16[4,128,128]{2,1,0:T(8,128)(2,1)S(1)}, bf16[4,128,128]{2,1,0:T(8,128)(2,1)S(1)}, u32[]{:S(2)}, u32[]{:S(2)}) %collective-permute-start.9) | collective-permute-done | bytes 131104 | tf_op jit(solution)/shard_map/ppermute | solution.py:274
  49.6 0.4 shard_map.71
  50.1 1.3 %collective-permute-done.10.got = bf16[128,512]{1,0:T(8,128)(2,1)S(1)} collective-permute-done((bf16[128,512]{1,0:T(8,128)(2,1)S(1)}, bf16[128,512]{1,0:T(8,128)(2,1)S(1)}, u32[]{:S(2)}, u32[]{:S(2)}) %collective-permute-start.10) | collective-permute-done | bytes 131104 | tf_op jit(solution)/shard_map/ppermute | solution.py:274
  51.4 0.8 %shard_map.73 = bf16[64,2048]{1,0:T(8,128)(2,1)S(1)} custom-call(bf16[128,512]{1,0:T(8,128)(2,1)S(1)} %get-tuple-element.39.own, bf16[128,512]{1,0:T(8,128)(2,1)S(1)} %collective-permute-done.10.got, bf16[512,2048]{1,0:T(8,128)(2,1)S(1)} %copy-done, bf16[512,2048]{1,0:T(8,128)(2,1)S(1)} %collective-permute-done.11.w_got), custom_call_target="tpu_custom_call" | custom-call | flops 536870912 | bytes 4456448 | tf_op jit(solution)/shard_map/pallas_call | solution.py:257
  52.2 0.6 collective-permute-start.12
  52.9 0.8 %shard_map.72 = f32[64,2048]{1,0:T(8,128)S(1)} custom-call(bf16[128,512]{1,0:T(8,128)(2,1)S(1)} %get-tuple-element.39.own, bf16[128,512]{1,0:T(8,128)(2,1)S(1)} %collective-permute-done.10.got, bf16[512,2048]{1,0:T(8,128)(2,1)S(1)} %copy-done, bf16[512,2048]{1,0:T(8,128)(2,1)S(1)} %collective-permute-done.11.w_got), custom_call_target="tpu_custom_call" | custom-call | flops 536870912 | bytes 4456448 | tf_op jit(solution)/shard_map/pallas_call | solution.py:257
  53.7 7.0 %collective-permute-done.12 = bf16[64,2048]{1,0:T(8,128)(2,1)S(1)} collective-permute-done((bf16[64,2048]{1,0:T(8,128)(2,1)S(1)}, bf16[64,2048]{1,0:T(8,128)(2,1)S(1)}, u32[]{:S(2)}, u32[]{:S(2)}) %collective-permute-start.12) | collective-permute-done | bytes 262176 | tf_op jit(solution)/shard_map/ppermute | solution.py:274
  60.7 0.8 %add_convert_fusion = bf16[64,2048]{1,0:T(8,128)(2,1)} fusion(f32[64,2048]{1,0:T(8,128)S(1)} %shard_map.72, bf16[64,2048]{1,0:T(8,128)(2,1)S(1)} %collective-permute-done.12), kind=kLoop, calls=%fused_computation | loop fusion | flops 393216 | bytes 1048576 | tf_op jit(solution)/shard_map/convert_element_type | solution.py:382
  (25 shorter events, 1.2 us)
Async XLA Ops:
  0.0 51.4 %collective-permute-start.11 = (bf16[512,2048]{1,0:T(8,128)(2,1)}, bf16[512,2048]{1,0:T(8,128)(2,1)S(1)}, u32[]{:S(2)}, u32[]{:S(2)}) collective-permute-start(bf16[512,2048]{1,0:T(8,128)(2,1)} %w_own.3), channel_id=1, source_target_pairs={{0,1},{1,0},{2,3},{3,2},{4,5},{5,4},{6,7},{7,6},{8,9},{9,8},{10,11... | collective-permute-start | bytes 6291464 | tf_op jit(solution)/shard_map/ppermute | solution.py:274
  0.5 9.1 %collective-permute-start.3 = (bf16[64,2048]{1,0:T(8,128)(2,1)}, bf16[64,2048]{1,0:T(8,128)(2,1)S(1)}, u32[]{:S(2)}, u32[]{:S(2)}) collective-permute-start(bf16[64,2048]{1,0:T(8,128)(2,1)} %refs_0_.1), channel_id=1, source_target_pairs={{3,5},{7,9},{11,13},{15,17},{19,21},{23,25},{27,29}} | collective-permute-start | bytes 786440 | tf_op jit(solution)/shard_map/ppermute | solution.py:300
  1.1 8.4 %collective-permute-start.4 = (bf16[64,2048]{1,0:T(8,128)(2,1)}, bf16[64,2048]{1,0:T(8,128)(2,1)S(1)}, u32[]{:S(2)}, u32[]{:S(2)}) collective-permute-start(bf16[64,2048]{1,0:T(8,128)(2,1)} %refs_0_.1), channel_id=1, source_target_pairs={{3,7},{7,11},{11,15},{15,19},{19,23},{23,27},{27,31}} | collective-permute-start | bytes 786440 | tf_op jit(solution)/shard_map/ppermute | solution.py:300
  1.8 7.9 %collective-permute-start.1 = (bf16[64,2048]{1,0:T(8,128)(2,1)}, bf16[64,2048]{1,0:T(8,128)(2,1)S(1)}, u32[]{:S(2)}, u32[]{:S(2)}) collective-permute-start(bf16[64,2048]{1,0:T(8,128)(2,1)} %refs_0_.1), channel_id=1, source_target_pairs={{0,2},{1,3},{2,0},{3,1},{4,6},{5,7},{6,4},{7,5},{8,10},{9,11},{10,... | collective-permute-start | bytes 786440 | tf_op jit(solution)/shard_map/ppermute | solution.py:274
  4.4 15.0 %collective-permute-start = (bf16[64,2048]{1,0:T(8,128)(2,1)}, bf16[64,2048]{1,0:T(8,128)(2,1)S(1)}, u32[]{:S(2)}, u32[]{:S(2)}) collective-permute-start(bf16[64,2048]{1,0:T(8,128)(2,1)} %refs_0_.1), channel_id=1, source_target_pairs={{0,1},{1,0},{2,3},{3,2},{4,5},{5,4},{6,7},{7,6},{8,9},{9,8},{10,11... | collective-permute-start | bytes 786440 | tf_op jit(solution)/shard_map/ppermute | solution.py:274
  9.6 9.8 %collective-permute-start.5 = (bf16[64,2048]{1,0:T(8,128)(2,1)S(1)}, bf16[64,2048]{1,0:T(8,128)(2,1)S(1)}, u32[]{:S(2)}, u32[]{:S(2)}) collective-permute-start(bf16[64,2048]{1,0:T(8,128)(2,1)S(1)} %add.6.refs_4_), channel_id=1, source_target_pairs={{0,1},{1,0},{2,3},{3,2},{4,5},{5,4},{6,7},{7,6},{8,9},{9,8},{10,11... | collective-permute-start | bytes 786440 | tf_op jit(solution)/shard_map/ppermute | solution.py:274
  9.7 9.7 %collective-permute-start.2 = (bf16[64,2048]{1,0:T(8,128)(2,1)S(1)}, bf16[64,2048]{1,0:T(8,128)(2,1)S(1)}, u32[]{:S(2)}, u32[]{:S(2)}) collective-permute-start(bf16[64,2048]{1,0:T(8,128)(2,1)S(1)} %collective-permute-done.1.refs_2_), channel_id=1, source_target_pairs={{0,1},{1,0},{2,3},{3,2},{4,5},{5,4},{6,7},{7,6},{8,9},{9,8},{10,11... | collective-permute-start | bytes 786440 | tf_op jit(solution)/shard_map/ppermute | solution.py:274
  13.5 0.7 %copy-start.3 = (f32[2,4,256]{2,1,0:T(4,128)S(1)}, f32[2,4,256]{2,1,0:T(4,128)}, u32[]{:S(2)}) copy-start(f32[2,4,256]{2,1,0:T(4,128)} %logits.1) | copy-start | bytes 24580
  15.2 4.2 %copy-start.1 = (bf16[64,2048]{1,0:T(8,128)(2,1)S(1)}, bf16[64,2048]{1,0:T(8,128)(2,1)}, u32[]{:S(2)}) copy-start(bf16[64,2048]{1,0:T(8,128)(2,1)} %refs_0_.1) | copy-start | bytes 786436
  15.2 4.2 %copy-start.2 = (f32[4,2,512]{2,1,0:T(2,128)S(1)}, f32[4,2,512]{2,1,0:T(2,128)}, u32[]{:S(2)}) copy-start(f32[4,2,512]{2,1,0:T(2,128)} %cw.1) | copy-start | bytes 49156
  19.5 25.1 %copy-start.4 = (f32[128]{0:T(128)S(1)}, f32[128]{0:T(128)}, u32[]{:S(2)}) copy-start(f32[128]{0:T(128)} %param.10) | copy-start | bytes 1540
  24.5 9.4 %collective-permute-start.6 = (bf16[4,128,256]{2,1,0:T(8,128)(2,1)S(1)}, bf16[4,128,256]{2,1,0:T(8,128)(2,1)S(1)}, u32[]{:S(2)}, u32[]{:S(2)}) collective-permute-start(bf16[4,128,256]{2,1,0:T(8,128)(2,1)S(1)} %get-tuple-element.31.own), channel_id=1, source_target_pairs={{0,4},{4,0},{8,12},{12,8},{16,20},{20,16},{24,28},{28,24},{1,5},{5... | collective-permute-start | bytes 786440 | tf_op jit(solution)/shard_map/ppermute | solution.py:274
  34.2 7.2 %collective-permute-start.7 = (bf16[4,128,128]{2,1,0:T(8,128)(2,1)S(1)}, bf16[4,128,128]{2,1,0:T(8,128)(2,1)S(1)}, u32[]{:S(2)}, u32[]{:S(2)}) collective-permute-start(bf16[4,128,128]{2,1,0:T(8,128)(2,1)S(1)} %get-tuple-element.34.b), channel_id=1, source_target_pairs={{0,8},{4,12},{8,16},{12,20},{16,24},{20,28},{1,9},{5,13},{9,17},{1... | collective-permute-start | bytes 393224 | tf_op jit(solution)/shard_map/ppermute | solution.py:279
  37.9 8.9 %collective-permute-start.8 = (bf16[4,128,128]{2,1,0:T(8,128)(2,1)S(1)}, bf16[4,128,128]{2,1,0:T(8,128)(2,1)S(1)}, u32[]{:S(2)}, u32[]{:S(2)}) collective-permute-start(bf16[4,128,128]{2,1,0:T(8,128)(2,1)S(1)} %get-tuple-element.35.t), channel_id=1, source_target_pairs={{0,8},{4,12},{8,16},{12,20},{16,24},{20,28},{1,9},{5,13},{9,17},{1... | collective-permute-start | bytes 393224 | tf_op jit(solution)/shard_map/ppermute | solution.py:279
  41.6 8.0 %collective-permute-start.9 = (bf16[4,128,128]{2,1,0:T(8,128)(2,1)S(1)}, bf16[4,128,128]{2,1,0:T(8,128)(2,1)S(1)}, u32[]{:S(2)}, u32[]{:S(2)}) collective-permute-start(bf16[4,128,128]{2,1,0:T(8,128)(2,1)S(1)} %shard_map.70), channel_id=1, source_target_pairs={{0,16},{4,20},{8,24},{12,28},{16,0},{20,4},{24,8},{28,12},{1,17},{... | collective-permute-start | bytes 393224 | tf_op jit(solution)/shard_map/ppermute | solution.py:274
  46.5 4.9 %copy-start = (bf16[512,2048]{1,0:T(8,128)(2,1)S(1)}, bf16[512,2048]{1,0:T(8,128)(2,1)}, u32[]{:S(2)}) copy-start(bf16[512,2048]{1,0:T(8,128)(2,1)} %w_own.3) | copy-start | bytes 6291460
  50.0 1.4 %collective-permute-start.10 = (bf16[128,512]{1,0:T(8,128)(2,1)S(1)}, bf16[128,512]{1,0:T(8,128)(2,1)S(1)}, u32[]{:S(2)}, u32[]{:S(2)}) collective-permute-start(bf16[128,512]{1,0:T(8,128)(2,1)S(1)} %get-tuple-element.40), channel_id=1, source_target_pairs={{0,1},{1,0},{2,3},{3,2},{4,5},{5,4},{6,7},{7,6},{8,9},{9,8},{10,11... | collective-permute-start | bytes 393224 | tf_op jit(solution)/shard_map/ppermute | solution.py:274
  52.2 8.4 %collective-permute-start.12 = (bf16[64,2048]{1,0:T(8,128)(2,1)S(1)}, bf16[64,2048]{1,0:T(8,128)(2,1)S(1)}, u32[]{:S(2)}, u32[]{:S(2)}) collective-permute-start(bf16[64,2048]{1,0:T(8,128)(2,1)S(1)} %shard_map.73), channel_id=1, source_target_pairs={{0,2},{1,3},{2,0},{3,1},{4,6},{5,7},{6,4},{7,5},{8,10},{9,11},{10,... | collective-permute-start | bytes 786440 | tf_op jit(solution)/shard_map/ppermute | solution.py:274

commit v3 on v2

--- a/solution.py
+++ b/solution.py
@@ -47,7 +47,9 @@
     return jnp.exp(jnp.minimum(gap, 0.0))
 
 
-def gates_kernel(logits, rows, cols, decays):
+def gates_kernel(logits, x_any, rows, cols, decays, tail, sem):
+    copy = pltpu.make_async_copy(x_any.at[pl.ds(x_any.shape[0] - HALO, HALO), :], tail, sem)
+    copy.start()
     toks = logits.shape[2]
     blocks = toks // HALF
     x = logits[0]
@@ -72,6 +74,7 @@
                 m = m * bcols[a * HALF : (a + 1) * HALF, j : j + 1]
                 decays[j, i] = jnp.where(below, m, 0.0) if a == b else m
                 i += 1
+    copy.wait()
 
 
 def keys_kernel(*refs, n_head, key_heads, ratio):
@@ -82,13 +85,14 @@
     toks = part * n_head
     blocks = toks // HALF
     heads = key_heads * ratio
-    x_out[0:HALO, :] = jnp.where(me % 2 == 1, halo[part - HALO :, :], halo_core[part - HALO :, :])
+    direct = (me % 2 == 1) != (me >= n_head - 2)
+    x_out[0:HALO, :] = jnp.where(direct, halo[...], halo_core[...])
     for s in range(n_head):
         at = pl.multiple_of(HALO + (me ^ s) * part, 16)
         x_out[pl.ds(at, part), :] = pieces[s][...]
-    group = 2 * DK + 2 * ratio * DV
+    width = DK + ratio * DV
     for g in range(key_heads):
-        proj = dot(x_out[...], w[:, g * group + DK : g * group + 2 * DK + ratio * DV])
+        proj = dot(x_out[...], w[:, g * width : (g + 1) * width])
         proj = proj.astype(BF16).astype(F32)
         for t in range(1 + ratio):
             padded[g * (1 + ratio) + t] = proj[:, t * 128 : (t + 1) * 128]
@@ -156,16 +160,15 @@
         s_out[j, :, DK:] = s[:, DK:].astype(BF16)
 
 
-def queries_kernel(x, w, cw, cols, rows, keys, ys, gain, q_out, o_out, g_out, padded, *, key_heads, ratio):
+def queries_kernel(x, wq, wz, cw, cols, rows, keys, ys, gain, q_out, o_out, g_out, padded, *, key_heads, ratio):
     toks = x.shape[0] - HALO
     blocks = toks // HALF
-    group = 2 * DK + 2 * ratio * DV
     ri = lax.broadcasted_iota(jnp.int32, (HALF, HALF), 0)
     ci = lax.broadcasted_iota(jnp.int32, (HALF, HALF), 1)
     upto = ri >= ci
     for g in range(key_heads):
-        padded[g] = dot(x[...], w[:, g * group : g * group + DK]).astype(BF16).astype(F32)
-        proj = dot(x[HALO:, :], w[:, g * group + 2 * DK + ratio * DV : (g + 1) * group]).astype(BF16).astype(F32)
+        padded[g] = dot(x[...], wq[:, g * DK : (g + 1) * DK]).astype(BF16).astype(F32)
+        proj = dot(x[HALO:, :], wz[:, g * ratio * DV : (g + 1) * ratio * DV]).astype(BF16).astype(F32)
         for r in range(ratio):
             z = proj[:, r * DV : (r + 1) * DV]
             g_out[g * ratio + r] = gain[...] * silu(z)
@@ -251,13 +254,13 @@
     out[...] = (dot(a, w_own[...]) + dot(b, w_got[...])).astype(out.dtype)
 
 
-def call(body, out_shape, args, scratch=(), flops=0, **static):
+def call(body, out_shape, args, scratch=(), flops=0, any_space=(), **static):
     nbytes = sum(a.size * a.dtype.itemsize for a in args)
     vmem = pl.BlockSpec(memory_space=pltpu.VMEM)
     return pl.pallas_call(
         functools.partial(body, **static),
         out_shape=out_shape,
-        in_specs=[vmem] * len(args),
+        in_specs=[pl.BlockSpec(memory_space=pl.ANY) if i in any_space else vmem for i in range(len(args))],
         out_specs=jax.tree.map(lambda _: vmem, out_shape),
         scratch_shapes=list(scratch),
         compiler_params=pltpu.CompilerParams(vmem_limit_bytes=VMEM_BYTES),
@@ -294,24 +297,33 @@
         for s in range(0, n_head, 2 * step):
             pieces[s + step] = xor_sent(pieces[s], "head", step)
         step //= 2
-    halo = None
-    for h in range(1, n_head, 2):
-        perm = [((c - 1) * n_head + n_head - 1, c * n_head + h) for c in range(1, n_ctx)]
-        got = lax.ppermute(layer_in, ctx_head, perm)
-        halo = got if halo is None else halo + got
-    halo_core = xor_sent(halo, "head", 1)
-    w_in = in_proj.reshape(width, key_heads * group)
     blocks = toks // HALF
-    rows, cols, decays = call(
+    rows, cols, decays, tail = call(
         gates_kernel,
         (
             shaped((heads, toks), F32),
             shaped((toks, 2 * heads), F32),
             shaped((heads, blocks * (blocks + 1) // 2, HALF, HALF), F32),
+            shaped((HALO, width), BF16),
         ),
-        [gate_logits],
+        [gate_logits, layer_in],
+        [pltpu.SemaphoreType.DMA],
+        any_space=(1,),
     )
-    w_other = xor_sent(out_proj, "head", 1)
+    me = lax.axis_index("head")
+    halo = jnp.zeros_like(tail)
+    for h in range(1, n_head, 2):
+        target = h if h < n_head - 1 else h - 1
+        perm = []
+        for c in range(1, n_ctx):
+            source, sink = (c - 1) * n_head + n_head - 1, c * n_head + target
+            perm += [(source, sink), (sink, source)]
+        halo = jnp.where(me == target, lax.ppermute(tail, ctx_head, perm), halo)
+    halo_core = xor_sent(halo, "head", 1)
+    v_end = 2 * DK + ratio * DV
+    w_kv = in_proj[:, :, DK:v_end].reshape(width, key_heads * (v_end - DK))
+    w_q = in_proj[:, :, 0:DK].reshape(width, key_heads * DK)
+    w_z = in_proj[:, :, v_end:].reshape(width, heads * DV)
 
     state = shaped((heads, DK, DV), BF16)
     s_own, ys, keys, x_full = call(
@@ -322,7 +334,7 @@
             shaped((key_heads, toks, DK), BF16),
             shaped((HALO + toks, width), BF16),
         ),
-        [*pieces, halo, halo_core, w_in, conv_weight, cols, rows, decays],
+        [*pieces, halo, halo_core, w_kv, conv_weight, cols, rows, decays],
         [pltpu.VMEM((key_heads * (1 + ratio), HALO + toks, 128), F32)],
         flops=2 * toks * width * group,
         n_head=n_head,
@@ -330,12 +342,13 @@
         ratio=ratio,
     )
     got = xor_sent(s_own, "ctx", 1)
+    w_other = xor_sent(lax.optimization_barrier((out_proj, s_own))[0], "head", 1)
     q_shape = shaped((heads, toks, DK), BF16)
     o_shape = shaped((heads, toks, DV), F32)
     q, o, gate = call(
         queries_kernel,
         (q_shape, o_shape, o_shape),
-        [x_full, w_in, conv_weight, cols, rows, keys, ys, norm_gain[None, :]],
+        [x_full, w_q, w_z, conv_weight, cols, rows, keys, ys, norm_gain[None, :]],
         [pltpu.VMEM((key_heads, HALO + toks, 128), F32)],
         flops=2 * toks * width * group,
         key_heads=key_heads,

time: 61.7 us -> 59.9 us (0.971)
  starting transfers between devices: 27.2 us -> 23.6 us
  Pallas kernels: 11 us -> 12.9 us
  waiting for transfers between devices: 17.3 us -> 16.3 us
  local copies, waits for them, and re-layouts: 4.9 us -> 5.65 us
    ppermute x9, starting transfers between devices: 18.6 us -> 14.2 us  [xor_sent(): return lax.ppermute(value, axis, [(i, i ^ step) for i in range(count)])]
    slice x0 -> x6, local copies, waits for them, and re-layouts: none -> 3.62 us  [the longest x2 1.59 us: local(): w_z = in_proj[:, :, v_end:].reshape(width, heads * DV)]
    unnamed x11, local copies, waits for them, and re-layouts: 4.9 us -> 2.03 us
    pallas_call x10, Pallas kernels: 11 us -> 12.9 us  [call(): pl.pallas_call(functools.partial(body, **static), out_shape=out_shape, in...]
    ppermute x9, waiting for transfers between devices: 17.3 us -> 16.3 us  [xor_sent(): return lax.ppermute(value, axis, [(i, i ^ step) for i in range(count)])]
    ppermute x2, starting transfers between devices: 7.22 us -> 8.11 us  [passed_along(): lax.ppermute(value, axis, [(i, i + steps) for i in range(count - steps)])]
  transfers between devices with their start and end apart: 13 -> 13, of which waited for: 4 -> 4; matrix products, arithmetic and copies ran while one was open for 7% -> 2% of each run, Pallas kernels for 17% -> 10%
where the time goes in v3:
time: 59.9 us; the launch traced here: 59.5 us
  starting transfers between devices  23.6 us (39%)
  waiting for transfers between devices  16.3 us (27%)
  Pallas kernels  12.9 us (22%)
  local copies, waits for them, and re-layouts  5.65 us (9%)
  other arithmetic  0.76 us (1%)
    ppermute x9, waiting for transfers between devices, xor_sent(): return lax.ppermute(value, axis, [(i, i ^ step) for i in range(count)])  16.3 us
    ppermute x9, starting transfers between devices, xor_sent(): return lax.ppermute(value, axis, [(i, i ^ step) for i in range(count)])  14.2 us
    pallas_call x10, Pallas kernels, call(): pl.pallas_call(functools.partial(body, **static), out_shape=out_shape, in...  12.9 us
    ppermute x2, starting transfers between devices, passed_along(): lax.ppermute(value, axis, [(i, i + steps) for i in range(count - steps)])  8.11 us
    unnamed x11, local copies, waits for them, and re-layouts  2.03 us
    slice x2, local copies, waits for them, and re-layouts, local(): w_z = in_proj[:, :, v_end:].reshape(width, heads * DV)  1.59 us
    ppermute x2, starting transfers between devices, local(): halo = jnp.where(me == target, lax.ppermute(tail, ctx_head, perm), halo)  1.33 us
    slice x2, local copies, waits for them, and re-layouts, local(): w_kv = in_proj[:, :, DK:v_end].reshape(width, key_heads * (v_end - DK))  1.32 us
  transfers between devices with their start and end apart: 13, of which 4 were waited for; matrix products, arithmetic and copies ran while one was open for 2% of the time, Pallas kernels for 10%

profile of v3, /device:TPU:0, one launch (start us, length us, event | category | flops | bytes accessed | tf_op | source)
XLA Modules:
  0.0 59.5 jit_solution(16259676789981511328)
XLA Ops:
  0.0 3.0 %collective-permute-start.1 = (bf16[64,2048]{1,0:T(8,128)(2,1)}, bf16[64,2048]{1,0:T(8,128)(2,1)S(1)}, u32[]{:S(2)}, u32[]{:S(2)}) collective-permute-start(bf16[64,2048]{1,0:T(8,128)(2,1)} %refs_0_.1), channel_id=1, source_target_pairs={{0,2},{1,3},{2,0},{3,1},{4,6},{5,7},{6,4},{7,5},{8,10},{9,11},{10,... | collective-permute-start | bytes 786440 | tf_op jit(solution)/shard_map/ppermute | solution.py:277
  3.0 0.7 %copy-done.2 = f32[2,4,256]{2,1,0:T(4,128)S(1)} copy-done((f32[2,4,256]{2,1,0:T(4,128)S(1)}, f32[2,4,256]{2,1,0:T(4,128)}, u32[]{:S(2)}) %copy-start.2) | copy-done | bytes 8216
  3.7 1.8 %shard_map.64 = (f32[4,256]{1,0:T(4,128)S(1)}, f32[256,8]{1,0:T(8,128)S(1)}, f32[4,3,128,128]{3,2,1,0:T(8,128)S(1)}, bf16[16,2048]{1,0:T(8,128)(2,1)S(1)}) custom-call(f32[2,4,256]{2,1,0:T(4,128)S(1)} %copy-done.2, bf16[64,2048]{1,0:T(8,128)(2,1)} %refs_0_.1), custom_call_target="tpu_custom_call" | custom-call | bytes 270336 | tf_op jit(solution)/shard_map/pallas_call | solution.py:260
  5.5 0.7 %collective-permute-start.3 = (bf16[16,2048]{1,0:T(8,128)(2,1)S(1)}, bf16[16,2048]{1,0:T(8,128)(2,1)S(1)}, u32[]{:S(2)}, u32[]{:S(2)}) collective-permute-start(bf16[16,2048]{1,0:T(8,128)(2,1)S(1)} %get-tuple-element.25), channel_id=1, source_target_pairs={{3,6},{6,3},{7,10},{10,7},{11,14},{14,11},{15,18},{18,15},{19,22},... | collective-permute-start | bytes 196616 | tf_op jit(solution)/shard_map/ppermute | solution.py:321
  6.1 0.7 %collective-permute-start.4 = (bf16[16,2048]{1,0:T(8,128)(2,1)S(1)}, bf16[16,2048]{1,0:T(8,128)(2,1)S(1)}, u32[]{:S(2)}, u32[]{:S(2)}) collective-permute-start(bf16[16,2048]{1,0:T(8,128)(2,1)S(1)} %get-tuple-element.25), channel_id=1, source_target_pairs={{3,5},{5,3},{7,9},{9,7},{11,13},{13,11},{15,17},{17,15},{19,21},{2... | collective-permute-start | bytes 196616 | tf_op jit(solution)/shard_map/ppermute | solution.py:321
  6.9 2.6 %collective-permute-done.1.refs_2_ = bf16[64,2048]{1,0:T(8,128)(2,1)S(1)} collective-permute-done((bf16[64,2048]{1,0:T(8,128)(2,1)}, bf16[64,2048]{1,0:T(8,128)(2,1)S(1)}, u32[]{:S(2)}, u32[]{:S(2)}) %collective-permute-start.1) | collective-permute-done | bytes 262176 | tf_op jit(solution)/shard_map/ppermute | solution.py:277
  10.1 1.3 %slice-done = bf16[2048,2,384]{2,1,0:T(2,128)(2,1)S(1)} async-done(((bf16[2048,2,768]{2,1,0:T(2,128)(2,1)}), bf16[2048,2,384]{2,1,0:T(2,128)(2,1)S(1)}, s32[]{:S(2)}) %slice-start) | async-done | bytes 3145752 | tf_op jit(solution)/shard_map/slice | solution.py:324
  11.4 0.7 %copy.7 = bf16[256,8,2,384]{3,1,2,0:T(8,128)(2,1)S(1)} copy(bf16[256,8,2,384]{3,2,1,0:T(2,128)(2,1)S(1)} %bitcast.13) | data formatting | bytes 6291456
  12.1 6.1 %shard_map.65 = (bf16[4,128,256]{2,1,0:T(8,128)(2,1)S(1)}, bf16[4,256,256]{2,1,0:T(8,128)(2,1)S(1)}, bf16[2,256,128]{2,1,0:T(8,128)(2,1)S(1)}, bf16[272,2048]{1,0:T(8,128)(2,1)S(1)}) custom-call(bf16[64,2048]{1,0:T(8,128)(2,1)} %refs_0_.1, bf16[64,2048]{1,0:T(8,128)(2,1)S(1)} %collective-permute-done.refs_1_, ...), custom_call_target="tpu_custom_call" | custom-call | flops 805306368 | bytes 5140480 | tf_op jit(solution)/shard_map/pallas_call | solution.py:260
  18.3 0.6 collective-permute-start.11
  18.8 4.2 %collective-permute-start.6 = (bf16[4,128,256]{2,1,0:T(8,128)(2,1)S(1)}, bf16[4,128,256]{2,1,0:T(8,128)(2,1)S(1)}, u32[]{:S(2)}, u32[]{:S(2)}) collective-permute-start(bf16[4,128,256]{2,1,0:T(8,128)(2,1)S(1)} %get-tuple-element.34.own), channel_id=1, source_target_pairs={{0,4},{4,0},{8,12},{12,8},{16,20},{20,16},{24,28},{28,24},{1,5},{5... | collective-permute-start | bytes 786440 | tf_op jit(solution)/shard_map/ppermute | solution.py:277
  23.1 6.5 %collective-permute-done.6.got = bf16[4,128,256]{2,1,0:T(8,128)(2,1)S(1)} collective-permute-done((bf16[4,128,256]{2,1,0:T(8,128)(2,1)S(1)}, bf16[4,128,256]{2,1,0:T(8,128)(2,1)S(1)}, u32[]{:S(2)}, u32[]{:S(2)}) %collective-permute-start.6) | collective-permute-done | bytes 262176 | tf_op jit(solution)/shard_map/ppermute | solution.py:277
  29.9 4.6 %collective-permute-start.7 = (bf16[4,128,128]{2,1,0:T(8,128)(2,1)S(1)}, bf16[4,128,128]{2,1,0:T(8,128)(2,1)S(1)}, u32[]{:S(2)}, u32[]{:S(2)}) collective-permute-start(bf16[4,128,128]{2,1,0:T(8,128)(2,1)S(1)} %get-tuple-element.37.b), channel_id=1, source_target_pairs={{0,8},{4,12},{8,16},{12,20},{16,24},{20,28},{1,9},{5,13},{9,17},{1... | collective-permute-start | bytes 393224 | tf_op jit(solution)/shard_map/ppermute | solution.py:282
  34.5 3.5 %collective-permute-start.8 = (bf16[4,128,128]{2,1,0:T(8,128)(2,1)S(1)}, bf16[4,128,128]{2,1,0:T(8,128)(2,1)S(1)}, u32[]{:S(2)}, u32[]{:S(2)}) collective-permute-start(bf16[4,128,128]{2,1,0:T(8,128)(2,1)S(1)} %get-tuple-element.38.t), channel_id=1, source_target_pairs={{0,8},{4,12},{8,16},{12,20},{16,24},{20,28},{1,9},{5,13},{9,17},{1... | collective-permute-start | bytes 393224 | tf_op jit(solution)/shard_map/ppermute | solution.py:282
  38.2 2.8 %collective-permute-start.9 = (bf16[4,128,128]{2,1,0:T(8,128)(2,1)S(1)}, bf16[4,128,128]{2,1,0:T(8,128)(2,1)S(1)}, u32[]{:S(2)}, u32[]{:S(2)}) collective-permute-start(bf16[4,128,128]{2,1,0:T(8,128)(2,1)S(1)} %shard_map.70), channel_id=1, source_target_pairs={{0,16},{4,20},{8,24},{12,28},{16,0},{20,4},{24,8},{28,12},{1,17},{... | collective-permute-start | bytes 393224 | tf_op jit(solution)/shard_map/ppermute | solution.py:277
  41.0 1.6 %slice-done.1 = bf16[2048,2,256]{2,1,0:T(2,128)(2,1)S(1)} async-done(((bf16[2048,2,768]{2,1,0:T(2,128)(2,1)}), bf16[2048,2,256]{2,1,0:T(2,128)(2,1)S(1)}, s32[]{:S(2)}) %slice-start.1) | async-done | bytes 2097176 | tf_op jit(solution)/shard_map/slice | solution.py:326
  43.1 0.7 %slice-done.2 = bf16[2048,2,128]{2,1,0:T(2,128)(2,1)S(1)} async-done(((bf16[2048,2,768]{2,1,0:T(2,128)(2,1)}), bf16[2048,2,128]{2,1,0:T(2,128)(2,1)S(1)}, s32[]{:S(2)}) %slice-start.2) | async-done | bytes 1048600 | tf_op jit(solution)/shard_map/slice | solution.py:325
  44.0 1.9 %shard_map.66 = (bf16[4,256,128]{2,1,0:T(8,128)(2,1)S(1)}, f32[4,256,128]{2,1,0:T(8,128)S(1)}, f32[4,256,128]{2,1,0:T(8,128)S(1)}) custom-call(bf16[272,2048]{1,0:T(8,128)(2,1)S(1)} %get-tuple-element.29.x, bf16[2048,256]{1,0:T(8,128)(2,1)S(1)} %bitcast.11, bf16[2048,512]{1,0:T(8,128)(2,1)S(1)} %bitcast.10, f32[4,2,512]{2,1,0:T(2,128)S(1)} %copy-done.1, ...), custom_call_target="tpu_custom_call" | custom-call | flops 805306368 | bytes 4944384 | tf_op jit(solution)/shard_map/pallas_call | solution.py:260
  47.0 1.3 %collective-permute-done.10.got = bf16[128,512]{1,0:T(8,128)(2,1)S(1)} collective-permute-done((bf16[128,512]{1,0:T(8,128)(2,1)S(1)}, bf16[128,512]{1,0:T(8,128)(2,1)S(1)}, u32[]{:S(2)}, u32[]{:S(2)}) %collective-permute-start.10) | collective-permute-done | bytes 131104 | tf_op jit(solution)/shard_map/ppermute | solution.py:277
  48.3 0.9 %shard_map.73 = bf16[64,2048]{1,0:T(8,128)(2,1)S(1)} custom-call(bf16[128,512]{1,0:T(8,128)(2,1)S(1)} %get-tuple-element.42.own, bf16[128,512]{1,0:T(8,128)(2,1)S(1)} %collective-permute-done.10.got, bf16[512,2048]{1,0:T(8,128)(2,1)S(1)} %copy-done, bf16[512,2048]{1,0:T(8,128)(2,1)S(1)} %collective-permute-done.11.w_got), custom_call_target="tpu_custom_call" | custom-call | flops 536870912 | bytes 4456448 | tf_op jit(solution)/shard_map/pallas_call | solution.py:260
  49.2 2.9 %collective-permute-start.12 = (bf16[64,2048]{1,0:T(8,128)(2,1)S(1)}, bf16[64,2048]{1,0:T(8,128)(2,1)S(1)}, u32[]{:S(2)}, u32[]{:S(2)}) collective-permute-start(bf16[64,2048]{1,0:T(8,128)(2,1)S(1)} %shard_map.73), channel_id=1, source_target_pairs={{0,2},{1,3},{2,0},{3,1},{4,6},{5,7},{6,4},{7,5},{8,10},{9,11},{10,... | collective-permute-start | bytes 786440 | tf_op jit(solution)/shard_map/ppermute | solution.py:277
  52.1 0.9 %shard_map.72 = f32[64,2048]{1,0:T(8,128)S(1)} custom-call(bf16[128,512]{1,0:T(8,128)(2,1)S(1)} %get-tuple-element.42.own, bf16[128,512]{1,0:T(8,128)(2,1)S(1)} %collective-permute-done.10.got, bf16[512,2048]{1,0:T(8,128)(2,1)S(1)} %copy-done, bf16[512,2048]{1,0:T(8,128)(2,1)S(1)} %collective-permute-done.11.w_got), custom_call_target="tpu_custom_call" | custom-call | flops 536870912 | bytes 4456448 | tf_op jit(solution)/shard_map/pallas_call | solution.py:260
  53.0 5.8 %collective-permute-done.12 = bf16[64,2048]{1,0:T(8,128)(2,1)S(1)} collective-permute-done((bf16[64,2048]{1,0:T(8,128)(2,1)S(1)}, bf16[64,2048]{1,0:T(8,128)(2,1)S(1)}, u32[]{:S(2)}, u32[]{:S(2)}) %collective-permute-start.12) | collective-permute-done | bytes 262176 | tf_op jit(solution)/shard_map/ppermute | solution.py:277
  58.7 0.8 %add_convert_fusion = bf16[64,2048]{1,0:T(8,128)(2,1)} fusion(f32[64,2048]{1,0:T(8,128)S(1)} %shard_map.72, bf16[64,2048]{1,0:T(8,128)(2,1)S(1)} %collective-permute-done.12), kind=kLoop, calls=%fused_computation.1 | loop fusion | flops 393216 | bytes 1048576 | tf_op jit(solution)/shard_map/convert_element_type | solution.py:395
  (31 shorter events, 2.8 us)
Async XLA Ops:
  0.0 9.5 %collective-permute-start.1 = (bf16[64,2048]{1,0:T(8,128)(2,1)}, bf16[64,2048]{1,0:T(8,128)(2,1)S(1)}, u32[]{:S(2)}, u32[]{:S(2)}) collective-permute-start(bf16[64,2048]{1,0:T(8,128)(2,1)} %refs_0_.1), channel_id=1, source_target_pairs={{0,2},{1,3},{2,0},{3,1},{4,6},{5,7},{6,4},{7,5},{8,10},{9,11},{10,... | collective-permute-start | bytes 786440 | tf_op jit(solution)/shard_map/ppermute | solution.py:277
  3.0 0.7 %copy-start.2 = (f32[2,4,256]{2,1,0:T(4,128)S(1)}, f32[2,4,256]{2,1,0:T(4,128)}, u32[]{:S(2)}) copy-start(f32[2,4,256]{2,1,0:T(4,128)} %logits.1) | copy-start | bytes 24580
  5.5 4.0 %collective-permute-start.3 = (bf16[16,2048]{1,0:T(8,128)(2,1)S(1)}, bf16[16,2048]{1,0:T(8,128)(2,1)S(1)}, u32[]{:S(2)}, u32[]{:S(2)}) collective-permute-start(bf16[16,2048]{1,0:T(8,128)(2,1)S(1)} %get-tuple-element.25), channel_id=1, source_target_pairs={{3,6},{6,3},{7,10},{10,7},{11,14},{14,11},{15,18},{18,15},{19,22},... | collective-permute-start | bytes 196616 | tf_op jit(solution)/shard_map/ppermute | solution.py:321
  6.1 3.4 %collective-permute-start.4 = (bf16[16,2048]{1,0:T(8,128)(2,1)S(1)}, bf16[16,2048]{1,0:T(8,128)(2,1)S(1)}, u32[]{:S(2)}, u32[]{:S(2)}) collective-permute-start(bf16[16,2048]{1,0:T(8,128)(2,1)S(1)} %get-tuple-element.25), channel_id=1, source_target_pairs={{3,5},{5,3},{7,9},{9,7},{11,13},{13,11},{15,17},{17,15},{19,21},{2... | collective-permute-start | bytes 196616 | tf_op jit(solution)/shard_map/ppermute | solution.py:321
  6.8 5.3 %collective-permute-start = (bf16[64,2048]{1,0:T(8,128)(2,1)}, bf16[64,2048]{1,0:T(8,128)(2,1)S(1)}, u32[]{:S(2)}, u32[]{:S(2)}) collective-permute-start(bf16[64,2048]{1,0:T(8,128)(2,1)} %refs_0_.1), channel_id=1, source_target_pairs={{0,1},{1,0},{2,3},{3,2},{4,5},{5,4},{6,7},{7,6},{8,9},{9,8},{10,11... | collective-permute-start | bytes 786440 | tf_op jit(solution)/shard_map/ppermute | solution.py:277
  9.5 2.6 %collective-permute-start.2 = (bf16[64,2048]{1,0:T(8,128)(2,1)S(1)}, bf16[64,2048]{1,0:T(8,128)(2,1)S(1)}, u32[]{:S(2)}, u32[]{:S(2)}) collective-permute-start(bf16[64,2048]{1,0:T(8,128)(2,1)S(1)} %collective-permute-done.1.refs_2_), channel_id=1, source_target_pairs={{0,1},{1,0},{2,3},{3,2},{4,5},{5,4},{6,7},{7,6},{8,9},{9,8},{10,11... | collective-permute-start | bytes 786440 | tf_op jit(solution)/shard_map/ppermute | solution.py:277
  9.5 1.9 %slice-start = ((bf16[2048,2,768]{2,1,0:T(2,128)(2,1)}), bf16[2048,2,384]{2,1,0:T(2,128)(2,1)S(1)}, s32[]{:S(2)}) async-start(bf16[2048,2,768]{2,1,0:T(2,128)(2,1)} %param.7), calls=%async_computation | async-start | bytes 6291456 | tf_op jit(solution)/shard_map/slice | solution.py:324
  9.5 2.6 %collective-permute-start.5 = (bf16[16,2048]{1,0:T(8,128)(2,1)S(1)}, bf16[16,2048]{1,0:T(8,128)(2,1)S(1)}, u32[]{:S(2)}, u32[]{:S(2)}) collective-permute-start(bf16[16,2048]{1,0:T(8,128)(2,1)S(1)} %select_select_fusion.refs_4_), channel_id=1, source_target_pairs={{0,1},{1,0},{2,3},{3,2},{4,5},{5,4},{6,7},{7,6},{8,9},{9,8},{10,11... | collective-permute-start | bytes 196616 | tf_op jit(solution)/shard_map/ppermute | solution.py:277
  11.4 0.7 %copy-start.1 = (f32[4,2,512]{2,1,0:T(2,128)S(1)}, f32[4,2,512]{2,1,0:T(2,128)}, u32[]{:S(2)}) copy-start(f32[4,2,512]{2,1,0:T(2,128)} %cw.1) | copy-start | bytes 49156
  12.1 6.1 %copy-start = (bf16[512,2048]{1,0:T(8,128)(2,1)S(1)}, bf16[512,2048]{1,0:T(8,128)(2,1)}, u32[]{:S(2)}) copy-start(bf16[512,2048]{1,0:T(8,128)(2,1)} %w_own.3) | copy-start | bytes 6291460
  18.3 30.1 %collective-permute-start.11 = (bf16[512,2048]{1,0:T(8,128)(2,1)S(1)}, bf16[512,2048]{1,0:T(8,128)(2,1)S(1)}, u32[]{:S(2)}, u32[]{:S(2)}) collective-permute-start(bf16[512,2048]{1,0:T(8,128)(2,1)S(1)} %copy-done), channel_id=1, source_target_pairs={{0,1},{1,0},{2,3},{3,2},{4,5},{5,4},{6,7},{7,6},{8,9},{9,8},{10,11... | collective-permute-start | bytes 6291464 | tf_op jit(solution)/shard_map/ppermute | solution.py:277
  18.8 10.8 %collective-permute-start.6 = (bf16[4,128,256]{2,1,0:T(8,128)(2,1)S(1)}, bf16[4,128,256]{2,1,0:T(8,128)(2,1)S(1)}, u32[]{:S(2)}, u32[]{:S(2)}) collective-permute-start(bf16[4,128,256]{2,1,0:T(8,128)(2,1)S(1)} %get-tuple-element.34.own), channel_id=1, source_target_pairs={{0,4},{4,0},{8,12},{12,8},{16,20},{20,16},{24,28},{28,24},{1,5},{5... | collective-permute-start | bytes 786440 | tf_op jit(solution)/shard_map/ppermute | solution.py:277
  29.9 8.1 %collective-permute-start.7 = (bf16[4,128,128]{2,1,0:T(8,128)(2,1)S(1)}, bf16[4,128,128]{2,1,0:T(8,128)(2,1)S(1)}, u32[]{:S(2)}, u32[]{:S(2)}) collective-permute-start(bf16[4,128,128]{2,1,0:T(8,128)(2,1)S(1)} %get-tuple-element.37.b), channel_id=1, source_target_pairs={{0,8},{4,12},{8,16},{12,20},{16,24},{20,28},{1,9},{5,13},{9,17},{1... | collective-permute-start | bytes 393224 | tf_op jit(solution)/shard_map/ppermute | solution.py:282
  34.5 11.7 %collective-permute-start.8 = (bf16[4,128,128]{2,1,0:T(8,128)(2,1)S(1)}, bf16[4,128,128]{2,1,0:T(8,128)(2,1)S(1)}, u32[]{:S(2)}, u32[]{:S(2)}) collective-permute-start(bf16[4,128,128]{2,1,0:T(8,128)(2,1)S(1)} %get-tuple-element.38.t), channel_id=1, source_target_pairs={{0,8},{4,12},{8,16},{12,20},{16,24},{20,28},{1,9},{5,13},{9,17},{1... | collective-permute-start | bytes 393224 | tf_op jit(solution)/shard_map/ppermute | solution.py:282
  38.2 8.3 %collective-permute-start.9 = (bf16[4,128,128]{2,1,0:T(8,128)(2,1)S(1)}, bf16[4,128,128]{2,1,0:T(8,128)(2,1)S(1)}, u32[]{:S(2)}, u32[]{:S(2)}) collective-permute-start(bf16[4,128,128]{2,1,0:T(8,128)(2,1)S(1)} %shard_map.70), channel_id=1, source_target_pairs={{0,16},{4,20},{8,24},{12,28},{16,0},{20,4},{24,8},{28,12},{1,17},{... | collective-permute-start | bytes 393224 | tf_op jit(solution)/shard_map/ppermute | solution.py:277
  41.0 1.6 %slice-start.1 = ((bf16[2048,2,768]{2,1,0:T(2,128)(2,1)}), bf16[2048,2,256]{2,1,0:T(2,128)(2,1)S(1)}, s32[]{:S(2)}) async-start(bf16[2048,2,768]{2,1,0:T(2,128)(2,1)} %param.7), calls=%async_computation.1 | async-start | bytes 4194304 | tf_op jit(solution)/shard_map/slice | solution.py:326
  42.6 1.2 %slice-start.2 = ((bf16[2048,2,768]{2,1,0:T(2,128)(2,1)}), bf16[2048,2,128]{2,1,0:T(2,128)(2,1)S(1)}, s32[]{:S(2)}) async-start(bf16[2048,2,768]{2,1,0:T(2,128)(2,1)} %param.7), calls=%async_computation.2 | async-start | bytes 2097152 | tf_op jit(solution)/shard_map/slice | solution.py:325
  43.1 0.9 %copy-start.3 = (f32[128]{0:T(128)S(1)}, f32[128]{0:T(128)}, u32[]{:S(2)}) copy-start(f32[128]{0:T(128)} %param.10) | copy-start | bytes 1540
  46.9 1.4 %collective-permute-start.10 = (bf16[128,512]{1,0:T(8,128)(2,1)S(1)}, bf16[128,512]{1,0:T(8,128)(2,1)S(1)}, u32[]{:S(2)}, u32[]{:S(2)}) collective-permute-start(bf16[128,512]{1,0:T(8,128)(2,1)S(1)} %get-tuple-element.43), channel_id=1, source_target_pairs={{0,1},{1,0},{2,3},{3,2},{4,5},{5,4},{6,7},{7,6},{8,9},{9,8},{10,11... | collective-permute-start | bytes 393224 | tf_op jit(solution)/shard_map/ppermute | solution.py:277
  49.2 9.5 %collective-permute-start.12 = (bf16[64,2048]{1,0:T(8,128)(2,1)S(1)}, bf16[64,2048]{1,0:T(8,128)(2,1)S(1)}, u32[]{:S(2)}, u32[]{:S(2)}) collective-permute-start(bf16[64,2048]{1,0:T(8,128)(2,1)S(1)} %shard_map.73), channel_id=1, source_target_pairs={{0,2},{1,3},{2,0},{3,1},{4,6},{5,7},{6,4},{7,5},{8,10},{9,11},{10,... | collective-permute-start | bytes 786440 | tf_op jit(solution)/shard_map/ppermute | solution.py:277

commit v4 on v3

--- a/solution.py
+++ b/solution.py
@@ -47,9 +47,11 @@
     return jnp.exp(jnp.minimum(gap, 0.0))
 
 
-def gates_kernel(logits, x_any, rows, cols, decays, tail, sem):
-    copy = pltpu.make_async_copy(x_any.at[pl.ds(x_any.shape[0] - HALO, HALO), :], tail, sem)
-    copy.start()
+def gates_kernel(logits, x_any, rows, cols, decays, tail, x_own, sems):
+    tail_copy = pltpu.make_async_copy(x_any.at[pl.ds(x_any.shape[0] - HALO, HALO), :], tail, sems.at[0])
+    own_copy = pltpu.make_async_copy(x_any, x_own, sems.at[1])
+    tail_copy.start()
+    own_copy.start()
     toks = logits.shape[2]
     blocks = toks // HALF
     x = logits[0]
@@ -74,12 +76,13 @@
                 m = m * bcols[a * HALF : (a + 1) * HALF, j : j + 1]
                 decays[j, i] = jnp.where(below, m, 0.0) if a == b else m
                 i += 1
-    copy.wait()
+    tail_copy.wait()
+    own_copy.wait()
 
 
 def keys_kernel(*refs, n_head, key_heads, ratio):
     pieces = refs[:n_head]
-    halo, halo_core, w, cw, cols, rows, decays, s_out, y_out, k_out, x_out, padded = refs[n_head:]
+    halo, halo_core, w, cw, cols, rows, decays, s_keep, s_send, y_out, k_out, x_out, padded, s_all = refs[n_head:]
     me = lax.axis_index("head")
     part = pieces[0].shape[0]
     toks = part * n_head
@@ -156,8 +159,12 @@
         last = crow[:, toks - 1 : toks]
         kd = (kts[j // ratio] * jnp.exp(last - crow)).astype(BF16)
         s = dot(kd, y)
-        s_out[j, :, 0:DK] = (eye * jnp.exp(last) - s[:, 0:DK]).astype(BF16)
-        s_out[j, :, DK:] = s[:, DK:].astype(BF16)
+        s_all[j, :, 0:DK] = (eye * jnp.exp(last) - s[:, 0:DK]).astype(BF16)
+        s_all[j, :, DK:] = s[:, DK:].astype(BF16)
+    odd = lax.axis_index("ctx") % 2
+    half = heads // 2
+    s_keep[...] = s_all[pl.ds(odd * half, half)]
+    s_send[...] = s_all[pl.ds((1 - odd) * half, half)]
 
 
 def queries_kernel(x, wq, wz, cw, cols, rows, keys, ys, gain, q_out, o_out, g_out, padded, *, key_heads, ratio):
@@ -198,46 +205,60 @@
                 o_out[j, at, :] = acc[:, DK:]
 
 
-def pair_kernel(own, got, b_out, t_out):
-    odd = lax.axis_index("ctx") % 2 == 1
+def placed(step):
+    return lax.axis_index("ctx") // step % 2 == 1
+
+
+def join_kernel(own, got, out, *, step):
+    upper = placed(step)
     for j in range(own.shape[0]):
         mine, other = own[j], got[j]
-        later = jnp.where(odd, mine, other)
-        earlier = jnp.where(odd, other, mine)
-        prod = dot(later[:, 0:DK], earlier)
-        t_out[j] = prod[:, 0:DK].astype(BF16)
-        b_out[j] = (prod[:, DK:] + later[:, DK:].astype(F32)).astype(BF16)
-
-
-def pair_absorb_kernel(q, o, got, q_out, o_out):
-    odd = lax.axis_index("ctx") % 2 == 1
+        later = jnp.where(upper, mine, other)
+        earlier = jnp.where(upper, other, mine)
+        if out.shape[-1] == DV:
+            out[j] = (dot(later[:, 0:DK], earlier[:, DK:]) + later[:, DK:].astype(F32)).astype(BF16)
+        else:
+            prod = dot(later[:, 0:DK], earlier)
+            out[j, :, 0:DK] = prod[:, 0:DK].astype(BF16)
+            out[j, :, DK:] = (prod[:, DK:] + later[:, DK:].astype(F32)).astype(BF16)
+
+
+def prefix_kernel(before, got, out, *, step):
+    upper = placed(step)
+    for j in range(before.shape[0]):
+        prod = dot(before[j, :, 0:DK], got[j])
+        prod_t, prod_b = prod[:, 0:DK], prod[:, DK:] + before[j, :, DK:].astype(F32)
+        out[j, :, 0:DK] = jnp.where(upper, prod_t.astype(BF16), before[j, :, 0:DK])
+        out[j, :, DK:] = jnp.where(upper, prod_b.astype(BF16), before[j, :, DK:])
+
+
+def states_kernel(own, pair, before, got, keep, send, *, before_step, step):
+    odd = placed(1)
+    began = placed(before_step)
+    upper = placed(step)
+    for j in range(own.shape[0]):
+        t, b = before[j, :, 0:DK], before[j, :, DK:].astype(F32)
+        if before_step == 2:
+            last = got[j].astype(F32)
+            entered = jnp.where(began, dot(t, got[j]), last)
+            b = jnp.where(began, b, 0.0)
+        else:
+            entered = dot(t, got[j])
+        entered = jnp.where(upper, entered, 0.0) + b
+        first = jnp.where(odd, pair[j], own[j])
+        passed = dot(first[:, 0:DK], entered.astype(BF16)) + first[:, DK:].astype(F32)
+        keep[j] = jnp.where(odd, passed, entered).astype(BF16)
+        send[j] = jnp.where(odd, entered, passed).astype(BF16)
+
+
+def normed_kernel(q, o, own, got, gate, keep, send, scratch, *, n_head):
+    me = lax.axis_index("head")
+    odd = placed(1)
+    half = own.shape[0]
     for j in range(q.shape[0]):
-        prod = dot(q[j], got[j])
-        q_out[j] = jnp.where(odd, prod[:, 0:DK], q[j].astype(F32)).astype(BF16)
-        o_out[j] = o[j] + jnp.where(odd, prod[:, DK:], 0.0)
-
-
-def absorb_kernel(q, o, jb, jt, q_out, o_out):
-    for j in range(q.shape[0]):
-        o_out[j] = o[j] + dot(q[j], jb[j])
-        q_out[j] = dot(q[j], jt[j]).astype(BF16)
-
-
-def join_b_kernel(t, b, jb, b_out):
-    for j in range(t.shape[0]):
-        b_out[j] = (dot(t[j], jb[j]) + b[j].astype(F32)).astype(BF16)
-
-
-def join_t_kernel(t, jt, t_out):
-    for j in range(t.shape[0]):
-        t_out[j] = dot(t[j], jt[j]).astype(BF16)
-
-
-def normed_kernel(q, o, jb, gate, keep, send, scratch, *, n_head, last_step):
-    me = lax.axis_index("head")
-    upper = lax.axis_index("ctx") // last_step % 2 == 1
-    for j in range(q.shape[0]):
-        att = o[j] + jnp.where(upper, dot(q[j], jb[j]), 0.0)
+        mine, other = own[j % half], got[j % half]
+        state = jnp.where(odd, mine, other) if j >= half else jnp.where(odd, other, mine)
+        att = o[j] + dot(q[j], state)
         scale = lax.rsqrt(jnp.mean(att * att, axis=-1, keepdims=True) + EPSILON)
         scratch[:, j * DV : (j + 1) * DV] = (att * scale * gate[j]).astype(BF16)
     part = scratch.shape[0] // n_head
@@ -298,16 +319,17 @@
             pieces[s + step] = xor_sent(pieces[s], "head", step)
         step //= 2
     blocks = toks // HALF
-    rows, cols, decays, tail = call(
+    rows, cols, decays, tail, x_own = call(
         gates_kernel,
         (
             shaped((heads, toks), F32),
             shaped((toks, 2 * heads), F32),
             shaped((heads, blocks * (blocks + 1) // 2, HALF, HALF), F32),
             shaped((HALO, width), BF16),
+            shaped((part, width), BF16),
         ),
         [gate_logits, layer_in],
-        [pltpu.SemaphoreType.DMA],
+        [pltpu.SemaphoreType.DMA((2,))],
         any_space=(1,),
     )
     me = lax.axis_index("head")
@@ -325,59 +347,72 @@
     w_q = in_proj[:, :, 0:DK].reshape(width, key_heads * DK)
     w_z = in_proj[:, :, v_end:].reshape(width, heads * DV)
 
-    state = shaped((heads, DK, DV), BF16)
-    s_own, ys, keys, x_full = call(
+    half = heads // 2
+    pair_shape = shaped((half, DK, DK + DV), BF16)
+    state_shape = shaped((half, DK, DV), BF16)
+    s_keep, s_send, ys, keys, x_full = call(
         keys_kernel,
         (
-            shaped((heads, DK, DK + DV), BF16),
+            pair_shape,
+            pair_shape,
             shaped((heads, toks, DK + DV), BF16),
             shaped((key_heads, toks, DK), BF16),
             shaped((HALO + toks, width), BF16),
         ),
-        [*pieces, halo, halo_core, w_kv, conv_weight, cols, rows, decays],
-        [pltpu.VMEM((key_heads * (1 + ratio), HALO + toks, 128), F32)],
+        [x_own, *pieces[1:], halo, halo_core, w_kv, conv_weight, cols, rows, decays],
+        [
+            pltpu.VMEM((key_heads * (1 + ratio), HALO + toks, 128), F32),
+            pltpu.VMEM((heads, DK, DK + DV), BF16),
+        ],
         flops=2 * toks * width * group,
         n_head=n_head,
         key_heads=key_heads,
         ratio=ratio,
     )
-    got = xor_sent(s_own, "ctx", 1)
-    w_other = xor_sent(lax.optimization_barrier((out_proj, s_own))[0], "head", 1)
-    q_shape = shaped((heads, toks, DK), BF16)
+    s_pair = xor_sent(s_send, "ctx", 1)
+    w_other = xor_sent(lax.optimization_barrier((out_proj, s_keep))[0], "head", 1)
     o_shape = shaped((heads, toks, DV), F32)
     q, o, gate = call(
         queries_kernel,
-        (q_shape, o_shape, o_shape),
+        (shaped((heads, toks, DK), BF16), o_shape, o_shape),
         [x_full, w_q, w_z, conv_weight, cols, rows, keys, ys, norm_gain[None, :]],
         [pltpu.VMEM((key_heads, HALO + toks, 128), F32)],
         flops=2 * toks * width * group,
         key_heads=key_heads,
         ratio=ratio,
     )
-    b, t = call(pair_kernel, (state, state), [s_own, got], flops=heads * 2**23)
-    step = 2
-    jb = passed_along(b, "ctx", step)
-    jt = passed_along(t, "ctx", step)
-    q, o = call(pair_absorb_kernel, (q_shape, o_shape), [q, o, got], flops=heads * 2**24)
+    total = call(join_kernel, pair_shape, [s_keep, s_pair], flops=heads * 2**22, step=1)
+    step, before, before_step = 2, None, 2
     while 2 * step < n_ctx:
-        b = call(join_b_kernel, state, [t, b, jb], flops=heads * 2**22)
+        got = xor_sent(total, "ctx", step)
+        more = 4 * step < n_ctx
+        total = call(join_kernel, pair_shape if more else state_shape, [total, got], flops=heads * 2**22, step=step)
+        if before is None:
+            before = got
+        else:
+            if before_step == 2:
+                entry = jnp.concatenate([jnp.eye(DK, dtype=BF16), jnp.zeros((DK, DV), BF16)], axis=1)
+                before = jnp.where(lax.axis_index("ctx") // 2 % 2 == 1, before, entry)
+                before_step = 1
+            before = call(prefix_kernel, pair_shape, [before, got], step=step)
         step *= 2
-        more = 2 * step < n_ctx
-        if more:
-            t = call(join_t_kernel, state, [t, jt], flops=heads * 2**22)
-        nb = passed_along(b, "ctx", step) if more else xor_sent(b, "ctx", step)
-        nt = passed_along(t, "ctx", step) if more else None
-        q, o = call(absorb_kernel, (q_shape, o_shape), [q, o, jb, jt], flops=heads * 2**24)
-        jb, jt = nb, nt
-    half = shaped((toks // 2, heads * DV), BF16)
+    got = xor_sent(total, "ctx", step)
+    own_state, out_state = call(
+        states_kernel,
+        (state_shape, state_shape),
+        [s_keep, s_pair, before, got],
+        before_step=before_step,
+        step=step,
+    )
+    got_state = xor_sent(out_state, "ctx", 1)
+    rows_shape = shaped((toks // 2, heads * DV), BF16)
     keep, send = call(
         normed_kernel,
-        (half, half),
-        [q, o, jb, gate],
+        (rows_shape, rows_shape),
+        [q, o, own_state, got_state, gate],
         [pltpu.VMEM((toks, heads * DV), BF16)],
         flops=heads * 2**23,
         n_head=n_head,
-        last_step=step,
     )
     other = xor_sent(send, "head", 1)
     out_args = [keep, other, out_proj, w_other]

time: 59.9 us -> 54.7 us (0.913)
  starting transfers between devices: 23.6 us -> 18.1 us
  waiting for transfers between devices: 16.3 us -> 18.9 us
  Pallas kernels: 12.9 us -> 10.8 us
    ppermute x2 -> x0, starting transfers between devices: 8.11 us -> none  [passed_along(): lax.ppermute(value, axis, [(i, i + steps) for i in range(count - steps)])]
    ppermute x9 -> x11, starting transfers between devices: 14.2 us -> 16.8 us  [xor_sent(): return lax.ppermute(value, axis, [(i, i ^ step) for i in range(count)])]
    ppermute x9 -> x11, waiting for transfers between devices: 16.3 us -> 18.9 us  [xor_sent(): return lax.ppermute(value, axis, [(i, i ^ step) for i in range(count)])]
    pallas_call x10 -> x9, Pallas kernels: 12.9 us -> 10.8 us  [call(): pl.pallas_call(functools.partial(body, **static), out_shape=out_shape, in...]
  transfers between devices with their start and end apart: 13 -> 13, of which waited for: 4 -> 6; matrix products, arithmetic and copies ran while one was open for 2% -> 2% of each run, Pallas kernels for 10% -> 9%
where the time goes in v4:
time: 54.7 us; the launch traced here: 54.4 us
  waiting for transfers between devices  18.9 us (35%)
  starting transfers between devices  18.1 us (33%)
  Pallas kernels  10.8 us (20%)
  local copies, waits for them, and re-layouts  5.65 us (10%)
  other arithmetic  0.76 us (1%)
    ppermute x11, waiting for transfers between devices, xor_sent(): return lax.ppermute(value, axis, [(i, i ^ step) for i in range(count)])  18.9 us
    ppermute x11, starting transfers between devices, xor_sent(): return lax.ppermute(value, axis, [(i, i ^ step) for i in range(count)])  16.8 us
    pallas_call x9, Pallas kernels, call(): pl.pallas_call(functools.partial(body, **static), out_shape=out_shape, in...  10.8 us
    unnamed x11, local copies, waits for them, and re-layouts  2.03 us
    slice x2, local copies, waits for them, and re-layouts, local(): w_z = in_proj[:, :, v_end:].reshape(width, heads * DV)  1.59 us
    ppermute x2, starting transfers between devices, local(): halo = jnp.where(me == target, lax.ppermute(tail, ctx_head, perm), halo)  1.33 us
    slice x2, local copies, waits for them, and re-layouts, local(): w_kv = in_proj[:, :, DK:v_end].reshape(width, key_heads * (v_end - DK))  1.32 us
  transfers between devices with their start and end apart: 13, of which 6 were waited for; matrix products, arithmetic and copies ran while one was open for 2% of the time, Pallas kernels for 9%

profile of v4, /device:TPU:0, one launch (start us, length us, event | category | flops | bytes accessed | tf_op | source)
XLA Modules:
  0.0 54.4 jit_solution(7662113722311267442)
XLA Ops:
  0.0 3.0 %collective-permute-start.1 = (bf16[64,2048]{1,0:T(8,128)(2,1)}, bf16[64,2048]{1,0:T(8,128)(2,1)S(1)}, u32[]{:S(2)}, u32[]{:S(2)}) collective-permute-start(bf16[64,2048]{1,0:T(8,128)(2,1)} %x_any.1), channel_id=1, source_target_pairs={{0,2},{1,3},{2,0},{3,1},{4,6},{5,7},{6,4},{7,5},{8,10},{9,11},{10,... | collective-permute-start | bytes 786440 | tf_op jit(solution)/shard_map/ppermute | solution.py:298
  3.0 0.7 %copy-done.2 = f32[2,4,256]{2,1,0:T(4,128)S(1)} copy-done((f32[2,4,256]{2,1,0:T(4,128)S(1)}, f32[2,4,256]{2,1,0:T(4,128)}, u32[]{:S(2)}) %copy-start.2) | copy-done | bytes 8216
  3.7 1.0 %shard_map.64 = (f32[4,256]{1,0:T(4,128)S(1)}, f32[256,8]{1,0:T(8,128)S(1)}, f32[4,3,128,128]{3,2,1,0:T(8,128)S(1)}, bf16[16,2048]{1,0:T(8,128)(2,1)S(1)}, bf16[64,2048]{1,0:T(8,128)(2,1)S(1)}) custom-call(f32[2,4,256]{2,1,0:T(4,128)S(1)} %copy-done.2, bf16[64,2048]{1,0:T(8,128)(2,1)} %x_any.1), custom_call_target="tpu_custom_call" | custom-call | bytes 270336 | tf_op jit(solution)/shard_map/pallas_call | solution.py:281
  4.7 0.7 %collective-permute-start.3 = (bf16[16,2048]{1,0:T(8,128)(2,1)S(1)}, bf16[16,2048]{1,0:T(8,128)(2,1)S(1)}, u32[]{:S(2)}, u32[]{:S(2)}) collective-permute-start(bf16[16,2048]{1,0:T(8,128)(2,1)S(1)} %get-tuple-element.24), channel_id=1, source_target_pairs={{3,6},{6,3},{7,10},{10,7},{11,14},{14,11},{15,18},{18,15},{19,22},... | collective-permute-start | bytes 196616 | tf_op jit(solution)/shard_map/ppermute | solution.py:343
  5.4 0.7 %collective-permute-start.4 = (bf16[16,2048]{1,0:T(8,128)(2,1)S(1)}, bf16[16,2048]{1,0:T(8,128)(2,1)S(1)}, u32[]{:S(2)}, u32[]{:S(2)}) collective-permute-start(bf16[16,2048]{1,0:T(8,128)(2,1)S(1)} %get-tuple-element.24), channel_id=1, source_target_pairs={{3,5},{5,3},{7,9},{9,7},{11,13},{13,11},{15,17},{17,15},{19,21},{2... | collective-permute-start | bytes 196616 | tf_op jit(solution)/shard_map/ppermute | solution.py:343
  6.2 3.3 %collective-permute-done.1.refs_2_ = bf16[64,2048]{1,0:T(8,128)(2,1)S(1)} collective-permute-done((bf16[64,2048]{1,0:T(8,128)(2,1)}, bf16[64,2048]{1,0:T(8,128)(2,1)S(1)}, u32[]{:S(2)}, u32[]{:S(2)}) %collective-permute-start.1) | collective-permute-done | bytes 262176 | tf_op jit(solution)/shard_map/ppermute | solution.py:298
  10.1 1.3 %slice-done = bf16[2048,2,384]{2,1,0:T(2,128)(2,1)S(1)} async-done(((bf16[2048,2,768]{2,1,0:T(2,128)(2,1)}), bf16[2048,2,384]{2,1,0:T(2,128)(2,1)S(1)}, s32[]{:S(2)}) %slice-start) | async-done | bytes 3145752 | tf_op jit(solution)/shard_map/slice | solution.py:346
  11.4 0.7 %copy.7 = bf16[256,8,2,384]{3,1,2,0:T(8,128)(2,1)S(1)} copy(bf16[256,8,2,384]{3,2,1,0:T(2,128)(2,1)S(1)} %bitcast.13) | data formatting | bytes 6291456
  12.1 5.1 %shard_map.65 = (bf16[2,128,256]{2,1,0:T(8,128)(2,1)S(1)}, bf16[2,128,256]{2,1,0:T(8,128)(2,1)S(1)}, bf16[4,256,256]{2,1,0:T(8,128)(2,1)S(1)}, bf16[2,256,128]{2,1,0:T(8,128)(2,1)S(1)}, bf16[272,2048]{1,0:T(8,128)(2,1)S(1)}) custom-call(bf16[64,2048]{1,0:T(8,128)(2,1)S(1)} %get-tuple-element.23.refs_0_, bf16[64,2048]{1,0:T(8,128)(2,1)S(1)} %collective-permute-done.refs_1_, ...), custom_call_target="tpu_custom_call" | custom-call | flops 805306368 | bytes 5140480 | tf_op jit(solution)/shard_map/pallas_call | solution.py:281
  17.8 3.5 %collective-permute-start.6 = (bf16[2,128,256]{2,1,0:T(8,128)(2,1)S(1)}, bf16[2,128,256]{2,1,0:T(8,128)(2,1)S(1)}, u32[]{:S(2)}, u32[]{:S(2)}) collective-permute-start(bf16[2,128,256]{2,1,0:T(8,128)(2,1)S(1)} %get-tuple-element.34), channel_id=1, source_target_pairs={{0,4},{4,0},{8,12},{12,8},{16,20},{20,16},{24,28},{28,24},{1,5},{5... | collective-permute-start | bytes 393224 | tf_op jit(solution)/shard_map/ppermute | solution.py:298
  21.3 3.7 %collective-permute-done.6.got.pair = bf16[2,128,256]{2,1,0:T(8,128)(2,1)S(1)} collective-permute-done((bf16[2,128,256]{2,1,0:T(8,128)(2,1)S(1)}, bf16[2,128,256]{2,1,0:T(8,128)(2,1)S(1)}, u32[]{:S(2)}, u32[]{:S(2)}) %collective-permute-start.6) | collective-permute-done | bytes 131104 | tf_op jit(solution)/shard_map/ppermute | solution.py:298
  25.2 2.8 %collective-permute-start.7 = (bf16[2,128,256]{2,1,0:T(8,128)(2,1)S(1)}, bf16[2,128,256]{2,1,0:T(8,128)(2,1)S(1)}, u32[]{:S(2)}, u32[]{:S(2)}) collective-permute-start(bf16[2,128,256]{2,1,0:T(8,128)(2,1)S(1)} %shard_map.67.own), channel_id=1, source_target_pairs={{0,8},{4,12},{8,0},{12,4},{16,24},{20,28},{24,16},{28,20},{1,9},{5... | collective-permute-start | bytes 393224 | tf_op jit(solution)/shard_map/ppermute | solution.py:298
  28.0 2.9 %collective-permute-done.7.got.before = bf16[2,128,256]{2,1,0:T(8,128)(2,1)S(1)} collective-permute-done((bf16[2,128,256]{2,1,0:T(8,128)(2,1)S(1)}, bf16[2,128,256]{2,1,0:T(8,128)(2,1)S(1)}, u32[]{:S(2)}, u32[]{:S(2)}) %collective-permute-start.7) | collective-permute-done | bytes 131104 | tf_op jit(solution)/shard_map/ppermute | solution.py:298
  31.1 3.1 %collective-permute-start.8 = (bf16[2,128,128]{2,1,0:T(8,128)(2,1)S(1)}, bf16[2,128,128]{2,1,0:T(8,128)(2,1)S(1)}, u32[]{:S(2)}, u32[]{:S(2)}) collective-permute-start(bf16[2,128,128]{2,1,0:T(8,128)(2,1)S(1)} %shard_map.68), channel_id=1, source_target_pairs={{0,16},{4,20},{8,24},{12,28},{16,0},{20,4},{24,8},{28,12},{1,17},{... | collective-permute-start | bytes 196616 | tf_op jit(solution)/shard_map/ppermute | solution.py:298
  34.2 1.6 %slice-done.1 = bf16[2048,2,256]{2,1,0:T(2,128)(2,1)S(1)} async-done(((bf16[2048,2,768]{2,1,0:T(2,128)(2,1)}), bf16[2048,2,256]{2,1,0:T(2,128)(2,1)S(1)}, s32[]{:S(2)}) %slice-start.1) | async-done | bytes 2097176 | tf_op jit(solution)/shard_map/slice | solution.py:348
  36.3 0.7 %slice-done.2 = bf16[2048,2,128]{2,1,0:T(2,128)(2,1)S(1)} async-done(((bf16[2048,2,768]{2,1,0:T(2,128)(2,1)}), bf16[2048,2,128]{2,1,0:T(2,128)(2,1)S(1)}, s32[]{:S(2)}) %slice-start.2) | async-done | bytes 1048600 | tf_op jit(solution)/shard_map/slice | solution.py:347
  38.1 1.9 %shard_map.66 = (bf16[4,256,128]{2,1,0:T(8,128)(2,1)S(1)}, f32[4,256,128]{2,1,0:T(8,128)S(1)}, f32[4,256,128]{2,1,0:T(8,128)S(1)}) custom-call(bf16[272,2048]{1,0:T(8,128)(2,1)S(1)} %get-tuple-element.28.x, bf16[2048,256]{1,0:T(8,128)(2,1)S(1)} %bitcast.11, bf16[2048,512]{1,0:T(8,128)(2,1)S(1)} %bitcast.10, f32[4,2,512]{2,1,0:T(2,128)S(1)} %copy-done.1, ...), custom_call_target="tpu_custom_call" | custom-call | flops 805306368 | bytes 4944384 | tf_op jit(solution)/shard_map/pallas_call | solution.py:281
  40.1 1.7 %collective-permute-done.9.got = bf16[2,128,128]{2,1,0:T(8,128)(2,1)S(1)} collective-permute-done((bf16[2,128,128]{2,1,0:T(8,128)(2,1)S(1)}, bf16[2,128,128]{2,1,0:T(8,128)(2,1)S(1)}, u32[]{:S(2)}, u32[]{:S(2)}) %collective-permute-start.9) | collective-permute-done | bytes 65568 | tf_op jit(solution)/shard_map/ppermute | solution.py:298
  42.3 1.3 %collective-permute-done.10.got = bf16[128,512]{1,0:T(8,128)(2,1)S(1)} collective-permute-done((bf16[128,512]{1,0:T(8,128)(2,1)S(1)}, bf16[128,512]{1,0:T(8,128)(2,1)S(1)}, u32[]{:S(2)}, u32[]{:S(2)}) %collective-permute-start.10) | collective-permute-done | bytes 131104 | tf_op jit(solution)/shard_map/ppermute | solution.py:298
  43.6 0.8 %shard_map.72 = bf16[64,2048]{1,0:T(8,128)(2,1)S(1)} custom-call(bf16[128,512]{1,0:T(8,128)(2,1)S(1)} %get-tuple-element.38.own, bf16[128,512]{1,0:T(8,128)(2,1)S(1)} %collective-permute-done.10.got, bf16[512,2048]{1,0:T(8,128)(2,1)S(1)} %copy-done, bf16[512,2048]{1,0:T(8,128)(2,1)S(1)} %collective-permute-done.11.w_got), custom_call_target="tpu_custom_call" | custom-call | flops 536870912 | bytes 4456448 | tf_op jit(solution)/shard_map/pallas_call | solution.py:281
  44.5 2.5 %collective-permute-start.12 = (bf16[64,2048]{1,0:T(8,128)(2,1)S(1)}, bf16[64,2048]{1,0:T(8,128)(2,1)S(1)}, u32[]{:S(2)}, u32[]{:S(2)}) collective-permute-start(bf16[64,2048]{1,0:T(8,128)(2,1)S(1)} %shard_map.72), channel_id=1, source_target_pairs={{0,2},{1,3},{2,0},{3,1},{4,6},{5,7},{6,4},{7,5},{8,10},{9,11},{10,... | collective-permute-start | bytes 786440 | tf_op jit(solution)/shard_map/ppermute | solution.py:298
  47.0 0.9 %shard_map.71 = f32[64,2048]{1,0:T(8,128)S(1)} custom-call(bf16[128,512]{1,0:T(8,128)(2,1)S(1)} %get-tuple-element.38.own, bf16[128,512]{1,0:T(8,128)(2,1)S(1)} %collective-permute-done.10.got, bf16[512,2048]{1,0:T(8,128)(2,1)S(1)} %copy-done, bf16[512,2048]{1,0:T(8,128)(2,1)S(1)} %collective-permute-done.11.w_got), custom_call_target="tpu_custom_call" | custom-call | flops 536870912 | bytes 4456448 | tf_op jit(solution)/shard_map/pallas_call | solution.py:281
  47.9 5.8 %collective-permute-done.12 = bf16[64,2048]{1,0:T(8,128)(2,1)S(1)} collective-permute-done((bf16[64,2048]{1,0:T(8,128)(2,1)S(1)}, bf16[64,2048]{1,0:T(8,128)(2,1)S(1)}, u32[]{:S(2)}, u32[]{:S(2)}) %collective-permute-start.12) | collective-permute-done | bytes 262176 | tf_op jit(solution)/shard_map/ppermute | solution.py:298
  53.7 0.8 %add_convert_fusion = bf16[64,2048]{1,0:T(8,128)(2,1)} fusion(f32[64,2048]{1,0:T(8,128)S(1)} %shard_map.71, bf16[64,2048]{1,0:T(8,128)(2,1)S(1)} %collective-permute-done.12), kind=kLoop, calls=%fused_computation.1 | loop fusion | flops 393216 | bytes 1048576 | tf_op jit(solution)/shard_map/convert_element_type | solution.py:430
  (30 shorter events, 3.7 us)
Async XLA Ops:
  0.0 9.5 %collective-permute-start.1 = (bf16[64,2048]{1,0:T(8,128)(2,1)}, bf16[64,2048]{1,0:T(8,128)(2,1)S(1)}, u32[]{:S(2)}, u32[]{:S(2)}) collective-permute-start(bf16[64,2048]{1,0:T(8,128)(2,1)} %x_any.1), channel_id=1, source_target_pairs={{0,2},{1,3},{2,0},{3,1},{4,6},{5,7},{6,4},{7,5},{8,10},{9,11},{10,... | collective-permute-start | bytes 786440 | tf_op jit(solution)/shard_map/ppermute | solution.py:298
  3.0 0.7 %copy-start.2 = (f32[2,4,256]{2,1,0:T(4,128)S(1)}, f32[2,4,256]{2,1,0:T(4,128)}, u32[]{:S(2)}) copy-start(f32[2,4,256]{2,1,0:T(4,128)} %logits.1) | copy-start | bytes 24580
  4.7 4.8 %collective-permute-start.3 = (bf16[16,2048]{1,0:T(8,128)(2,1)S(1)}, bf16[16,2048]{1,0:T(8,128)(2,1)S(1)}, u32[]{:S(2)}, u32[]{:S(2)}) collective-permute-start(bf16[16,2048]{1,0:T(8,128)(2,1)S(1)} %get-tuple-element.24), channel_id=1, source_target_pairs={{3,6},{6,3},{7,10},{10,7},{11,14},{14,11},{15,18},{18,15},{19,22},... | collective-permute-start | bytes 196616 | tf_op jit(solution)/shard_map/ppermute | solution.py:343
  5.4 4.1 %collective-permute-start.4 = (bf16[16,2048]{1,0:T(8,128)(2,1)S(1)}, bf16[16,2048]{1,0:T(8,128)(2,1)S(1)}, u32[]{:S(2)}, u32[]{:S(2)}) collective-permute-start(bf16[16,2048]{1,0:T(8,128)(2,1)S(1)} %get-tuple-element.24), channel_id=1, source_target_pairs={{3,5},{5,3},{7,9},{9,7},{11,13},{13,11},{15,17},{17,15},{19,21},{2... | collective-permute-start | bytes 196616 | tf_op jit(solution)/shard_map/ppermute | solution.py:343
  6.1 6.0 %collective-permute-start = (bf16[64,2048]{1,0:T(8,128)(2,1)}, bf16[64,2048]{1,0:T(8,128)(2,1)S(1)}, u32[]{:S(2)}, u32[]{:S(2)}) collective-permute-start(bf16[64,2048]{1,0:T(8,128)(2,1)} %x_any.1), channel_id=1, source_target_pairs={{0,1},{1,0},{2,3},{3,2},{4,5},{5,4},{6,7},{7,6},{8,9},{9,8},{10,11... | collective-permute-start | bytes 786440 | tf_op jit(solution)/shard_map/ppermute | solution.py:298
  9.5 2.6 %collective-permute-start.2 = (bf16[64,2048]{1,0:T(8,128)(2,1)S(1)}, bf16[64,2048]{1,0:T(8,128)(2,1)S(1)}, u32[]{:S(2)}, u32[]{:S(2)}) collective-permute-start(bf16[64,2048]{1,0:T(8,128)(2,1)S(1)} %collective-permute-done.1.refs_2_), channel_id=1, source_target_pairs={{0,1},{1,0},{2,3},{3,2},{4,5},{5,4},{6,7},{7,6},{8,9},{9,8},{10,11... | collective-permute-start | bytes 786440 | tf_op jit(solution)/shard_map/ppermute | solution.py:298
  9.5 1.9 %slice-start = ((bf16[2048,2,768]{2,1,0:T(2,128)(2,1)}), bf16[2048,2,384]{2,1,0:T(2,128)(2,1)S(1)}, s32[]{:S(2)}) async-start(bf16[2048,2,768]{2,1,0:T(2,128)(2,1)} %param.7), calls=%async_computation | async-start | bytes 6291456 | tf_op jit(solution)/shard_map/slice | solution.py:346
  9.5 2.6 %collective-permute-start.5 = (bf16[16,2048]{1,0:T(8,128)(2,1)S(1)}, bf16[16,2048]{1,0:T(8,128)(2,1)S(1)}, u32[]{:S(2)}, u32[]{:S(2)}) collective-permute-start(bf16[16,2048]{1,0:T(8,128)(2,1)S(1)} %select_select_fusion.refs_4_), channel_id=1, source_target_pairs={{0,1},{1,0},{2,3},{3,2},{4,5},{5,4},{6,7},{7,6},{8,9},{9,8},{10,11... | collective-permute-start | bytes 196616 | tf_op jit(solution)/shard_map/ppermute | solution.py:298
  11.4 0.7 %copy-start.1 = (f32[4,2,512]{2,1,0:T(2,128)S(1)}, f32[4,2,512]{2,1,0:T(2,128)}, u32[]{:S(2)}) copy-start(f32[4,2,512]{2,1,0:T(2,128)} %cw.1) | copy-start | bytes 49156
  12.1 5.1 %copy-start = (bf16[512,2048]{1,0:T(8,128)(2,1)S(1)}, bf16[512,2048]{1,0:T(8,128)(2,1)}, u32[]{:S(2)}) copy-start(bf16[512,2048]{1,0:T(8,128)(2,1)} %w_own.3) | copy-start | bytes 6291460
  17.2 26.4 %collective-permute-start.11 = (bf16[512,2048]{1,0:T(8,128)(2,1)S(1)}, bf16[512,2048]{1,0:T(8,128)(2,1)S(1)}, u32[]{:S(2)}, u32[]{:S(2)}) collective-permute-start(bf16[512,2048]{1,0:T(8,128)(2,1)S(1)} %copy-done), channel_id=1, source_target_pairs={{0,1},{1,0},{2,3},{3,2},{4,5},{5,4},{6,7},{7,6},{8,9},{9,8},{10,11... | collective-permute-start | bytes 6291464 | tf_op jit(solution)/shard_map/ppermute | solution.py:298
  17.8 7.2 %collective-permute-start.6 = (bf16[2,128,256]{2,1,0:T(8,128)(2,1)S(1)}, bf16[2,128,256]{2,1,0:T(8,128)(2,1)S(1)}, u32[]{:S(2)}, u32[]{:S(2)}) collective-permute-start(bf16[2,128,256]{2,1,0:T(8,128)(2,1)S(1)} %get-tuple-element.34), channel_id=1, source_target_pairs={{0,4},{4,0},{8,12},{12,8},{16,20},{20,16},{24,28},{28,24},{1,5},{5... | collective-permute-start | bytes 393224 | tf_op jit(solution)/shard_map/ppermute | solution.py:298
  25.2 5.7 %collective-permute-start.7 = (bf16[2,128,256]{2,1,0:T(8,128)(2,1)S(1)}, bf16[2,128,256]{2,1,0:T(8,128)(2,1)S(1)}, u32[]{:S(2)}, u32[]{:S(2)}) collective-permute-start(bf16[2,128,256]{2,1,0:T(8,128)(2,1)S(1)} %shard_map.67.own), channel_id=1, source_target_pairs={{0,8},{4,12},{8,0},{12,4},{16,24},{20,28},{24,16},{28,20},{1,9},{5... | collective-permute-start | bytes 393224 | tf_op jit(solution)/shard_map/ppermute | solution.py:298
  31.1 6.1 %collective-permute-start.8 = (bf16[2,128,128]{2,1,0:T(8,128)(2,1)S(1)}, bf16[2,128,128]{2,1,0:T(8,128)(2,1)S(1)}, u32[]{:S(2)}, u32[]{:S(2)}) collective-permute-start(bf16[2,128,128]{2,1,0:T(8,128)(2,1)S(1)} %shard_map.68), channel_id=1, source_target_pairs={{0,16},{4,20},{8,24},{12,28},{16,0},{20,4},{24,8},{28,12},{1,17},{... | collective-permute-start | bytes 196616 | tf_op jit(solution)/shard_map/ppermute | solution.py:298
  34.2 1.6 %slice-start.1 = ((bf16[2048,2,768]{2,1,0:T(2,128)(2,1)}), bf16[2048,2,256]{2,1,0:T(2,128)(2,1)S(1)}, s32[]{:S(2)}) async-start(bf16[2048,2,768]{2,1,0:T(2,128)(2,1)} %param.7), calls=%async_computation.1 | async-start | bytes 4194304 | tf_op jit(solution)/shard_map/slice | solution.py:348
  35.8 1.2 %slice-start.2 = ((bf16[2048,2,768]{2,1,0:T(2,128)(2,1)}), bf16[2048,2,128]{2,1,0:T(2,128)(2,1)S(1)}, s32[]{:S(2)}) async-start(bf16[2048,2,768]{2,1,0:T(2,128)(2,1)} %param.7), calls=%async_computation.2 | async-start | bytes 2097152 | tf_op jit(solution)/shard_map/slice | solution.py:347
  36.3 1.8 %copy-start.3 = (f32[128]{0:T(128)S(1)}, f32[128]{0:T(128)}, u32[]{:S(2)}) copy-start(f32[128]{0:T(128)} %param.10) | copy-start | bytes 1540
  37.5 4.3 %collective-permute-start.9 = (bf16[2,128,128]{2,1,0:T(8,128)(2,1)S(1)}, bf16[2,128,128]{2,1,0:T(8,128)(2,1)S(1)}, u32[]{:S(2)}, u32[]{:S(2)}) collective-permute-start(bf16[2,128,128]{2,1,0:T(8,128)(2,1)S(1)} %get-tuple-element.36), channel_id=1, source_target_pairs={{0,4},{4,0},{8,12},{12,8},{16,20},{20,16},{24,28},{28,24},{1,5},{5... | collective-permute-start | bytes 196616 | tf_op jit(solution)/shard_map/ppermute | solution.py:298
  42.2 1.4 %collective-permute-start.10 = (bf16[128,512]{1,0:T(8,128)(2,1)S(1)}, bf16[128,512]{1,0:T(8,128)(2,1)S(1)}, u32[]{:S(2)}, u32[]{:S(2)}) collective-permute-start(bf16[128,512]{1,0:T(8,128)(2,1)S(1)} %get-tuple-element.39), channel_id=1, source_target_pairs={{0,1},{1,0},{2,3},{3,2},{4,5},{5,4},{6,7},{7,6},{8,9},{9,8},{10,11... | collective-permute-start | bytes 393224 | tf_op jit(solution)/shard_map/ppermute | solution.py:298
  44.5 9.2 %collective-permute-start.12 = (bf16[64,2048]{1,0:T(8,128)(2,1)S(1)}, bf16[64,2048]{1,0:T(8,128)(2,1)S(1)}, u32[]{:S(2)}, u32[]{:S(2)}) collective-permute-start(bf16[64,2048]{1,0:T(8,128)(2,1)S(1)} %shard_map.72), channel_id=1, source_target_pairs={{0,2},{1,3},{2,0},{3,1},{4,6},{5,7},{6,4},{7,5},{8,10},{9,11},{10,... | collective-permute-start | bytes 786440 | tf_op jit(solution)/shard_map/ppermute | solution.py:298

commit v5 on v4

--- a/solution.py
+++ b/solution.py
@@ -15,7 +15,7 @@
 EPSILON = 1e-06
 F32 = jnp.float32
 BF16 = jnp.bfloat16
-VMEM_BYTES = 40 * 1024 * 1024
+VMEM_BYTES = 24 * 1024 * 1024
 
 
 def dot(a, b):
@@ -47,11 +47,14 @@
     return jnp.exp(jnp.minimum(gap, 0.0))
 
 
-def gates_kernel(logits, x_any, rows, cols, decays, tail, x_own, sems):
+def gates_kernel(logits_any, x_any, rows, cols, decays, tail, x_own, logits, sems):
+    logits_copy = pltpu.make_async_copy(logits_any, logits, sems.at[3])
+    logits_copy.start()
     tail_copy = pltpu.make_async_copy(x_any.at[pl.ds(x_any.shape[0] - HALO, HALO), :], tail, sems.at[0])
     own_copy = pltpu.make_async_copy(x_any, x_own, sems.at[1])
     tail_copy.start()
     own_copy.start()
+    logits_copy.wait()
     toks = logits.shape[2]
     blocks = toks // HALF
     x = logits[0]
@@ -275,17 +278,18 @@
     out[...] = (dot(a, w_own[...]) + dot(b, w_got[...])).astype(out.dtype)
 
 
-def call(body, out_shape, args, scratch=(), flops=0, any_space=(), **static):
+def call(body, out_shape, args, us, scratch=(), any_space=(), **static):
     nbytes = sum(a.size * a.dtype.itemsize for a in args)
     vmem = pl.BlockSpec(memory_space=pltpu.VMEM)
+    args = [pltpu.with_memory_space_constraint(a, pltpu.HBM) if i in any_space else a for i, a in enumerate(args)]
     return pl.pallas_call(
         functools.partial(body, **static),
         out_shape=out_shape,
-        in_specs=[pl.BlockSpec(memory_space=pl.ANY) if i in any_space else vmem for i in range(len(args))],
+        in_specs=[pl.BlockSpec(memory_space=pltpu.HBM) if i in any_space else vmem for i in range(len(args))],
         out_specs=jax.tree.map(lambda _: vmem, out_shape),
         scratch_shapes=list(scratch),
         compiler_params=pltpu.CompilerParams(vmem_limit_bytes=VMEM_BYTES),
-        cost_estimate=pl.CostEstimate(flops=flops, bytes_accessed=nbytes, transcendentals=0),
+        cost_estimate=pl.CostEstimate(flops=int(us * 1.15e9), bytes_accessed=nbytes, transcendentals=0),
     )(*args)
 
 
@@ -329,21 +333,23 @@
             shaped((part, width), BF16),
         ),
         [gate_logits, layer_in],
-        [pltpu.SemaphoreType.DMA((2,))],
-        any_space=(1,),
+        1.1,
+        [pltpu.VMEM(gate_logits.shape, F32), pltpu.SemaphoreType.DMA((4,))],
+        any_space=(0, 1),
     )
     me = lax.axis_index("head")
     halo = jnp.zeros_like(tail)
-    for h in range(1, n_head, 2):
+    for h in range(n_head - 1, 0, -2):
         target = h if h < n_head - 1 else h - 1
         perm = []
         for c in range(1, n_ctx):
             source, sink = (c - 1) * n_head + n_head - 1, c * n_head + target
             perm += [(source, sink), (sink, source)]
         halo = jnp.where(me == target, lax.ppermute(tail, ctx_head, perm), halo)
-    halo_core = xor_sent(halo, "head", 1)
     v_end = 2 * DK + ratio * DV
     w_kv = in_proj[:, :, DK:v_end].reshape(width, key_heads * (v_end - DK))
+    halo, w_kv = lax.optimization_barrier((halo, w_kv))
+    halo_core = xor_sent(halo, "head", 1)
     w_q = in_proj[:, :, 0:DK].reshape(width, key_heads * DK)
     w_z = in_proj[:, :, v_end:].reshape(width, heads * DV)
 
@@ -360,11 +366,11 @@
             shaped((HALO + toks, width), BF16),
         ),
         [x_own, *pieces[1:], halo, halo_core, w_kv, conv_weight, cols, rows, decays],
+        5.0,
         [
             pltpu.VMEM((key_heads * (1 + ratio), HALO + toks, 128), F32),
             pltpu.VMEM((heads, DK, DK + DV), BF16),
         ],
-        flops=2 * toks * width * group,
         n_head=n_head,
         key_heads=key_heads,
         ratio=ratio,
@@ -376,17 +382,17 @@
         queries_kernel,
         (shaped((heads, toks, DK), BF16), o_shape, o_shape),
         [x_full, w_q, w_z, conv_weight, cols, rows, keys, ys, norm_gain[None, :]],
+        1.9,
         [pltpu.VMEM((key_heads, HALO + toks, 128), F32)],
-        flops=2 * toks * width * group,
         key_heads=key_heads,
         ratio=ratio,
     )
-    total = call(join_kernel, pair_shape, [s_keep, s_pair], flops=heads * 2**22, step=1)
+    total = call(join_kernel, pair_shape, [s_keep, s_pair], 0.2, step=1)
     step, before, before_step = 2, None, 2
     while 2 * step < n_ctx:
         got = xor_sent(total, "ctx", step)
         more = 4 * step < n_ctx
-        total = call(join_kernel, pair_shape if more else state_shape, [total, got], flops=heads * 2**22, step=step)
+        total = call(join_kernel, pair_shape if more else state_shape, [total, got], 0.2, step=step)
         if before is None:
             before = got
         else:
@@ -394,13 +400,14 @@
                 entry = jnp.concatenate([jnp.eye(DK, dtype=BF16), jnp.zeros((DK, DV), BF16)], axis=1)
                 before = jnp.where(lax.axis_index("ctx") // 2 % 2 == 1, before, entry)
                 before_step = 1
-            before = call(prefix_kernel, pair_shape, [before, got], step=step)
+            before = call(prefix_kernel, pair_shape, [before, got], 0.2, step=step)
         step *= 2
     got = xor_sent(total, "ctx", step)
     own_state, out_state = call(
         states_kernel,
         (state_shape, state_shape),
         [s_keep, s_pair, before, got],
+        0.3,
         before_step=before_step,
         step=step,
     )
@@ -410,8 +417,8 @@
         normed_kernel,
         (rows_shape, rows_shape),
         [q, o, own_state, got_state, gate],
+        0.4,
         [pltpu.VMEM((toks, heads * DV), BF16)],
-        flops=heads * 2**23,
         n_head=n_head,
     )
     other = xor_sent(send, "head", 1)
@@ -421,7 +428,7 @@
     for i in reversed(range(n_head // 2)):
         dtype = F32 if i == 0 else BF16
         partial[i] = call(
-            out_kernel, shaped((part, width), dtype), out_args, flops=part * width * 2**12, first=i, part=part
+            out_kernel, shaped((part, width), dtype), out_args, 0.8, first=i, part=part
         )
         if i:
             partial[i] = xor_sent(partial[i], "head", 2 * i)

time: 54.7 us -> 53.5 us (0.978)
  waiting for transfers between devices: 18.9 us -> 17.8 us
  Pallas kernels: 10.8 us -> 11.5 us
  starting transfers between devices: 18.1 us -> 17.5 us
    ppermute x11, waiting for transfers between devices: 18.9 us -> 17.8 us  [xor_sent(): return lax.ppermute(value, axis, [(i, i ^ step) for i in range(count)])]
    pallas_call x9, Pallas kernels: 10.8 us -> 11.5 us  [call(): pl.pallas_call(functools.partial(body, **static), out_shape=out_shape, in...]
    unnamed x11, local copies, waits for them, and re-layouts: 2.03 us -> 1.36 us
    ppermute x11, starting transfers between devices: 16.8 us -> 16.2 us  [xor_sent(): return lax.ppermute(value, axis, [(i, i ^ step) for i in range(count)])]
    slice x2, local copies, waits for them, and re-layouts: 1.32 us -> 1.89 us  [local(): w_kv = in_proj[:, :, DK:v_end].reshape(width, key_heads * (v_end - DK))]
  transfers between devices with their start and end apart: 13 -> 13, of which waited for: 6 -> 7; matrix products, arithmetic and copies ran while one was open for 2% -> 3% of each run, Pallas kernels for 9% -> 11%
where the time goes in v5:
time: 53.5 us; the launch traced here: 53.2 us
  waiting for transfers between devices  17.8 us (33%)
  starting transfers between devices  17.5 us (33%)
  Pallas kernels  11.5 us (21%)
  local copies, waits for them, and re-layouts  5.51 us (10%)
  other arithmetic  0.76 us (1%)
    ppermute x11, waiting for transfers between devices, xor_sent(): return lax.ppermute(value, axis, [(i, i ^ step) for i in range(count)])  17.8 us
    ppermute x11, starting transfers between devices, xor_sent(): return lax.ppermute(value, axis, [(i, i ^ step) for i in range(count)])  16.2 us
    pallas_call x9, Pallas kernels, call(): pl.pallas_call(functools.partial(body, **static), out_shape=out_shape, in...  11.5 us
    slice x2, local copies, waits for them, and re-layouts, local(): w_kv = in_proj[:, :, DK:v_end].reshape(width, key_heads * (v_end - DK))  1.89 us
    slice x2, local copies, waits for them, and re-layouts, local(): w_z = in_proj[:, :, v_end:].reshape(width, heads * DV)  1.59 us
    unnamed x11, local copies, waits for them, and re-layouts  1.36 us
    ppermute x2, starting transfers between devices, local(): halo = jnp.where(me == target, lax.ppermute(tail, ctx_head, perm), halo)  1.33 us
  transfers between devices with their start and end apart: 13, of which 7 were waited for; matrix products, arithmetic and copies ran while one was open for 3% of the time, Pallas kernels for 11%

profile of v5, /device:TPU:0, one launch (start us, length us, event | category | flops | bytes accessed | tf_op | source)
XLA Modules:
  0.0 53.2 jit_solution(17719063279676096441)
XLA Ops:
  0.0 3.0 %collective-permute-start.1 = (bf16[64,2048]{1,0:T(8,128)(2,1)}, bf16[64,2048]{1,0:T(8,128)(2,1)S(1)}, u32[]{:S(2)}, u32[]{:S(2)}) collective-permute-start(bf16[64,2048]{1,0:T(8,128)(2,1)} %x_any.1), channel_id=1, source_target_pairs={{0,2},{1,3},{2,0},{3,1},{4,6},{5,7},{6,4},{7,5},{8,10},{9,11},{10,... | collective-permute-start | bytes 786440 | tf_op jit(solution)/shard_map/ppermute | solution.py:302
  3.0 1.7 %shard_map.64 = (f32[4,256]{1,0:T(4,128)S(1)}, f32[256,8]{1,0:T(8,128)S(1)}, f32[4,3,128,128]{3,2,1,0:T(8,128)S(1)}, bf16[16,2048]{1,0:T(8,128)(2,1)S(1)}, bf16[64,2048]{1,0:T(8,128)(2,1)S(1)}) custom-call(f32[2,4,256]{2,1,0:T(4,128)} %logits_any.1, bf16[64,2048]{1,0:T(8,128)(2,1)} %x_any.1), custom_call_target="tpu_custom_call" | custom-call | flops 1264999936 | bytes 270336 | tf_op jit(solution)/shard_map/pallas_call | solution.py:285
  4.7 0.7 %collective-permute-start.3 = (bf16[16,2048]{1,0:T(8,128)(2,1)S(1)}, bf16[16,2048]{1,0:T(8,128)(2,1)S(1)}, u32[]{:S(2)}, u32[]{:S(2)}) collective-permute-start(bf16[16,2048]{1,0:T(8,128)(2,1)S(1)} %get-tuple-element.26), channel_id=1, source_target_pairs={{3,5},{5,3},{7,9},{9,7},{11,13},{13,11},{15,17},{17,15},{19,21},{2... | collective-permute-start | bytes 196616 | tf_op jit(solution)/shard_map/ppermute | solution.py:348
  6.2 1.9 %slice-done = bf16[2048,2,384]{2,1,0:T(2,128)(2,1)S(1)} async-done(((bf16[2048,2,768]{2,1,0:T(2,128)(2,1)}), bf16[2048,2,384]{2,1,0:T(2,128)(2,1)S(1)}, s32[]{:S(2)}) %slice-start) | async-done | bytes 3145752 | tf_op jit(solution)/shard_map/slice | solution.py:350
  8.1 0.7 %copy.7 = bf16[256,8,2,384]{3,1,2,0:T(8,128)(2,1)S(1)} copy(bf16[256,8,2,384]{3,2,1,0:T(2,128)(2,1)S(1)} %bitcast.13) | data formatting | bytes 6291456
  8.7 0.8 %collective-permute-done.1.refs_2_ = bf16[64,2048]{1,0:T(8,128)(2,1)S(1)} collective-permute-done((bf16[64,2048]{1,0:T(8,128)(2,1)}, bf16[64,2048]{1,0:T(8,128)(2,1)S(1)}, u32[]{:S(2)}, u32[]{:S(2)}) %collective-permute-start.1) | collective-permute-done | bytes 262176 | tf_op jit(solution)/shard_map/ppermute | solution.py:302
  10.2 1.0 %collective-permute-done.5.refs_5_ = bf16[16,2048]{1,0:T(8,128)(2,1)S(1)} collective-permute-done((bf16[16,2048]{1,0:T(8,128)(2,1)S(1)}, bf16[16,2048]{1,0:T(8,128)(2,1)S(1)}, u32[]{:S(2)}, u32[]{:S(2)}) %collective-permute-start.5) | collective-permute-done | bytes 65568 | tf_op jit(solution)/shard_map/ppermute | solution.py:302
  11.2 5.1 %shard_map.65 = (bf16[2,128,256]{2,1,0:T(8,128)(2,1)S(1)}, bf16[2,128,256]{2,1,0:T(8,128)(2,1)S(1)}, bf16[4,256,256]{2,1,0:T(8,128)(2,1)S(1)}, bf16[2,256,128]{2,1,0:T(8,128)(2,1)S(1)}, bf16[272,2048]{1,0:T(8,128)(2,1)S(1)}) custom-call(bf16[64,2048]{1,0:T(8,128)(2,1)S(1)} %get-tuple-element.25.refs_0_, bf16[64,2048]{1,0:T(8,128)(2,1)S(1)} %collective-permute-done.refs_1_, ...), custom_call_target="tpu_custom_call" | custom-call | flops 5750000128 | bytes 5140480 | tf_op jit(solution)/shard_map/pallas_call | solution.py:285
  16.6 1.7 %collective-permute-start.6 = (bf16[2,128,256]{2,1,0:T(8,128)(2,1)S(1)}, bf16[2,128,256]{2,1,0:T(8,128)(2,1)S(1)}, u32[]{:S(2)}, u32[]{:S(2)}) collective-permute-start(bf16[2,128,256]{2,1,0:T(8,128)(2,1)S(1)} %get-tuple-element.38), channel_id=1, source_target_pairs={{0,4},{4,0},{8,12},{12,8},{16,20},{20,16},{24,28},{28,24},{1,5},{5... | collective-permute-start | bytes 393224 | tf_op jit(solution)/shard_map/ppermute | solution.py:302
  18.2 4.0 %collective-permute-done.6.got.pair = bf16[2,128,256]{2,1,0:T(8,128)(2,1)S(1)} collective-permute-done((bf16[2,128,256]{2,1,0:T(8,128)(2,1)S(1)}, bf16[2,128,256]{2,1,0:T(8,128)(2,1)S(1)}, u32[]{:S(2)}, u32[]{:S(2)}) %collective-permute-start.6) | collective-permute-done | bytes 131104 | tf_op jit(solution)/shard_map/ppermute | solution.py:302
  22.4 2.7 %collective-permute-start.7 = (bf16[2,128,256]{2,1,0:T(8,128)(2,1)S(1)}, bf16[2,128,256]{2,1,0:T(8,128)(2,1)S(1)}, u32[]{:S(2)}, u32[]{:S(2)}) collective-permute-start(bf16[2,128,256]{2,1,0:T(8,128)(2,1)S(1)} %shard_map.67.own), channel_id=1, source_target_pairs={{0,8},{4,12},{8,0},{12,4},{16,24},{20,28},{24,16},{28,20},{1,9},{5... | collective-permute-start | bytes 393224 | tf_op jit(solution)/shard_map/ppermute | solution.py:302
  25.1 3.1 %collective-permute-done.7.got.before = bf16[2,128,256]{2,1,0:T(8,128)(2,1)S(1)} collective-permute-done((bf16[2,128,256]{2,1,0:T(8,128)(2,1)S(1)}, bf16[2,128,256]{2,1,0:T(8,128)(2,1)S(1)}, u32[]{:S(2)}, u32[]{:S(2)}) %collective-permute-start.7) | collective-permute-done | bytes 131104 | tf_op jit(solution)/shard_map/ppermute | solution.py:302
  28.5 2.9 %collective-permute-start.8 = (bf16[2,128,128]{2,1,0:T(8,128)(2,1)S(1)}, bf16[2,128,128]{2,1,0:T(8,128)(2,1)S(1)}, u32[]{:S(2)}, u32[]{:S(2)}) collective-permute-start(bf16[2,128,128]{2,1,0:T(8,128)(2,1)S(1)} %shard_map.68), channel_id=1, source_target_pairs={{0,16},{4,20},{8,24},{12,28},{16,0},{20,4},{24,8},{28,12},{1,17},{... | collective-permute-start | bytes 196616 | tf_op jit(solution)/shard_map/ppermute | solution.py:302
  31.4 1.6 %slice-done.1 = bf16[2048,2,256]{2,1,0:T(2,128)(2,1)S(1)} async-done(((bf16[2048,2,768]{2,1,0:T(2,128)(2,1)}), bf16[2048,2,256]{2,1,0:T(2,128)(2,1)S(1)}, s32[]{:S(2)}) %slice-start.1) | async-done | bytes 2097176 | tf_op jit(solution)/shard_map/slice | solution.py:354
  33.5 0.7 %slice-done.2 = bf16[2048,2,128]{2,1,0:T(2,128)(2,1)S(1)} async-done(((bf16[2048,2,768]{2,1,0:T(2,128)(2,1)}), bf16[2048,2,128]{2,1,0:T(2,128)(2,1)S(1)}, s32[]{:S(2)}) %slice-start.2) | async-done | bytes 1048600 | tf_op jit(solution)/shard_map/slice | solution.py:353
  34.6 0.7 %collective-permute-start.9 = (bf16[2,128,128]{2,1,0:T(8,128)(2,1)S(1)}, bf16[2,128,128]{2,1,0:T(8,128)(2,1)S(1)}, u32[]{:S(2)}, u32[]{:S(2)}) collective-permute-start(bf16[2,128,128]{2,1,0:T(8,128)(2,1)S(1)} %get-tuple-element.40), channel_id=1, source_target_pairs={{0,4},{4,0},{8,12},{12,8},{16,20},{20,16},{24,28},{28,24},{1,5},{5... | collective-permute-start | bytes 196616 | tf_op jit(solution)/shard_map/ppermute | solution.py:302
  35.4 1.9 %shard_map.66 = (bf16[4,256,128]{2,1,0:T(8,128)(2,1)S(1)}, f32[4,256,128]{2,1,0:T(8,128)S(1)}, f32[4,256,128]{2,1,0:T(8,128)S(1)}) custom-call(bf16[272,2048]{1,0:T(8,128)(2,1)S(1)} %get-tuple-element.32.x, bf16[2048,256]{1,0:T(8,128)(2,1)S(1)} %bitcast.11, bf16[2048,512]{1,0:T(8,128)(2,1)S(1)} %bitcast.10, f32[4,2,512]{2,1,0:T(2,128)S(1)} %copy-done.1, ...), custom_call_target="tpu_custom_call" | custom-call | flops 2184999936 | bytes 4944384 | tf_op jit(solution)/shard_map/pallas_call | solution.py:285
  37.3 1.7 %collective-permute-done.9.got = bf16[2,128,128]{2,1,0:T(8,128)(2,1)S(1)} collective-permute-done((bf16[2,128,128]{2,1,0:T(8,128)(2,1)S(1)}, bf16[2,128,128]{2,1,0:T(8,128)(2,1)S(1)}, u32[]{:S(2)}, u32[]{:S(2)}) %collective-permute-start.9) | collective-permute-done | bytes 65568 | tf_op jit(solution)/shard_map/ppermute | solution.py:302
  39.5 1.3 %collective-permute-done.10.got = bf16[128,512]{1,0:T(8,128)(2,1)S(1)} collective-permute-done((bf16[128,512]{1,0:T(8,128)(2,1)S(1)}, bf16[128,512]{1,0:T(8,128)(2,1)S(1)}, u32[]{:S(2)}, u32[]{:S(2)}) %collective-permute-start.10) | collective-permute-done | bytes 131104 | tf_op jit(solution)/shard_map/ppermute | solution.py:302
  40.8 0.8 %shard_map.72 = bf16[64,2048]{1,0:T(8,128)(2,1)S(1)} custom-call(bf16[128,512]{1,0:T(8,128)(2,1)S(1)} %get-tuple-element.42.own, bf16[128,512]{1,0:T(8,128)(2,1)S(1)} %collective-permute-done.10.got, bf16[512,2048]{1,0:T(8,128)(2,1)S(1)} %copy-done, bf16[512,2048]{1,0:T(8,128)(2,1)S(1)} %collective-permute-done.11.w_got), custom_call_target="tpu_custom_call" | custom-call | flops 920000000 | bytes 4456448 | tf_op jit(solution)/shard_map/pallas_call | solution.py:285
  41.7 4.2 %collective-permute-start.12 = (bf16[64,2048]{1,0:T(8,128)(2,1)S(1)}, bf16[64,2048]{1,0:T(8,128)(2,1)S(1)}, u32[]{:S(2)}, u32[]{:S(2)}) collective-permute-start(bf16[64,2048]{1,0:T(8,128)(2,1)S(1)} %shard_map.72), channel_id=1, source_target_pairs={{0,2},{1,3},{2,0},{3,1},{4,6},{5,7},{6,4},{7,5},{8,10},{9,11},{10,... | collective-permute-start | bytes 786440 | tf_op jit(solution)/shard_map/ppermute | solution.py:302
  45.9 0.9 %shard_map.71 = f32[64,2048]{1,0:T(8,128)S(1)} custom-call(bf16[128,512]{1,0:T(8,128)(2,1)S(1)} %get-tuple-element.42.own, bf16[128,512]{1,0:T(8,128)(2,1)S(1)} %collective-permute-done.10.got, bf16[512,2048]{1,0:T(8,128)(2,1)S(1)} %copy-done, bf16[512,2048]{1,0:T(8,128)(2,1)S(1)} %collective-permute-done.11.w_got), custom_call_target="tpu_custom_call" | custom-call | flops 920000000 | bytes 4456448 | tf_op jit(solution)/shard_map/pallas_call | solution.py:285
  46.7 5.8 %collective-permute-done.12 = bf16[64,2048]{1,0:T(8,128)(2,1)S(1)} collective-permute-done((bf16[64,2048]{1,0:T(8,128)(2,1)S(1)}, bf16[64,2048]{1,0:T(8,128)(2,1)S(1)}, u32[]{:S(2)}, u32[]{:S(2)}) %collective-permute-start.12) | collective-permute-done | bytes 262176 | tf_op jit(solution)/shard_map/ppermute | solution.py:302
  52.5 0.8 %add_convert_fusion = bf16[64,2048]{1,0:T(8,128)(2,1)} fusion(f32[64,2048]{1,0:T(8,128)S(1)} %shard_map.71, bf16[64,2048]{1,0:T(8,128)(2,1)S(1)} %collective-permute-done.12), kind=kLoop, calls=%fused_computation.1 | loop fusion | flops 393216 | bytes 1048576 | tf_op jit(solution)/shard_map/convert_element_type | solution.py:437
  (30 shorter events, 3.4 us)
Async XLA Ops:
  0.0 6.1 %copy-start.3 = (bf16[64,2048]{1,0:T(8,128)(2,1)S(1)}, bf16[64,2048]{1,0:T(8,128)(2,1)}, u32[]{:S(2)}) copy-start(bf16[64,2048]{1,0:T(8,128)(2,1)} %x_any.1) | copy-start | bytes 786436
  0.0 9.6 %collective-permute-start.1 = (bf16[64,2048]{1,0:T(8,128)(2,1)}, bf16[64,2048]{1,0:T(8,128)(2,1)S(1)}, u32[]{:S(2)}, u32[]{:S(2)}) collective-permute-start(bf16[64,2048]{1,0:T(8,128)(2,1)} %x_any.1), channel_id=1, source_target_pairs={{0,2},{1,3},{2,0},{3,1},{4,6},{5,7},{6,4},{7,5},{8,10},{9,11},{10,... | collective-permute-start | bytes 786440 | tf_op jit(solution)/shard_map/ppermute | solution.py:302
  4.7 4.8 %collective-permute-start.3 = (bf16[16,2048]{1,0:T(8,128)(2,1)S(1)}, bf16[16,2048]{1,0:T(8,128)(2,1)S(1)}, u32[]{:S(2)}, u32[]{:S(2)}) collective-permute-start(bf16[16,2048]{1,0:T(8,128)(2,1)S(1)} %get-tuple-element.26), channel_id=1, source_target_pairs={{3,5},{5,3},{7,9},{9,7},{11,13},{13,11},{15,17},{17,15},{19,21},{2... | collective-permute-start | bytes 196616 | tf_op jit(solution)/shard_map/ppermute | solution.py:348
  5.4 4.2 %collective-permute-start.4 = (bf16[16,2048]{1,0:T(8,128)(2,1)S(1)}, bf16[16,2048]{1,0:T(8,128)(2,1)S(1)}, u32[]{:S(2)}, u32[]{:S(2)}) collective-permute-start(bf16[16,2048]{1,0:T(8,128)(2,1)S(1)} %get-tuple-element.26), channel_id=1, source_target_pairs={{3,6},{6,3},{7,10},{10,7},{11,14},{14,11},{15,18},{18,15},{19,22},... | collective-permute-start | bytes 196616 | tf_op jit(solution)/shard_map/ppermute | solution.py:348
  6.1 5.1 %collective-permute-start = (bf16[64,2048]{1,0:T(8,128)(2,1)S(1)}, bf16[64,2048]{1,0:T(8,128)(2,1)S(1)}, u32[]{:S(2)}, u32[]{:S(2)}) collective-permute-start(bf16[64,2048]{1,0:T(8,128)(2,1)S(1)} %copy-done.3), channel_id=1, source_target_pairs={{0,1},{1,0},{2,3},{3,2},{4,5},{5,4},{6,7},{7,6},{8,9},{9,8},{10,11... | collective-permute-start | bytes 786440 | tf_op jit(solution)/shard_map/ppermute | solution.py:302
  6.2 1.9 %slice-start = ((bf16[2048,2,768]{2,1,0:T(2,128)(2,1)}), bf16[2048,2,384]{2,1,0:T(2,128)(2,1)S(1)}, s32[]{:S(2)}) async-start(bf16[2048,2,768]{2,1,0:T(2,128)(2,1)} %param.7), calls=%async_computation | async-start | bytes 6291456 | tf_op jit(solution)/shard_map/slice | solution.py:350
  8.1 3.1 %copy-start.1 = (f32[4,2,512]{2,1,0:T(2,128)S(1)}, f32[4,2,512]{2,1,0:T(2,128)}, u32[]{:S(2)}) copy-start(f32[4,2,512]{2,1,0:T(2,128)} %cw.1) | copy-start | bytes 49156
  9.6 1.6 %collective-permute-start.2 = (bf16[64,2048]{1,0:T(8,128)(2,1)S(1)}, bf16[64,2048]{1,0:T(8,128)(2,1)S(1)}, u32[]{:S(2)}, u32[]{:S(2)}) collective-permute-start(bf16[64,2048]{1,0:T(8,128)(2,1)S(1)} %collective-permute-done.1.refs_2_), channel_id=1, source_target_pairs={{0,1},{1,0},{2,3},{3,2},{4,5},{5,4},{6,7},{7,6},{8,9},{9,8},{10,11... | collective-permute-start | bytes 786440 | tf_op jit(solution)/shard_map/ppermute | solution.py:302
  9.6 1.6 %collective-permute-start.5 = (bf16[16,2048]{1,0:T(8,128)(2,1)S(1)}, bf16[16,2048]{1,0:T(8,128)(2,1)S(1)}, u32[]{:S(2)}, u32[]{:S(2)}) collective-permute-start(bf16[16,2048]{1,0:T(8,128)(2,1)S(1)} %select_select_fusion.refs_4_), channel_id=1, source_target_pairs={{0,1},{1,0},{2,3},{3,2},{4,5},{5,4},{6,7},{7,6},{8,9},{9,8},{10,11... | collective-permute-start | bytes 196616 | tf_op jit(solution)/shard_map/ppermute | solution.py:302
  11.2 5.1 %copy-start = (bf16[512,2048]{1,0:T(8,128)(2,1)S(1)}, bf16[512,2048]{1,0:T(8,128)(2,1)}, u32[]{:S(2)}) copy-start(bf16[512,2048]{1,0:T(8,128)(2,1)} %w_own.3) | copy-start | bytes 6291460
  16.3 24.5 %collective-permute-start.11 = (bf16[512,2048]{1,0:T(8,128)(2,1)S(1)}, bf16[512,2048]{1,0:T(8,128)(2,1)S(1)}, u32[]{:S(2)}, u32[]{:S(2)}) collective-permute-start(bf16[512,2048]{1,0:T(8,128)(2,1)S(1)} %copy-done), channel_id=1, source_target_pairs={{0,1},{1,0},{2,3},{3,2},{4,5},{5,4},{6,7},{7,6},{8,9},{9,8},{10,11... | collective-permute-start | bytes 6291464 | tf_op jit(solution)/shard_map/ppermute | solution.py:302
  16.6 5.7 %collective-permute-start.6 = (bf16[2,128,256]{2,1,0:T(8,128)(2,1)S(1)}, bf16[2,128,256]{2,1,0:T(8,128)(2,1)S(1)}, u32[]{:S(2)}, u32[]{:S(2)}) collective-permute-start(bf16[2,128,256]{2,1,0:T(8,128)(2,1)S(1)} %get-tuple-element.38), channel_id=1, source_target_pairs={{0,4},{4,0},{8,12},{12,8},{16,20},{20,16},{24,28},{28,24},{1,5},{5... | collective-permute-start | bytes 393224 | tf_op jit(solution)/shard_map/ppermute | solution.py:302
  22.4 5.9 %collective-permute-start.7 = (bf16[2,128,256]{2,1,0:T(8,128)(2,1)S(1)}, bf16[2,128,256]{2,1,0:T(8,128)(2,1)S(1)}, u32[]{:S(2)}, u32[]{:S(2)}) collective-permute-start(bf16[2,128,256]{2,1,0:T(8,128)(2,1)S(1)} %shard_map.67.own), channel_id=1, source_target_pairs={{0,8},{4,12},{8,0},{12,4},{16,24},{20,28},{24,16},{28,20},{1,9},{5... | collective-permute-start | bytes 393224 | tf_op jit(solution)/shard_map/ppermute | solution.py:302
  28.5 5.9 %collective-permute-start.8 = (bf16[2,128,128]{2,1,0:T(8,128)(2,1)S(1)}, bf16[2,128,128]{2,1,0:T(8,128)(2,1)S(1)}, u32[]{:S(2)}, u32[]{:S(2)}) collective-permute-start(bf16[2,128,128]{2,1,0:T(8,128)(2,1)S(1)} %shard_map.68), channel_id=1, source_target_pairs={{0,16},{4,20},{8,24},{12,28},{16,0},{20,4},{24,8},{28,12},{1,17},{... | collective-permute-start | bytes 196616 | tf_op jit(solution)/shard_map/ppermute | solution.py:302
  31.4 1.6 %slice-start.1 = ((bf16[2048,2,768]{2,1,0:T(2,128)(2,1)}), bf16[2048,2,256]{2,1,0:T(2,128)(2,1)S(1)}, s32[]{:S(2)}) async-start(bf16[2048,2,768]{2,1,0:T(2,128)(2,1)} %param.7), calls=%async_computation.1 | async-start | bytes 4194304 | tf_op jit(solution)/shard_map/slice | solution.py:354
  33.0 1.2 %slice-start.2 = ((bf16[2048,2,768]{2,1,0:T(2,128)(2,1)}), bf16[2048,2,128]{2,1,0:T(2,128)(2,1)S(1)}, s32[]{:S(2)}) async-start(bf16[2048,2,768]{2,1,0:T(2,128)(2,1)} %param.7), calls=%async_computation.2 | async-start | bytes 2097152 | tf_op jit(solution)/shard_map/slice | solution.py:353
  33.5 1.9 %copy-start.2 = (f32[128]{0:T(128)S(1)}, f32[128]{0:T(128)}, u32[]{:S(2)}) copy-start(f32[128]{0:T(128)} %param.10) | copy-start | bytes 1540
  34.6 4.3 %collective-permute-start.9 = (bf16[2,128,128]{2,1,0:T(8,128)(2,1)S(1)}, bf16[2,128,128]{2,1,0:T(8,128)(2,1)S(1)}, u32[]{:S(2)}, u32[]{:S(2)}) collective-permute-start(bf16[2,128,128]{2,1,0:T(8,128)(2,1)S(1)} %get-tuple-element.40), channel_id=1, source_target_pairs={{0,4},{4,0},{8,12},{12,8},{16,20},{20,16},{24,28},{28,24},{1,5},{5... | collective-permute-start | bytes 196616 | tf_op jit(solution)/shard_map/ppermute | solution.py:302
  39.4 1.4 %collective-permute-start.10 = (bf16[128,512]{1,0:T(8,128)(2,1)S(1)}, bf16[128,512]{1,0:T(8,128)(2,1)S(1)}, u32[]{:S(2)}, u32[]{:S(2)}) collective-permute-start(bf16[128,512]{1,0:T(8,128)(2,1)S(1)} %get-tuple-element.43), channel_id=1, source_target_pairs={{0,1},{1,0},{2,3},{3,2},{4,5},{5,4},{6,7},{7,6},{8,9},{9,8},{10,11... | collective-permute-start | bytes 393224 | tf_op jit(solution)/shard_map/ppermute | solution.py:302
  41.7 10.8 %collective-permute-start.12 = (bf16[64,2048]{1,0:T(8,128)(2,1)S(1)}, bf16[64,2048]{1,0:T(8,128)(2,1)S(1)}, u32[]{:S(2)}, u32[]{:S(2)}) collective-permute-start(bf16[64,2048]{1,0:T(8,128)(2,1)S(1)} %shard_map.72), channel_id=1, source_target_pairs={{0,2},{1,3},{2,0},{3,1},{4,6},{5,7},{6,4},{7,5},{8,10},{9,11},{10,... | collective-permute-start | bytes 786440 | tf_op jit(solution)/shard_map/ppermute | solution.py:302

commit v6 on v5

--- a/solution.py
+++ b/solution.py
@@ -34,11 +34,11 @@
     return x * lax.rsqrt(jnp.sum(x * x, axis=-1, keepdims=True) + EPSILON)
 
 
-def conv_silu(padded, slot, weight, g, lanes, rows):
-    acc = padded[slot, HALO - KERNEL + 1 : HALO - KERNEL + 1 + rows, :] * weight[0, g : g + 1, lanes]
+def conv_silu(padded, slot, weights, rows):
+    acc = padded[slot, HALO - KERNEL + 1 : HALO - KERNEL + 1 + rows, :] * weights[0]
     for i in range(1, KERNEL):
         lo = HALO - KERNEL + 1 + i
-        acc = acc + padded[slot, lo : lo + rows, :] * weight[i, g : g + 1, lanes]
+        acc = acc + padded[slot, lo : lo + rows, :] * weights[i]
     return silu(acc)
 
 
@@ -47,19 +47,37 @@
     return jnp.exp(jnp.minimum(gap, 0.0))
 
 
-def gates_kernel(logits_any, x_any, rows, cols, decays, tail, x_own, logits, sems):
-    logits_copy = pltpu.make_async_copy(logits_any, logits, sems.at[3])
-    logits_copy.start()
+def placed(step):
+    return lax.axis_index("ctx") // step % 2 == 1
+
+
+def true_index(local, count):
+    half = count // 2
+    odd = lax.axis_index("ctx") % 2
+    return (1 - odd if local < half else odd) * half + local % half
+
+
+def fetch_kernel(x_any, logits_any, tail, x_own, logits, sems):
+    logits_copy = pltpu.make_async_copy(logits_any, logits, sems.at[2])
     tail_copy = pltpu.make_async_copy(x_any.at[pl.ds(x_any.shape[0] - HALO, HALO), :], tail, sems.at[0])
     own_copy = pltpu.make_async_copy(x_any, x_own, sems.at[1])
     tail_copy.start()
     own_copy.start()
+    logits_copy.start()
+    tail_copy.wait()
+    own_copy.wait()
     logits_copy.wait()
+
+
+def gates_kernel(logits, rows, cols, decays):
     toks = logits.shape[2]
     blocks = toks // HALF
-    x = logits[0]
+    half = logits.shape[1] // 2
+    given = [logits[i] for i in range(2)]
+    given = [jnp.where(placed(1), a, jnp.concatenate([a[half:], a[:half]], axis=0)) for a in given]
+    x = given[0]
     log_decay = -(jnp.maximum(x, 0.0) + jnp.log1p(jnp.exp(-jnp.abs(x))))
-    beta = 1.0 / (1.0 + jnp.exp(-logits[1]))
+    beta = 1.0 / (1.0 + jnp.exp(-given[1]))
     heads = x.shape[0]
     ri = lax.broadcasted_iota(jnp.int32, (toks, toks), 0)
     ci = lax.broadcasted_iota(jnp.int32, (toks, toks), 1)
@@ -79,38 +97,38 @@
                 m = m * bcols[a * HALF : (a + 1) * HALF, j : j + 1]
                 decays[j, i] = jnp.where(below, m, 0.0) if a == b else m
                 i += 1
-    tail_copy.wait()
-    own_copy.wait()
-
-
-def keys_kernel(*refs, n_head, key_heads, ratio):
-    pieces = refs[:n_head]
-    halo, halo_core, w, cw, cols, rows, decays, s_keep, s_send, y_out, k_out, x_out, padded, s_all = refs[n_head:]
-    me = lax.axis_index("head")
-    part = pieces[0].shape[0]
-    toks = part * n_head
+
+
+def conv_weights(weight, g, lanes):
+    taps = []
+    for i in range(KERNEL):
+        tap = weight[i, 0:1, lanes]
+        for h in range(1, weight.shape[1]):
+            tap = jnp.where(g == h, weight[i, h : h + 1, lanes], tap)
+        taps.append(tap)
+    return taps
+
+
+def keys_terms(x, w, cw, cols, rows, decays, s_out, y_out, k_out, padded, *, first, key_heads, ratio):
+    toks = x.shape[0] - HALO
     blocks = toks // HALF
+    count = key_heads // 2
     heads = key_heads * ratio
-    direct = (me % 2 == 1) != (me >= n_head - 2)
-    x_out[0:HALO, :] = jnp.where(direct, halo[...], halo_core[...])
-    for s in range(n_head):
-        at = pl.multiple_of(HALO + (me ^ s) * part, 16)
-        x_out[pl.ds(at, part), :] = pieces[s][...]
     width = DK + ratio * DV
-    for g in range(key_heads):
-        proj = dot(x_out[...], w[:, g * width : (g + 1) * width])
-        proj = proj.astype(BF16).astype(F32)
+    ri = lax.broadcasted_iota(jnp.int32, (HALF, HALF), 0)
+    ci = lax.broadcasted_iota(jnp.int32, (HALF, HALF), 1)
+    level = jnp.where(ri > ci, ri ^ ci, 0)
+    eye = jnp.where(ri == ci, 1.0, 0.0).astype(F32)
+    for g in range(count):
+        at = pl.multiple_of(true_index(first + g, key_heads) * width, 128)
+        proj = dot(x[...], w[:, pl.ds(at, width)]).astype(BF16).astype(F32)
         for t in range(1 + ratio):
             padded[g * (1 + ratio) + t] = proj[:, t * 128 : (t + 1) * 128]
-    ri = lax.broadcasted_iota(jnp.int32, (HALF, HALF), 0)
-    ci = lax.broadcasted_iota(jnp.int32, (HALF, HALF), 1)
-    below = ri > ci
-    level = jnp.where(below, ri ^ ci, 0)
-    eye = jnp.where(ri == ci, 1.0, 0.0).astype(F32)
     kts, rhs, lowers, offs = [], [], [], []
-    for g in range(key_heads):
+    for g in range(count):
         base = g * (1 + ratio)
-        k = l2_normed(conv_silu(padded, base, cw, g, slice(DK, 2 * DK), toks))
+        group = true_index(first + g, key_heads)
+        k = l2_normed(conv_silu(padded, base, conv_weights(cw, group, slice(DK, 2 * DK)), toks))
         kb = k.astype(BF16)
         k_out[g] = kb
         kf = kb.astype(F32)
@@ -118,24 +136,23 @@
         ks = [kb[b * HALF : (b + 1) * HALF] for b in range(blocks)]
         grams = {(a, b): dot_t(ks[a], ks[b]) for a in range(blocks) for b in range(a + 1)}
         for r in range(ratio):
-            j = g * ratio + r
+            j = (first + g) * ratio + r
             lanes = slice(2 * DK + r * DV, 2 * DK + (r + 1) * DV)
-            v = conv_silu(padded, base + 1 + r, cw, g, lanes, toks)
+            v = conv_silu(padded, base + 1 + r, conv_weights(cw, group, lanes), toks)
             ccol = cols[:, j : j + 1]
             bcol = cols[:, heads + j : heads + j + 1]
             rk = (kf * (bcol * jnp.exp(ccol))).astype(BF16)
             rv = (v * bcol).astype(BF16)
             rhs.append(jnp.concatenate([rk, rv], axis=1))
-            low, off, i = [], {}, 0
+            off, i = {}, 0
             for a in range(blocks):
                 for b in range(a + 1):
                     m = grams[(a, b)] * decays[j, i]
                     i += 1
                     if a == b:
-                        low.append(m)
+                        lowers.append(m)
                     else:
                         off[(a, b)] = m.astype(BF16)
-            lowers += low
             offs.append(off)
     inv = [eye - jnp.where(level == 1, m, 0.0) for m in lowers]
     size = 2
@@ -146,46 +163,73 @@
         inv = [x - dot(xb, c) for x, xb, c in zip(inv, inv_b, cx)]
         size *= 2
     inv_b = [m.astype(BF16) for m in inv]
-    for j in range(heads):
-        ys = []
-        for a in range(blocks):
-            r = rhs[j][a * HALF : (a + 1) * HALF]
+    solved = [[] for _ in rhs]
+    for a in range(blocks):
+        for j, given in enumerate(rhs):
+            r = given[a * HALF : (a + 1) * HALF]
             if a:
                 acc = r.astype(F32)
                 for b in range(a):
-                    acc = acc - dot(offs[j][(a, b)], ys[b])
+                    acc = acc - dot(offs[j][(a, b)], solved[j][b])
                 r = acc.astype(BF16)
-            ys.append(dot(inv_b[j * blocks + a], r).astype(BF16))
-        y = jnp.concatenate(ys, axis=0)
+            solved[j].append(dot(inv_b[j * blocks + a], r).astype(BF16))
+    for j in range(len(rhs)):
+        y = jnp.concatenate(solved[j], axis=0)
         y_out[j] = y
-        crow = rows[j : j + 1, :]
+        at = first * ratio + j
+        crow = rows[at : at + 1, :]
         last = crow[:, toks - 1 : toks]
         kd = (kts[j // ratio] * jnp.exp(last - crow)).astype(BF16)
         s = dot(kd, y)
-        s_all[j, :, 0:DK] = (eye * jnp.exp(last) - s[:, 0:DK]).astype(BF16)
-        s_all[j, :, DK:] = s[:, DK:].astype(BF16)
-    odd = lax.axis_index("ctx") % 2
-    half = heads // 2
-    s_keep[...] = s_all[pl.ds(odd * half, half)]
-    s_send[...] = s_all[pl.ds((1 - odd) * half, half)]
-
-
-def queries_kernel(x, wq, wz, cw, cols, rows, keys, ys, gain, q_out, o_out, g_out, padded, *, key_heads, ratio):
+        s_out[j, :, 0:DK] = (eye * jnp.exp(last) - s[:, 0:DK]).astype(BF16)
+        s_out[j, :, DK:] = s[:, DK:].astype(BF16)
+
+
+def keys_first_kernel(*refs, n_head, key_heads, ratio):
+    pieces = refs[:n_head]
+    halo, halo_core, w, cw, cols, rows, decays, s_out, y_out, k_out, x_out, padded = refs[n_head:]
+    me = lax.axis_index("head")
+    part = pieces[0].shape[0]
+    direct = (me % 2 == 1) != (me >= n_head - 2)
+    x_out[0:HALO, :] = jnp.where(direct, halo[...], halo_core[...])
+    for s in range(n_head):
+        at = pl.multiple_of(HALO + (me ^ s) * part, 16)
+        x_out[pl.ds(at, part), :] = pieces[s][...]
+    keys_terms(
+        x_out, w, cw, cols, rows, decays, s_out, y_out, k_out, padded, first=0, key_heads=key_heads, ratio=ratio
+    )
+
+
+def keys_second_kernel(x, w, cw, cols, rows, decays, s_out, y_out, k_out, padded, *, key_heads, ratio):
+    keys_terms(
+        x, w, cw, cols, rows, decays, s_out, y_out, k_out, padded,
+        first=key_heads // 2, key_heads=key_heads, ratio=ratio,
+    )
+
+
+def queries_kernel(
+    x, wq, wz, cw, cols, rows, keys_a, keys_b, ys_a, ys_b, gain, q_out, o_out, g_out, padded, *, key_heads, ratio
+):
     toks = x.shape[0] - HALO
     blocks = toks // HALF
     ri = lax.broadcasted_iota(jnp.int32, (HALF, HALF), 0)
     ci = lax.broadcasted_iota(jnp.int32, (HALF, HALF), 1)
     upto = ri >= ci
     for g in range(key_heads):
-        padded[g] = dot(x[...], wq[:, g * DK : (g + 1) * DK]).astype(BF16).astype(F32)
-        proj = dot(x[HALO:, :], wz[:, g * ratio * DV : (g + 1) * ratio * DV]).astype(BF16).astype(F32)
+        group = true_index(g, key_heads)
+        at = pl.multiple_of(group * DK, 128)
+        padded[g] = dot(x[...], wq[:, pl.ds(at, DK)]).astype(BF16).astype(F32)
+        at = pl.multiple_of(group * ratio * DV, 128)
+        proj = dot(x[HALO:, :], wz[:, pl.ds(at, ratio * DV)]).astype(BF16).astype(F32)
         for r in range(ratio):
             z = proj[:, r * DV : (r + 1) * DV]
             g_out[g * ratio + r] = gain[...] * silu(z)
     for g in range(key_heads):
-        q = l2_normed(conv_silu(padded, g, cw, g, slice(0, DK), toks)) * DK ** (-0.5)
+        weights = conv_weights(cw, true_index(g, key_heads), slice(0, DK))
+        q = l2_normed(conv_silu(padded, g, weights, toks)) * DK ** (-0.5)
         qb = q.astype(BF16)
-        kb = keys[g]
+        count = key_heads // 2
+        kb = keys_b[g - count] if g >= count else keys_a[g]
         grams = {
             (a, b): dot_t(qb[a * HALF : (a + 1) * HALF], kb[b * HALF : (b + 1) * HALF])
             for a in range(blocks)
@@ -195,6 +239,7 @@
             j = g * ratio + r
             ccol = cols[:, j : j + 1]
             crow = rows[j : j + 1, :]
+            ys, i = (ys_b, j - count * ratio) if g >= count else (ys_a, j)
             for a in range(blocks):
                 at = slice(a * HALF, (a + 1) * HALF)
                 acc = None
@@ -202,14 +247,10 @@
                     m = grams[(a, b)] * block_decay(ccol, crow, a, b)
                     if a == b:
                         m = jnp.where(upto, m, 0.0)
-                    term = dot(m.astype(BF16), ys[j, b * HALF : (b + 1) * HALF, :])
+                    term = dot(m.astype(BF16), ys[i, b * HALF : (b + 1) * HALF, :])
                     acc = term if acc is None else acc + term
                 q_out[j, at, :] = (q[at] * jnp.exp(ccol[at]) - acc[:, 0:DK]).astype(BF16)
                 o_out[j, at, :] = acc[:, DK:]
-
-
-def placed(step):
-    return lax.axis_index("ctx") // step % 2 == 1
 
 
 def join_kernel(own, got, out, *, step):
@@ -256,14 +297,13 @@
 
 def normed_kernel(q, o, own, got, gate, keep, send, scratch, *, n_head):
     me = lax.axis_index("head")
-    odd = placed(1)
-    half = own.shape[0]
-    for j in range(q.shape[0]):
-        mine, other = own[j % half], got[j % half]
-        state = jnp.where(odd, mine, other) if j >= half else jnp.where(odd, other, mine)
-        att = o[j] + dot(q[j], state)
+    heads = q.shape[0]
+    half = heads // 2
+    for j in range(heads):
+        att = o[j] + dot(q[j], own[j - half] if j >= half else got[j])
         scale = lax.rsqrt(jnp.mean(att * att, axis=-1, keepdims=True) + EPSILON)
-        scratch[:, j * DV : (j + 1) * DV] = (att * scale * gate[j]).astype(BF16)
+        at = pl.multiple_of(true_index(j, heads) * DV, 128)
+        scratch[:, pl.ds(at, DV)] = (att * scale * gate[j]).astype(BF16)
     part = scratch.shape[0] // n_head
     for i in range(n_head // 2):
         at = pl.multiple_of((me ^ (2 * i)) * part, 16)
@@ -272,10 +312,16 @@
         send[i * part : (i + 1) * part, :] = scratch[pl.ds(at, part), :]
 
 
-def out_kernel(own, got, w_own, w_got, out, *, first, part):
+def out_own_kernel(own, w, *outs):
+    part = outs[0].shape[0]
+    for i, out in enumerate(outs):
+        out[...] = dot(own[i * part : (i + 1) * part, :], w[...])
+
+
+def out_kernel(got, w, before, out, *, first):
+    part = out.shape[0]
     rows = slice(first * part, (first + 1) * part)
-    a, b = own[rows, :], got[rows, :]
-    out[...] = (dot(a, w_own[...]) + dot(b, w_got[...])).astype(out.dtype)
+    out[...] = (before[...] + dot(got[rows, :], w[...])).astype(out.dtype)
 
 
 def call(body, out_shape, args, us, scratch=(), any_space=(), **static):
@@ -323,19 +369,23 @@
             pieces[s + step] = xor_sent(pieces[s], "head", step)
         step //= 2
     blocks = toks // HALF
-    rows, cols, decays, tail, x_own = call(
+    tail, x_own, logits = call(
+        fetch_kernel,
+        (shaped((HALO, width), BF16), shaped((part, width), BF16), shaped(gate_logits.shape, F32)),
+        [layer_in, gate_logits],
+        6.0,
+        [pltpu.SemaphoreType.DMA((3,))],
+        any_space=(0, 1),
+    )
+    rows, cols, decays = call(
         gates_kernel,
         (
             shaped((heads, toks), F32),
             shaped((toks, 2 * heads), F32),
             shaped((heads, blocks * (blocks + 1) // 2, HALF, HALF), F32),
-            shaped((HALO, width), BF16),
-            shaped((part, width), BF16),
         ),
-        [gate_logits, layer_in],
-        1.1,
-        [pltpu.VMEM(gate_logits.shape, F32), pltpu.SemaphoreType.DMA((4,))],
-        any_space=(0, 1),
+        [logits],
+        1.0,
     )
     me = lax.axis_index("head")
     halo = jnp.zeros_like(tail)
@@ -348,7 +398,6 @@
         halo = jnp.where(me == target, lax.ppermute(tail, ctx_head, perm), halo)
     v_end = 2 * DK + ratio * DV
     w_kv = in_proj[:, :, DK:v_end].reshape(width, key_heads * (v_end - DK))
-    halo, w_kv = lax.optimization_barrier((halo, w_kv))
     halo_core = xor_sent(halo, "head", 1)
     w_q = in_proj[:, :, 0:DK].reshape(width, key_heads * DK)
     w_z = in_proj[:, :, v_end:].reshape(width, heads * DV)
@@ -356,32 +405,36 @@
     half = heads // 2
     pair_shape = shaped((half, DK, DK + DV), BF16)
     state_shape = shaped((half, DK, DV), BF16)
-    s_keep, s_send, ys, keys, x_full = call(
-        keys_kernel,
-        (
-            pair_shape,
-            pair_shape,
-            shaped((heads, toks, DK + DV), BF16),
-            shaped((key_heads, toks, DK), BF16),
-            shaped((HALO + toks, width), BF16),
-        ),
+    key_count = key_heads // 2
+    ys_shape = shaped((half, toks, DK + DV), BF16)
+    keys_shape = shaped((key_count, toks, DK), BF16)
+    padded = pltpu.VMEM((key_count * (1 + ratio), HALO + toks, 128), F32)
+    s_send, ys_a, keys_a, x_full = call(
+        keys_first_kernel,
+        (pair_shape, ys_shape, keys_shape, shaped((HALO + toks, width), BF16)),
         [x_own, *pieces[1:], halo, halo_core, w_kv, conv_weight, cols, rows, decays],
-        5.0,
-        [
-            pltpu.VMEM((key_heads * (1 + ratio), HALO + toks, 128), F32),
-            pltpu.VMEM((heads, DK, DK + DV), BF16),
-        ],
+        3.0,
+        [padded],
         n_head=n_head,
         key_heads=key_heads,
         ratio=ratio,
     )
     s_pair = xor_sent(s_send, "ctx", 1)
-    w_other = xor_sent(lax.optimization_barrier((out_proj, s_keep))[0], "head", 1)
+    s_keep, ys_b, keys_b = call(
+        keys_second_kernel,
+        (pair_shape, ys_shape, keys_shape),
+        [x_full, w_kv, conv_weight, cols, rows, decays],
+        3.0,
+        [padded],
+        key_heads=key_heads,
+        ratio=ratio,
+    )
+    w_other = xor_sent(lax.optimization_barrier((out_proj, s_send))[0], "head", 1)
     o_shape = shaped((heads, toks, DV), F32)
     q, o, gate = call(
         queries_kernel,
         (shaped((heads, toks, DK), BF16), o_shape, o_shape),
-        [x_full, w_q, w_z, conv_weight, cols, rows, keys, ys, norm_gain[None, :]],
+        [x_full, w_q, w_z, conv_weight, cols, rows, keys_a, keys_b, ys_a, ys_b, norm_gain[None, :]],
         1.9,
         [pltpu.VMEM((key_heads, HALO + toks, 128), F32)],
         key_heads=key_heads,
@@ -422,14 +475,13 @@
         n_head=n_head,
     )
     other = xor_sent(send, "head", 1)
-    out_args = [keep, other, out_proj, w_other]
+    out_shape = shaped((part, width), F32)
+    sums = call(out_own_kernel, (out_shape,) * (n_head // 2), [keep, out_proj], 0.8)
     out = None
     partial = {}
     for i in reversed(range(n_head // 2)):
-        dtype = F32 if i == 0 else BF16
-        partial[i] = call(
-            out_kernel, shaped((part, width), dtype), out_args, 0.8, first=i, part=part
-        )
+        shape = out_shape if i == 0 else shaped((part, width), BF16)
+        partial[i] = call(out_kernel, shape, [other, w_other, sums[i]], 0.5, first=i)
         if i:
             partial[i] = xor_sent(partial[i], "head", 2 * i)
     for i in range(n_head // 2):

time: 53.5 us -> 50.7 us (0.948)
  waiting for transfers between devices: 17.8 us -> 13.2 us
  Pallas kernels: 11.5 us -> 13.5 us
    ppermute x11, waiting for transfers between devices: 17.8 us -> 13.2 us  [xor_sent(): return lax.ppermute(value, axis, [(i, i ^ step) for i in range(count)])]
    pallas_call x9 -> x12, Pallas kernels: 11.5 us -> 13.5 us  [call(): pl.pallas_call(functools.partial(body, **static), out_shape=out_shape, in...]
  transfers between devices with their start and end apart: 13 -> 13, of which waited for: 7 -> 6; matrix products, arithmetic and copies ran while one was open for 3% -> 3% of each run, Pallas kernels for 11% -> 19%
where the time goes in v6:
time: 50.7 us; the launch traced here: 50.5 us
  starting transfers between devices  17.3 us (34%)
  Pallas kernels  13.5 us (27%)
  waiting for transfers between devices  13.2 us (26%)
  local copies, waits for them, and re-layouts  5.51 us (11%)
  other arithmetic  0.76 us (1%)
    ppermute x11, starting transfers between devices, xor_sent(): return lax.ppermute(value, axis, [(i, i ^ step) for i in range(count)])  16 us
    pallas_call x12, Pallas kernels, call(): pl.pallas_call(functools.partial(body, **static), out_shape=out_shape, in...  13.5 us
    ppermute x11, waiting for transfers between devices, xor_sent(): return lax.ppermute(value, axis, [(i, i ^ step) for i in range(count)])  13.2 us
    slice x2, local copies, waits for them, and re-layouts, local(): w_kv = in_proj[:, :, DK:v_end].reshape(width, key_heads * (v_end - DK))  1.89 us
    slice x2, local copies, waits for them, and re-layouts, local(): w_z = in_proj[:, :, v_end:].reshape(width, heads * DV)  1.59 us
    unnamed x11, local copies, waits for them, and re-layouts  1.36 us
    ppermute x2, starting transfers between devices, local(): halo = jnp.where(me == target, lax.ppermute(tail, ctx_head, perm), halo)  1.33 us
  transfers between devices with their start and end apart: 13, of which 6 were waited for; matrix products, arithmetic and copies ran while one was open for 3% of the time, Pallas kernels for 19%

profile of v6, /device:TPU:0, one launch (start us, length us, event | category | flops | bytes accessed | tf_op | source)
XLA Modules:
  0.0 50.5 jit_solution(13195062108294063632)
XLA Ops:
  0.0 3.0 %collective-permute-start.1 = (bf16[64,2048]{1,0:T(8,128)(2,1)}, bf16[64,2048]{1,0:T(8,128)(2,1)S(1)}, u32[]{:S(2)}, u32[]{:S(2)}) collective-permute-start(bf16[64,2048]{1,0:T(8,128)(2,1)} %x_any.1), channel_id=1, source_target_pairs={{0,2},{1,3},{2,0},{3,1},{4,6},{5,7},{6,4},{7,5},{8,10},{9,11},{10,... | collective-permute-start | bytes 786440 | tf_op jit(solution)/shard_map/ppermute | solution.py:348
  3.0 1.1 %shard_map.64 = (bf16[16,2048]{1,0:T(8,128)(2,1)S(1)}, bf16[64,2048]{1,0:T(8,128)(2,1)S(1)}, f32[2,4,256]{2,1,0:T(4,128)S(1)}) custom-call(bf16[64,2048]{1,0:T(8,128)(2,1)} %x_any.1, f32[2,4,256]{2,1,0:T(4,128)} %logits_any.1), custom_call_target="tpu_custom_call" | custom-call | flops 6899999744 | bytes 270336 | tf_op jit(solution)/shard_map/pallas_call | solution.py:331
  4.0 0.7 %collective-permute-start.3 = (bf16[16,2048]{1,0:T(8,128)(2,1)S(1)}, bf16[16,2048]{1,0:T(8,128)(2,1)S(1)}, u32[]{:S(2)}, u32[]{:S(2)}) collective-permute-start(bf16[16,2048]{1,0:T(8,128)(2,1)S(1)} %get-tuple-element.29), channel_id=1, source_target_pairs={{3,5},{5,3},{7,9},{9,7},{11,13},{13,11},{15,17},{17,15},{19,21},{2... | collective-permute-start | bytes 196616 | tf_op jit(solution)/shard_map/ppermute | solution.py:398
  4.7 0.7 %collective-permute-start.4 = (bf16[16,2048]{1,0:T(8,128)(2,1)S(1)}, bf16[16,2048]{1,0:T(8,128)(2,1)S(1)}, u32[]{:S(2)}, u32[]{:S(2)}) collective-permute-start(bf16[16,2048]{1,0:T(8,128)(2,1)S(1)} %get-tuple-element.29), channel_id=1, source_target_pairs={{3,6},{6,3},{7,10},{10,7},{11,14},{14,11},{15,18},{18,15},{19,22},... | collective-permute-start | bytes 196616 | tf_op jit(solution)/shard_map/ppermute | solution.py:398
  5.5 1.9 %slice-done = bf16[2048,2,384]{2,1,0:T(2,128)(2,1)S(1)} async-done(((bf16[2048,2,768]{2,1,0:T(2,128)(2,1)}), bf16[2048,2,384]{2,1,0:T(2,128)(2,1)S(1)}, s32[]{:S(2)}) %slice-start) | async-done | bytes 3145752 | tf_op jit(solution)/shard_map/slice | solution.py:400
  7.4 0.7 %copy.7 = bf16[256,8,2,384]{3,1,2,0:T(8,128)(2,1)S(1)} copy(bf16[256,8,2,384]{3,2,1,0:T(2,128)(2,1)S(1)} %bitcast.14) | data formatting | bytes 6291456
  8.0 1.5 %collective-permute-done.1.refs_2_ = bf16[64,2048]{1,0:T(8,128)(2,1)S(1)} collective-permute-done((bf16[64,2048]{1,0:T(8,128)(2,1)}, bf16[64,2048]{1,0:T(8,128)(2,1)S(1)}, u32[]{:S(2)}, u32[]{:S(2)}) %collective-permute-start.1) | collective-permute-done | bytes 262176 | tf_op jit(solution)/shard_map/ppermute | solution.py:348
  10.2 1.0 %shard_map.65 = (f32[4,256]{1,0:T(4,128)S(1)}, f32[256,8]{1,0:T(8,128)S(1)}, f32[4,3,128,128]{3,2,1,0:T(8,128)S(1)}) custom-call(f32[2,4,256]{2,1,0:T(4,128)S(1)} %get-tuple-element.30.logits), custom_call_target="tpu_custom_call" | custom-call | flops 1150000000 | bytes 8192 | tf_op jit(solution)/shard_map/pallas_call | solution.py:331
  11.2 3.4 %shard_map.66 = (bf16[2,128,256]{2,1,0:T(8,128)(2,1)S(1)}, bf16[2,256,256]{2,1,0:T(8,128)(2,1)S(1)}, bf16[1,256,128]{2,1,0:T(8,128)(2,1)S(1)}, bf16[272,2048]{1,0:T(8,128)(2,1)S(1)}) custom-call(bf16[64,2048]{1,0:T(8,128)(2,1)S(1)} %get-tuple-element.28.refs_0_, bf16[64,2048]{1,0:T(8,128)(2,1)S(1)} %collective-permute-done.refs_1_, ...), custom_call_target="tpu_custom_call" | custom-call | flops 3449999872 | bytes 5140480 | tf_op jit(solution)/shard_map/pallas_call | solution.py:331
  14.9 2.4 %collective-permute-start.6 = (bf16[2,128,256]{2,1,0:T(8,128)(2,1)S(1)}, bf16[2,128,256]{2,1,0:T(8,128)(2,1)S(1)}, u32[]{:S(2)}, u32[]{:S(2)}) collective-permute-start(bf16[2,128,256]{2,1,0:T(8,128)(2,1)S(1)} %get-tuple-element.42), channel_id=1, source_target_pairs={{0,4},{4,0},{8,12},{12,8},{16,20},{20,16},{24,28},{28,24},{1,5},{5... | collective-permute-start | bytes 393224 | tf_op jit(solution)/shard_map/ppermute | solution.py:348
  17.2 3.3 %shard_map.67 = (bf16[2,128,256]{2,1,0:T(8,128)(2,1)S(1)}, bf16[2,256,256]{2,1,0:T(8,128)(2,1)S(1)}, bf16[1,256,128]{2,1,0:T(8,128)(2,1)S(1)}) custom-call(bf16[272,2048]{1,0:T(8,128)(2,1)S(1)} %get-tuple-element.34.x, bf16[2048,768]{1,0:T(8,128)(2,1)S(1)} %bitcast.10, f32[4,2,512]{2,1,0:T(2,128)S(1)} %copy-done.1, ...), custom_call_target="tpu_custom_call" | custom-call | flops 3449999872 | bytes 5074944 | tf_op jit(solution)/shard_map/pallas_call | solution.py:331
  20.5 0.7 %collective-permute-done.6.got.pair = bf16[2,128,256]{2,1,0:T(8,128)(2,1)S(1)} collective-permute-done((bf16[2,128,256]{2,1,0:T(8,128)(2,1)S(1)}, bf16[2,128,256]{2,1,0:T(8,128)(2,1)S(1)}, u32[]{:S(2)}, u32[]{:S(2)}) %collective-permute-start.6) | collective-permute-done | bytes 131104 | tf_op jit(solution)/shard_map/ppermute | solution.py:348
  21.4 1.6 %collective-permute-start.7 = (bf16[2,128,256]{2,1,0:T(8,128)(2,1)S(1)}, bf16[2,128,256]{2,1,0:T(8,128)(2,1)S(1)}, u32[]{:S(2)}, u32[]{:S(2)}) collective-permute-start(bf16[2,128,256]{2,1,0:T(8,128)(2,1)S(1)} %shard_map.69.own), channel_id=1, source_target_pairs={{0,8},{4,12},{8,0},{12,4},{16,24},{20,28},{24,16},{28,20},{1,9},{5... | collective-permute-start | bytes 393224 | tf_op jit(solution)/shard_map/ppermute | solution.py:348
  23.0 3.6 %collective-permute-done.7.got.before = bf16[2,128,256]{2,1,0:T(8,128)(2,1)S(1)} collective-permute-done((bf16[2,128,256]{2,1,0:T(8,128)(2,1)S(1)}, bf16[2,128,256]{2,1,0:T(8,128)(2,1)S(1)}, u32[]{:S(2)}, u32[]{:S(2)}) %collective-permute-start.7) | collective-permute-done | bytes 131104 | tf_op jit(solution)/shard_map/ppermute | solution.py:348
  26.8 2.6 %collective-permute-start.8 = (bf16[2,128,128]{2,1,0:T(8,128)(2,1)S(1)}, bf16[2,128,128]{2,1,0:T(8,128)(2,1)S(1)}, u32[]{:S(2)}, u32[]{:S(2)}) collective-permute-start(bf16[2,128,128]{2,1,0:T(8,128)(2,1)S(1)} %shard_map.70), channel_id=1, source_target_pairs={{0,16},{4,20},{8,24},{12,28},{16,0},{20,4},{24,8},{28,12},{1,17},{... | collective-permute-start | bytes 196616 | tf_op jit(solution)/shard_map/ppermute | solution.py:348
  29.4 1.6 %slice-done.1 = bf16[2048,2,256]{2,1,0:T(2,128)(2,1)S(1)} async-done(((bf16[2048,2,768]{2,1,0:T(2,128)(2,1)}), bf16[2048,2,256]{2,1,0:T(2,128)(2,1)S(1)}, s32[]{:S(2)}) %slice-start.1) | async-done | bytes 2097176 | tf_op jit(solution)/shard_map/slice | solution.py:403
  31.6 0.7 %slice-done.2 = bf16[2048,2,128]{2,1,0:T(2,128)(2,1)S(1)} async-done(((bf16[2048,2,768]{2,1,0:T(2,128)(2,1)}), bf16[2048,2,128]{2,1,0:T(2,128)(2,1)S(1)}, s32[]{:S(2)}) %slice-start.2) | async-done | bytes 1048600 | tf_op jit(solution)/shard_map/slice | solution.py:402
  32.7 1.6 %collective-permute-start.9 = (bf16[2,128,128]{2,1,0:T(8,128)(2,1)S(1)}, bf16[2,128,128]{2,1,0:T(8,128)(2,1)S(1)}, u32[]{:S(2)}, u32[]{:S(2)}) collective-permute-start(bf16[2,128,128]{2,1,0:T(8,128)(2,1)S(1)} %get-tuple-element.44), channel_id=1, source_target_pairs={{0,4},{4,0},{8,12},{12,8},{16,20},{20,16},{24,28},{28,24},{1,5},{5... | collective-permute-start | bytes 196616 | tf_op jit(solution)/shard_map/ppermute | solution.py:348
  34.3 2.0 %shard_map.68 = (bf16[4,256,128]{2,1,0:T(8,128)(2,1)S(1)}, f32[4,256,128]{2,1,0:T(8,128)S(1)}, f32[4,256,128]{2,1,0:T(8,128)S(1)}) custom-call(bf16[272,2048]{1,0:T(8,128)(2,1)S(1)} %get-tuple-element.34.x, bf16[2048,256]{1,0:T(8,128)(2,1)S(1)} %bitcast.12, bf16[2048,512]{1,0:T(8,128)(2,1)S(1)} %bitcast.11, f32[4,2,512]{2,1,0:T(2,128)S(1)} %copy-done.1, ...), custom_call_target="tpu_custom_call" | custom-call | flops 2184999936 | bytes 4944384 | tf_op jit(solution)/shard_map/pallas_call | solution.py:331
  36.3 0.7 %collective-permute-done.9.got = bf16[2,128,128]{2,1,0:T(8,128)(2,1)S(1)} collective-permute-done((bf16[2,128,128]{2,1,0:T(8,128)(2,1)S(1)}, bf16[2,128,128]{2,1,0:T(8,128)(2,1)S(1)}, u32[]{:S(2)}, u32[]{:S(2)}) %collective-permute-start.9) | collective-permute-done | bytes 65568 | tf_op jit(solution)/shard_map/ppermute | solution.py:348
  37.5 0.8 %shard_map.73 = (f32[64,2048]{1,0:T(8,128)S(1)}, f32[64,2048]{1,0:T(8,128)S(1)}) custom-call(bf16[128,512]{1,0:T(8,128)(2,1)S(1)} %get-tuple-element.48.own, bf16[512,2048]{1,0:T(8,128)(2,1)S(1)} %copy-done), custom_call_target="tpu_custom_call" | custom-call | flops 920000000 | bytes 2228224 | tf_op jit(solution)/shard_map/pallas_call | solution.py:331
  39.3 3.8 %collective-permute-start.12 = (bf16[64,2048]{1,0:T(8,128)(2,1)S(1)}, bf16[64,2048]{1,0:T(8,128)(2,1)S(1)}, u32[]{:S(2)}, u32[]{:S(2)}) collective-permute-start(bf16[64,2048]{1,0:T(8,128)(2,1)S(1)} %shard_map.75), channel_id=1, source_target_pairs={{0,2},{1,3},{2,0},{3,1},{4,6},{5,7},{6,4},{7,5},{8,10},{9,11},{10,... | collective-permute-start | bytes 786440 | tf_op jit(solution)/shard_map/ppermute | solution.py:348
  43.6 6.1 %collective-permute-done.12 = bf16[64,2048]{1,0:T(8,128)(2,1)S(1)} collective-permute-done((bf16[64,2048]{1,0:T(8,128)(2,1)S(1)}, bf16[64,2048]{1,0:T(8,128)(2,1)S(1)}, u32[]{:S(2)}, u32[]{:S(2)}) %collective-permute-start.12) | collective-permute-done | bytes 262176 | tf_op jit(solution)/shard_map/ppermute | solution.py:348
  49.8 0.8 %add_convert_fusion = bf16[64,2048]{1,0:T(8,128)(2,1)} fusion(f32[64,2048]{1,0:T(8,128)S(1)} %shard_map.74, bf16[64,2048]{1,0:T(8,128)(2,1)S(1)} %collective-permute-done.12), kind=kLoop, calls=%fused_computation.1 | loop fusion | flops 393216 | bytes 1048576 | tf_op jit(solution)/shard_map/convert_element_type | solution.py:489
  (33 shorter events, 4.2 us)
Async XLA Ops:
  0.0 5.4 %copy-start.3 = (bf16[64,2048]{1,0:T(8,128)(2,1)S(1)}, bf16[64,2048]{1,0:T(8,128)(2,1)}, u32[]{:S(2)}) copy-start(bf16[64,2048]{1,0:T(8,128)(2,1)} %x_any.1) | copy-start | bytes 786436
  0.0 9.6 %collective-permute-start.1 = (bf16[64,2048]{1,0:T(8,128)(2,1)}, bf16[64,2048]{1,0:T(8,128)(2,1)S(1)}, u32[]{:S(2)}, u32[]{:S(2)}) collective-permute-start(bf16[64,2048]{1,0:T(8,128)(2,1)} %x_any.1), channel_id=1, source_target_pairs={{0,2},{1,3},{2,0},{3,1},{4,6},{5,7},{6,4},{7,5},{8,10},{9,11},{10,... | collective-permute-start | bytes 786440 | tf_op jit(solution)/shard_map/ppermute | solution.py:348
  4.0 5.5 %collective-permute-start.3 = (bf16[16,2048]{1,0:T(8,128)(2,1)S(1)}, bf16[16,2048]{1,0:T(8,128)(2,1)S(1)}, u32[]{:S(2)}, u32[]{:S(2)}) collective-permute-start(bf16[16,2048]{1,0:T(8,128)(2,1)S(1)} %get-tuple-element.29), channel_id=1, source_target_pairs={{3,5},{5,3},{7,9},{9,7},{11,13},{13,11},{15,17},{17,15},{19,21},{2... | collective-permute-start | bytes 196616 | tf_op jit(solution)/shard_map/ppermute | solution.py:398
  4.7 4.9 %collective-permute-start.4 = (bf16[16,2048]{1,0:T(8,128)(2,1)S(1)}, bf16[16,2048]{1,0:T(8,128)(2,1)S(1)}, u32[]{:S(2)}, u32[]{:S(2)}) collective-permute-start(bf16[16,2048]{1,0:T(8,128)(2,1)S(1)} %get-tuple-element.29), channel_id=1, source_target_pairs={{3,6},{6,3},{7,10},{10,7},{11,14},{14,11},{15,18},{18,15},{19,22},... | collective-permute-start | bytes 196616 | tf_op jit(solution)/shard_map/ppermute | solution.py:398
  5.4 5.8 %collective-permute-start = (bf16[64,2048]{1,0:T(8,128)(2,1)S(1)}, bf16[64,2048]{1,0:T(8,128)(2,1)S(1)}, u32[]{:S(2)}, u32[]{:S(2)}) collective-permute-start(bf16[64,2048]{1,0:T(8,128)(2,1)S(1)} %copy-done.3), channel_id=1, source_target_pairs={{0,1},{1,0},{2,3},{3,2},{4,5},{5,4},{6,7},{7,6},{8,9},{9,8},{10,11... | collective-permute-start | bytes 786440 | tf_op jit(solution)/shard_map/ppermute | solution.py:348
  5.5 1.9 %slice-start = ((bf16[2048,2,768]{2,1,0:T(2,128)(2,1)}), bf16[2048,2,384]{2,1,0:T(2,128)(2,1)S(1)}, s32[]{:S(2)}) async-start(bf16[2048,2,768]{2,1,0:T(2,128)(2,1)} %param.7), calls=%async_computation | async-start | bytes 6291456 | tf_op jit(solution)/shard_map/slice | solution.py:400
  9.6 1.6 %collective-permute-start.2 = (bf16[64,2048]{1,0:T(8,128)(2,1)S(1)}, bf16[64,2048]{1,0:T(8,128)(2,1)S(1)}, u32[]{:S(2)}, u32[]{:S(2)}) collective-permute-start(bf16[64,2048]{1,0:T(8,128)(2,1)S(1)} %collective-permute-done.1.refs_2_), channel_id=1, source_target_pairs={{0,1},{1,0},{2,3},{3,2},{4,5},{5,4},{6,7},{7,6},{8,9},{9,8},{10,11... | collective-permute-start | bytes 786440 | tf_op jit(solution)/shard_map/ppermute | solution.py:348
  9.6 1.6 %collective-permute-start.5 = (bf16[16,2048]{1,0:T(8,128)(2,1)S(1)}, bf16[16,2048]{1,0:T(8,128)(2,1)S(1)}, u32[]{:S(2)}, u32[]{:S(2)}) collective-permute-start(bf16[16,2048]{1,0:T(8,128)(2,1)S(1)} %select_select_fusion.refs_4_), channel_id=1, source_target_pairs={{0,1},{1,0},{2,3},{3,2},{4,5},{5,4},{6,7},{7,6},{8,9},{9,8},{10,11... | collective-permute-start | bytes 196616 | tf_op jit(solution)/shard_map/ppermute | solution.py:348
  10.2 1.0 %copy-start.1 = (f32[4,2,512]{2,1,0:T(2,128)S(1)}, f32[4,2,512]{2,1,0:T(2,128)}, u32[]{:S(2)}) copy-start(f32[4,2,512]{2,1,0:T(2,128)} %cw.3) | copy-start | bytes 49156
  11.2 3.4 %copy-start = (bf16[512,2048]{1,0:T(8,128)(2,1)S(1)}, bf16[512,2048]{1,0:T(8,128)(2,1)}, u32[]{:S(2)}) copy-start(bf16[512,2048]{1,0:T(8,128)(2,1)} %w.1) | copy-start | bytes 6291460
  14.6 24.3 %collective-permute-start.11 = (bf16[512,2048]{1,0:T(8,128)(2,1)S(1)}, bf16[512,2048]{1,0:T(8,128)(2,1)S(1)}, u32[]{:S(2)}, u32[]{:S(2)}) collective-permute-start(bf16[512,2048]{1,0:T(8,128)(2,1)S(1)} %copy-done), channel_id=1, source_target_pairs={{0,1},{1,0},{2,3},{3,2},{4,5},{5,4},{6,7},{7,6},{8,9},{9,8},{10,11... | collective-permute-start | bytes 6291464 | tf_op jit(solution)/shard_map/ppermute | solution.py:348
  14.9 6.3 %collective-permute-start.6 = (bf16[2,128,256]{2,1,0:T(8,128)(2,1)S(1)}, bf16[2,128,256]{2,1,0:T(8,128)(2,1)S(1)}, u32[]{:S(2)}, u32[]{:S(2)}) collective-permute-start(bf16[2,128,256]{2,1,0:T(8,128)(2,1)S(1)} %get-tuple-element.42), channel_id=1, source_target_pairs={{0,4},{4,0},{8,12},{12,8},{16,20},{20,16},{24,28},{28,24},{1,5},{5... | collective-permute-start | bytes 393224 | tf_op jit(solution)/shard_map/ppermute | solution.py:348
  21.4 5.3 %collective-permute-start.7 = (bf16[2,128,256]{2,1,0:T(8,128)(2,1)S(1)}, bf16[2,128,256]{2,1,0:T(8,128)(2,1)S(1)}, u32[]{:S(2)}, u32[]{:S(2)}) collective-permute-start(bf16[2,128,256]{2,1,0:T(8,128)(2,1)S(1)} %shard_map.69.own), channel_id=1, source_target_pairs={{0,8},{4,12},{8,0},{12,4},{16,24},{20,28},{24,16},{28,20},{1,9},{5... | collective-permute-start | bytes 393224 | tf_op jit(solution)/shard_map/ppermute | solution.py:348
  26.8 5.6 %collective-permute-start.8 = (bf16[2,128,128]{2,1,0:T(8,128)(2,1)S(1)}, bf16[2,128,128]{2,1,0:T(8,128)(2,1)S(1)}, u32[]{:S(2)}, u32[]{:S(2)}) collective-permute-start(bf16[2,128,128]{2,1,0:T(8,128)(2,1)S(1)} %shard_map.70), channel_id=1, source_target_pairs={{0,16},{4,20},{8,24},{12,28},{16,0},{20,4},{24,8},{28,12},{1,17},{... | collective-permute-start | bytes 196616 | tf_op jit(solution)/shard_map/ppermute | solution.py:348
  29.4 1.6 %slice-start.1 = ((bf16[2048,2,768]{2,1,0:T(2,128)(2,1)}), bf16[2048,2,256]{2,1,0:T(2,128)(2,1)S(1)}, s32[]{:S(2)}) async-start(bf16[2048,2,768]{2,1,0:T(2,128)(2,1)} %param.7), calls=%async_computation.1 | async-start | bytes 4194304 | tf_op jit(solution)/shard_map/slice | solution.py:403
  31.0 1.2 %slice-start.2 = ((bf16[2048,2,768]{2,1,0:T(2,128)(2,1)}), bf16[2048,2,128]{2,1,0:T(2,128)(2,1)S(1)}, s32[]{:S(2)}) async-start(bf16[2048,2,768]{2,1,0:T(2,128)(2,1)} %param.7), calls=%async_computation.2 | async-start | bytes 2097152 | tf_op jit(solution)/shard_map/slice | solution.py:402
  31.5 2.8 %copy-start.2 = (f32[128]{0:T(128)S(1)}, f32[128]{0:T(128)}, u32[]{:S(2)}) copy-start(f32[128]{0:T(128)} %param.10) | copy-start | bytes 1540
  32.7 4.3 %collective-permute-start.9 = (bf16[2,128,128]{2,1,0:T(8,128)(2,1)S(1)}, bf16[2,128,128]{2,1,0:T(8,128)(2,1)S(1)}, u32[]{:S(2)}, u32[]{:S(2)}) collective-permute-start(bf16[2,128,128]{2,1,0:T(8,128)(2,1)S(1)} %get-tuple-element.44), channel_id=1, source_target_pairs={{0,4},{4,0},{8,12},{12,8},{16,20},{20,16},{24,28},{28,24},{1,5},{5... | collective-permute-start | bytes 196616 | tf_op jit(solution)/shard_map/ppermute | solution.py:348
  37.4 1.4 %collective-permute-start.10 = (bf16[128,512]{1,0:T(8,128)(2,1)S(1)}, bf16[128,512]{1,0:T(8,128)(2,1)S(1)}, u32[]{:S(2)}, u32[]{:S(2)}) collective-permute-start(bf16[128,512]{1,0:T(8,128)(2,1)S(1)} %get-tuple-element.46), channel_id=1, source_target_pairs={{0,1},{1,0},{2,3},{3,2},{4,5},{5,4},{6,7},{7,6},{8,9},{9,8},{10,11... | collective-permute-start | bytes 393224 | tf_op jit(solution)/shard_map/ppermute | solution.py:348
  39.3 10.4 %collective-permute-start.12 = (bf16[64,2048]{1,0:T(8,128)(2,1)S(1)}, bf16[64,2048]{1,0:T(8,128)(2,1)S(1)}, u32[]{:S(2)}, u32[]{:S(2)}) collective-permute-start(bf16[64,2048]{1,0:T(8,128)(2,1)S(1)} %shard_map.75), channel_id=1, source_target_pairs={{0,2},{1,3},{2,0},{3,1},{4,6},{5,7},{6,4},{7,5},{8,10},{9,11},{10,... | collective-permute-start | bytes 786440 | tf_op jit(solution)/shard_map/ppermute | solution.py:348

commit v7 on v6

--- a/solution.py
+++ b/solution.py
@@ -312,6 +312,12 @@
         send[i * part : (i + 1) * part, :] = scratch[pl.ds(at, part), :]
 
 
+def early_kernel(keep, send, w, out):
+    even = lax.axis_index("head") % 2 == 0
+    part = keep.shape[0] - out.shape[0]
+    out[...] = dot(jnp.where(even, keep[part:, :], send[part:, :]), w[...]).astype(BF16)
+
+
 def out_own_kernel(own, w, *outs):
     part = outs[0].shape[0]
     for i, out in enumerate(outs):
@@ -322,6 +328,16 @@
     part = out.shape[0]
     rows = slice(first * part, (first + 1) * part)
     out[...] = (before[...] + dot(got[rows, :], w[...])).astype(out.dtype)
+
+
+def total_kernel(*refs):
+    even = lax.axis_index("head") % 2 == 0
+    count = (len(refs) - 2) // 3
+    acc = refs[0][...]
+    for i in range(count):
+        mine, passed, late = (refs[1 + i + t * count][...].astype(F32) for t in range(3))
+        acc = acc + jnp.where(even, mine + passed, late)
+    refs[-1][...] = acc.astype(BF16)
 
 
 def call(body, out_shape, args, us, scratch=(), any_space=(), **static):
@@ -348,9 +364,17 @@
     return lax.ppermute(value, axis, [(i, i ^ step) for i in range(count)])
 
 
-def passed_along(value, axis, steps):
-    count = lax.axis_size(axis)
-    return lax.ppermute(value, axis, [(i, i + steps) for i in range(count - steps)])
+def halo_pairs(n_ctx, n_head, target):
+    source = n_head - 1
+    pairs = [((c - 1, source), (c, target)) for c in range(1, n_ctx)]
+    spare = [h for h in range(n_head) if h not in (source, target)]
+    if n_ctx % 4 == 0 and len(spare) == 2:
+        a, b = spare
+        pairs += [((0, target), (0, a)), ((n_ctx - 1, source), (n_ctx - 1, b)), ((1, a), (1, b)), ((0, b), (2, b))]
+        pairs += [((c, a), (c + 1, a)) for c in range(2, n_ctx, 2)]
+        pairs += [((c + i, b), (c + i + 2, b)) for c in range(3, n_ctx - 1, 4) for i in range(2)]
+    flat = [(c * n_head + h, d * n_head + k) for (c, h), (d, k) in pairs]
+    return sorted(flat + [(d, c) for c, d in flat])
 
 
 def local(layer_in, in_proj, conv_weight, gate_logits, norm_gain, out_proj):
@@ -391,11 +415,8 @@
     halo = jnp.zeros_like(tail)
     for h in range(n_head - 1, 0, -2):
         target = h if h < n_head - 1 else h - 1
-        perm = []
-        for c in range(1, n_ctx):
-            source, sink = (c - 1) * n_head + n_head - 1, c * n_head + target
-            perm += [(source, sink), (sink, source)]
-        halo = jnp.where(me == target, lax.ppermute(tail, ctx_head, perm), halo)
+        wanted = (me == target) & (lax.axis_index("ctx") > 0)
+        halo = jnp.where(wanted, lax.ppermute(tail, ctx_head, halo_pairs(n_ctx, n_head, target)), halo)
     v_end = 2 * DK + ratio * DV
     w_kv = in_proj[:, :, DK:v_end].reshape(width, key_heads * (v_end - DK))
     halo_core = xor_sent(halo, "head", 1)
@@ -475,18 +496,25 @@
         n_head=n_head,
     )
     other = xor_sent(send, "head", 1)
+    early = call(early_kernel, shaped((toks // 2 - part, width), BF16), [keep, send, out_proj], 0.4)
+    early_got = [
+        xor_sent(early[(i - 1) * part : i * part], "head", 2 * i) for i in range(1, n_head // 2)
+    ]
     out_shape = shaped((part, width), F32)
     sums = call(out_own_kernel, (out_shape,) * (n_head // 2), [keep, out_proj], 0.8)
-    out = None
-    partial = {}
-    for i in reversed(range(n_head // 2)):
-        shape = out_shape if i == 0 else shaped((part, width), BF16)
-        partial[i] = call(out_kernel, shape, [other, w_other, sums[i]], 0.5, first=i)
-        if i:
-            partial[i] = xor_sent(partial[i], "head", 2 * i)
-    for i in range(n_head // 2):
-        out = partial[i].astype(F32) if out is None else out + partial[i].astype(F32)
-    return out.astype(BF16)
+    late_got = []
+    for i in range(1, n_head // 2):
+        late = call(out_kernel, shaped((part, width), BF16), [other, w_other, sums[i]], 0.5, first=i)
+        late_perm = [
+            (c * n_head + h, c * n_head + (h ^ (2 * i)) if h % 2 else (c ^ 1) * n_head + h)
+            for c in range(n_ctx)
+            for h in range(n_head)
+        ]
+        late_got.append(lax.ppermute(late, ctx_head, late_perm))
+    out = call(out_kernel, out_shape, [other, w_other, sums[0]], 0.5, first=0)
+    out, *early_got = lax.optimization_barrier((out, *early_got))
+    passed = [xor_sent(mine, "head", 1) for mine in early_got]
+    return call(total_kernel, shaped((part, width), BF16), [out, *early_got, *passed, *late_got], 0.5)
 
 
 def solution(mesh):

time: 50.7 us -> 48.9 us (0.964)
  waiting for transfers between devices: 13.2 us -> 11.8 us
  Pallas kernels: 13.5 us -> 14.8 us
  starting transfers between devices: 17.3 us -> 16.4 us
  other arithmetic: 0.76 us -> 0.01 us
    ppermute x11 -> x12, waiting for transfers between devices: 13.2 us -> 8.81 us  [xor_sent(): return lax.ppermute(value, axis, [(i, i ^ step) for i in range(count)])]
    ppermute x11 -> x12, starting transfers between devices: 16 us -> 12.7 us  [xor_sent(): return lax.ppermute(value, axis, [(i, i ^ step) for i in range(count)])]
    ppermute x2 -> x3, waiting for transfers between devices: 0.01 us -> 2.96 us  [the longest x1 2.26 us: local(): late_got.append(lax.ppermute(late, ctx_head, late_perm))]
    ppermute x2 -> x3, starting transfers between devices: 1.33 us -> 3.7 us  [the longest x2 2.14 us: local(): lax.ppermute(tail, ctx_head, halo_pairs(n_ctx, n_head, target))]
    pallas_call x12 -> x14, Pallas kernels: 13.5 us -> 14.8 us  [call(): pl.pallas_call(functools.partial(body, **static), out_shape=out_shape, in...]
    convert_element_type x1 -> x0, other arithmetic: 0.75 us -> none  [local(): return out.astype(BF16)]
  transfers between devices with their start and end apart: 13 -> 15, of which waited for: 6 -> 9; matrix products, arithmetic and copies ran while one was open for 3% -> 3% of each run, Pallas kernels for 19% -> 22%
where the time goes in v7:
time: 48.9 us; the launch traced here: 48.7 us
  starting transfers between devices  16.4 us (34%)
  Pallas kernels  14.8 us (30%)
  waiting for transfers between devices  11.8 us (24%)
  local copies, waits for them, and re-layouts  5.52 us (11%)
    pallas_call x14, Pallas kernels, call(): pl.pallas_call(functools.partial(body, **static), out_shape=out_shape, in...  14.8 us
    ppermute x12, starting transfers between devices, xor_sent(): return lax.ppermute(value, axis, [(i, i ^ step) for i in range(count)])  12.7 us
    ppermute x12, waiting for transfers between devices, xor_sent(): return lax.ppermute(value, axis, [(i, i ^ step) for i in range(count)])  8.81 us
    ppermute x1, waiting for transfers between devices, local(): late_got.append(lax.ppermute(late, ctx_head, late_perm))  2.26 us
    ppermute x2, starting transfers between devices, local(): lax.ppermute(tail, ctx_head, halo_pairs(n_ctx, n_head, target))  2.14 us
    slice x2, local copies, waits for them, and re-layouts, local(): w_kv = in_proj[:, :, DK:v_end].reshape(width, key_heads * (v_end - DK))  1.89 us
    slice x2, local copies, waits for them, and re-layouts, local(): w_z = in_proj[:, :, v_end:].reshape(width, heads * DV)  1.59 us
    ppermute x1, starting transfers between devices, local(): late_got.append(lax.ppermute(late, ctx_head, late_perm))  1.56 us
  transfers between devices with their start and end apart: 15, of which 9 were waited for; matrix products, arithmetic and copies ran while one was open for 3% of the time, Pallas kernels for 22%

profile of v7, /device:TPU:0, one launch (start us, length us, event | category | flops | bytes accessed | tf_op | source)
XLA Modules:
  0.0 48.7 jit_solution(15039128144756710278)
XLA Ops:
  0.0 3.0 %collective-permute-start.1 = (bf16[64,2048]{1,0:T(8,128)(2,1)}, bf16[64,2048]{1,0:T(8,128)(2,1)S(1)}, u32[]{:S(2)}, u32[]{:S(2)}) collective-permute-start(bf16[64,2048]{1,0:T(8,128)(2,1)} %x_any.1), channel_id=1, source_target_pairs={{0,2},{1,3},{2,0},{3,1},{4,6},{5,7},{6,4},{7,5},{8,10},{9,11},{10,... | collective-permute-start | bytes 786440 | tf_op jit(solution)/shard_map/ppermute | solution.py:364
  3.0 1.1 %shard_map.64 = (bf16[16,2048]{1,0:T(8,128)(2,1)S(1)}, bf16[64,2048]{1,0:T(8,128)(2,1)S(1)}, f32[2,4,256]{2,1,0:T(4,128)S(1)}) custom-call(bf16[64,2048]{1,0:T(8,128)(2,1)} %x_any.1, f32[2,4,256]{2,1,0:T(4,128)} %logits_any.1), custom_call_target="tpu_custom_call" | custom-call | flops 6899999744 | bytes 270336 | tf_op jit(solution)/shard_map/pallas_call | solution.py:347
  4.1 2.1 %collective-permute-start.4 = (bf16[16,2048]{1,0:T(8,128)(2,1)S(1)}, bf16[16,2048]{1,0:T(8,128)(2,1)S(1)}, u32[]{:S(2)}, u32[]{:S(2)}) collective-permute-start(bf16[16,2048]{1,0:T(8,128)(2,1)S(1)} %get-tuple-element.31), channel_id=1, source_target_pairs={{0,2},{1,9},{2,0},{3,6},{4,5},{5,4},{6,3},{7,10},{8,12},{9,1},{10,... | collective-permute-start | bytes 196616 | tf_op jit(solution)/shard_map/ppermute | solution.py:419
  6.2 1.9 %slice-done = bf16[2048,2,384]{2,1,0:T(2,128)(2,1)S(1)} async-done(((bf16[2048,2,768]{2,1,0:T(2,128)(2,1)}), bf16[2048,2,384]{2,1,0:T(2,128)(2,1)S(1)}, s32[]{:S(2)}) %slice-start) | async-done | bytes 3145752 | tf_op jit(solution)/shard_map/slice | solution.py:421
  8.8 0.8 %collective-permute-done.1.refs_2_ = bf16[64,2048]{1,0:T(8,128)(2,1)S(1)} collective-permute-done((bf16[64,2048]{1,0:T(8,128)(2,1)}, bf16[64,2048]{1,0:T(8,128)(2,1)S(1)}, u32[]{:S(2)}, u32[]{:S(2)}) %collective-permute-start.1) | collective-permute-done | bytes 262176 | tf_op jit(solution)/shard_map/ppermute | solution.py:364
  9.6 0.7 %collective-permute-done.4 = bf16[16,2048]{1,0:T(8,128)(2,1)S(1)} collective-permute-done((bf16[16,2048]{1,0:T(8,128)(2,1)S(1)}, bf16[16,2048]{1,0:T(8,128)(2,1)S(1)}, u32[]{:S(2)}, u32[]{:S(2)}) %collective-permute-start.4) | collective-permute-done | bytes 65568 | tf_op jit(solution)/shard_map/ppermute | solution.py:419
  10.4 1.0 %shard_map.65 = (f32[4,256]{1,0:T(4,128)S(1)}, f32[256,8]{1,0:T(8,128)S(1)}, f32[4,3,128,128]{3,2,1,0:T(8,128)S(1)}) custom-call(f32[2,4,256]{2,1,0:T(4,128)S(1)} %get-tuple-element.32.logits), custom_call_target="tpu_custom_call" | custom-call | flops 1150000000 | bytes 8192 | tf_op jit(solution)/shard_map/pallas_call | solution.py:347
  11.6 3.4 %shard_map.66 = (bf16[2,128,256]{2,1,0:T(8,128)(2,1)S(1)}, bf16[2,256,256]{2,1,0:T(8,128)(2,1)S(1)}, bf16[1,256,128]{2,1,0:T(8,128)(2,1)S(1)}, bf16[272,2048]{1,0:T(8,128)(2,1)S(1)}) custom-call(bf16[64,2048]{1,0:T(8,128)(2,1)S(1)} %get-tuple-element.30.refs_0_, bf16[64,2048]{1,0:T(8,128)(2,1)S(1)} %collective-permute-done.refs_1_, ...), custom_call_target="tpu_custom_call" | custom-call | flops 3449999872 | bytes 5140480 | tf_op jit(solution)/shard_map/pallas_call | solution.py:347
  15.4 2.4 %collective-permute-start.6 = (bf16[2,128,256]{2,1,0:T(8,128)(2,1)S(1)}, bf16[2,128,256]{2,1,0:T(8,128)(2,1)S(1)}, u32[]{:S(2)}, u32[]{:S(2)}) collective-permute-start(bf16[2,128,256]{2,1,0:T(8,128)(2,1)S(1)} %get-tuple-element.44), channel_id=1, source_target_pairs={{0,4},{4,0},{8,12},{12,8},{16,20},{20,16},{24,28},{28,24},{1,5},{5... | collective-permute-start | bytes 393224 | tf_op jit(solution)/shard_map/ppermute | solution.py:364
  17.7 3.3 %shard_map.67 = (bf16[2,128,256]{2,1,0:T(8,128)(2,1)S(1)}, bf16[2,256,256]{2,1,0:T(8,128)(2,1)S(1)}, bf16[1,256,128]{2,1,0:T(8,128)(2,1)S(1)}) custom-call(bf16[272,2048]{1,0:T(8,128)(2,1)S(1)} %get-tuple-element.36.x, bf16[2048,768]{1,0:T(8,128)(2,1)S(1)} %bitcast.10, f32[4,2,512]{2,1,0:T(2,128)S(1)} %copy-done.1, ...), custom_call_target="tpu_custom_call" | custom-call | flops 3449999872 | bytes 5074944 | tf_op jit(solution)/shard_map/pallas_call | solution.py:347
  21.8 1.5 %collective-permute-start.7 = (bf16[2,128,256]{2,1,0:T(8,128)(2,1)S(1)}, bf16[2,128,256]{2,1,0:T(8,128)(2,1)S(1)}, u32[]{:S(2)}, u32[]{:S(2)}) collective-permute-start(bf16[2,128,256]{2,1,0:T(8,128)(2,1)S(1)} %shard_map.69.own), channel_id=1, source_target_pairs={{0,8},{4,12},{8,0},{12,4},{16,24},{20,28},{24,16},{28,20},{1,9},{5... | collective-permute-start | bytes 393224 | tf_op jit(solution)/shard_map/ppermute | solution.py:364
  23.3 3.7 %collective-permute-done.7.got.before = bf16[2,128,256]{2,1,0:T(8,128)(2,1)S(1)} collective-permute-done((bf16[2,128,256]{2,1,0:T(8,128)(2,1)S(1)}, bf16[2,128,256]{2,1,0:T(8,128)(2,1)S(1)}, u32[]{:S(2)}, u32[]{:S(2)}) %collective-permute-start.7) | collective-permute-done | bytes 131104 | tf_op jit(solution)/shard_map/ppermute | solution.py:364
  27.1 2.9 %collective-permute-start.8 = (bf16[2,128,128]{2,1,0:T(8,128)(2,1)S(1)}, bf16[2,128,128]{2,1,0:T(8,128)(2,1)S(1)}, u32[]{:S(2)}, u32[]{:S(2)}) collective-permute-start(bf16[2,128,128]{2,1,0:T(8,128)(2,1)S(1)} %shard_map.70), channel_id=1, source_target_pairs={{0,16},{4,20},{8,24},{12,28},{16,0},{20,4},{24,8},{28,12},{1,17},{... | collective-permute-start | bytes 196616 | tf_op jit(solution)/shard_map/ppermute | solution.py:364
  30.0 1.6 %slice-done.1 = bf16[2048,2,256]{2,1,0:T(2,128)(2,1)S(1)} async-done(((bf16[2048,2,768]{2,1,0:T(2,128)(2,1)}), bf16[2048,2,256]{2,1,0:T(2,128)(2,1)S(1)}, s32[]{:S(2)}) %slice-start.1) | async-done | bytes 2097176 | tf_op jit(solution)/shard_map/slice | solution.py:424
  32.1 0.7 %slice-done.2 = bf16[2048,2,128]{2,1,0:T(2,128)(2,1)S(1)} async-done(((bf16[2048,2,768]{2,1,0:T(2,128)(2,1)}), bf16[2048,2,128]{2,1,0:T(2,128)(2,1)S(1)}, s32[]{:S(2)}) %slice-start.2) | async-done | bytes 1048600 | tf_op jit(solution)/shard_map/slice | solution.py:423
  33.3 1.5 %collective-permute-start.9 = (bf16[2,128,128]{2,1,0:T(8,128)(2,1)S(1)}, bf16[2,128,128]{2,1,0:T(8,128)(2,1)S(1)}, u32[]{:S(2)}, u32[]{:S(2)}) collective-permute-start(bf16[2,128,128]{2,1,0:T(8,128)(2,1)S(1)} %get-tuple-element.46), channel_id=1, source_target_pairs={{0,4},{4,0},{8,12},{12,8},{16,20},{20,16},{24,28},{28,24},{1,5},{5... | collective-permute-start | bytes 196616 | tf_op jit(solution)/shard_map/ppermute | solution.py:364
  34.8 1.9 %shard_map.68 = (bf16[4,256,128]{2,1,0:T(8,128)(2,1)S(1)}, f32[4,256,128]{2,1,0:T(8,128)S(1)}, f32[4,256,128]{2,1,0:T(8,128)S(1)}) custom-call(bf16[272,2048]{1,0:T(8,128)(2,1)S(1)} %get-tuple-element.36.x, bf16[2048,256]{1,0:T(8,128)(2,1)S(1)} %bitcast.12, bf16[2048,512]{1,0:T(8,128)(2,1)S(1)} %bitcast.11, f32[4,2,512]{2,1,0:T(2,128)S(1)} %copy-done.1, ...), custom_call_target="tpu_custom_call" | custom-call | flops 2184999936 | bytes 4944384 | tf_op jit(solution)/shard_map/pallas_call | solution.py:347
  36.7 0.9 %collective-permute-done.9.got = bf16[2,128,128]{2,1,0:T(8,128)(2,1)S(1)} collective-permute-done((bf16[2,128,128]{2,1,0:T(8,128)(2,1)S(1)}, bf16[2,128,128]{2,1,0:T(8,128)(2,1)S(1)}, u32[]{:S(2)}, u32[]{:S(2)}) %collective-permute-start.9) | collective-permute-done | bytes 65568 | tf_op jit(solution)/shard_map/ppermute | solution.py:364
  38.5 1.1 %collective-permute-start.12 = (bf16[64,2048]{1,0:T(8,128)(2,1)S(1)}, bf16[64,2048]{1,0:T(8,128)(2,1)S(1)}, u32[]{:S(2)}, u32[]{:S(2)}) collective-permute-start(bf16[64,2048]{1,0:T(8,128)(2,1)S(1)} %shard_map.75), channel_id=1, source_target_pairs={{0,2},{1,3},{2,0},{3,1},{4,6},{5,7},{6,4},{7,5},{8,10},{9,11},{10,... | collective-permute-start | bytes 786440 | tf_op jit(solution)/shard_map/ppermute | solution.py:364
  39.6 0.8 %shard_map.73 = (f32[64,2048]{1,0:T(8,128)S(1)}, f32[64,2048]{1,0:T(8,128)S(1)}) custom-call(bf16[128,512]{1,0:T(8,128)(2,1)S(1)} %get-tuple-element.50.own.keep, bf16[512,2048]{1,0:T(8,128)(2,1)S(1)} %copy-done), custom_call_target="tpu_custom_call" | custom-call | flops 920000000 | bytes 2228224 | tf_op jit(solution)/shard_map/pallas_call | solution.py:347
  41.4 1.6 %collective-permute-start.14 = (bf16[64,2048]{1,0:T(8,128)(2,1)S(1)}, bf16[64,2048]{1,0:T(8,128)(2,1)S(1)}, u32[]{:S(2)}, u32[]{:S(2)}) collective-permute-start(bf16[64,2048]{1,0:T(8,128)(2,1)S(1)} %shard_map.76), channel_id=1, source_target_pairs={{0,4},{1,3},{2,6},{3,1},{4,0},{5,7},{6,2},{7,5},{8,12},{9,11},{10,... | collective-permute-start | bytes 786440 | tf_op jit(solution)/shard_map/ppermute | solution.py:513
  43.5 2.1 %collective-permute-done.12.refs_1_ = bf16[64,2048]{1,0:T(8,128)(2,1)S(1)} collective-permute-done((bf16[64,2048]{1,0:T(8,128)(2,1)S(1)}, bf16[64,2048]{1,0:T(8,128)(2,1)S(1)}, u32[]{:S(2)}, u32[]{:S(2)}) %collective-permute-start.12) | collective-permute-done | bytes 262176 | tf_op jit(solution)/shard_map/ppermute | solution.py:364
  45.6 2.3 %collective-permute-done.14.refs_3_ = bf16[64,2048]{1,0:T(8,128)(2,1)S(1)} collective-permute-done((bf16[64,2048]{1,0:T(8,128)(2,1)S(1)}, bf16[64,2048]{1,0:T(8,128)(2,1)S(1)}, u32[]{:S(2)}, u32[]{:S(2)}) %collective-permute-start.14) | collective-permute-done | bytes 262176 | tf_op jit(solution)/shard_map/ppermute | solution.py:513
  47.9 0.8 %shard_map.77 = bf16[64,2048]{1,0:T(8,128)(2,1)} custom-call(f32[64,2048]{1,0:T(8,128)S(1)} %shard_map.74.refs_0_, bf16[64,2048]{1,0:T(8,128)(2,1)S(1)} %collective-permute-done.12.refs_1_, bf16[64,2048]{1,0:T(8,128)(2,1)S(1)} %collective-permute-done.13.refs_2_, bf16[64,2048]{1,0:T(8,128)(2,1)S(1)} %collective-permute-done.14.refs_3_), custom_call_target="tpu_custom_call" | custom-call | flops 575000000 | bytes 1310720 | tf_op jit(solution)/shard_map/pallas_call | solution.py:347
  (38 shorter events, 5.7 us)
Async XLA Ops:
  0.0 6.2 %copy-start.3 = (bf16[64,2048]{1,0:T(8,128)(2,1)S(1)}, bf16[64,2048]{1,0:T(8,128)(2,1)}, u32[]{:S(2)}) copy-start(bf16[64,2048]{1,0:T(8,128)(2,1)} %x_any.1) | copy-start | bytes 786436
  0.0 9.6 %collective-permute-start.1 = (bf16[64,2048]{1,0:T(8,128)(2,1)}, bf16[64,2048]{1,0:T(8,128)(2,1)S(1)}, u32[]{:S(2)}, u32[]{:S(2)}) collective-permute-start(bf16[64,2048]{1,0:T(8,128)(2,1)} %x_any.1), channel_id=1, source_target_pairs={{0,2},{1,3},{2,0},{3,1},{4,6},{5,7},{6,4},{7,5},{8,10},{9,11},{10,... | collective-permute-start | bytes 786440 | tf_op jit(solution)/shard_map/ppermute | solution.py:364
  4.0 5.5 %collective-permute-start.3 = (bf16[16,2048]{1,0:T(8,128)(2,1)S(1)}, bf16[16,2048]{1,0:T(8,128)(2,1)S(1)}, u32[]{:S(2)}, u32[]{:S(2)}) collective-permute-start(bf16[16,2048]{1,0:T(8,128)(2,1)S(1)} %get-tuple-element.31), channel_id=1, source_target_pairs={{0,1},{1,0},{2,10},{3,5},{4,6},{5,3},{6,4},{7,9},{8,12},{9,7},{10,... | collective-permute-start | bytes 196616 | tf_op jit(solution)/shard_map/ppermute | solution.py:419
  4.1 6.1 %collective-permute-start.4 = (bf16[16,2048]{1,0:T(8,128)(2,1)S(1)}, bf16[16,2048]{1,0:T(8,128)(2,1)S(1)}, u32[]{:S(2)}, u32[]{:S(2)}) collective-permute-start(bf16[16,2048]{1,0:T(8,128)(2,1)S(1)} %get-tuple-element.31), channel_id=1, source_target_pairs={{0,2},{1,9},{2,0},{3,6},{4,5},{5,4},{6,3},{7,10},{8,12},{9,1},{10,... | collective-permute-start | bytes 196616 | tf_op jit(solution)/shard_map/ppermute | solution.py:419
  6.2 5.4 %collective-permute-start = (bf16[64,2048]{1,0:T(8,128)(2,1)S(1)}, bf16[64,2048]{1,0:T(8,128)(2,1)S(1)}, u32[]{:S(2)}, u32[]{:S(2)}) collective-permute-start(bf16[64,2048]{1,0:T(8,128)(2,1)S(1)} %copy-done.3), channel_id=1, source_target_pairs={{0,1},{1,0},{2,3},{3,2},{4,5},{5,4},{6,7},{7,6},{8,9},{9,8},{10,11... | collective-permute-start | bytes 786440 | tf_op jit(solution)/shard_map/ppermute | solution.py:364
  6.2 1.9 %slice-start = ((bf16[2048,2,768]{2,1,0:T(2,128)(2,1)}), bf16[2048,2,384]{2,1,0:T(2,128)(2,1)S(1)}, s32[]{:S(2)}) async-start(bf16[2048,2,768]{2,1,0:T(2,128)(2,1)} %param.7), calls=%async_computation | async-start | bytes 6291456 | tf_op jit(solution)/shard_map/slice | solution.py:421
  9.6 2.0 %collective-permute-start.2 = (bf16[64,2048]{1,0:T(8,128)(2,1)S(1)}, bf16[64,2048]{1,0:T(8,128)(2,1)S(1)}, u32[]{:S(2)}, u32[]{:S(2)}) collective-permute-start(bf16[64,2048]{1,0:T(8,128)(2,1)S(1)} %collective-permute-done.1.refs_2_), channel_id=1, source_target_pairs={{0,1},{1,0},{2,3},{3,2},{4,5},{5,4},{6,7},{7,6},{8,9},{9,8},{10,11... | collective-permute-start | bytes 786440 | tf_op jit(solution)/shard_map/ppermute | solution.py:364
  10.3 1.3 %collective-permute-start.5 = (bf16[16,2048]{1,0:T(8,128)(2,1)S(1)}, bf16[16,2048]{1,0:T(8,128)(2,1)S(1)}, u32[]{:S(2)}, u32[]{:S(2)}) collective-permute-start(bf16[16,2048]{1,0:T(8,128)(2,1)S(1)} %select_select_fusion.refs_4_), channel_id=1, source_target_pairs={{0,1},{1,0},{2,3},{3,2},{4,5},{5,4},{6,7},{7,6},{8,9},{9,8},{10,11... | collective-permute-start | bytes 196616 | tf_op jit(solution)/shard_map/ppermute | solution.py:364
  10.3 1.2 %copy-start.1 = (f32[4,2,512]{2,1,0:T(2,128)S(1)}, f32[4,2,512]{2,1,0:T(2,128)}, u32[]{:S(2)}) copy-start(f32[4,2,512]{2,1,0:T(2,128)} %cw.3) | copy-start | bytes 49156
  11.6 3.4 %copy-start = (bf16[512,2048]{1,0:T(8,128)(2,1)S(1)}, bf16[512,2048]{1,0:T(8,128)(2,1)}, u32[]{:S(2)}) copy-start(bf16[512,2048]{1,0:T(8,128)(2,1)} %w.3) | copy-start | bytes 6291460
  15.0 25.9 %collective-permute-start.11 = (bf16[512,2048]{1,0:T(8,128)(2,1)S(1)}, bf16[512,2048]{1,0:T(8,128)(2,1)S(1)}, u32[]{:S(2)}, u32[]{:S(2)}) collective-permute-start(bf16[512,2048]{1,0:T(8,128)(2,1)S(1)} %copy-done), channel_id=1, source_target_pairs={{0,1},{1,0},{2,3},{3,2},{4,5},{5,4},{6,7},{7,6},{8,9},{9,8},{10,11... | collective-permute-start | bytes 6291464 | tf_op jit(solution)/shard_map/ppermute | solution.py:364
  15.4 6.2 %collective-permute-start.6 = (bf16[2,128,256]{2,1,0:T(8,128)(2,1)S(1)}, bf16[2,128,256]{2,1,0:T(8,128)(2,1)S(1)}, u32[]{:S(2)}, u32[]{:S(2)}) collective-permute-start(bf16[2,128,256]{2,1,0:T(8,128)(2,1)S(1)} %get-tuple-element.44), channel_id=1, source_target_pairs={{0,4},{4,0},{8,12},{12,8},{16,20},{20,16},{24,28},{28,24},{1,5},{5... | collective-permute-start | bytes 393224 | tf_op jit(solution)/shard_map/ppermute | solution.py:364
  21.8 5.2 %collective-permute-start.7 = (bf16[2,128,256]{2,1,0:T(8,128)(2,1)S(1)}, bf16[2,128,256]{2,1,0:T(8,128)(2,1)S(1)}, u32[]{:S(2)}, u32[]{:S(2)}) collective-permute-start(bf16[2,128,256]{2,1,0:T(8,128)(2,1)S(1)} %shard_map.69.own), channel_id=1, source_target_pairs={{0,8},{4,12},{8,0},{12,4},{16,24},{20,28},{24,16},{28,20},{1,9},{5... | collective-permute-start | bytes 393224 | tf_op jit(solution)/shard_map/ppermute | solution.py:364
  27.1 5.8 %collective-permute-start.8 = (bf16[2,128,128]{2,1,0:T(8,128)(2,1)S(1)}, bf16[2,128,128]{2,1,0:T(8,128)(2,1)S(1)}, u32[]{:S(2)}, u32[]{:S(2)}) collective-permute-start(bf16[2,128,128]{2,1,0:T(8,128)(2,1)S(1)} %shard_map.70), channel_id=1, source_target_pairs={{0,16},{4,20},{8,24},{12,28},{16,0},{20,4},{24,8},{28,12},{1,17},{... | collective-permute-start | bytes 196616 | tf_op jit(solution)/shard_map/ppermute | solution.py:364
  30.0 1.6 %slice-start.1 = ((bf16[2048,2,768]{2,1,0:T(2,128)(2,1)}), bf16[2048,2,256]{2,1,0:T(2,128)(2,1)S(1)}, s32[]{:S(2)}) async-start(bf16[2048,2,768]{2,1,0:T(2,128)(2,1)} %param.7), calls=%async_computation.1 | async-start | bytes 4194304 | tf_op jit(solution)/shard_map/slice | solution.py:424
  31.6 1.2 %slice-start.2 = ((bf16[2048,2,768]{2,1,0:T(2,128)(2,1)}), bf16[2048,2,128]{2,1,0:T(2,128)(2,1)S(1)}, s32[]{:S(2)}) async-start(bf16[2048,2,768]{2,1,0:T(2,128)(2,1)} %param.7), calls=%async_computation.2 | async-start | bytes 2097152 | tf_op jit(solution)/shard_map/slice | solution.py:423
  32.1 2.7 %copy-start.2 = (f32[128]{0:T(128)S(1)}, f32[128]{0:T(128)}, u32[]{:S(2)}) copy-start(f32[128]{0:T(128)} %param.10) | copy-start | bytes 1540
  33.3 4.3 %collective-permute-start.9 = (bf16[2,128,128]{2,1,0:T(8,128)(2,1)S(1)}, bf16[2,128,128]{2,1,0:T(8,128)(2,1)S(1)}, u32[]{:S(2)}, u32[]{:S(2)}) collective-permute-start(bf16[2,128,128]{2,1,0:T(8,128)(2,1)S(1)} %get-tuple-element.46), channel_id=1, source_target_pairs={{0,4},{4,0},{8,12},{12,8},{16,20},{20,16},{24,28},{28,24},{1,5},{5... | collective-permute-start | bytes 196616 | tf_op jit(solution)/shard_map/ppermute | solution.py:364
  38.5 7.1 %collective-permute-start.12 = (bf16[64,2048]{1,0:T(8,128)(2,1)S(1)}, bf16[64,2048]{1,0:T(8,128)(2,1)S(1)}, u32[]{:S(2)}, u32[]{:S(2)}) collective-permute-start(bf16[64,2048]{1,0:T(8,128)(2,1)S(1)} %shard_map.75), channel_id=1, source_target_pairs={{0,2},{1,3},{2,0},{3,1},{4,6},{5,7},{6,4},{7,5},{8,10},{9,11},{10,... | collective-permute-start | bytes 786440 | tf_op jit(solution)/shard_map/ppermute | solution.py:364
  39.6 1.3 %collective-permute-start.10 = (bf16[128,512]{1,0:T(8,128)(2,1)S(1)}, bf16[128,512]{1,0:T(8,128)(2,1)S(1)}, u32[]{:S(2)}, u32[]{:S(2)}) collective-permute-start(bf16[128,512]{1,0:T(8,128)(2,1)S(1)} %get-tuple-element.48.send), channel_id=1, source_target_pairs={{0,1},{1,0},{2,3},{3,2},{4,5},{5,4},{6,7},{7,6},{8,9},{9,8},{10,11... | collective-permute-start | bytes 393224 | tf_op jit(solution)/shard_map/ppermute | solution.py:364
  41.4 6.4 %collective-permute-start.14 = (bf16[64,2048]{1,0:T(8,128)(2,1)S(1)}, bf16[64,2048]{1,0:T(8,128)(2,1)S(1)}, u32[]{:S(2)}, u32[]{:S(2)}) collective-permute-start(bf16[64,2048]{1,0:T(8,128)(2,1)S(1)} %shard_map.76), channel_id=1, source_target_pairs={{0,4},{1,3},{2,6},{3,1},{4,0},{5,7},{6,2},{7,5},{8,12},{9,11},{10,... | collective-permute-start | bytes 786440 | tf_op jit(solution)/shard_map/ppermute | solution.py:513
  45.6 2.3 %collective-permute-start.13 = (bf16[64,2048]{1,0:T(8,128)(2,1)S(1)}, bf16[64,2048]{1,0:T(8,128)(2,1)S(1)}, u32[]{:S(2)}, u32[]{:S(2)}) collective-permute-start(bf16[64,2048]{1,0:T(8,128)(2,1)S(1)} %collective-permute-done.12.refs_1_), channel_id=1, source_target_pairs={{0,1},{1,0},{2,3},{3,2},{4,5},{5,4},{6,7},{7,6},{8,9},{9,8},{10,11... | collective-permute-start | bytes 786440 | tf_op jit(solution)/shard_map/ppermute | solution.py:364

commit v8 on v7

--- a/solution.py
+++ b/solution.py
@@ -57,7 +57,7 @@
     return (1 - odd if local < half else odd) * half + local % half
 
 
-def fetch_kernel(x_any, logits_any, tail, x_own, logits, sems):
+def fetch_kernel(x_any, logits_any, packed, x_own, logits, tail, rows, sems):
     logits_copy = pltpu.make_async_copy(logits_any, logits, sems.at[2])
     tail_copy = pltpu.make_async_copy(x_any.at[pl.ds(x_any.shape[0] - HALO, HALO), :], tail, sems.at[0])
     own_copy = pltpu.make_async_copy(x_any, x_own, sems.at[1])
@@ -65,6 +65,14 @@
     own_copy.start()
     logits_copy.start()
     tail_copy.wait()
+    width = tail.shape[1]
+    last = tail[...].astype(F32)
+    taps = KERNEL - 1
+    for r in range(taps):
+        for t in range(width // 128):
+            at = r * (width // 128) + t
+            rows[at : at + 1, :] = last[HALO - taps + r : HALO - taps + r + 1, t * 128 : (t + 1) * 128]
+    packed[...] = rows[...].astype(BF16)
     own_copy.wait()
     logits_copy.wait()
 
@@ -187,11 +195,18 @@
 
 def keys_first_kernel(*refs, n_head, key_heads, ratio):
     pieces = refs[:n_head]
-    halo, halo_core, w, cw, cols, rows, decays, s_out, y_out, k_out, x_out, padded = refs[n_head:]
+    halo, halo_core, w, cw, cols, rows, decays, s_out, y_out, k_out, x_out, padded, halo_rows = refs[n_head:]
     me = lax.axis_index("head")
     part = pieces[0].shape[0]
     direct = (me % 2 == 1) != (me >= n_head - 2)
-    x_out[0:HALO, :] = jnp.where(direct, halo[...], halo_core[...])
+    given = jnp.where(direct, halo[...].astype(F32), halo_core[...].astype(F32))
+    taps, tiles = KERNEL - 1, x_out.shape[1] // 128
+    halo_rows[...] = jnp.zeros_like(halo_rows)
+    for r in range(taps):
+        for t in range(tiles):
+            at = HALO - taps + r
+            halo_rows[at : at + 1, t * 128 : (t + 1) * 128] = given[r * tiles + t : r * tiles + t + 1, :]
+    x_out[0:HALO, :] = halo_rows[...].astype(BF16)
     for s in range(n_head):
         at = pl.multiple_of(HALO + (me ^ s) * part, 16)
         x_out[pl.ds(at, part), :] = pieces[s][...]
@@ -393,12 +408,13 @@
             pieces[s + step] = xor_sent(pieces[s], "head", step)
         step //= 2
     blocks = toks // HALF
+    packed_shape = shaped(((KERNEL - 1) * (width // 128), 128), BF16)
     tail, x_own, logits = call(
         fetch_kernel,
-        (shaped((HALO, width), BF16), shaped((part, width), BF16), shaped(gate_logits.shape, F32)),
+        (packed_shape, shaped((part, width), BF16), shaped(gate_logits.shape, F32)),
         [layer_in, gate_logits],
         6.0,
-        [pltpu.SemaphoreType.DMA((3,))],
+        [pltpu.VMEM((HALO, width), BF16), pltpu.VMEM(packed_shape.shape, F32), pltpu.SemaphoreType.DMA((3,))],
         any_space=(0, 1),
     )
     rows, cols, decays = call(
@@ -419,6 +435,7 @@
         halo = jnp.where(wanted, lax.ppermute(tail, ctx_head, halo_pairs(n_ctx, n_head, target)), halo)
     v_end = 2 * DK + ratio * DV
     w_kv = in_proj[:, :, DK:v_end].reshape(width, key_heads * (v_end - DK))
+    halo, w_kv = lax.optimization_barrier((halo, w_kv))
     halo_core = xor_sent(halo, "head", 1)
     w_q = in_proj[:, :, 0:DK].reshape(width, key_heads * DK)
     w_z = in_proj[:, :, v_end:].reshape(width, heads * DV)
@@ -435,7 +452,7 @@
         (pair_shape, ys_shape, keys_shape, shaped((HALO + toks, width), BF16)),
         [x_own, *pieces[1:], halo, halo_core, w_kv, conv_weight, cols, rows, decays],
         3.0,
-        [padded],
+        [padded, pltpu.VMEM((HALO, width), F32)],
         n_head=n_head,
         key_heads=key_heads,
         ratio=ratio,
@@ -451,20 +468,12 @@
         ratio=ratio,
     )
     w_other = xor_sent(lax.optimization_barrier((out_proj, s_send))[0], "head", 1)
-    o_shape = shaped((heads, toks, DV), F32)
-    q, o, gate = call(
-        queries_kernel,
-        (shaped((heads, toks, DK), BF16), o_shape, o_shape),
-        [x_full, w_q, w_z, conv_weight, cols, rows, keys_a, keys_b, ys_a, ys_b, norm_gain[None, :]],
-        1.9,
-        [pltpu.VMEM((key_heads, HALO + toks, 128), F32)],
-        key_heads=key_heads,
-        ratio=ratio,
-    )
     total = call(join_kernel, pair_shape, [s_keep, s_pair], 0.2, step=1)
     step, before, before_step = 2, None, 2
     while 2 * step < n_ctx:
         got = xor_sent(total, "ctx", step)
+        if step == 2:
+            got, w_q, w_z = lax.optimization_barrier((got, w_q, w_z))
         more = 4 * step < n_ctx
         total = call(join_kernel, pair_shape if more else state_shape, [total, got], 0.2, step=step)
         if before is None:
@@ -486,6 +495,16 @@
         step=step,
     )
     got_state = xor_sent(out_state, "ctx", 1)
+    o_shape = shaped((heads, toks, DV), F32)
+    q, o, gate = call(
+        queries_kernel,
+        (shaped((heads, toks, DK), BF16), o_shape, o_shape),
+        [x_full, w_q, w_z, conv_weight, cols, rows, keys_a, keys_b, ys_a, ys_b, norm_gain[None, :]],
+        1.9,
+        [pltpu.VMEM((key_heads, HALO + toks, 128), F32)],
+        key_heads=key_heads,
+        ratio=ratio,
+    )
     rows_shape = shaped((toks // 2, heads * DV), BF16)
     keep, send = call(
         normed_kernel,

time: 48.9 us -> 48 us (0.982)
  waiting for transfers between devices: 11.8 us -> 9.86 us
  starting transfers between devices: 16.4 us -> 17.3 us
    ppermute x12, waiting for transfers between devices: 8.81 us -> 6.67 us  [xor_sent(): return lax.ppermute(value, axis, [(i, i ^ step) for i in range(count)])]
    ppermute x12, starting transfers between devices: 12.7 us -> 13.6 us  [xor_sent(): return lax.ppermute(value, axis, [(i, i ^ step) for i in range(count)])]
    ppermute x1, waiting for transfers between devices: 2.26 us -> 3.06 us  [local(): late_got.append(lax.ppermute(late, ctx_head, late_perm))]
    ppermute x2, waiting for transfers between devices: 0.7 us -> 0.13 us  [local(): lax.ppermute(tail, ctx_head, halo_pairs(n_ctx, n_head, target))]
where the time goes in v8:
time: 48 us; the launch traced here: 47.7 us
  starting transfers between devices  17.3 us (36%)
  Pallas kernels  14.8 us (31%)
  waiting for transfers between devices  9.86 us (21%)
  local copies, waits for them, and re-layouts  5.53 us (12%)
    pallas_call x14, Pallas kernels, call(): pl.pallas_call(functools.partial(body, **static), out_shape=out_shape, in...  14.8 us
    ppermute x12, starting transfers between devices, xor_sent(): return lax.ppermute(value, axis, [(i, i ^ step) for i in range(count)])  13.6 us
    ppermute x12, waiting for transfers between devices, xor_sent(): return lax.ppermute(value, axis, [(i, i ^ step) for i in range(count)])  6.67 us
    ppermute x1, waiting for transfers between devices, local(): late_got.append(lax.ppermute(late, ctx_head, late_perm))  3.06 us
    ppermute x2, starting transfers between devices, local(): lax.ppermute(tail, ctx_head, halo_pairs(n_ctx, n_head, target))  2.14 us
    slice x2, local copies, waits for them, and re-layouts, local(): w_kv = in_proj[:, :, DK:v_end].reshape(width, key_heads * (v_end - DK))  1.89 us
    slice x2, local copies, waits for them, and re-layouts, local(): w_z = in_proj[:, :, v_end:].reshape(width, heads * DV)  1.59 us
    ppermute x1, starting transfers between devices, local(): late_got.append(lax.ppermute(late, ctx_head, late_perm))  1.57 us
  transfers between devices with their start and end apart: 15, of which 9 were waited for; matrix products, arithmetic and copies ran while one was open for 3% of the time, Pallas kernels for 22%

profile of v8, /device:TPU:0, one launch (start us, length us, event | category | flops | bytes accessed | tf_op | source)
XLA Modules:
  0.0 47.7 jit_solution(17576771440493048309)
XLA Ops:
  0.0 3.0 %collective-permute-start.1 = (bf16[64,2048]{1,0:T(8,128)(2,1)}, bf16[64,2048]{1,0:T(8,128)(2,1)S(1)}, u32[]{:S(2)}, u32[]{:S(2)}) collective-permute-start(bf16[64,2048]{1,0:T(8,128)(2,1)} %x_any.1), channel_id=1, source_target_pairs={{0,2},{1,3},{2,0},{3,1},{4,6},{5,7},{6,4},{7,5},{8,10},{9,11},{10,... | collective-permute-start | bytes 786440 | tf_op jit(solution)/shard_map/ppermute | solution.py:379
  3.0 1.1 %shard_map.64 = (bf16[48,128]{1,0:T(8,128)(2,1)S(1)}, bf16[64,2048]{1,0:T(8,128)(2,1)S(1)}, f32[2,4,256]{2,1,0:T(4,128)S(1)}) custom-call(bf16[64,2048]{1,0:T(8,128)(2,1)} %x_any.1, f32[2,4,256]{2,1,0:T(4,128)} %logits_any.1), custom_call_target="tpu_custom_call" | custom-call | flops 6899999744 | bytes 270336 | tf_op jit(solution)/shard_map/pallas_call | solution.py:362
  4.1 2.1 %collective-permute-start.4 = (bf16[48,128]{1,0:T(8,128)(2,1)S(1)}, bf16[48,128]{1,0:T(8,128)(2,1)S(1)}, u32[]{:S(2)}, u32[]{:S(2)}) collective-permute-start(bf16[48,128]{1,0:T(8,128)(2,1)S(1)} %get-tuple-element.36), channel_id=1, source_target_pairs={{0,2},{1,9},{2,0},{3,6},{4,5},{5,4},{6,3},{7,10},{8,12},{9,1},{10,... | collective-permute-start | bytes 36872 | tf_op jit(solution)/shard_map/ppermute | solution.py:435
  6.2 1.9 %slice-done = bf16[2048,2,384]{2,1,0:T(2,128)(2,1)S(1)} async-done(((bf16[2048,2,768]{2,1,0:T(2,128)(2,1)}), bf16[2048,2,384]{2,1,0:T(2,128)(2,1)S(1)}, s32[]{:S(2)}) %slice-start) | async-done | bytes 3145752 | tf_op jit(solution)/shard_map/slice | solution.py:437
  8.1 0.7 %copy.7 = bf16[256,8,2,384]{3,1,2,0:T(8,128)(2,1)S(1)} copy(bf16[256,8,2,384]{3,2,1,0:T(2,128)(2,1)S(1)} %bitcast.14) | data formatting | bytes 6291456
  8.8 0.8 %collective-permute-done.1.refs_2_ = bf16[64,2048]{1,0:T(8,128)(2,1)S(1)} collective-permute-done((bf16[64,2048]{1,0:T(8,128)(2,1)}, bf16[64,2048]{1,0:T(8,128)(2,1)S(1)}, u32[]{:S(2)}, u32[]{:S(2)}) %collective-permute-start.1) | collective-permute-done | bytes 262176 | tf_op jit(solution)/shard_map/ppermute | solution.py:379
  10.1 1.0 %shard_map.65 = (f32[4,256]{1,0:T(4,128)S(1)}, f32[256,8]{1,0:T(8,128)S(1)}, f32[4,3,128,128]{3,2,1,0:T(8,128)S(1)}) custom-call(f32[2,4,256]{2,1,0:T(4,128)S(1)} %get-tuple-element.39.logits), custom_call_target="tpu_custom_call" | custom-call | flops 1150000000 | bytes 8192 | tf_op jit(solution)/shard_map/pallas_call | solution.py:362
  11.2 3.4 %shard_map.66 = (bf16[2,128,256]{2,1,0:T(8,128)(2,1)S(1)}, bf16[2,256,256]{2,1,0:T(8,128)(2,1)S(1)}, bf16[1,256,128]{2,1,0:T(8,128)(2,1)S(1)}, bf16[272,2048]{1,0:T(8,128)(2,1)S(1)}) custom-call(bf16[64,2048]{1,0:T(8,128)(2,1)S(1)} %get-tuple-element.35.refs_0_, bf16[64,2048]{1,0:T(8,128)(2,1)S(1)} %collective-permute-done.refs_1_, ...), custom_call_target="tpu_custom_call" | custom-call | flops 3449999872 | bytes 5033984 | tf_op jit(solution)/shard_map/pallas_call | solution.py:362
  14.8 1.8 %collective-permute-start.6 = (bf16[2,128,256]{2,1,0:T(8,128)(2,1)S(1)}, bf16[2,128,256]{2,1,0:T(8,128)(2,1)S(1)}, u32[]{:S(2)}, u32[]{:S(2)}) collective-permute-start(bf16[2,128,256]{2,1,0:T(8,128)(2,1)S(1)} %get-tuple-element.45), channel_id=1, source_target_pairs={{0,4},{4,0},{8,12},{12,8},{16,20},{20,16},{24,28},{28,24},{1,5},{5... | collective-permute-start | bytes 393224 | tf_op jit(solution)/shard_map/ppermute | solution.py:379
  16.6 3.3 %shard_map.67 = (bf16[2,128,256]{2,1,0:T(8,128)(2,1)S(1)}, bf16[2,256,256]{2,1,0:T(8,128)(2,1)S(1)}, bf16[1,256,128]{2,1,0:T(8,128)(2,1)S(1)}) custom-call(bf16[272,2048]{1,0:T(8,128)(2,1)S(1)} %get-tuple-element.43.x, bf16[2048,768]{1,0:T(8,128)(2,1)S(1)} %bitcast.10, f32[4,2,512]{2,1,0:T(2,128)S(1)} %copy-done.1, ...), custom_call_target="tpu_custom_call" | custom-call | flops 3449999872 | bytes 5074944 | tf_op jit(solution)/shard_map/pallas_call | solution.py:362
  19.9 0.7 %collective-permute-done.6.got.pair = bf16[2,128,256]{2,1,0:T(8,128)(2,1)S(1)} collective-permute-done((bf16[2,128,256]{2,1,0:T(8,128)(2,1)S(1)}, bf16[2,128,256]{2,1,0:T(8,128)(2,1)S(1)}, u32[]{:S(2)}, u32[]{:S(2)}) %collective-permute-start.6) | collective-permute-done | bytes 131104 | tf_op jit(solution)/shard_map/ppermute | solution.py:379
  20.8 1.9 %collective-permute-start.7 = (bf16[2,128,256]{2,1,0:T(8,128)(2,1)S(1)}, bf16[2,128,256]{2,1,0:T(8,128)(2,1)S(1)}, u32[]{:S(2)}, u32[]{:S(2)}) collective-permute-start(bf16[2,128,256]{2,1,0:T(8,128)(2,1)S(1)} %shard_map.68.own), channel_id=1, source_target_pairs={{0,8},{4,12},{8,0},{12,4},{16,24},{20,28},{24,16},{28,20},{1,9},{5... | collective-permute-start | bytes 393224 | tf_op jit(solution)/shard_map/ppermute | solution.py:379
  22.7 1.6 %slice-done.1 = bf16[2048,2,256]{2,1,0:T(2,128)(2,1)S(1)} async-done(((bf16[2048,2,768]{2,1,0:T(2,128)(2,1)}), bf16[2048,2,256]{2,1,0:T(2,128)(2,1)S(1)}, s32[]{:S(2)}) %slice-start.1) | async-done | bytes 2097176 | tf_op jit(solution)/shard_map/slice | solution.py:441
  24.8 0.7 %slice-done.2 = bf16[2048,2,128]{2,1,0:T(2,128)(2,1)S(1)} async-done(((bf16[2048,2,768]{2,1,0:T(2,128)(2,1)}), bf16[2048,2,128]{2,1,0:T(2,128)(2,1)S(1)}, s32[]{:S(2)}) %slice-start.2) | async-done | bytes 1048600 | tf_op jit(solution)/shard_map/slice | solution.py:440
  26.1 2.8 %collective-permute-start.8 = (bf16[2,128,128]{2,1,0:T(8,128)(2,1)S(1)}, bf16[2,128,128]{2,1,0:T(8,128)(2,1)S(1)}, u32[]{:S(2)}, u32[]{:S(2)}) collective-permute-start(bf16[2,128,128]{2,1,0:T(8,128)(2,1)S(1)} %shard_map.70), channel_id=1, source_target_pairs={{0,16},{4,20},{8,24},{12,28},{16,0},{20,4},{24,8},{28,12},{1,17},{... | collective-permute-start | bytes 196616 | tf_op jit(solution)/shard_map/ppermute | solution.py:379
  28.9 2.4 %collective-permute-done.8.got = bf16[2,128,128]{2,1,0:T(8,128)(2,1)S(1)} collective-permute-done((bf16[2,128,128]{2,1,0:T(8,128)(2,1)S(1)}, bf16[2,128,128]{2,1,0:T(8,128)(2,1)S(1)}, u32[]{:S(2)}, u32[]{:S(2)}) %collective-permute-start.8) | collective-permute-done | bytes 65568 | tf_op jit(solution)/shard_map/ppermute | solution.py:379
  31.6 1.7 %collective-permute-start.9 = (bf16[2,128,128]{2,1,0:T(8,128)(2,1)S(1)}, bf16[2,128,128]{2,1,0:T(8,128)(2,1)S(1)}, u32[]{:S(2)}, u32[]{:S(2)}) collective-permute-start(bf16[2,128,128]{2,1,0:T(8,128)(2,1)S(1)} %get-tuple-element.56), channel_id=1, source_target_pairs={{0,4},{4,0},{8,12},{12,8},{16,20},{20,16},{24,28},{28,24},{1,5},{5... | collective-permute-start | bytes 196616 | tf_op jit(solution)/shard_map/ppermute | solution.py:379
  33.4 2.0 %shard_map.69 = (bf16[4,256,128]{2,1,0:T(8,128)(2,1)S(1)}, f32[4,256,128]{2,1,0:T(8,128)S(1)}, f32[4,256,128]{2,1,0:T(8,128)S(1)}) custom-call(bf16[272,2048]{1,0:T(8,128)(2,1)S(1)} %get-tuple-element.43.x, bf16[2048,256]{1,0:T(8,128)(2,1)S(1)} %bitcast.12, bf16[2048,512]{1,0:T(8,128)(2,1)S(1)} %bitcast.11, f32[4,2,512]{2,1,0:T(2,128)S(1)} %copy-done.1, ...), custom_call_target="tpu_custom_call" | custom-call | flops 2184999936 | bytes 4944384 | tf_op jit(solution)/shard_map/pallas_call | solution.py:362
  36.9 1.8 %collective-permute-start.12 = (bf16[64,2048]{1,0:T(8,128)(2,1)S(1)}, bf16[64,2048]{1,0:T(8,128)(2,1)S(1)}, u32[]{:S(2)}, u32[]{:S(2)}) collective-permute-start(bf16[64,2048]{1,0:T(8,128)(2,1)S(1)} %shard_map.75), channel_id=1, source_target_pairs={{0,2},{1,3},{2,0},{3,1},{4,6},{5,7},{6,4},{7,5},{8,10},{9,11},{10,... | collective-permute-start | bytes 786440 | tf_op jit(solution)/shard_map/ppermute | solution.py:379
  38.6 0.8 %shard_map.73 = (f32[64,2048]{1,0:T(8,128)S(1)}, f32[64,2048]{1,0:T(8,128)S(1)}) custom-call(bf16[128,512]{1,0:T(8,128)(2,1)S(1)} %get-tuple-element.60.own.keep, bf16[512,2048]{1,0:T(8,128)(2,1)S(1)} %copy-done), custom_call_target="tpu_custom_call" | custom-call | flops 920000000 | bytes 2228224 | tf_op jit(solution)/shard_map/pallas_call | solution.py:362
  40.5 1.6 %collective-permute-start.14 = (bf16[64,2048]{1,0:T(8,128)(2,1)S(1)}, bf16[64,2048]{1,0:T(8,128)(2,1)S(1)}, u32[]{:S(2)}, u32[]{:S(2)}) collective-permute-start(bf16[64,2048]{1,0:T(8,128)(2,1)S(1)} %shard_map.76), channel_id=1, source_target_pairs={{0,4},{1,3},{2,6},{3,1},{4,0},{5,7},{6,2},{7,5},{8,12},{9,11},{10,... | collective-permute-start | bytes 786440 | tf_op jit(solution)/shard_map/ppermute | solution.py:532
  42.5 1.3 %collective-permute-done.12.refs_1_ = bf16[64,2048]{1,0:T(8,128)(2,1)S(1)} collective-permute-done((bf16[64,2048]{1,0:T(8,128)(2,1)S(1)}, bf16[64,2048]{1,0:T(8,128)(2,1)S(1)}, u32[]{:S(2)}, u32[]{:S(2)}) %collective-permute-start.12) | collective-permute-done | bytes 262176 | tf_op jit(solution)/shard_map/ppermute | solution.py:379
  43.8 3.1 %collective-permute-done.14.refs_3_ = bf16[64,2048]{1,0:T(8,128)(2,1)S(1)} collective-permute-done((bf16[64,2048]{1,0:T(8,128)(2,1)S(1)}, bf16[64,2048]{1,0:T(8,128)(2,1)S(1)}, u32[]{:S(2)}, u32[]{:S(2)}) %collective-permute-start.14) | collective-permute-done | bytes 262176 | tf_op jit(solution)/shard_map/ppermute | solution.py:532
  46.9 0.8 %shard_map.77 = bf16[64,2048]{1,0:T(8,128)(2,1)} custom-call(f32[64,2048]{1,0:T(8,128)S(1)} %shard_map.74.refs_0_, bf16[64,2048]{1,0:T(8,128)(2,1)S(1)} %collective-permute-done.12.refs_1_, bf16[64,2048]{1,0:T(8,128)(2,1)S(1)} %collective-permute-done.13.refs_2_, bf16[64,2048]{1,0:T(8,128)(2,1)S(1)} %collective-permute-done.14.refs_3_), custom_call_target="tpu_custom_call" | custom-call | flops 575000000 | bytes 1310720 | tf_op jit(solution)/shard_map/pallas_call | solution.py:362
  (38 shorter events, 5.5 us)
Async XLA Ops:
  0.0 6.2 %copy-start.3 = (bf16[64,2048]{1,0:T(8,128)(2,1)S(1)}, bf16[64,2048]{1,0:T(8,128)(2,1)}, u32[]{:S(2)}) copy-start(bf16[64,2048]{1,0:T(8,128)(2,1)} %x_any.1) | copy-start | bytes 786436
  0.0 9.6 %collective-permute-start.1 = (bf16[64,2048]{1,0:T(8,128)(2,1)}, bf16[64,2048]{1,0:T(8,128)(2,1)S(1)}, u32[]{:S(2)}, u32[]{:S(2)}) collective-permute-start(bf16[64,2048]{1,0:T(8,128)(2,1)} %x_any.1), channel_id=1, source_target_pairs={{0,2},{1,3},{2,0},{3,1},{4,6},{5,7},{6,4},{7,5},{8,10},{9,11},{10,... | collective-permute-start | bytes 786440 | tf_op jit(solution)/shard_map/ppermute | solution.py:379
  4.0 5.5 %collective-permute-start.3 = (bf16[48,128]{1,0:T(8,128)(2,1)S(1)}, bf16[48,128]{1,0:T(8,128)(2,1)S(1)}, u32[]{:S(2)}, u32[]{:S(2)}) collective-permute-start(bf16[48,128]{1,0:T(8,128)(2,1)S(1)} %get-tuple-element.36), channel_id=1, source_target_pairs={{0,1},{1,0},{2,10},{3,5},{4,6},{5,3},{6,4},{7,9},{8,12},{9,7},{10,... | collective-permute-start | bytes 36872 | tf_op jit(solution)/shard_map/ppermute | solution.py:435
  4.1 5.6 %collective-permute-start.4 = (bf16[48,128]{1,0:T(8,128)(2,1)S(1)}, bf16[48,128]{1,0:T(8,128)(2,1)S(1)}, u32[]{:S(2)}, u32[]{:S(2)}) collective-permute-start(bf16[48,128]{1,0:T(8,128)(2,1)S(1)} %get-tuple-element.36), channel_id=1, source_target_pairs={{0,2},{1,9},{2,0},{3,6},{4,5},{5,4},{6,3},{7,10},{8,12},{9,1},{10,... | collective-permute-start | bytes 36872 | tf_op jit(solution)/shard_map/ppermute | solution.py:435
  6.2 5.0 %collective-permute-start = (bf16[64,2048]{1,0:T(8,128)(2,1)S(1)}, bf16[64,2048]{1,0:T(8,128)(2,1)S(1)}, u32[]{:S(2)}, u32[]{:S(2)}) collective-permute-start(bf16[64,2048]{1,0:T(8,128)(2,1)S(1)} %copy-done.3), channel_id=1, source_target_pairs={{0,1},{1,0},{2,3},{3,2},{4,5},{5,4},{6,7},{7,6},{8,9},{9,8},{10,11... | collective-permute-start | bytes 786440 | tf_op jit(solution)/shard_map/ppermute | solution.py:379
  6.2 1.9 %slice-start = ((bf16[2048,2,768]{2,1,0:T(2,128)(2,1)}), bf16[2048,2,384]{2,1,0:T(2,128)(2,1)S(1)}, s32[]{:S(2)}) async-start(bf16[2048,2,768]{2,1,0:T(2,128)(2,1)} %param.7), calls=%async_computation | async-start | bytes 6291456 | tf_op jit(solution)/shard_map/slice | solution.py:437
  9.6 1.6 %collective-permute-start.2 = (bf16[64,2048]{1,0:T(8,128)(2,1)S(1)}, bf16[64,2048]{1,0:T(8,128)(2,1)S(1)}, u32[]{:S(2)}, u32[]{:S(2)}) collective-permute-start(bf16[64,2048]{1,0:T(8,128)(2,1)S(1)} %collective-permute-done.1.refs_2_), channel_id=1, source_target_pairs={{0,1},{1,0},{2,3},{3,2},{4,5},{5,4},{6,7},{7,6},{8,9},{9,8},{10,11... | collective-permute-start | bytes 786440 | tf_op jit(solution)/shard_map/ppermute | solution.py:379
  9.7 1.5 %collective-permute-start.5 = (bf16[48,128]{1,0:T(8,128)(2,1)S(1)}, bf16[48,128]{1,0:T(8,128)(2,1)S(1)}, u32[]{:S(2)}, u32[]{:S(2)}) collective-permute-start(bf16[48,128]{1,0:T(8,128)(2,1)S(1)} %select_select_fusion.refs_4_), channel_id=1, source_target_pairs={{0,1},{1,0},{2,3},{3,2},{4,5},{5,4},{6,7},{7,6},{8,9},{9,8},{10,11... | collective-permute-start | bytes 36872 | tf_op jit(solution)/shard_map/ppermute | solution.py:379
  10.1 1.0 %copy-start.1 = (f32[4,2,512]{2,1,0:T(2,128)S(1)}, f32[4,2,512]{2,1,0:T(2,128)}, u32[]{:S(2)}) copy-start(f32[4,2,512]{2,1,0:T(2,128)} %cw.3) | copy-start | bytes 49156
  11.2 3.4 %copy-start = (bf16[512,2048]{1,0:T(8,128)(2,1)S(1)}, bf16[512,2048]{1,0:T(8,128)(2,1)}, u32[]{:S(2)}) copy-start(bf16[512,2048]{1,0:T(8,128)(2,1)} %w.3) | copy-start | bytes 6291460
  14.6 25.4 %collective-permute-start.11 = (bf16[512,2048]{1,0:T(8,128)(2,1)S(1)}, bf16[512,2048]{1,0:T(8,128)(2,1)S(1)}, u32[]{:S(2)}, u32[]{:S(2)}) collective-permute-start(bf16[512,2048]{1,0:T(8,128)(2,1)S(1)} %copy-done), channel_id=1, source_target_pairs={{0,1},{1,0},{2,3},{3,2},{4,5},{5,4},{6,7},{7,6},{8,9},{9,8},{10,11... | collective-permute-start | bytes 6291464 | tf_op jit(solution)/shard_map/ppermute | solution.py:379
  14.8 5.8 %collective-permute-start.6 = (bf16[2,128,256]{2,1,0:T(8,128)(2,1)S(1)}, bf16[2,128,256]{2,1,0:T(8,128)(2,1)S(1)}, u32[]{:S(2)}, u32[]{:S(2)}) collective-permute-start(bf16[2,128,256]{2,1,0:T(8,128)(2,1)S(1)} %get-tuple-element.45), channel_id=1, source_target_pairs={{0,4},{4,0},{8,12},{12,8},{16,20},{20,16},{24,28},{28,24},{1,5},{5... | collective-permute-start | bytes 393224 | tf_op jit(solution)/shard_map/ppermute | solution.py:379
  20.8 5.1 %collective-permute-start.7 = (bf16[2,128,256]{2,1,0:T(8,128)(2,1)S(1)}, bf16[2,128,256]{2,1,0:T(8,128)(2,1)S(1)}, u32[]{:S(2)}, u32[]{:S(2)}) collective-permute-start(bf16[2,128,256]{2,1,0:T(8,128)(2,1)S(1)} %shard_map.68.own), channel_id=1, source_target_pairs={{0,8},{4,12},{8,0},{12,4},{16,24},{20,28},{24,16},{28,20},{1,9},{5... | collective-permute-start | bytes 393224 | tf_op jit(solution)/shard_map/ppermute | solution.py:379
  22.7 1.6 %slice-start.1 = ((bf16[2048,2,768]{2,1,0:T(2,128)(2,1)}), bf16[2048,2,256]{2,1,0:T(2,128)(2,1)S(1)}, s32[]{:S(2)}) async-start(bf16[2048,2,768]{2,1,0:T(2,128)(2,1)} %param.7), calls=%async_computation.1 | async-start | bytes 4194304 | tf_op jit(solution)/shard_map/slice | solution.py:441
  24.3 1.2 %slice-start.2 = ((bf16[2048,2,768]{2,1,0:T(2,128)(2,1)}), bf16[2048,2,128]{2,1,0:T(2,128)(2,1)S(1)}, s32[]{:S(2)}) async-start(bf16[2048,2,768]{2,1,0:T(2,128)(2,1)} %param.7), calls=%async_computation.2 | async-start | bytes 2097152 | tf_op jit(solution)/shard_map/slice | solution.py:440
  25.5 7.8 %copy-start.2 = (f32[128]{0:T(128)S(1)}, f32[128]{0:T(128)}, u32[]{:S(2)}) copy-start(f32[128]{0:T(128)} %param.10) | copy-start | bytes 1540
  26.1 5.2 %collective-permute-start.8 = (bf16[2,128,128]{2,1,0:T(8,128)(2,1)S(1)}, bf16[2,128,128]{2,1,0:T(8,128)(2,1)S(1)}, u32[]{:S(2)}, u32[]{:S(2)}) collective-permute-start(bf16[2,128,128]{2,1,0:T(8,128)(2,1)S(1)} %shard_map.70), channel_id=1, source_target_pairs={{0,16},{4,20},{8,24},{12,28},{16,0},{20,4},{24,8},{28,12},{1,17},{... | collective-permute-start | bytes 196616 | tf_op jit(solution)/shard_map/ppermute | solution.py:379
  31.6 4.3 %collective-permute-start.9 = (bf16[2,128,128]{2,1,0:T(8,128)(2,1)S(1)}, bf16[2,128,128]{2,1,0:T(8,128)(2,1)S(1)}, u32[]{:S(2)}, u32[]{:S(2)}) collective-permute-start(bf16[2,128,128]{2,1,0:T(8,128)(2,1)S(1)} %get-tuple-element.56), channel_id=1, source_target_pairs={{0,4},{4,0},{8,12},{12,8},{16,20},{20,16},{24,28},{28,24},{1,5},{5... | collective-permute-start | bytes 196616 | tf_op jit(solution)/shard_map/ppermute | solution.py:379
  36.9 7.0 %collective-permute-start.12 = (bf16[64,2048]{1,0:T(8,128)(2,1)S(1)}, bf16[64,2048]{1,0:T(8,128)(2,1)S(1)}, u32[]{:S(2)}, u32[]{:S(2)}) collective-permute-start(bf16[64,2048]{1,0:T(8,128)(2,1)S(1)} %shard_map.75), channel_id=1, source_target_pairs={{0,2},{1,3},{2,0},{3,1},{4,6},{5,7},{6,4},{7,5},{8,10},{9,11},{10,... | collective-permute-start | bytes 786440 | tf_op jit(solution)/shard_map/ppermute | solution.py:379
  38.6 1.3 %collective-permute-start.10 = (bf16[128,512]{1,0:T(8,128)(2,1)S(1)}, bf16[128,512]{1,0:T(8,128)(2,1)S(1)}, u32[]{:S(2)}, u32[]{:S(2)}) collective-permute-start(bf16[128,512]{1,0:T(8,128)(2,1)S(1)} %get-tuple-element.58.send), channel_id=1, source_target_pairs={{0,1},{1,0},{2,3},{3,2},{4,5},{5,4},{6,7},{7,6},{8,9},{9,8},{10,11... | collective-permute-start | bytes 393224 | tf_op jit(solution)/shard_map/ppermute | solution.py:379
  40.5 6.4 %collective-permute-start.14 = (bf16[64,2048]{1,0:T(8,128)(2,1)S(1)}, bf16[64,2048]{1,0:T(8,128)(2,1)S(1)}, u32[]{:S(2)}, u32[]{:S(2)}) collective-permute-start(bf16[64,2048]{1,0:T(8,128)(2,1)S(1)} %shard_map.76), channel_id=1, source_target_pairs={{0,4},{1,3},{2,6},{3,1},{4,0},{5,7},{6,2},{7,5},{8,12},{9,11},{10,... | collective-permute-start | bytes 786440 | tf_op jit(solution)/shard_map/ppermute | solution.py:532
  43.8 3.1 %collective-permute-start.13 = (bf16[64,2048]{1,0:T(8,128)(2,1)S(1)}, bf16[64,2048]{1,0:T(8,128)(2,1)S(1)}, u32[]{:S(2)}, u32[]{:S(2)}) collective-permute-start(bf16[64,2048]{1,0:T(8,128)(2,1)S(1)} %collective-permute-done.12.refs_1_), channel_id=1, source_target_pairs={{0,1},{1,0},{2,3},{3,2},{4,5},{5,4},{6,7},{7,6},{8,9},{9,8},{10,11... | collective-permute-start | bytes 786440 | tf_op jit(solution)/shard_map/ppermute | solution.py:379

commit v9 on v8

--- a/solution.py
+++ b/solution.py
@@ -163,14 +163,16 @@
                         off[(a, b)] = m.astype(BF16)
             offs.append(off)
     inv = [eye - jnp.where(level == 1, m, 0.0) for m in lowers]
+    inv_b = [m.astype(BF16) for m in inv]
     size = 2
     while size < HALF:
-        here = (level >= size) & (level < 2 * size)
+        here = (level >= size) & (level < 4 * size)
+        steps = [dot(x, jnp.where(here, m, 0.0).astype(BF16)).astype(BF16) for m, x in zip(lowers, inv_b)]
+        squares = [dot(n, n).astype(BF16) for n in steps]
+        inv = [x - dot(n, xb) for x, xb, n in zip(inv, inv_b, steps)]
+        inv = [x + dot(n, x.astype(BF16)) for x, n in zip(inv, squares)]
         inv_b = [m.astype(BF16) for m in inv]
-        cx = [dot(jnp.where(here, m, 0.0).astype(BF16), x).astype(BF16) for m, x in zip(lowers, inv_b)]
-        inv = [x - dot(xb, c) for x, xb, c in zip(inv, inv_b, cx)]
-        size *= 2
-    inv_b = [m.astype(BF16) for m in inv]
+        size *= 4
     solved = [[] for _ in rhs]
     for a in range(blocks):
         for j, given in enumerate(rhs):

time: 48 us -> 47.7 us (level)
  Pallas kernels: 14.8 us -> 14.2 us
    pallas_call x14, Pallas kernels: 14.8 us -> 14.2 us  [call(): pl.pallas_call(functools.partial(body, **static), out_shape=out_shape, in...]
where the time goes in v9:
time: 47.7 us; the launch traced here: 47.4 us
  starting transfers between devices  17.3 us (36%)
  Pallas kernels  14.2 us (30%)
  waiting for transfers between devices  10.1 us (21%)
  local copies, waits for them, and re-layouts  5.53 us (12%)
    pallas_call x14, Pallas kernels, call(): pl.pallas_call(functools.partial(body, **static), out_shape=out_shape, in...  14.2 us
    ppermute x12, starting transfers between devices, xor_sent(): return lax.ppermute(value, axis, [(i, i ^ step) for i in range(count)])  13.6 us
    ppermute x12, waiting for transfers between devices, xor_sent(): return lax.ppermute(value, axis, [(i, i ^ step) for i in range(count)])  6.98 us
    ppermute x1, waiting for transfers between devices, local(): late_got.append(lax.ppermute(late, ctx_head, late_perm))  3.04 us
    ppermute x2, starting transfers between devices, local(): lax.ppermute(tail, ctx_head, halo_pairs(n_ctx, n_head, target))  2.14 us
    slice x2, local copies, waits for them, and re-layouts, local(): w_kv = in_proj[:, :, DK:v_end].reshape(width, key_heads * (v_end - DK))  1.89 us
    slice x2, local copies, waits for them, and re-layouts, local(): w_z = in_proj[:, :, v_end:].reshape(width, heads * DV)  1.59 us
    ppermute x1, starting transfers between devices, local(): late_got.append(lax.ppermute(late, ctx_head, late_perm))  1.55 us
  transfers between devices with their start and end apart: 15, of which 9 were waited for; matrix products, arithmetic and copies ran while one was open for 3% of the time, Pallas kernels for 22%

profile of v9, /device:TPU:0, one launch (start us, length us, event | category | flops | bytes accessed | tf_op | source)
XLA Modules:
  0.0 47.4 jit_solution(6137110527194331608)
XLA Ops:
  0.0 3.0 %collective-permute-start.1 = (bf16[64,2048]{1,0:T(8,128)(2,1)}, bf16[64,2048]{1,0:T(8,128)(2,1)S(1)}, u32[]{:S(2)}, u32[]{:S(2)}) collective-permute-start(bf16[64,2048]{1,0:T(8,128)(2,1)} %x_any.1), channel_id=1, source_target_pairs={{0,2},{1,3},{2,0},{3,1},{4,6},{5,7},{6,4},{7,5},{8,10},{9,11},{10,... | collective-permute-start | bytes 786440 | tf_op jit(solution)/shard_map/ppermute | solution.py:381
  3.0 1.1 %shard_map.64 = (bf16[48,128]{1,0:T(8,128)(2,1)S(1)}, bf16[64,2048]{1,0:T(8,128)(2,1)S(1)}, f32[2,4,256]{2,1,0:T(4,128)S(1)}) custom-call(bf16[64,2048]{1,0:T(8,128)(2,1)} %x_any.1, f32[2,4,256]{2,1,0:T(4,128)} %logits_any.1), custom_call_target="tpu_custom_call" | custom-call | flops 6899999744 | bytes 270336 | tf_op jit(solution)/shard_map/pallas_call | solution.py:364
  4.1 2.1 %collective-permute-start.4 = (bf16[48,128]{1,0:T(8,128)(2,1)S(1)}, bf16[48,128]{1,0:T(8,128)(2,1)S(1)}, u32[]{:S(2)}, u32[]{:S(2)}) collective-permute-start(bf16[48,128]{1,0:T(8,128)(2,1)S(1)} %get-tuple-element.36), channel_id=1, source_target_pairs={{0,2},{1,9},{2,0},{3,6},{4,5},{5,4},{6,3},{7,10},{8,12},{9,1},{10,... | collective-permute-start | bytes 36872 | tf_op jit(solution)/shard_map/ppermute | solution.py:437
  6.2 1.9 %slice-done = bf16[2048,2,384]{2,1,0:T(2,128)(2,1)S(1)} async-done(((bf16[2048,2,768]{2,1,0:T(2,128)(2,1)}), bf16[2048,2,384]{2,1,0:T(2,128)(2,1)S(1)}, s32[]{:S(2)}) %slice-start) | async-done | bytes 3145752 | tf_op jit(solution)/shard_map/slice | solution.py:439
  8.1 0.7 %copy.7 = bf16[256,8,2,384]{3,1,2,0:T(8,128)(2,1)S(1)} copy(bf16[256,8,2,384]{3,2,1,0:T(2,128)(2,1)S(1)} %bitcast.14) | data formatting | bytes 6291456
  8.8 0.8 %collective-permute-done.1.refs_2_ = bf16[64,2048]{1,0:T(8,128)(2,1)S(1)} collective-permute-done((bf16[64,2048]{1,0:T(8,128)(2,1)}, bf16[64,2048]{1,0:T(8,128)(2,1)S(1)}, u32[]{:S(2)}, u32[]{:S(2)}) %collective-permute-start.1) | collective-permute-done | bytes 262176 | tf_op jit(solution)/shard_map/ppermute | solution.py:381
  10.1 1.0 %shard_map.65 = (f32[4,256]{1,0:T(4,128)S(1)}, f32[256,8]{1,0:T(8,128)S(1)}, f32[4,3,128,128]{3,2,1,0:T(8,128)S(1)}) custom-call(f32[2,4,256]{2,1,0:T(4,128)S(1)} %get-tuple-element.39.logits), custom_call_target="tpu_custom_call" | custom-call | flops 1150000000 | bytes 8192 | tf_op jit(solution)/shard_map/pallas_call | solution.py:364
  11.2 3.1 %shard_map.66 = (bf16[2,128,256]{2,1,0:T(8,128)(2,1)S(1)}, bf16[2,256,256]{2,1,0:T(8,128)(2,1)S(1)}, bf16[1,256,128]{2,1,0:T(8,128)(2,1)S(1)}, bf16[272,2048]{1,0:T(8,128)(2,1)S(1)}) custom-call(bf16[64,2048]{1,0:T(8,128)(2,1)S(1)} %get-tuple-element.35.refs_0_, bf16[64,2048]{1,0:T(8,128)(2,1)S(1)} %collective-permute-done.refs_1_, ...), custom_call_target="tpu_custom_call" | custom-call | flops 3449999872 | bytes 5033984 | tf_op jit(solution)/shard_map/pallas_call | solution.py:364
  14.5 1.8 %collective-permute-start.6 = (bf16[2,128,256]{2,1,0:T(8,128)(2,1)S(1)}, bf16[2,128,256]{2,1,0:T(8,128)(2,1)S(1)}, u32[]{:S(2)}, u32[]{:S(2)}) collective-permute-start(bf16[2,128,256]{2,1,0:T(8,128)(2,1)S(1)} %get-tuple-element.45), channel_id=1, source_target_pairs={{0,4},{4,0},{8,12},{12,8},{16,20},{20,16},{24,28},{28,24},{1,5},{5... | collective-permute-start | bytes 393224 | tf_op jit(solution)/shard_map/ppermute | solution.py:381
  16.3 3.0 %shard_map.67 = (bf16[2,128,256]{2,1,0:T(8,128)(2,1)S(1)}, bf16[2,256,256]{2,1,0:T(8,128)(2,1)S(1)}, bf16[1,256,128]{2,1,0:T(8,128)(2,1)S(1)}) custom-call(bf16[272,2048]{1,0:T(8,128)(2,1)S(1)} %get-tuple-element.43.x, bf16[2048,768]{1,0:T(8,128)(2,1)S(1)} %bitcast.10, f32[4,2,512]{2,1,0:T(2,128)S(1)} %copy-done.1, ...), custom_call_target="tpu_custom_call" | custom-call | flops 3449999872 | bytes 5074944 | tf_op jit(solution)/shard_map/pallas_call | solution.py:364
  19.3 1.0 %collective-permute-done.6.got.pair = bf16[2,128,256]{2,1,0:T(8,128)(2,1)S(1)} collective-permute-done((bf16[2,128,256]{2,1,0:T(8,128)(2,1)S(1)}, bf16[2,128,256]{2,1,0:T(8,128)(2,1)S(1)}, u32[]{:S(2)}, u32[]{:S(2)}) %collective-permute-start.6) | collective-permute-done | bytes 131104 | tf_op jit(solution)/shard_map/ppermute | solution.py:381
  20.5 1.9 %collective-permute-start.7 = (bf16[2,128,256]{2,1,0:T(8,128)(2,1)S(1)}, bf16[2,128,256]{2,1,0:T(8,128)(2,1)S(1)}, u32[]{:S(2)}, u32[]{:S(2)}) collective-permute-start(bf16[2,128,256]{2,1,0:T(8,128)(2,1)S(1)} %shard_map.68.own), channel_id=1, source_target_pairs={{0,8},{4,12},{8,0},{12,4},{16,24},{20,28},{24,16},{28,20},{1,9},{5... | collective-permute-start | bytes 393224 | tf_op jit(solution)/shard_map/ppermute | solution.py:381
  22.4 1.6 %slice-done.1 = bf16[2048,2,256]{2,1,0:T(2,128)(2,1)S(1)} async-done(((bf16[2048,2,768]{2,1,0:T(2,128)(2,1)}), bf16[2048,2,256]{2,1,0:T(2,128)(2,1)S(1)}, s32[]{:S(2)}) %slice-start.1) | async-done | bytes 2097176 | tf_op jit(solution)/shard_map/slice | solution.py:443
  24.5 0.7 %slice-done.2 = bf16[2048,2,128]{2,1,0:T(2,128)(2,1)S(1)} async-done(((bf16[2048,2,768]{2,1,0:T(2,128)(2,1)}), bf16[2048,2,128]{2,1,0:T(2,128)(2,1)S(1)}, s32[]{:S(2)}) %slice-start.2) | async-done | bytes 1048600 | tf_op jit(solution)/shard_map/slice | solution.py:442
  25.8 2.8 %collective-permute-start.8 = (bf16[2,128,128]{2,1,0:T(8,128)(2,1)S(1)}, bf16[2,128,128]{2,1,0:T(8,128)(2,1)S(1)}, u32[]{:S(2)}, u32[]{:S(2)}) collective-permute-start(bf16[2,128,128]{2,1,0:T(8,128)(2,1)S(1)} %shard_map.70), channel_id=1, source_target_pairs={{0,16},{4,20},{8,24},{12,28},{16,0},{20,4},{24,8},{28,12},{1,17},{... | collective-permute-start | bytes 196616 | tf_op jit(solution)/shard_map/ppermute | solution.py:381
  28.6 2.4 %collective-permute-done.8.got = bf16[2,128,128]{2,1,0:T(8,128)(2,1)S(1)} collective-permute-done((bf16[2,128,128]{2,1,0:T(8,128)(2,1)S(1)}, bf16[2,128,128]{2,1,0:T(8,128)(2,1)S(1)}, u32[]{:S(2)}, u32[]{:S(2)}) %collective-permute-start.8) | collective-permute-done | bytes 65568 | tf_op jit(solution)/shard_map/ppermute | solution.py:381
  31.3 1.7 %collective-permute-start.9 = (bf16[2,128,128]{2,1,0:T(8,128)(2,1)S(1)}, bf16[2,128,128]{2,1,0:T(8,128)(2,1)S(1)}, u32[]{:S(2)}, u32[]{:S(2)}) collective-permute-start(bf16[2,128,128]{2,1,0:T(8,128)(2,1)S(1)} %get-tuple-element.56), channel_id=1, source_target_pairs={{0,4},{4,0},{8,12},{12,8},{16,20},{20,16},{24,28},{28,24},{1,5},{5... | collective-permute-start | bytes 196616 | tf_op jit(solution)/shard_map/ppermute | solution.py:381
  33.0 2.0 %shard_map.69 = (bf16[4,256,128]{2,1,0:T(8,128)(2,1)S(1)}, f32[4,256,128]{2,1,0:T(8,128)S(1)}, f32[4,256,128]{2,1,0:T(8,128)S(1)}) custom-call(bf16[272,2048]{1,0:T(8,128)(2,1)S(1)} %get-tuple-element.43.x, bf16[2048,256]{1,0:T(8,128)(2,1)S(1)} %bitcast.12, bf16[2048,512]{1,0:T(8,128)(2,1)S(1)} %bitcast.11, f32[4,2,512]{2,1,0:T(2,128)S(1)} %copy-done.1, ...), custom_call_target="tpu_custom_call" | custom-call | flops 2184999936 | bytes 4944384 | tf_op jit(solution)/shard_map/pallas_call | solution.py:364
  36.5 1.8 %collective-permute-start.12 = (bf16[64,2048]{1,0:T(8,128)(2,1)S(1)}, bf16[64,2048]{1,0:T(8,128)(2,1)S(1)}, u32[]{:S(2)}, u32[]{:S(2)}) collective-permute-start(bf16[64,2048]{1,0:T(8,128)(2,1)S(1)} %shard_map.75), channel_id=1, source_target_pairs={{0,2},{1,3},{2,0},{3,1},{4,6},{5,7},{6,4},{7,5},{8,10},{9,11},{10,... | collective-permute-start | bytes 786440 | tf_op jit(solution)/shard_map/ppermute | solution.py:381
  38.3 0.8 %shard_map.73 = (f32[64,2048]{1,0:T(8,128)S(1)}, f32[64,2048]{1,0:T(8,128)S(1)}) custom-call(bf16[128,512]{1,0:T(8,128)(2,1)S(1)} %get-tuple-element.60.own.keep, bf16[512,2048]{1,0:T(8,128)(2,1)S(1)} %copy-done), custom_call_target="tpu_custom_call" | custom-call | flops 920000000 | bytes 2228224 | tf_op jit(solution)/shard_map/pallas_call | solution.py:364
  40.2 1.6 %collective-permute-start.14 = (bf16[64,2048]{1,0:T(8,128)(2,1)S(1)}, bf16[64,2048]{1,0:T(8,128)(2,1)S(1)}, u32[]{:S(2)}, u32[]{:S(2)}) collective-permute-start(bf16[64,2048]{1,0:T(8,128)(2,1)S(1)} %shard_map.76), channel_id=1, source_target_pairs={{0,4},{1,3},{2,6},{3,1},{4,0},{5,7},{6,2},{7,5},{8,12},{9,11},{10,... | collective-permute-start | bytes 786440 | tf_op jit(solution)/shard_map/ppermute | solution.py:534
  42.2 1.4 %collective-permute-done.12.refs_1_ = bf16[64,2048]{1,0:T(8,128)(2,1)S(1)} collective-permute-done((bf16[64,2048]{1,0:T(8,128)(2,1)S(1)}, bf16[64,2048]{1,0:T(8,128)(2,1)S(1)}, u32[]{:S(2)}, u32[]{:S(2)}) %collective-permute-start.12) | collective-permute-done | bytes 262176 | tf_op jit(solution)/shard_map/ppermute | solution.py:381
  43.6 3.0 %collective-permute-done.14.refs_3_ = bf16[64,2048]{1,0:T(8,128)(2,1)S(1)} collective-permute-done((bf16[64,2048]{1,0:T(8,128)(2,1)S(1)}, bf16[64,2048]{1,0:T(8,128)(2,1)S(1)}, u32[]{:S(2)}, u32[]{:S(2)}) %collective-permute-start.14) | collective-permute-done | bytes 262176 | tf_op jit(solution)/shard_map/ppermute | solution.py:534
  46.6 0.8 %shard_map.77 = bf16[64,2048]{1,0:T(8,128)(2,1)} custom-call(f32[64,2048]{1,0:T(8,128)S(1)} %shard_map.74.refs_0_, bf16[64,2048]{1,0:T(8,128)(2,1)S(1)} %collective-permute-done.12.refs_1_, bf16[64,2048]{1,0:T(8,128)(2,1)S(1)} %collective-permute-done.13.refs_2_, bf16[64,2048]{1,0:T(8,128)(2,1)S(1)} %collective-permute-done.14.refs_3_), custom_call_target="tpu_custom_call" | custom-call | flops 575000000 | bytes 1310720 | tf_op jit(solution)/shard_map/pallas_call | solution.py:364
  (38 shorter events, 5.4 us)
Async XLA Ops:
  0.0 6.2 %copy-start.3 = (bf16[64,2048]{1,0:T(8,128)(2,1)S(1)}, bf16[64,2048]{1,0:T(8,128)(2,1)}, u32[]{:S(2)}) copy-start(bf16[64,2048]{1,0:T(8,128)(2,1)} %x_any.1) | copy-start | bytes 786436
  0.0 9.6 %collective-permute-start.1 = (bf16[64,2048]{1,0:T(8,128)(2,1)}, bf16[64,2048]{1,0:T(8,128)(2,1)S(1)}, u32[]{:S(2)}, u32[]{:S(2)}) collective-permute-start(bf16[64,2048]{1,0:T(8,128)(2,1)} %x_any.1), channel_id=1, source_target_pairs={{0,2},{1,3},{2,0},{3,1},{4,6},{5,7},{6,4},{7,5},{8,10},{9,11},{10,... | collective-permute-start | bytes 786440 | tf_op jit(solution)/shard_map/ppermute | solution.py:381
  4.0 5.5 %collective-permute-start.3 = (bf16[48,128]{1,0:T(8,128)(2,1)S(1)}, bf16[48,128]{1,0:T(8,128)(2,1)S(1)}, u32[]{:S(2)}, u32[]{:S(2)}) collective-permute-start(bf16[48,128]{1,0:T(8,128)(2,1)S(1)} %get-tuple-element.36), channel_id=1, source_target_pairs={{0,1},{1,0},{2,10},{3,5},{4,6},{5,3},{6,4},{7,9},{8,12},{9,7},{10,... | collective-permute-start | bytes 36872 | tf_op jit(solution)/shard_map/ppermute | solution.py:437
  4.1 5.6 %collective-permute-start.4 = (bf16[48,128]{1,0:T(8,128)(2,1)S(1)}, bf16[48,128]{1,0:T(8,128)(2,1)S(1)}, u32[]{:S(2)}, u32[]{:S(2)}) collective-permute-start(bf16[48,128]{1,0:T(8,128)(2,1)S(1)} %get-tuple-element.36), channel_id=1, source_target_pairs={{0,2},{1,9},{2,0},{3,6},{4,5},{5,4},{6,3},{7,10},{8,12},{9,1},{10,... | collective-permute-start | bytes 36872 | tf_op jit(solution)/shard_map/ppermute | solution.py:437
  6.2 5.0 %collective-permute-start = (bf16[64,2048]{1,0:T(8,128)(2,1)S(1)}, bf16[64,2048]{1,0:T(8,128)(2,1)S(1)}, u32[]{:S(2)}, u32[]{:S(2)}) collective-permute-start(bf16[64,2048]{1,0:T(8,128)(2,1)S(1)} %copy-done.3), channel_id=1, source_target_pairs={{0,1},{1,0},{2,3},{3,2},{4,5},{5,4},{6,7},{7,6},{8,9},{9,8},{10,11... | collective-permute-start | bytes 786440 | tf_op jit(solution)/shard_map/ppermute | solution.py:381
  6.2 1.9 %slice-start = ((bf16[2048,2,768]{2,1,0:T(2,128)(2,1)}), bf16[2048,2,384]{2,1,0:T(2,128)(2,1)S(1)}, s32[]{:S(2)}) async-start(bf16[2048,2,768]{2,1,0:T(2,128)(2,1)} %param.7), calls=%async_computation | async-start | bytes 6291456 | tf_op jit(solution)/shard_map/slice | solution.py:439
  9.6 1.6 %collective-permute-start.2 = (bf16[64,2048]{1,0:T(8,128)(2,1)S(1)}, bf16[64,2048]{1,0:T(8,128)(2,1)S(1)}, u32[]{:S(2)}, u32[]{:S(2)}) collective-permute-start(bf16[64,2048]{1,0:T(8,128)(2,1)S(1)} %collective-permute-done.1.refs_2_), channel_id=1, source_target_pairs={{0,1},{1,0},{2,3},{3,2},{4,5},{5,4},{6,7},{7,6},{8,9},{9,8},{10,11... | collective-permute-start | bytes 786440 | tf_op jit(solution)/shard_map/ppermute | solution.py:381
  9.7 1.5 %collective-permute-start.5 = (bf16[48,128]{1,0:T(8,128)(2,1)S(1)}, bf16[48,128]{1,0:T(8,128)(2,1)S(1)}, u32[]{:S(2)}, u32[]{:S(2)}) collective-permute-start(bf16[48,128]{1,0:T(8,128)(2,1)S(1)} %select_select_fusion.refs_4_), channel_id=1, source_target_pairs={{0,1},{1,0},{2,3},{3,2},{4,5},{5,4},{6,7},{7,6},{8,9},{9,8},{10,11... | collective-permute-start | bytes 36872 | tf_op jit(solution)/shard_map/ppermute | solution.py:381
  10.1 1.0 %copy-start.1 = (f32[4,2,512]{2,1,0:T(2,128)S(1)}, f32[4,2,512]{2,1,0:T(2,128)}, u32[]{:S(2)}) copy-start(f32[4,2,512]{2,1,0:T(2,128)} %cw.3) | copy-start | bytes 49156
  11.2 3.1 %copy-start = (bf16[512,2048]{1,0:T(8,128)(2,1)S(1)}, bf16[512,2048]{1,0:T(8,128)(2,1)}, u32[]{:S(2)}) copy-start(bf16[512,2048]{1,0:T(8,128)(2,1)} %w.3) | copy-start | bytes 6291460
  14.3 25.4 %collective-permute-start.11 = (bf16[512,2048]{1,0:T(8,128)(2,1)S(1)}, bf16[512,2048]{1,0:T(8,128)(2,1)S(1)}, u32[]{:S(2)}, u32[]{:S(2)}) collective-permute-start(bf16[512,2048]{1,0:T(8,128)(2,1)S(1)} %copy-done), channel_id=1, source_target_pairs={{0,1},{1,0},{2,3},{3,2},{4,5},{5,4},{6,7},{7,6},{8,9},{9,8},{10,11... | collective-permute-start | bytes 6291464 | tf_op jit(solution)/shard_map/ppermute | solution.py:381
  14.5 5.8 %collective-permute-start.6 = (bf16[2,128,256]{2,1,0:T(8,128)(2,1)S(1)}, bf16[2,128,256]{2,1,0:T(8,128)(2,1)S(1)}, u32[]{:S(2)}, u32[]{:S(2)}) collective-permute-start(bf16[2,128,256]{2,1,0:T(8,128)(2,1)S(1)} %get-tuple-element.45), channel_id=1, source_target_pairs={{0,4},{4,0},{8,12},{12,8},{16,20},{20,16},{24,28},{28,24},{1,5},{5... | collective-permute-start | bytes 393224 | tf_op jit(solution)/shard_map/ppermute | solution.py:381
  20.5 5.1 %collective-permute-start.7 = (bf16[2,128,256]{2,1,0:T(8,128)(2,1)S(1)}, bf16[2,128,256]{2,1,0:T(8,128)(2,1)S(1)}, u32[]{:S(2)}, u32[]{:S(2)}) collective-permute-start(bf16[2,128,256]{2,1,0:T(8,128)(2,1)S(1)} %shard_map.68.own), channel_id=1, source_target_pairs={{0,8},{4,12},{8,0},{12,4},{16,24},{20,28},{24,16},{28,20},{1,9},{5... | collective-permute-start | bytes 393224 | tf_op jit(solution)/shard_map/ppermute | solution.py:381
  22.4 1.6 %slice-start.1 = ((bf16[2048,2,768]{2,1,0:T(2,128)(2,1)}), bf16[2048,2,256]{2,1,0:T(2,128)(2,1)S(1)}, s32[]{:S(2)}) async-start(bf16[2048,2,768]{2,1,0:T(2,128)(2,1)} %param.7), calls=%async_computation.1 | async-start | bytes 4194304 | tf_op jit(solution)/shard_map/slice | solution.py:443
  24.0 1.2 %slice-start.2 = ((bf16[2048,2,768]{2,1,0:T(2,128)(2,1)}), bf16[2048,2,128]{2,1,0:T(2,128)(2,1)S(1)}, s32[]{:S(2)}) async-start(bf16[2048,2,768]{2,1,0:T(2,128)(2,1)} %param.7), calls=%async_computation.2 | async-start | bytes 2097152 | tf_op jit(solution)/shard_map/slice | solution.py:442
  25.2 7.8 %copy-start.2 = (f32[128]{0:T(128)S(1)}, f32[128]{0:T(128)}, u32[]{:S(2)}) copy-start(f32[128]{0:T(128)} %param.10) | copy-start | bytes 1540
  25.8 5.2 %collective-permute-start.8 = (bf16[2,128,128]{2,1,0:T(8,128)(2,1)S(1)}, bf16[2,128,128]{2,1,0:T(8,128)(2,1)S(1)}, u32[]{:S(2)}, u32[]{:S(2)}) collective-permute-start(bf16[2,128,128]{2,1,0:T(8,128)(2,1)S(1)} %shard_map.70), channel_id=1, source_target_pairs={{0,16},{4,20},{8,24},{12,28},{16,0},{20,4},{24,8},{28,12},{1,17},{... | collective-permute-start | bytes 196616 | tf_op jit(solution)/shard_map/ppermute | solution.py:381
  31.3 4.3 %collective-permute-start.9 = (bf16[2,128,128]{2,1,0:T(8,128)(2,1)S(1)}, bf16[2,128,128]{2,1,0:T(8,128)(2,1)S(1)}, u32[]{:S(2)}, u32[]{:S(2)}) collective-permute-start(bf16[2,128,128]{2,1,0:T(8,128)(2,1)S(1)} %get-tuple-element.56), channel_id=1, source_target_pairs={{0,4},{4,0},{8,12},{12,8},{16,20},{20,16},{24,28},{28,24},{1,5},{5... | collective-permute-start | bytes 196616 | tf_op jit(solution)/shard_map/ppermute | solution.py:381
  36.5 7.0 %collective-permute-start.12 = (bf16[64,2048]{1,0:T(8,128)(2,1)S(1)}, bf16[64,2048]{1,0:T(8,128)(2,1)S(1)}, u32[]{:S(2)}, u32[]{:S(2)}) collective-permute-start(bf16[64,2048]{1,0:T(8,128)(2,1)S(1)} %shard_map.75), channel_id=1, source_target_pairs={{0,2},{1,3},{2,0},{3,1},{4,6},{5,7},{6,4},{7,5},{8,10},{9,11},{10,... | collective-permute-start | bytes 786440 | tf_op jit(solution)/shard_map/ppermute | solution.py:381
  38.3 1.3 %collective-permute-start.10 = (bf16[128,512]{1,0:T(8,128)(2,1)S(1)}, bf16[128,512]{1,0:T(8,128)(2,1)S(1)}, u32[]{:S(2)}, u32[]{:S(2)}) collective-permute-start(bf16[128,512]{1,0:T(8,128)(2,1)S(1)} %get-tuple-element.58.send), channel_id=1, source_target_pairs={{0,1},{1,0},{2,3},{3,2},{4,5},{5,4},{6,7},{7,6},{8,9},{9,8},{10,11... | collective-permute-start | bytes 393224 | tf_op jit(solution)/shard_map/ppermute | solution.py:381
  40.2 6.4 %collective-permute-start.14 = (bf16[64,2048]{1,0:T(8,128)(2,1)S(1)}, bf16[64,2048]{1,0:T(8,128)(2,1)S(1)}, u32[]{:S(2)}, u32[]{:S(2)}) collective-permute-start(bf16[64,2048]{1,0:T(8,128)(2,1)S(1)} %shard_map.76), channel_id=1, source_target_pairs={{0,4},{1,3},{2,6},{3,1},{4,0},{5,7},{6,2},{7,5},{8,12},{9,11},{10,... | collective-permute-start | bytes 786440 | tf_op jit(solution)/shard_map/ppermute | solution.py:534
  43.6 3.0 %collective-permute-start.13 = (bf16[64,2048]{1,0:T(8,128)(2,1)S(1)}, bf16[64,2048]{1,0:T(8,128)(2,1)S(1)}, u32[]{:S(2)}, u32[]{:S(2)}) collective-permute-start(bf16[64,2048]{1,0:T(8,128)(2,1)S(1)} %collective-permute-done.12.refs_1_), channel_id=1, source_target_pairs={{0,1},{1,0},{2,3},{3,2},{4,5},{5,4},{6,7},{7,6},{8,9},{9,8},{10,11... | collective-permute-start | bytes 786440 | tf_op jit(solution)/shard_map/ppermute | solution.py:381

commit v10 on v9

--- a/solution.py
+++ b/solution.py
@@ -90,12 +90,11 @@
     ri = lax.broadcasted_iota(jnp.int32, (toks, toks), 0)
     ci = lax.broadcasted_iota(jnp.int32, (toks, toks), 1)
     exact = lax.Precision.HIGHEST
-    rows[...] = jnp.dot(log_decay, (ri <= ci).astype(F32), precision=exact, preferred_element_type=F32)
-    last_dims = (((1,), (1,)), ((), ()))
-    ccols = lax.dot_general((ri >= ci).astype(F32), log_decay, last_dims, precision=exact, preferred_element_type=F32)
-    bcols = lax.dot_general((ri == ci).astype(F32), beta, last_dims, precision=exact, preferred_element_type=F32)
-    cols[:, 0:heads] = ccols
-    cols[:, heads : 2 * heads] = bcols
+    cum = jnp.dot(log_decay, (ri <= ci).astype(F32), precision=exact, preferred_element_type=F32)
+    rows[...] = cum
+    both = jnp.concatenate([cum, beta], axis=0).T
+    cols[...] = both
+    ccols, bcols = both[:, 0:heads], both[:, heads:]
     below = ri[:HALF, :HALF] > ci[:HALF, :HALF]
     for j in range(heads):
         i = 0
@@ -312,15 +311,29 @@
         send[j] = jnp.where(odd, entered, passed).astype(BF16)
 
 
-def normed_kernel(q, o, own, got, gate, keep, send, scratch, *, n_head):
+def gated_norm(q, o, state, gate):
+    att = o + dot(q, state)
+    scale = lax.rsqrt(jnp.mean(att * att, axis=-1, keepdims=True) + EPSILON)
+    return (att * scale * gate).astype(BF16)
+
+
+def own_normed_kernel(q, o, own, gate, out):
+    half = own.shape[0]
+    for j in range(half):
+        i = half + j
+        out[:, j * DV : (j + 1) * DV] = gated_norm(q[i], o[i], own[j], gate[i])
+
+
+def normed_kernel(q, o, got, gate, own, keep, send, scratch, *, n_head):
     me = lax.axis_index("head")
     heads = q.shape[0]
     half = heads // 2
     for j in range(heads):
-        att = o[j] + dot(q[j], own[j - half] if j >= half else got[j])
-        scale = lax.rsqrt(jnp.mean(att * att, axis=-1, keepdims=True) + EPSILON)
         at = pl.multiple_of(true_index(j, heads) * DV, 128)
-        scratch[:, pl.ds(at, DV)] = (att * scale * gate[j]).astype(BF16)
+        if j < half:
+            scratch[:, pl.ds(at, DV)] = gated_norm(q[j], o[j], got[j], gate[j])
+        else:
+            scratch[:, pl.ds(at, DV)] = own[:, (j - half) * DV : (j - half + 1) * DV]
     part = scratch.shape[0] // n_head
     for i in range(n_head // 2):
         at = pl.multiple_of((me ^ (2 * i)) * part, 16)
@@ -508,10 +521,11 @@
         ratio=ratio,
     )
     rows_shape = shaped((toks // 2, heads * DV), BF16)
+    own_normed = call(own_normed_kernel, shaped((toks, half * DV), BF16), [q, o, own_state, gate], 0.2)
     keep, send = call(
         normed_kernel,
         (rows_shape, rows_shape),
-        [q, o, own_state, got_state, gate],
+        [q, o, got_state, gate, own_normed],
         0.4,
         [pltpu.VMEM((toks, heads * DV), BF16)],
         n_head=n_head,

time: 47.7 us -> 47.5 us (level)
    pallas_call x14 -> x15, Pallas kernels: 14.2 us -> 14.2 us  [call(): pl.pallas_call(functools.partial(body, **static), out_shape=out_shape, in...]
  transfers between devices with their start and end apart: 15 -> 15, of which waited for: 9 -> 10; matrix products, arithmetic and copies ran while one was open for 3% -> 3% of each run, Pallas kernels for 22% -> 22%
where the time goes in v10:
time: 47.5 us; the launch traced here: 47.3 us
  starting transfers between devices  17.6 us (37%)
  Pallas kernels  14.2 us (30%)
  waiting for transfers between devices  9.74 us (21%)
  local copies, waits for them, and re-layouts  5.53 us (12%)
    pallas_call x15, Pallas kernels, call(): pl.pallas_call(functools.partial(body, **static), out_shape=out_shape, in...  14.2 us
    ppermute x12, starting transfers between devices, xor_sent(): return lax.ppermute(value, axis, [(i, i ^ step) for i in range(count)])  13.9 us
    ppermute x12, waiting for transfers between devices, xor_sent(): return lax.ppermute(value, axis, [(i, i ^ step) for i in range(count)])  6.61 us
    ppermute x1, waiting for transfers between devices, local(): late_got.append(lax.ppermute(late, ctx_head, late_perm))  3 us
    ppermute x2, starting transfers between devices, local(): lax.ppermute(tail, ctx_head, halo_pairs(n_ctx, n_head, target))  2.14 us
    slice x2, local copies, waits for them, and re-layouts, local(): w_kv = in_proj[:, :, DK:v_end].reshape(width, key_heads * (v_end - DK))  1.89 us
    slice x2, local copies, waits for them, and re-layouts, local(): w_z = in_proj[:, :, v_end:].reshape(width, heads * DV)  1.59 us
    ppermute x1, starting transfers between devices, local(): late_got.append(lax.ppermute(late, ctx_head, late_perm))  1.55 us
  transfers between devices with their start and end apart: 15, of which 10 were waited for; matrix products, arithmetic and copies ran while one was open for 3% of the time, Pallas kernels for 22%

profile of v10, /device:TPU:0, one launch (start us, length us, event | category | flops | bytes accessed | tf_op | source)
XLA Modules:
  0.0 47.3 jit_solution(15481182700911752411)
XLA Ops:
  0.0 3.0 %collective-permute-start.1 = (bf16[64,2048]{1,0:T(8,128)(2,1)}, bf16[64,2048]{1,0:T(8,128)(2,1)S(1)}, u32[]{:S(2)}, u32[]{:S(2)}) collective-permute-start(bf16[64,2048]{1,0:T(8,128)(2,1)} %x_any.1), channel_id=1, source_target_pairs={{0,2},{1,3},{2,0},{3,1},{4,6},{5,7},{6,4},{7,5},{8,10},{9,11},{10,... | collective-permute-start | bytes 786440 | tf_op jit(solution)/shard_map/ppermute | solution.py:394
  3.0 1.1 %shard_map.64 = (bf16[48,128]{1,0:T(8,128)(2,1)S(1)}, bf16[64,2048]{1,0:T(8,128)(2,1)S(1)}, f32[2,4,256]{2,1,0:T(4,128)S(1)}) custom-call(bf16[64,2048]{1,0:T(8,128)(2,1)} %x_any.1, f32[2,4,256]{2,1,0:T(4,128)} %logits_any.1), custom_call_target="tpu_custom_call" | custom-call | flops 6899999744 | bytes 270336 | tf_op jit(solution)/shard_map/pallas_call | solution.py:377
  4.1 2.1 %collective-permute-start.4 = (bf16[48,128]{1,0:T(8,128)(2,1)S(1)}, bf16[48,128]{1,0:T(8,128)(2,1)S(1)}, u32[]{:S(2)}, u32[]{:S(2)}) collective-permute-start(bf16[48,128]{1,0:T(8,128)(2,1)S(1)} %get-tuple-element.36), channel_id=1, source_target_pairs={{0,2},{1,9},{2,0},{3,6},{4,5},{5,4},{6,3},{7,10},{8,12},{9,1},{10,... | collective-permute-start | bytes 36872 | tf_op jit(solution)/shard_map/ppermute | solution.py:450
  6.2 1.9 %slice-done = bf16[2048,2,384]{2,1,0:T(2,128)(2,1)S(1)} async-done(((bf16[2048,2,768]{2,1,0:T(2,128)(2,1)}), bf16[2048,2,384]{2,1,0:T(2,128)(2,1)S(1)}, s32[]{:S(2)}) %slice-start) | async-done | bytes 3145752 | tf_op jit(solution)/shard_map/slice | solution.py:452
  8.1 0.7 %copy.7 = bf16[256,8,2,384]{3,1,2,0:T(8,128)(2,1)S(1)} copy(bf16[256,8,2,384]{3,2,1,0:T(2,128)(2,1)S(1)} %bitcast.14) | data formatting | bytes 6291456
  8.8 0.8 %collective-permute-done.1.refs_2_ = bf16[64,2048]{1,0:T(8,128)(2,1)S(1)} collective-permute-done((bf16[64,2048]{1,0:T(8,128)(2,1)}, bf16[64,2048]{1,0:T(8,128)(2,1)S(1)}, u32[]{:S(2)}, u32[]{:S(2)}) %collective-permute-start.1) | collective-permute-done | bytes 262176 | tf_op jit(solution)/shard_map/ppermute | solution.py:394
  10.1 0.8 %shard_map.65 = (f32[4,256]{1,0:T(4,128)S(1)}, f32[256,8]{1,0:T(8,128)S(1)}, f32[4,3,128,128]{3,2,1,0:T(8,128)S(1)}) custom-call(f32[2,4,256]{2,1,0:T(4,128)S(1)} %get-tuple-element.39.logits), custom_call_target="tpu_custom_call" | custom-call | flops 1150000000 | bytes 8192 | tf_op jit(solution)/shard_map/pallas_call | solution.py:377
  11.1 3.1 %shard_map.66 = (bf16[2,128,256]{2,1,0:T(8,128)(2,1)S(1)}, bf16[2,256,256]{2,1,0:T(8,128)(2,1)S(1)}, bf16[1,256,128]{2,1,0:T(8,128)(2,1)S(1)}, bf16[272,2048]{1,0:T(8,128)(2,1)S(1)}) custom-call(bf16[64,2048]{1,0:T(8,128)(2,1)S(1)} %get-tuple-element.35.refs_0_, bf16[64,2048]{1,0:T(8,128)(2,1)S(1)} %collective-permute-done.refs_1_, ...), custom_call_target="tpu_custom_call" | custom-call | flops 3449999872 | bytes 5033984 | tf_op jit(solution)/shard_map/pallas_call | solution.py:377
  14.5 1.8 %collective-permute-start.6 = (bf16[2,128,256]{2,1,0:T(8,128)(2,1)S(1)}, bf16[2,128,256]{2,1,0:T(8,128)(2,1)S(1)}, u32[]{:S(2)}, u32[]{:S(2)}) collective-permute-start(bf16[2,128,256]{2,1,0:T(8,128)(2,1)S(1)} %get-tuple-element.45), channel_id=1, source_target_pairs={{0,4},{4,0},{8,12},{12,8},{16,20},{20,16},{24,28},{28,24},{1,5},{5... | collective-permute-start | bytes 393224 | tf_op jit(solution)/shard_map/ppermute | solution.py:394
  16.3 3.0 %shard_map.67 = (bf16[2,128,256]{2,1,0:T(8,128)(2,1)S(1)}, bf16[2,256,256]{2,1,0:T(8,128)(2,1)S(1)}, bf16[1,256,128]{2,1,0:T(8,128)(2,1)S(1)}) custom-call(bf16[272,2048]{1,0:T(8,128)(2,1)S(1)} %get-tuple-element.43.x, bf16[2048,768]{1,0:T(8,128)(2,1)S(1)} %bitcast.10, f32[4,2,512]{2,1,0:T(2,128)S(1)} %copy-done.1, ...), custom_call_target="tpu_custom_call" | custom-call | flops 3449999872 | bytes 5074944 | tf_op jit(solution)/shard_map/pallas_call | solution.py:377
  19.2 1.0 %collective-permute-done.6.got.pair = bf16[2,128,256]{2,1,0:T(8,128)(2,1)S(1)} collective-permute-done((bf16[2,128,256]{2,1,0:T(8,128)(2,1)S(1)}, bf16[2,128,256]{2,1,0:T(8,128)(2,1)S(1)}, u32[]{:S(2)}, u32[]{:S(2)}) %collective-permute-start.6) | collective-permute-done | bytes 131104 | tf_op jit(solution)/shard_map/ppermute | solution.py:394
  20.4 1.9 %collective-permute-start.7 = (bf16[2,128,256]{2,1,0:T(8,128)(2,1)S(1)}, bf16[2,128,256]{2,1,0:T(8,128)(2,1)S(1)}, u32[]{:S(2)}, u32[]{:S(2)}) collective-permute-start(bf16[2,128,256]{2,1,0:T(8,128)(2,1)S(1)} %shard_map.68.own), channel_id=1, source_target_pairs={{0,8},{4,12},{8,0},{12,4},{16,24},{20,28},{24,16},{28,20},{1,9},{5... | collective-permute-start | bytes 393224 | tf_op jit(solution)/shard_map/ppermute | solution.py:394
  22.3 1.6 %slice-done.1 = bf16[2048,2,256]{2,1,0:T(2,128)(2,1)S(1)} async-done(((bf16[2048,2,768]{2,1,0:T(2,128)(2,1)}), bf16[2048,2,256]{2,1,0:T(2,128)(2,1)S(1)}, s32[]{:S(2)}) %slice-start.1) | async-done | bytes 2097176 | tf_op jit(solution)/shard_map/slice | solution.py:456
  24.4 0.7 %slice-done.2 = bf16[2048,2,128]{2,1,0:T(2,128)(2,1)S(1)} async-done(((bf16[2048,2,768]{2,1,0:T(2,128)(2,1)}), bf16[2048,2,128]{2,1,0:T(2,128)(2,1)S(1)}, s32[]{:S(2)}) %slice-start.2) | async-done | bytes 1048600 | tf_op jit(solution)/shard_map/slice | solution.py:455
  25.6 2.9 %collective-permute-start.8 = (bf16[2,128,128]{2,1,0:T(8,128)(2,1)S(1)}, bf16[2,128,128]{2,1,0:T(8,128)(2,1)S(1)}, u32[]{:S(2)}, u32[]{:S(2)}) collective-permute-start(bf16[2,128,128]{2,1,0:T(8,128)(2,1)S(1)} %shard_map.70), channel_id=1, source_target_pairs={{0,16},{4,20},{8,24},{12,28},{16,0},{20,4},{24,8},{28,12},{1,17},{... | collective-permute-start | bytes 196616 | tf_op jit(solution)/shard_map/ppermute | solution.py:394
  28.5 2.3 %collective-permute-done.8.got = bf16[2,128,128]{2,1,0:T(8,128)(2,1)S(1)} collective-permute-done((bf16[2,128,128]{2,1,0:T(8,128)(2,1)S(1)}, bf16[2,128,128]{2,1,0:T(8,128)(2,1)S(1)}, u32[]{:S(2)}, u32[]{:S(2)}) %collective-permute-start.8) | collective-permute-done | bytes 65568 | tf_op jit(solution)/shard_map/ppermute | solution.py:394
  31.2 1.8 %collective-permute-start.9 = (bf16[2,128,128]{2,1,0:T(8,128)(2,1)S(1)}, bf16[2,128,128]{2,1,0:T(8,128)(2,1)S(1)}, u32[]{:S(2)}, u32[]{:S(2)}) collective-permute-start(bf16[2,128,128]{2,1,0:T(8,128)(2,1)S(1)} %get-tuple-element.55), channel_id=1, source_target_pairs={{0,4},{4,0},{8,12},{12,8},{16,20},{20,16},{24,28},{28,24},{1,5},{5... | collective-permute-start | bytes 196616 | tf_op jit(solution)/shard_map/ppermute | solution.py:394
  33.0 2.0 %shard_map.69 = (bf16[4,256,128]{2,1,0:T(8,128)(2,1)S(1)}, f32[4,256,128]{2,1,0:T(8,128)S(1)}, f32[4,256,128]{2,1,0:T(8,128)S(1)}) custom-call(bf16[272,2048]{1,0:T(8,128)(2,1)S(1)} %get-tuple-element.43.x, bf16[2048,256]{1,0:T(8,128)(2,1)S(1)} %bitcast.12, bf16[2048,512]{1,0:T(8,128)(2,1)S(1)} %bitcast.11, f32[4,2,512]{2,1,0:T(2,128)S(1)} %copy-done.1, ...), custom_call_target="tpu_custom_call" | custom-call | flops 2184999936 | bytes 4944384 | tf_op jit(solution)/shard_map/pallas_call | solution.py:377
  36.3 1.8 %collective-permute-start.12 = (bf16[64,2048]{1,0:T(8,128)(2,1)S(1)}, bf16[64,2048]{1,0:T(8,128)(2,1)S(1)}, u32[]{:S(2)}, u32[]{:S(2)}) collective-permute-start(bf16[64,2048]{1,0:T(8,128)(2,1)S(1)} %shard_map.76), channel_id=1, source_target_pairs={{0,2},{1,3},{2,0},{3,1},{4,6},{5,7},{6,4},{7,5},{8,10},{9,11},{10,... | collective-permute-start | bytes 786440 | tf_op jit(solution)/shard_map/ppermute | solution.py:394
  38.2 0.8 %shard_map.74 = (f32[64,2048]{1,0:T(8,128)S(1)}, f32[64,2048]{1,0:T(8,128)S(1)}) custom-call(bf16[128,512]{1,0:T(8,128)(2,1)S(1)} %get-tuple-element.60.own.keep, bf16[512,2048]{1,0:T(8,128)(2,1)S(1)} %copy-done), custom_call_target="tpu_custom_call" | custom-call | flops 920000000 | bytes 2228224 | tf_op jit(solution)/shard_map/pallas_call | solution.py:377
  40.0 1.6 %collective-permute-start.14 = (bf16[64,2048]{1,0:T(8,128)(2,1)S(1)}, bf16[64,2048]{1,0:T(8,128)(2,1)S(1)}, u32[]{:S(2)}, u32[]{:S(2)}) collective-permute-start(bf16[64,2048]{1,0:T(8,128)(2,1)S(1)} %shard_map.77), channel_id=1, source_target_pairs={{0,4},{1,3},{2,6},{3,1},{4,0},{5,7},{6,2},{7,5},{8,12},{9,11},{10,... | collective-permute-start | bytes 786440 | tf_op jit(solution)/shard_map/ppermute | solution.py:548
  42.0 1.4 %collective-permute-done.12.refs_1_ = bf16[64,2048]{1,0:T(8,128)(2,1)S(1)} collective-permute-done((bf16[64,2048]{1,0:T(8,128)(2,1)S(1)}, bf16[64,2048]{1,0:T(8,128)(2,1)S(1)}, u32[]{:S(2)}, u32[]{:S(2)}) %collective-permute-start.12) | collective-permute-done | bytes 262176 | tf_op jit(solution)/shard_map/ppermute | solution.py:394
  43.4 3.0 %collective-permute-done.14.refs_3_ = bf16[64,2048]{1,0:T(8,128)(2,1)S(1)} collective-permute-done((bf16[64,2048]{1,0:T(8,128)(2,1)S(1)}, bf16[64,2048]{1,0:T(8,128)(2,1)S(1)}, u32[]{:S(2)}, u32[]{:S(2)}) %collective-permute-start.14) | collective-permute-done | bytes 262176 | tf_op jit(solution)/shard_map/ppermute | solution.py:548
  46.4 0.8 %shard_map.78 = bf16[64,2048]{1,0:T(8,128)(2,1)} custom-call(f32[64,2048]{1,0:T(8,128)S(1)} %shard_map.75.refs_0_, bf16[64,2048]{1,0:T(8,128)(2,1)S(1)} %collective-permute-done.12.refs_1_, bf16[64,2048]{1,0:T(8,128)(2,1)S(1)} %collective-permute-done.13.refs_2_, bf16[64,2048]{1,0:T(8,128)(2,1)S(1)} %collective-permute-done.14.refs_3_), custom_call_target="tpu_custom_call" | custom-call | flops 575000000 | bytes 1310720 | tf_op jit(solution)/shard_map/pallas_call | solution.py:377
  (39 shorter events, 5.4 us)
Async XLA Ops:
  0.0 6.2 %copy-start.3 = (bf16[64,2048]{1,0:T(8,128)(2,1)S(1)}, bf16[64,2048]{1,0:T(8,128)(2,1)}, u32[]{:S(2)}) copy-start(bf16[64,2048]{1,0:T(8,128)(2,1)} %x_any.1) | copy-start | bytes 786436
  0.0 9.6 %collective-permute-start.1 = (bf16[64,2048]{1,0:T(8,128)(2,1)}, bf16[64,2048]{1,0:T(8,128)(2,1)S(1)}, u32[]{:S(2)}, u32[]{:S(2)}) collective-permute-start(bf16[64,2048]{1,0:T(8,128)(2,1)} %x_any.1), channel_id=1, source_target_pairs={{0,2},{1,3},{2,0},{3,1},{4,6},{5,7},{6,4},{7,5},{8,10},{9,11},{10,... | collective-permute-start | bytes 786440 | tf_op jit(solution)/shard_map/ppermute | solution.py:394
  4.0 5.5 %collective-permute-start.3 = (bf16[48,128]{1,0:T(8,128)(2,1)S(1)}, bf16[48,128]{1,0:T(8,128)(2,1)S(1)}, u32[]{:S(2)}, u32[]{:S(2)}) collective-permute-start(bf16[48,128]{1,0:T(8,128)(2,1)S(1)} %get-tuple-element.36), channel_id=1, source_target_pairs={{0,1},{1,0},{2,10},{3,5},{4,6},{5,3},{6,4},{7,9},{8,12},{9,7},{10,... | collective-permute-start | bytes 36872 | tf_op jit(solution)/shard_map/ppermute | solution.py:450
  4.1 5.6 %collective-permute-start.4 = (bf16[48,128]{1,0:T(8,128)(2,1)S(1)}, bf16[48,128]{1,0:T(8,128)(2,1)S(1)}, u32[]{:S(2)}, u32[]{:S(2)}) collective-permute-start(bf16[48,128]{1,0:T(8,128)(2,1)S(1)} %get-tuple-element.36), channel_id=1, source_target_pairs={{0,2},{1,9},{2,0},{3,6},{4,5},{5,4},{6,3},{7,10},{8,12},{9,1},{10,... | collective-permute-start | bytes 36872 | tf_op jit(solution)/shard_map/ppermute | solution.py:450
  6.2 4.9 %collective-permute-start = (bf16[64,2048]{1,0:T(8,128)(2,1)S(1)}, bf16[64,2048]{1,0:T(8,128)(2,1)S(1)}, u32[]{:S(2)}, u32[]{:S(2)}) collective-permute-start(bf16[64,2048]{1,0:T(8,128)(2,1)S(1)} %copy-done.3), channel_id=1, source_target_pairs={{0,1},{1,0},{2,3},{3,2},{4,5},{5,4},{6,7},{7,6},{8,9},{9,8},{10,11... | collective-permute-start | bytes 786440 | tf_op jit(solution)/shard_map/ppermute | solution.py:394
  6.2 1.9 %slice-start = ((bf16[2048,2,768]{2,1,0:T(2,128)(2,1)}), bf16[2048,2,384]{2,1,0:T(2,128)(2,1)S(1)}, s32[]{:S(2)}) async-start(bf16[2048,2,768]{2,1,0:T(2,128)(2,1)} %param.7), calls=%async_computation | async-start | bytes 6291456 | tf_op jit(solution)/shard_map/slice | solution.py:452
  9.6 1.6 %collective-permute-start.2 = (bf16[64,2048]{1,0:T(8,128)(2,1)S(1)}, bf16[64,2048]{1,0:T(8,128)(2,1)S(1)}, u32[]{:S(2)}, u32[]{:S(2)}) collective-permute-start(bf16[64,2048]{1,0:T(8,128)(2,1)S(1)} %collective-permute-done.1.refs_2_), channel_id=1, source_target_pairs={{0,1},{1,0},{2,3},{3,2},{4,5},{5,4},{6,7},{7,6},{8,9},{9,8},{10,11... | collective-permute-start | bytes 786440 | tf_op jit(solution)/shard_map/ppermute | solution.py:394
  9.7 1.4 %collective-permute-start.5 = (bf16[48,128]{1,0:T(8,128)(2,1)S(1)}, bf16[48,128]{1,0:T(8,128)(2,1)S(1)}, u32[]{:S(2)}, u32[]{:S(2)}) collective-permute-start(bf16[48,128]{1,0:T(8,128)(2,1)S(1)} %select_select_fusion.refs_4_), channel_id=1, source_target_pairs={{0,1},{1,0},{2,3},{3,2},{4,5},{5,4},{6,7},{7,6},{8,9},{9,8},{10,11... | collective-permute-start | bytes 36872 | tf_op jit(solution)/shard_map/ppermute | solution.py:394
  10.1 1.0 %copy-start.1 = (f32[4,2,512]{2,1,0:T(2,128)S(1)}, f32[4,2,512]{2,1,0:T(2,128)}, u32[]{:S(2)}) copy-start(f32[4,2,512]{2,1,0:T(2,128)} %cw.3) | copy-start | bytes 49156
  11.1 3.1 %copy-start = (bf16[512,2048]{1,0:T(8,128)(2,1)S(1)}, bf16[512,2048]{1,0:T(8,128)(2,1)}, u32[]{:S(2)}) copy-start(bf16[512,2048]{1,0:T(8,128)(2,1)} %w.3) | copy-start | bytes 6291460
  14.2 25.3 %collective-permute-start.11 = (bf16[512,2048]{1,0:T(8,128)(2,1)S(1)}, bf16[512,2048]{1,0:T(8,128)(2,1)S(1)}, u32[]{:S(2)}, u32[]{:S(2)}) collective-permute-start(bf16[512,2048]{1,0:T(8,128)(2,1)S(1)} %copy-done), channel_id=1, source_target_pairs={{0,1},{1,0},{2,3},{3,2},{4,5},{5,4},{6,7},{7,6},{8,9},{9,8},{10,11... | collective-permute-start | bytes 6291464 | tf_op jit(solution)/shard_map/ppermute | solution.py:394
  14.5 5.7 %collective-permute-start.6 = (bf16[2,128,256]{2,1,0:T(8,128)(2,1)S(1)}, bf16[2,128,256]{2,1,0:T(8,128)(2,1)S(1)}, u32[]{:S(2)}, u32[]{:S(2)}) collective-permute-start(bf16[2,128,256]{2,1,0:T(8,128)(2,1)S(1)} %get-tuple-element.45), channel_id=1, source_target_pairs={{0,4},{4,0},{8,12},{12,8},{16,20},{20,16},{24,28},{28,24},{1,5},{5... | collective-permute-start | bytes 393224 | tf_op jit(solution)/shard_map/ppermute | solution.py:394
  20.4 5.0 %collective-permute-start.7 = (bf16[2,128,256]{2,1,0:T(8,128)(2,1)S(1)}, bf16[2,128,256]{2,1,0:T(8,128)(2,1)S(1)}, u32[]{:S(2)}, u32[]{:S(2)}) collective-permute-start(bf16[2,128,256]{2,1,0:T(8,128)(2,1)S(1)} %shard_map.68.own), channel_id=1, source_target_pairs={{0,8},{4,12},{8,0},{12,4},{16,24},{20,28},{24,16},{28,20},{1,9},{5... | collective-permute-start | bytes 393224 | tf_op jit(solution)/shard_map/ppermute | solution.py:394
  22.3 1.6 %slice-start.1 = ((bf16[2048,2,768]{2,1,0:T(2,128)(2,1)}), bf16[2048,2,256]{2,1,0:T(2,128)(2,1)S(1)}, s32[]{:S(2)}) async-start(bf16[2048,2,768]{2,1,0:T(2,128)(2,1)} %param.7), calls=%async_computation.1 | async-start | bytes 4194304 | tf_op jit(solution)/shard_map/slice | solution.py:456
  23.9 1.2 %slice-start.2 = ((bf16[2048,2,768]{2,1,0:T(2,128)(2,1)}), bf16[2048,2,128]{2,1,0:T(2,128)(2,1)S(1)}, s32[]{:S(2)}) async-start(bf16[2048,2,768]{2,1,0:T(2,128)(2,1)} %param.7), calls=%async_computation.2 | async-start | bytes 2097152 | tf_op jit(solution)/shard_map/slice | solution.py:455
  25.1 7.8 %copy-start.2 = (f32[128]{0:T(128)S(1)}, f32[128]{0:T(128)}, u32[]{:S(2)}) copy-start(f32[128]{0:T(128)} %param.10) | copy-start | bytes 1540
  25.6 5.2 %collective-permute-start.8 = (bf16[2,128,128]{2,1,0:T(8,128)(2,1)S(1)}, bf16[2,128,128]{2,1,0:T(8,128)(2,1)S(1)}, u32[]{:S(2)}, u32[]{:S(2)}) collective-permute-start(bf16[2,128,128]{2,1,0:T(8,128)(2,1)S(1)} %shard_map.70), channel_id=1, source_target_pairs={{0,16},{4,20},{8,24},{12,28},{16,0},{20,4},{24,8},{28,12},{1,17},{... | collective-permute-start | bytes 196616 | tf_op jit(solution)/shard_map/ppermute | solution.py:394
  31.2 4.3 %collective-permute-start.9 = (bf16[2,128,128]{2,1,0:T(8,128)(2,1)S(1)}, bf16[2,128,128]{2,1,0:T(8,128)(2,1)S(1)}, u32[]{:S(2)}, u32[]{:S(2)}) collective-permute-start(bf16[2,128,128]{2,1,0:T(8,128)(2,1)S(1)} %get-tuple-element.55), channel_id=1, source_target_pairs={{0,4},{4,0},{8,12},{12,8},{16,20},{20,16},{24,28},{28,24},{1,5},{5... | collective-permute-start | bytes 196616 | tf_op jit(solution)/shard_map/ppermute | solution.py:394
  36.3 7.1 %collective-permute-start.12 = (bf16[64,2048]{1,0:T(8,128)(2,1)S(1)}, bf16[64,2048]{1,0:T(8,128)(2,1)S(1)}, u32[]{:S(2)}, u32[]{:S(2)}) collective-permute-start(bf16[64,2048]{1,0:T(8,128)(2,1)S(1)} %shard_map.76), channel_id=1, source_target_pairs={{0,2},{1,3},{2,0},{3,1},{4,6},{5,7},{6,4},{7,5},{8,10},{9,11},{10,... | collective-permute-start | bytes 786440 | tf_op jit(solution)/shard_map/ppermute | solution.py:394
  38.2 1.3 %collective-permute-start.10 = (bf16[128,512]{1,0:T(8,128)(2,1)S(1)}, bf16[128,512]{1,0:T(8,128)(2,1)S(1)}, u32[]{:S(2)}, u32[]{:S(2)}) collective-permute-start(bf16[128,512]{1,0:T(8,128)(2,1)S(1)} %get-tuple-element.58.send), channel_id=1, source_target_pairs={{0,1},{1,0},{2,3},{3,2},{4,5},{5,4},{6,7},{7,6},{8,9},{9,8},{10,11... | collective-permute-start | bytes 393224 | tf_op jit(solution)/shard_map/ppermute | solution.py:394
  40.0 6.4 %collective-permute-start.14 = (bf16[64,2048]{1,0:T(8,128)(2,1)S(1)}, bf16[64,2048]{1,0:T(8,128)(2,1)S(1)}, u32[]{:S(2)}, u32[]{:S(2)}) collective-permute-start(bf16[64,2048]{1,0:T(8,128)(2,1)S(1)} %shard_map.77), channel_id=1, source_target_pairs={{0,4},{1,3},{2,6},{3,1},{4,0},{5,7},{6,2},{7,5},{8,12},{9,11},{10,... | collective-permute-start | bytes 786440 | tf_op jit(solution)/shard_map/ppermute | solution.py:548
  43.4 3.0 %collective-permute-start.13 = (bf16[64,2048]{1,0:T(8,128)(2,1)S(1)}, bf16[64,2048]{1,0:T(8,128)(2,1)S(1)}, u32[]{:S(2)}, u32[]{:S(2)}) collective-permute-start(bf16[64,2048]{1,0:T(8,128)(2,1)S(1)} %collective-permute-done.12.refs_1_), channel_id=1, source_target_pairs={{0,1},{1,0},{2,3},{3,2},{4,5},{5,4},{6,7},{7,6},{8,9},{9,8},{10,11... | collective-permute-start | bytes 786440 | tf_op jit(solution)/shard_map/ppermute | solution.py:394

commit v11 on v10

--- a/solution.py
+++ b/solution.py
@@ -501,15 +501,6 @@
             before = call(prefix_kernel, pair_shape, [before, got], 0.2, step=step)
         step *= 2
     got = xor_sent(total, "ctx", step)
-    own_state, out_state = call(
-        states_kernel,
-        (state_shape, state_shape),
-        [s_keep, s_pair, before, got],
-        0.3,
-        before_step=before_step,
-        step=step,
-    )
-    got_state = xor_sent(out_state, "ctx", 1)
     o_shape = shaped((heads, toks, DV), F32)
     q, o, gate = call(
         queries_kernel,
@@ -520,6 +511,16 @@
         key_heads=key_heads,
         ratio=ratio,
     )
+    got, q, o, gate = lax.optimization_barrier((got, q, o, gate))
+    own_state, out_state = call(
+        states_kernel,
+        (state_shape, state_shape),
+        [s_keep, s_pair, before, got],
+        0.3,
+        before_step=before_step,
+        step=step,
+    )
+    got_state = xor_sent(out_state, "ctx", 1)
     rows_shape = shaped((toks // 2, heads * DV), BF16)
     own_normed = call(own_normed_kernel, shaped((toks, half * DV), BF16), [q, o, own_state, gate], 0.2)
     keep, send = call(

time: 47.5 us -> 47.5 us (level)
  no operation moved by 1% of the time
where the time goes in v11:
time: 47.5 us; the launch traced here: 47.3 us
  starting transfers between devices  17.6 us (37%)
  Pallas kernels  14.2 us (30%)
  waiting for transfers between devices  9.73 us (20%)
  local copies, waits for them, and re-layouts  5.52 us (12%)
    pallas_call x15, Pallas kernels, call(): pl.pallas_call(functools.partial(body, **static), out_shape=out_shape, in...  14.2 us
    ppermute x12, starting transfers between devices, xor_sent(): return lax.ppermute(value, axis, [(i, i ^ step) for i in range(count)])  13.9 us
    ppermute x12, waiting for transfers between devices, xor_sent(): return lax.ppermute(value, axis, [(i, i ^ step) for i in range(count)])  6.6 us
    ppermute x1, waiting for transfers between devices, local(): late_got.append(lax.ppermute(late, ctx_head, late_perm))  3 us
    ppermute x2, starting transfers between devices, local(): lax.ppermute(tail, ctx_head, halo_pairs(n_ctx, n_head, target))  2.14 us
    slice x2, local copies, waits for them, and re-layouts, local(): w_kv = in_proj[:, :, DK:v_end].reshape(width, key_heads * (v_end - DK))  1.89 us
    slice x2, local copies, waits for them, and re-layouts, local(): w_z = in_proj[:, :, v_end:].reshape(width, heads * DV)  1.59 us
    ppermute x1, starting transfers between devices, local(): late_got.append(lax.ppermute(late, ctx_head, late_perm))  1.55 us
  transfers between devices with their start and end apart: 15, of which 10 were waited for; matrix products, arithmetic and copies ran while one was open for 3% of the time, Pallas kernels for 22%

profile of v11, /device:TPU:0, one launch (start us, length us, event | category | flops | bytes accessed | tf_op | source)
XLA Modules:
  0.0 47.3 jit_solution(6368362920723218005)
XLA Ops:
  0.0 3.0 %collective-permute-start.1 = (bf16[64,2048]{1,0:T(8,128)(2,1)}, bf16[64,2048]{1,0:T(8,128)(2,1)S(1)}, u32[]{:S(2)}, u32[]{:S(2)}) collective-permute-start(bf16[64,2048]{1,0:T(8,128)(2,1)} %x_any.1), channel_id=1, source_target_pairs={{0,2},{1,3},{2,0},{3,1},{4,6},{5,7},{6,4},{7,5},{8,10},{9,11},{10,... | collective-permute-start | bytes 786440 | tf_op jit(solution)/shard_map/ppermute | solution.py:394
  3.0 1.1 %shard_map.64 = (bf16[48,128]{1,0:T(8,128)(2,1)S(1)}, bf16[64,2048]{1,0:T(8,128)(2,1)S(1)}, f32[2,4,256]{2,1,0:T(4,128)S(1)}) custom-call(bf16[64,2048]{1,0:T(8,128)(2,1)} %x_any.1, f32[2,4,256]{2,1,0:T(4,128)} %logits_any.1), custom_call_target="tpu_custom_call" | custom-call | flops 6899999744 | bytes 270336 | tf_op jit(solution)/shard_map/pallas_call | solution.py:377
  4.1 2.1 %collective-permute-start.4 = (bf16[48,128]{1,0:T(8,128)(2,1)S(1)}, bf16[48,128]{1,0:T(8,128)(2,1)S(1)}, u32[]{:S(2)}, u32[]{:S(2)}) collective-permute-start(bf16[48,128]{1,0:T(8,128)(2,1)S(1)} %get-tuple-element.40), channel_id=1, source_target_pairs={{0,2},{1,9},{2,0},{3,6},{4,5},{5,4},{6,3},{7,10},{8,12},{9,1},{10,... | collective-permute-start | bytes 36872 | tf_op jit(solution)/shard_map/ppermute | solution.py:450
  6.2 1.9 %slice-done = bf16[2048,2,384]{2,1,0:T(2,128)(2,1)S(1)} async-done(((bf16[2048,2,768]{2,1,0:T(2,128)(2,1)}), bf16[2048,2,384]{2,1,0:T(2,128)(2,1)S(1)}, s32[]{:S(2)}) %slice-start) | async-done | bytes 3145752 | tf_op jit(solution)/shard_map/slice | solution.py:452
  8.1 0.7 %copy.7 = bf16[256,8,2,384]{3,1,2,0:T(8,128)(2,1)S(1)} copy(bf16[256,8,2,384]{3,2,1,0:T(2,128)(2,1)S(1)} %bitcast.14) | data formatting | bytes 6291456
  8.8 0.8 %collective-permute-done.1.refs_2_ = bf16[64,2048]{1,0:T(8,128)(2,1)S(1)} collective-permute-done((bf16[64,2048]{1,0:T(8,128)(2,1)}, bf16[64,2048]{1,0:T(8,128)(2,1)S(1)}, u32[]{:S(2)}, u32[]{:S(2)}) %collective-permute-start.1) | collective-permute-done | bytes 262176 | tf_op jit(solution)/shard_map/ppermute | solution.py:394
  10.1 0.8 %shard_map.65 = (f32[4,256]{1,0:T(4,128)S(1)}, f32[256,8]{1,0:T(8,128)S(1)}, f32[4,3,128,128]{3,2,1,0:T(8,128)S(1)}) custom-call(f32[2,4,256]{2,1,0:T(4,128)S(1)} %get-tuple-element.43.logits), custom_call_target="tpu_custom_call" | custom-call | flops 1150000000 | bytes 8192 | tf_op jit(solution)/shard_map/pallas_call | solution.py:377
  11.1 3.1 %shard_map.66 = (bf16[2,128,256]{2,1,0:T(8,128)(2,1)S(1)}, bf16[2,256,256]{2,1,0:T(8,128)(2,1)S(1)}, bf16[1,256,128]{2,1,0:T(8,128)(2,1)S(1)}, bf16[272,2048]{1,0:T(8,128)(2,1)S(1)}) custom-call(bf16[64,2048]{1,0:T(8,128)(2,1)S(1)} %get-tuple-element.39.refs_0_, bf16[64,2048]{1,0:T(8,128)(2,1)S(1)} %collective-permute-done.refs_1_, ...), custom_call_target="tpu_custom_call" | custom-call | flops 3449999872 | bytes 5033984 | tf_op jit(solution)/shard_map/pallas_call | solution.py:377
  14.5 1.8 %collective-permute-start.6 = (bf16[2,128,256]{2,1,0:T(8,128)(2,1)S(1)}, bf16[2,128,256]{2,1,0:T(8,128)(2,1)S(1)}, u32[]{:S(2)}, u32[]{:S(2)}) collective-permute-start(bf16[2,128,256]{2,1,0:T(8,128)(2,1)S(1)} %get-tuple-element.49), channel_id=1, source_target_pairs={{0,4},{4,0},{8,12},{12,8},{16,20},{20,16},{24,28},{28,24},{1,5},{5... | collective-permute-start | bytes 393224 | tf_op jit(solution)/shard_map/ppermute | solution.py:394
  16.3 3.0 %shard_map.67 = (bf16[2,128,256]{2,1,0:T(8,128)(2,1)S(1)}, bf16[2,256,256]{2,1,0:T(8,128)(2,1)S(1)}, bf16[1,256,128]{2,1,0:T(8,128)(2,1)S(1)}) custom-call(bf16[272,2048]{1,0:T(8,128)(2,1)S(1)} %get-tuple-element.47.x, bf16[2048,768]{1,0:T(8,128)(2,1)S(1)} %bitcast.10, f32[4,2,512]{2,1,0:T(2,128)S(1)} %copy-done.1, ...), custom_call_target="tpu_custom_call" | custom-call | flops 3449999872 | bytes 5074944 | tf_op jit(solution)/shard_map/pallas_call | solution.py:377
  19.3 1.0 %collective-permute-done.6.got.pair = bf16[2,128,256]{2,1,0:T(8,128)(2,1)S(1)} collective-permute-done((bf16[2,128,256]{2,1,0:T(8,128)(2,1)S(1)}, bf16[2,128,256]{2,1,0:T(8,128)(2,1)S(1)}, u32[]{:S(2)}, u32[]{:S(2)}) %collective-permute-start.6) | collective-permute-done | bytes 131104 | tf_op jit(solution)/shard_map/ppermute | solution.py:394
  20.4 1.9 %collective-permute-start.7 = (bf16[2,128,256]{2,1,0:T(8,128)(2,1)S(1)}, bf16[2,128,256]{2,1,0:T(8,128)(2,1)S(1)}, u32[]{:S(2)}, u32[]{:S(2)}) collective-permute-start(bf16[2,128,256]{2,1,0:T(8,128)(2,1)S(1)} %shard_map.68.own), channel_id=1, source_target_pairs={{0,8},{4,12},{8,0},{12,4},{16,24},{20,28},{24,16},{28,20},{1,9},{5... | collective-permute-start | bytes 393224 | tf_op jit(solution)/shard_map/ppermute | solution.py:394
  22.3 1.6 %slice-done.1 = bf16[2048,2,256]{2,1,0:T(2,128)(2,1)S(1)} async-done(((bf16[2048,2,768]{2,1,0:T(2,128)(2,1)}), bf16[2048,2,256]{2,1,0:T(2,128)(2,1)S(1)}, s32[]{:S(2)}) %slice-start.1) | async-done | bytes 2097176 | tf_op jit(solution)/shard_map/slice | solution.py:456
  24.4 0.7 %slice-done.2 = bf16[2048,2,128]{2,1,0:T(2,128)(2,1)S(1)} async-done(((bf16[2048,2,768]{2,1,0:T(2,128)(2,1)}), bf16[2048,2,128]{2,1,0:T(2,128)(2,1)S(1)}, s32[]{:S(2)}) %slice-start.2) | async-done | bytes 1048600 | tf_op jit(solution)/shard_map/slice | solution.py:455
  25.6 2.9 %collective-permute-start.8 = (bf16[2,128,128]{2,1,0:T(8,128)(2,1)S(1)}, bf16[2,128,128]{2,1,0:T(8,128)(2,1)S(1)}, u32[]{:S(2)}, u32[]{:S(2)}) collective-permute-start(bf16[2,128,128]{2,1,0:T(8,128)(2,1)S(1)} %shard_map.69), channel_id=1, source_target_pairs={{0,16},{4,20},{8,24},{12,28},{16,0},{20,4},{24,8},{28,12},{1,17},{... | collective-permute-start | bytes 196616 | tf_op jit(solution)/shard_map/ppermute | solution.py:394
  28.5 1.9 %shard_map.70 = (bf16[4,256,128]{2,1,0:T(8,128)(2,1)S(1)}, f32[4,256,128]{2,1,0:T(8,128)S(1)}, f32[4,256,128]{2,1,0:T(8,128)S(1)}) custom-call(bf16[272,2048]{1,0:T(8,128)(2,1)S(1)} %get-tuple-element.47.x, bf16[2048,256]{1,0:T(8,128)(2,1)S(1)} %bitcast.12, bf16[2048,512]{1,0:T(8,128)(2,1)S(1)} %bitcast.11, f32[4,2,512]{2,1,0:T(2,128)S(1)} %copy-done.1, ...), custom_call_target="tpu_custom_call" | custom-call | flops 2184999936 | bytes 4944384 | tf_op jit(solution)/shard_map/pallas_call | solution.py:377
  31.2 1.8 %collective-permute-start.9 = (bf16[2,128,128]{2,1,0:T(8,128)(2,1)S(1)}, bf16[2,128,128]{2,1,0:T(8,128)(2,1)S(1)}, u32[]{:S(2)}, u32[]{:S(2)}) collective-permute-start(bf16[2,128,128]{2,1,0:T(8,128)(2,1)S(1)} %get-tuple-element.63), channel_id=1, source_target_pairs={{0,4},{4,0},{8,12},{12,8},{16,20},{20,16},{24,28},{28,24},{1,5},{5... | collective-permute-start | bytes 196616 | tf_op jit(solution)/shard_map/ppermute | solution.py:394
  33.3 2.2 %collective-permute-done.9.got = bf16[2,128,128]{2,1,0:T(8,128)(2,1)S(1)} collective-permute-done((bf16[2,128,128]{2,1,0:T(8,128)(2,1)S(1)}, bf16[2,128,128]{2,1,0:T(8,128)(2,1)S(1)}, u32[]{:S(2)}, u32[]{:S(2)}) %collective-permute-start.9) | collective-permute-done | bytes 65568 | tf_op jit(solution)/shard_map/ppermute | solution.py:394
  36.3 1.8 %collective-permute-start.12 = (bf16[64,2048]{1,0:T(8,128)(2,1)S(1)}, bf16[64,2048]{1,0:T(8,128)(2,1)S(1)}, u32[]{:S(2)}, u32[]{:S(2)}) collective-permute-start(bf16[64,2048]{1,0:T(8,128)(2,1)S(1)} %shard_map.76), channel_id=1, source_target_pairs={{0,2},{1,3},{2,0},{3,1},{4,6},{5,7},{6,4},{7,5},{8,10},{9,11},{10,... | collective-permute-start | bytes 786440 | tf_op jit(solution)/shard_map/ppermute | solution.py:394
  38.2 0.8 %shard_map.74 = (f32[64,2048]{1,0:T(8,128)S(1)}, f32[64,2048]{1,0:T(8,128)S(1)}) custom-call(bf16[128,512]{1,0:T(8,128)(2,1)S(1)} %get-tuple-element.68.own.keep, bf16[512,2048]{1,0:T(8,128)(2,1)S(1)} %copy-done), custom_call_target="tpu_custom_call" | custom-call | flops 920000000 | bytes 2228224 | tf_op jit(solution)/shard_map/pallas_call | solution.py:377
  40.0 1.6 %collective-permute-start.14 = (bf16[64,2048]{1,0:T(8,128)(2,1)S(1)}, bf16[64,2048]{1,0:T(8,128)(2,1)S(1)}, u32[]{:S(2)}, u32[]{:S(2)}) collective-permute-start(bf16[64,2048]{1,0:T(8,128)(2,1)S(1)} %shard_map.77), channel_id=1, source_target_pairs={{0,4},{1,3},{2,6},{3,1},{4,0},{5,7},{6,2},{7,5},{8,12},{9,11},{10,... | collective-permute-start | bytes 786440 | tf_op jit(solution)/shard_map/ppermute | solution.py:549
  42.0 1.4 %collective-permute-done.12.refs_1_ = bf16[64,2048]{1,0:T(8,128)(2,1)S(1)} collective-permute-done((bf16[64,2048]{1,0:T(8,128)(2,1)S(1)}, bf16[64,2048]{1,0:T(8,128)(2,1)S(1)}, u32[]{:S(2)}, u32[]{:S(2)}) %collective-permute-start.12) | collective-permute-done | bytes 262176 | tf_op jit(solution)/shard_map/ppermute | solution.py:394
  43.4 3.0 %collective-permute-done.14.refs_3_ = bf16[64,2048]{1,0:T(8,128)(2,1)S(1)} collective-permute-done((bf16[64,2048]{1,0:T(8,128)(2,1)S(1)}, bf16[64,2048]{1,0:T(8,128)(2,1)S(1)}, u32[]{:S(2)}, u32[]{:S(2)}) %collective-permute-start.14) | collective-permute-done | bytes 262176 | tf_op jit(solution)/shard_map/ppermute | solution.py:549
  46.4 0.8 %shard_map.78 = bf16[64,2048]{1,0:T(8,128)(2,1)} custom-call(f32[64,2048]{1,0:T(8,128)S(1)} %shard_map.75.refs_0_, bf16[64,2048]{1,0:T(8,128)(2,1)S(1)} %collective-permute-done.12.refs_1_, bf16[64,2048]{1,0:T(8,128)(2,1)S(1)} %collective-permute-done.13.refs_2_, bf16[64,2048]{1,0:T(8,128)(2,1)S(1)} %collective-permute-done.14.refs_3_), custom_call_target="tpu_custom_call" | custom-call | flops 575000000 | bytes 1310720 | tf_op jit(solution)/shard_map/pallas_call | solution.py:377
  (39 shorter events, 5.6 us)
Async XLA Ops:
  0.0 6.2 %copy-start.3 = (bf16[64,2048]{1,0:T(8,128)(2,1)S(1)}, bf16[64,2048]{1,0:T(8,128)(2,1)}, u32[]{:S(2)}) copy-start(bf16[64,2048]{1,0:T(8,128)(2,1)} %x_any.1) | copy-start | bytes 786436
  0.0 9.6 %collective-permute-start.1 = (bf16[64,2048]{1,0:T(8,128)(2,1)}, bf16[64,2048]{1,0:T(8,128)(2,1)S(1)}, u32[]{:S(2)}, u32[]{:S(2)}) collective-permute-start(bf16[64,2048]{1,0:T(8,128)(2,1)} %x_any.1), channel_id=1, source_target_pairs={{0,2},{1,3},{2,0},{3,1},{4,6},{5,7},{6,4},{7,5},{8,10},{9,11},{10,... | collective-permute-start | bytes 786440 | tf_op jit(solution)/shard_map/ppermute | solution.py:394
  4.0 5.5 %collective-permute-start.3 = (bf16[48,128]{1,0:T(8,128)(2,1)S(1)}, bf16[48,128]{1,0:T(8,128)(2,1)S(1)}, u32[]{:S(2)}, u32[]{:S(2)}) collective-permute-start(bf16[48,128]{1,0:T(8,128)(2,1)S(1)} %get-tuple-element.40), channel_id=1, source_target_pairs={{0,1},{1,0},{2,10},{3,5},{4,6},{5,3},{6,4},{7,9},{8,12},{9,7},{10,... | collective-permute-start | bytes 36872 | tf_op jit(solution)/shard_map/ppermute | solution.py:450
  4.1 5.6 %collective-permute-start.4 = (bf16[48,128]{1,0:T(8,128)(2,1)S(1)}, bf16[48,128]{1,0:T(8,128)(2,1)S(1)}, u32[]{:S(2)}, u32[]{:S(2)}) collective-permute-start(bf16[48,128]{1,0:T(8,128)(2,1)S(1)} %get-tuple-element.40), channel_id=1, source_target_pairs={{0,2},{1,9},{2,0},{3,6},{4,5},{5,4},{6,3},{7,10},{8,12},{9,1},{10,... | collective-permute-start | bytes 36872 | tf_op jit(solution)/shard_map/ppermute | solution.py:450
  6.2 4.9 %collective-permute-start = (bf16[64,2048]{1,0:T(8,128)(2,1)S(1)}, bf16[64,2048]{1,0:T(8,128)(2,1)S(1)}, u32[]{:S(2)}, u32[]{:S(2)}) collective-permute-start(bf16[64,2048]{1,0:T(8,128)(2,1)S(1)} %copy-done.3), channel_id=1, source_target_pairs={{0,1},{1,0},{2,3},{3,2},{4,5},{5,4},{6,7},{7,6},{8,9},{9,8},{10,11... | collective-permute-start | bytes 786440 | tf_op jit(solution)/shard_map/ppermute | solution.py:394
  6.2 1.9 %slice-start = ((bf16[2048,2,768]{2,1,0:T(2,128)(2,1)}), bf16[2048,2,384]{2,1,0:T(2,128)(2,1)S(1)}, s32[]{:S(2)}) async-start(bf16[2048,2,768]{2,1,0:T(2,128)(2,1)} %param.7), calls=%async_computation | async-start | bytes 6291456 | tf_op jit(solution)/shard_map/slice | solution.py:452
  9.6 1.6 %collective-permute-start.2 = (bf16[64,2048]{1,0:T(8,128)(2,1)S(1)}, bf16[64,2048]{1,0:T(8,128)(2,1)S(1)}, u32[]{:S(2)}, u32[]{:S(2)}) collective-permute-start(bf16[64,2048]{1,0:T(8,128)(2,1)S(1)} %collective-permute-done.1.refs_2_), channel_id=1, source_target_pairs={{0,1},{1,0},{2,3},{3,2},{4,5},{5,4},{6,7},{7,6},{8,9},{9,8},{10,11... | collective-permute-start | bytes 786440 | tf_op jit(solution)/shard_map/ppermute | solution.py:394
  9.7 1.4 %collective-permute-start.5 = (bf16[48,128]{1,0:T(8,128)(2,1)S(1)}, bf16[48,128]{1,0:T(8,128)(2,1)S(1)}, u32[]{:S(2)}, u32[]{:S(2)}) collective-permute-start(bf16[48,128]{1,0:T(8,128)(2,1)S(1)} %select_select_fusion.refs_4_), channel_id=1, source_target_pairs={{0,1},{1,0},{2,3},{3,2},{4,5},{5,4},{6,7},{7,6},{8,9},{9,8},{10,11... | collective-permute-start | bytes 36872 | tf_op jit(solution)/shard_map/ppermute | solution.py:394
  10.1 1.0 %copy-start.1 = (f32[4,2,512]{2,1,0:T(2,128)S(1)}, f32[4,2,512]{2,1,0:T(2,128)}, u32[]{:S(2)}) copy-start(f32[4,2,512]{2,1,0:T(2,128)} %cw.3) | copy-start | bytes 49156
  11.1 3.1 %copy-start = (bf16[512,2048]{1,0:T(8,128)(2,1)S(1)}, bf16[512,2048]{1,0:T(8,128)(2,1)}, u32[]{:S(2)}) copy-start(bf16[512,2048]{1,0:T(8,128)(2,1)} %w.3) | copy-start | bytes 6291460
  14.2 25.3 %collective-permute-start.11 = (bf16[512,2048]{1,0:T(8,128)(2,1)S(1)}, bf16[512,2048]{1,0:T(8,128)(2,1)S(1)}, u32[]{:S(2)}, u32[]{:S(2)}) collective-permute-start(bf16[512,2048]{1,0:T(8,128)(2,1)S(1)} %copy-done), channel_id=1, source_target_pairs={{0,1},{1,0},{2,3},{3,2},{4,5},{5,4},{6,7},{7,6},{8,9},{9,8},{10,11... | collective-permute-start | bytes 6291464 | tf_op jit(solution)/shard_map/ppermute | solution.py:394
  14.5 5.7 %collective-permute-start.6 = (bf16[2,128,256]{2,1,0:T(8,128)(2,1)S(1)}, bf16[2,128,256]{2,1,0:T(8,128)(2,1)S(1)}, u32[]{:S(2)}, u32[]{:S(2)}) collective-permute-start(bf16[2,128,256]{2,1,0:T(8,128)(2,1)S(1)} %get-tuple-element.49), channel_id=1, source_target_pairs={{0,4},{4,0},{8,12},{12,8},{16,20},{20,16},{24,28},{28,24},{1,5},{5... | collective-permute-start | bytes 393224 | tf_op jit(solution)/shard_map/ppermute | solution.py:394
  20.4 5.0 %collective-permute-start.7 = (bf16[2,128,256]{2,1,0:T(8,128)(2,1)S(1)}, bf16[2,128,256]{2,1,0:T(8,128)(2,1)S(1)}, u32[]{:S(2)}, u32[]{:S(2)}) collective-permute-start(bf16[2,128,256]{2,1,0:T(8,128)(2,1)S(1)} %shard_map.68.own), channel_id=1, source_target_pairs={{0,8},{4,12},{8,0},{12,4},{16,24},{20,28},{24,16},{28,20},{1,9},{5... | collective-permute-start | bytes 393224 | tf_op jit(solution)/shard_map/ppermute | solution.py:394
  22.3 1.6 %slice-start.1 = ((bf16[2048,2,768]{2,1,0:T(2,128)(2,1)}), bf16[2048,2,256]{2,1,0:T(2,128)(2,1)S(1)}, s32[]{:S(2)}) async-start(bf16[2048,2,768]{2,1,0:T(2,128)(2,1)} %param.7), calls=%async_computation.1 | async-start | bytes 4194304 | tf_op jit(solution)/shard_map/slice | solution.py:456
  23.9 1.2 %slice-start.2 = ((bf16[2048,2,768]{2,1,0:T(2,128)(2,1)}), bf16[2048,2,128]{2,1,0:T(2,128)(2,1)S(1)}, s32[]{:S(2)}) async-start(bf16[2048,2,768]{2,1,0:T(2,128)(2,1)} %param.7), calls=%async_computation.2 | async-start | bytes 2097152 | tf_op jit(solution)/shard_map/slice | solution.py:455
  24.4 4.1 %copy-start.2 = (f32[128]{0:T(128)S(1)}, f32[128]{0:T(128)}, u32[]{:S(2)}) copy-start(f32[128]{0:T(128)} %param.10) | copy-start | bytes 1540
  25.6 5.2 %collective-permute-start.8 = (bf16[2,128,128]{2,1,0:T(8,128)(2,1)S(1)}, bf16[2,128,128]{2,1,0:T(8,128)(2,1)S(1)}, u32[]{:S(2)}, u32[]{:S(2)}) collective-permute-start(bf16[2,128,128]{2,1,0:T(8,128)(2,1)S(1)} %shard_map.69), channel_id=1, source_target_pairs={{0,16},{4,20},{8,24},{12,28},{16,0},{20,4},{24,8},{28,12},{1,17},{... | collective-permute-start | bytes 196616 | tf_op jit(solution)/shard_map/ppermute | solution.py:394
  31.2 4.3 %collective-permute-start.9 = (bf16[2,128,128]{2,1,0:T(8,128)(2,1)S(1)}, bf16[2,128,128]{2,1,0:T(8,128)(2,1)S(1)}, u32[]{:S(2)}, u32[]{:S(2)}) collective-permute-start(bf16[2,128,128]{2,1,0:T(8,128)(2,1)S(1)} %get-tuple-element.63), channel_id=1, source_target_pairs={{0,4},{4,0},{8,12},{12,8},{16,20},{20,16},{24,28},{28,24},{1,5},{5... | collective-permute-start | bytes 196616 | tf_op jit(solution)/shard_map/ppermute | solution.py:394
  36.3 7.1 %collective-permute-start.12 = (bf16[64,2048]{1,0:T(8,128)(2,1)S(1)}, bf16[64,2048]{1,0:T(8,128)(2,1)S(1)}, u32[]{:S(2)}, u32[]{:S(2)}) collective-permute-start(bf16[64,2048]{1,0:T(8,128)(2,1)S(1)} %shard_map.76), channel_id=1, source_target_pairs={{0,2},{1,3},{2,0},{3,1},{4,6},{5,7},{6,4},{7,5},{8,10},{9,11},{10,... | collective-permute-start | bytes 786440 | tf_op jit(solution)/shard_map/ppermute | solution.py:394
  38.2 1.3 %collective-permute-start.10 = (bf16[128,512]{1,0:T(8,128)(2,1)S(1)}, bf16[128,512]{1,0:T(8,128)(2,1)S(1)}, u32[]{:S(2)}, u32[]{:S(2)}) collective-permute-start(bf16[128,512]{1,0:T(8,128)(2,1)S(1)} %get-tuple-element.66.send), channel_id=1, source_target_pairs={{0,1},{1,0},{2,3},{3,2},{4,5},{5,4},{6,7},{7,6},{8,9},{9,8},{10,11... | collective-permute-start | bytes 393224 | tf_op jit(solution)/shard_map/ppermute | solution.py:394
  40.0 6.4 %collective-permute-start.14 = (bf16[64,2048]{1,0:T(8,128)(2,1)S(1)}, bf16[64,2048]{1,0:T(8,128)(2,1)S(1)}, u32[]{:S(2)}, u32[]{:S(2)}) collective-permute-start(bf16[64,2048]{1,0:T(8,128)(2,1)S(1)} %shard_map.77), channel_id=1, source_target_pairs={{0,4},{1,3},{2,6},{3,1},{4,0},{5,7},{6,2},{7,5},{8,12},{9,11},{10,... | collective-permute-start | bytes 786440 | tf_op jit(solution)/shard_map/ppermute | solution.py:549
  43.4 3.0 %collective-permute-start.13 = (bf16[64,2048]{1,0:T(8,128)(2,1)S(1)}, bf16[64,2048]{1,0:T(8,128)(2,1)S(1)}, u32[]{:S(2)}, u32[]{:S(2)}) collective-permute-start(bf16[64,2048]{1,0:T(8,128)(2,1)S(1)} %collective-permute-done.12.refs_1_), channel_id=1, source_target_pairs={{0,1},{1,0},{2,3},{3,2},{4,5},{5,4},{6,7},{7,6},{8,9},{9,8},{10,11... | collective-permute-start | bytes 786440 | tf_op jit(solution)/shard_map/ppermute | solution.py:394

commit v12 on v11

--- a/solution.py
+++ b/solution.py
@@ -542,7 +542,7 @@
     for i in range(1, n_head // 2):
         late = call(out_kernel, shaped((part, width), BF16), [other, w_other, sums[i]], 0.5, first=i)
         late_perm = [
-            (c * n_head + h, c * n_head + (h ^ (2 * i)) if h % 2 else (c ^ 1) * n_head + h)
+            (c * n_head + h, c * n_head + (h ^ (2 * i)) if h % 2 else (c ^ 2) * n_head + h)
             for c in range(n_ctx)
             for h in range(n_head)
         ]

time: 47.5 us -> 47.5 us (level)
  no operation moved by 1% of the time
where the time goes in v12:
time: 47.5 us; the launch traced here: 47.3 us
  starting transfers between devices  17.7 us (37%)
  Pallas kernels  14.2 us (30%)
  waiting for transfers between devices  9.64 us (20%)
  local copies, waits for them, and re-layouts  5.52 us (12%)
    pallas_call x15, Pallas kernels, call(): pl.pallas_call(functools.partial(body, **static), out_shape=out_shape, in...  14.2 us
    ppermute x12, starting transfers between devices, xor_sent(): return lax.ppermute(value, axis, [(i, i ^ step) for i in range(count)])  13.9 us
    ppermute x12, waiting for transfers between devices, xor_sent(): return lax.ppermute(value, axis, [(i, i ^ step) for i in range(count)])  6.51 us
    ppermute x1, waiting for transfers between devices, local(): late_got.append(lax.ppermute(late, ctx_head, late_perm))  3 us
    ppermute x2, starting transfers between devices, local(): lax.ppermute(tail, ctx_head, halo_pairs(n_ctx, n_head, target))  2.14 us
    slice x2, local copies, waits for them, and re-layouts, local(): w_kv = in_proj[:, :, DK:v_end].reshape(width, key_heads * (v_end - DK))  1.89 us
    ppermute x1, starting transfers between devices, local(): late_got.append(lax.ppermute(late, ctx_head, late_perm))  1.64 us
    slice x2, local copies, waits for them, and re-layouts, local(): w_z = in_proj[:, :, v_end:].reshape(width, heads * DV)  1.59 us
  transfers between devices with their start and end apart: 15, of which 10 were waited for; matrix products, arithmetic and copies ran while one was open for 3% of the time, Pallas kernels for 22%

profile of v12, /device:TPU:0, one launch (start us, length us, event | category | flops | bytes accessed | tf_op | source)
XLA Modules:
  0.0 47.3 jit_solution(15661394580716421962)
XLA Ops:
  0.0 3.0 %collective-permute-start.1 = (bf16[64,2048]{1,0:T(8,128)(2,1)}, bf16[64,2048]{1,0:T(8,128)(2,1)S(1)}, u32[]{:S(2)}, u32[]{:S(2)}) collective-permute-start(bf16[64,2048]{1,0:T(8,128)(2,1)} %x_any.1), channel_id=1, source_target_pairs={{0,2},{1,3},{2,0},{3,1},{4,6},{5,7},{6,4},{7,5},{8,10},{9,11},{10,... | collective-permute-start | bytes 786440 | tf_op jit(solution)/shard_map/ppermute | solution.py:394
  3.0 1.1 %shard_map.64 = (bf16[48,128]{1,0:T(8,128)(2,1)S(1)}, bf16[64,2048]{1,0:T(8,128)(2,1)S(1)}, f32[2,4,256]{2,1,0:T(4,128)S(1)}) custom-call(bf16[64,2048]{1,0:T(8,128)(2,1)} %x_any.1, f32[2,4,256]{2,1,0:T(4,128)} %logits_any.1), custom_call_target="tpu_custom_call" | custom-call | flops 6899999744 | bytes 270336 | tf_op jit(solution)/shard_map/pallas_call | solution.py:377
  4.1 2.1 %collective-permute-start.4 = (bf16[48,128]{1,0:T(8,128)(2,1)S(1)}, bf16[48,128]{1,0:T(8,128)(2,1)S(1)}, u32[]{:S(2)}, u32[]{:S(2)}) collective-permute-start(bf16[48,128]{1,0:T(8,128)(2,1)S(1)} %get-tuple-element.40), channel_id=1, source_target_pairs={{0,2},{1,9},{2,0},{3,6},{4,5},{5,4},{6,3},{7,10},{8,12},{9,1},{10,... | collective-permute-start | bytes 36872 | tf_op jit(solution)/shard_map/ppermute | solution.py:450
  6.2 1.9 %slice-done = bf16[2048,2,384]{2,1,0:T(2,128)(2,1)S(1)} async-done(((bf16[2048,2,768]{2,1,0:T(2,128)(2,1)}), bf16[2048,2,384]{2,1,0:T(2,128)(2,1)S(1)}, s32[]{:S(2)}) %slice-start) | async-done | bytes 3145752 | tf_op jit(solution)/shard_map/slice | solution.py:452
  8.1 0.7 %copy.7 = bf16[256,8,2,384]{3,1,2,0:T(8,128)(2,1)S(1)} copy(bf16[256,8,2,384]{3,2,1,0:T(2,128)(2,1)S(1)} %bitcast.14) | data formatting | bytes 6291456
  8.8 0.8 %collective-permute-done.1.refs_2_ = bf16[64,2048]{1,0:T(8,128)(2,1)S(1)} collective-permute-done((bf16[64,2048]{1,0:T(8,128)(2,1)}, bf16[64,2048]{1,0:T(8,128)(2,1)S(1)}, u32[]{:S(2)}, u32[]{:S(2)}) %collective-permute-start.1) | collective-permute-done | bytes 262176 | tf_op jit(solution)/shard_map/ppermute | solution.py:394
  10.1 0.8 %shard_map.65 = (f32[4,256]{1,0:T(4,128)S(1)}, f32[256,8]{1,0:T(8,128)S(1)}, f32[4,3,128,128]{3,2,1,0:T(8,128)S(1)}) custom-call(f32[2,4,256]{2,1,0:T(4,128)S(1)} %get-tuple-element.43.logits), custom_call_target="tpu_custom_call" | custom-call | flops 1150000000 | bytes 8192 | tf_op jit(solution)/shard_map/pallas_call | solution.py:377
  11.1 3.1 %shard_map.66 = (bf16[2,128,256]{2,1,0:T(8,128)(2,1)S(1)}, bf16[2,256,256]{2,1,0:T(8,128)(2,1)S(1)}, bf16[1,256,128]{2,1,0:T(8,128)(2,1)S(1)}, bf16[272,2048]{1,0:T(8,128)(2,1)S(1)}) custom-call(bf16[64,2048]{1,0:T(8,128)(2,1)S(1)} %get-tuple-element.39.refs_0_, bf16[64,2048]{1,0:T(8,128)(2,1)S(1)} %collective-permute-done.refs_1_, ...), custom_call_target="tpu_custom_call" | custom-call | flops 3449999872 | bytes 5033984 | tf_op jit(solution)/shard_map/pallas_call | solution.py:377
  14.5 1.8 %collective-permute-start.6 = (bf16[2,128,256]{2,1,0:T(8,128)(2,1)S(1)}, bf16[2,128,256]{2,1,0:T(8,128)(2,1)S(1)}, u32[]{:S(2)}, u32[]{:S(2)}) collective-permute-start(bf16[2,128,256]{2,1,0:T(8,128)(2,1)S(1)} %get-tuple-element.49), channel_id=1, source_target_pairs={{0,4},{4,0},{8,12},{12,8},{16,20},{20,16},{24,28},{28,24},{1,5},{5... | collective-permute-start | bytes 393224 | tf_op jit(solution)/shard_map/ppermute | solution.py:394
  16.3 3.0 %shard_map.67 = (bf16[2,128,256]{2,1,0:T(8,128)(2,1)S(1)}, bf16[2,256,256]{2,1,0:T(8,128)(2,1)S(1)}, bf16[1,256,128]{2,1,0:T(8,128)(2,1)S(1)}) custom-call(bf16[272,2048]{1,0:T(8,128)(2,1)S(1)} %get-tuple-element.47.x, bf16[2048,768]{1,0:T(8,128)(2,1)S(1)} %bitcast.10, f32[4,2,512]{2,1,0:T(2,128)S(1)} %copy-done.1, ...), custom_call_target="tpu_custom_call" | custom-call | flops 3449999872 | bytes 5074944 | tf_op jit(solution)/shard_map/pallas_call | solution.py:377
  19.3 1.0 %collective-permute-done.6.got.pair = bf16[2,128,256]{2,1,0:T(8,128)(2,1)S(1)} collective-permute-done((bf16[2,128,256]{2,1,0:T(8,128)(2,1)S(1)}, bf16[2,128,256]{2,1,0:T(8,128)(2,1)S(1)}, u32[]{:S(2)}, u32[]{:S(2)}) %collective-permute-start.6) | collective-permute-done | bytes 131104 | tf_op jit(solution)/shard_map/ppermute | solution.py:394
  20.4 1.9 %collective-permute-start.7 = (bf16[2,128,256]{2,1,0:T(8,128)(2,1)S(1)}, bf16[2,128,256]{2,1,0:T(8,128)(2,1)S(1)}, u32[]{:S(2)}, u32[]{:S(2)}) collective-permute-start(bf16[2,128,256]{2,1,0:T(8,128)(2,1)S(1)} %shard_map.68.own), channel_id=1, source_target_pairs={{0,8},{4,12},{8,0},{12,4},{16,24},{20,28},{24,16},{28,20},{1,9},{5... | collective-permute-start | bytes 393224 | tf_op jit(solution)/shard_map/ppermute | solution.py:394
  22.3 1.6 %slice-done.1 = bf16[2048,2,256]{2,1,0:T(2,128)(2,1)S(1)} async-done(((bf16[2048,2,768]{2,1,0:T(2,128)(2,1)}), bf16[2048,2,256]{2,1,0:T(2,128)(2,1)S(1)}, s32[]{:S(2)}) %slice-start.1) | async-done | bytes 2097176 | tf_op jit(solution)/shard_map/slice | solution.py:456
  24.4 0.7 %slice-done.2 = bf16[2048,2,128]{2,1,0:T(2,128)(2,1)S(1)} async-done(((bf16[2048,2,768]{2,1,0:T(2,128)(2,1)}), bf16[2048,2,128]{2,1,0:T(2,128)(2,1)S(1)}, s32[]{:S(2)}) %slice-start.2) | async-done | bytes 1048600 | tf_op jit(solution)/shard_map/slice | solution.py:455
  25.6 2.9 %collective-permute-start.8 = (bf16[2,128,128]{2,1,0:T(8,128)(2,1)S(1)}, bf16[2,128,128]{2,1,0:T(8,128)(2,1)S(1)}, u32[]{:S(2)}, u32[]{:S(2)}) collective-permute-start(bf16[2,128,128]{2,1,0:T(8,128)(2,1)S(1)} %shard_map.69), channel_id=1, source_target_pairs={{0,16},{4,20},{8,24},{12,28},{16,0},{20,4},{24,8},{28,12},{1,17},{... | collective-permute-start | bytes 196616 | tf_op jit(solution)/shard_map/ppermute | solution.py:394
  28.5 1.9 %shard_map.70 = (bf16[4,256,128]{2,1,0:T(8,128)(2,1)S(1)}, f32[4,256,128]{2,1,0:T(8,128)S(1)}, f32[4,256,128]{2,1,0:T(8,128)S(1)}) custom-call(bf16[272,2048]{1,0:T(8,128)(2,1)S(1)} %get-tuple-element.47.x, bf16[2048,256]{1,0:T(8,128)(2,1)S(1)} %bitcast.12, bf16[2048,512]{1,0:T(8,128)(2,1)S(1)} %bitcast.11, f32[4,2,512]{2,1,0:T(2,128)S(1)} %copy-done.1, ...), custom_call_target="tpu_custom_call" | custom-call | flops 2184999936 | bytes 4944384 | tf_op jit(solution)/shard_map/pallas_call | solution.py:377
  31.2 1.8 %collective-permute-start.9 = (bf16[2,128,128]{2,1,0:T(8,128)(2,1)S(1)}, bf16[2,128,128]{2,1,0:T(8,128)(2,1)S(1)}, u32[]{:S(2)}, u32[]{:S(2)}) collective-permute-start(bf16[2,128,128]{2,1,0:T(8,128)(2,1)S(1)} %get-tuple-element.63), channel_id=1, source_target_pairs={{0,4},{4,0},{8,12},{12,8},{16,20},{20,16},{24,28},{28,24},{1,5},{5... | collective-permute-start | bytes 196616 | tf_op jit(solution)/shard_map/ppermute | solution.py:394
  33.3 2.2 %collective-permute-done.9.got = bf16[2,128,128]{2,1,0:T(8,128)(2,1)S(1)} collective-permute-done((bf16[2,128,128]{2,1,0:T(8,128)(2,1)S(1)}, bf16[2,128,128]{2,1,0:T(8,128)(2,1)S(1)}, u32[]{:S(2)}, u32[]{:S(2)}) %collective-permute-start.9) | collective-permute-done | bytes 65568 | tf_op jit(solution)/shard_map/ppermute | solution.py:394
  36.3 1.8 %collective-permute-start.12 = (bf16[64,2048]{1,0:T(8,128)(2,1)S(1)}, bf16[64,2048]{1,0:T(8,128)(2,1)S(1)}, u32[]{:S(2)}, u32[]{:S(2)}) collective-permute-start(bf16[64,2048]{1,0:T(8,128)(2,1)S(1)} %shard_map.76), channel_id=1, source_target_pairs={{0,2},{1,3},{2,0},{3,1},{4,6},{5,7},{6,4},{7,5},{8,10},{9,11},{10,... | collective-permute-start | bytes 786440 | tf_op jit(solution)/shard_map/ppermute | solution.py:394
  38.2 0.8 %shard_map.74 = (f32[64,2048]{1,0:T(8,128)S(1)}, f32[64,2048]{1,0:T(8,128)S(1)}) custom-call(bf16[128,512]{1,0:T(8,128)(2,1)S(1)} %get-tuple-element.68.own.keep, bf16[512,2048]{1,0:T(8,128)(2,1)S(1)} %copy-done), custom_call_target="tpu_custom_call" | custom-call | flops 920000000 | bytes 2228224 | tf_op jit(solution)/shard_map/pallas_call | solution.py:377
  40.0 1.6 %collective-permute-start.14 = (bf16[64,2048]{1,0:T(8,128)(2,1)S(1)}, bf16[64,2048]{1,0:T(8,128)(2,1)S(1)}, u32[]{:S(2)}, u32[]{:S(2)}) collective-permute-start(bf16[64,2048]{1,0:T(8,128)(2,1)S(1)} %shard_map.77), channel_id=1, source_target_pairs={{0,8},{1,3},{2,10},{3,1},{4,12},{5,7},{6,14},{7,5},{8,0},{9,11},{1... | collective-permute-start | bytes 786440 | tf_op jit(solution)/shard_map/ppermute | solution.py:549
  42.1 1.3 %collective-permute-done.12.refs_1_ = bf16[64,2048]{1,0:T(8,128)(2,1)S(1)} collective-permute-done((bf16[64,2048]{1,0:T(8,128)(2,1)S(1)}, bf16[64,2048]{1,0:T(8,128)(2,1)S(1)}, u32[]{:S(2)}, u32[]{:S(2)}) %collective-permute-start.12) | collective-permute-done | bytes 262176 | tf_op jit(solution)/shard_map/ppermute | solution.py:394
  43.4 3.0 %collective-permute-done.14.refs_3_ = bf16[64,2048]{1,0:T(8,128)(2,1)S(1)} collective-permute-done((bf16[64,2048]{1,0:T(8,128)(2,1)S(1)}, bf16[64,2048]{1,0:T(8,128)(2,1)S(1)}, u32[]{:S(2)}, u32[]{:S(2)}) %collective-permute-start.14) | collective-permute-done | bytes 262176 | tf_op jit(solution)/shard_map/ppermute | solution.py:549
  46.4 0.8 %shard_map.78 = bf16[64,2048]{1,0:T(8,128)(2,1)} custom-call(f32[64,2048]{1,0:T(8,128)S(1)} %shard_map.75.refs_0_, bf16[64,2048]{1,0:T(8,128)(2,1)S(1)} %collective-permute-done.12.refs_1_, bf16[64,2048]{1,0:T(8,128)(2,1)S(1)} %collective-permute-done.13.refs_2_, bf16[64,2048]{1,0:T(8,128)(2,1)S(1)} %collective-permute-done.14.refs_3_), custom_call_target="tpu_custom_call" | custom-call | flops 575000000 | bytes 1310720 | tf_op jit(solution)/shard_map/pallas_call | solution.py:377
  (39 shorter events, 5.6 us)
Async XLA Ops:
  0.0 6.2 %copy-start.3 = (bf16[64,2048]{1,0:T(8,128)(2,1)S(1)}, bf16[64,2048]{1,0:T(8,128)(2,1)}, u32[]{:S(2)}) copy-start(bf16[64,2048]{1,0:T(8,128)(2,1)} %x_any.1) | copy-start | bytes 786436
  0.0 9.6 %collective-permute-start.1 = (bf16[64,2048]{1,0:T(8,128)(2,1)}, bf16[64,2048]{1,0:T(8,128)(2,1)S(1)}, u32[]{:S(2)}, u32[]{:S(2)}) collective-permute-start(bf16[64,2048]{1,0:T(8,128)(2,1)} %x_any.1), channel_id=1, source_target_pairs={{0,2},{1,3},{2,0},{3,1},{4,6},{5,7},{6,4},{7,5},{8,10},{9,11},{10,... | collective-permute-start | bytes 786440 | tf_op jit(solution)/shard_map/ppermute | solution.py:394
  4.0 5.5 %collective-permute-start.3 = (bf16[48,128]{1,0:T(8,128)(2,1)S(1)}, bf16[48,128]{1,0:T(8,128)(2,1)S(1)}, u32[]{:S(2)}, u32[]{:S(2)}) collective-permute-start(bf16[48,128]{1,0:T(8,128)(2,1)S(1)} %get-tuple-element.40), channel_id=1, source_target_pairs={{0,1},{1,0},{2,10},{3,5},{4,6},{5,3},{6,4},{7,9},{8,12},{9,7},{10,... | collective-permute-start | bytes 36872 | tf_op jit(solution)/shard_map/ppermute | solution.py:450
  4.1 5.6 %collective-permute-start.4 = (bf16[48,128]{1,0:T(8,128)(2,1)S(1)}, bf16[48,128]{1,0:T(8,128)(2,1)S(1)}, u32[]{:S(2)}, u32[]{:S(2)}) collective-permute-start(bf16[48,128]{1,0:T(8,128)(2,1)S(1)} %get-tuple-element.40), channel_id=1, source_target_pairs={{0,2},{1,9},{2,0},{3,6},{4,5},{5,4},{6,3},{7,10},{8,12},{9,1},{10,... | collective-permute-start | bytes 36872 | tf_op jit(solution)/shard_map/ppermute | solution.py:450
  6.2 4.9 %collective-permute-start = (bf16[64,2048]{1,0:T(8,128)(2,1)S(1)}, bf16[64,2048]{1,0:T(8,128)(2,1)S(1)}, u32[]{:S(2)}, u32[]{:S(2)}) collective-permute-start(bf16[64,2048]{1,0:T(8,128)(2,1)S(1)} %copy-done.3), channel_id=1, source_target_pairs={{0,1},{1,0},{2,3},{3,2},{4,5},{5,4},{6,7},{7,6},{8,9},{9,8},{10,11... | collective-permute-start | bytes 786440 | tf_op jit(solution)/shard_map/ppermute | solution.py:394
  6.2 1.9 %slice-start = ((bf16[2048,2,768]{2,1,0:T(2,128)(2,1)}), bf16[2048,2,384]{2,1,0:T(2,128)(2,1)S(1)}, s32[]{:S(2)}) async-start(bf16[2048,2,768]{2,1,0:T(2,128)(2,1)} %param.7), calls=%async_computation | async-start | bytes 6291456 | tf_op jit(solution)/shard_map/slice | solution.py:452
  9.6 1.6 %collective-permute-start.2 = (bf16[64,2048]{1,0:T(8,128)(2,1)S(1)}, bf16[64,2048]{1,0:T(8,128)(2,1)S(1)}, u32[]{:S(2)}, u32[]{:S(2)}) collective-permute-start(bf16[64,2048]{1,0:T(8,128)(2,1)S(1)} %collective-permute-done.1.refs_2_), channel_id=1, source_target_pairs={{0,1},{1,0},{2,3},{3,2},{4,5},{5,4},{6,7},{7,6},{8,9},{9,8},{10,11... | collective-permute-start | bytes 786440 | tf_op jit(solution)/shard_map/ppermute | solution.py:394
  9.7 1.4 %collective-permute-start.5 = (bf16[48,128]{1,0:T(8,128)(2,1)S(1)}, bf16[48,128]{1,0:T(8,128)(2,1)S(1)}, u32[]{:S(2)}, u32[]{:S(2)}) collective-permute-start(bf16[48,128]{1,0:T(8,128)(2,1)S(1)} %select_select_fusion.refs_4_), channel_id=1, source_target_pairs={{0,1},{1,0},{2,3},{3,2},{4,5},{5,4},{6,7},{7,6},{8,9},{9,8},{10,11... | collective-permute-start | bytes 36872 | tf_op jit(solution)/shard_map/ppermute | solution.py:394
  10.1 1.0 %copy-start.1 = (f32[4,2,512]{2,1,0:T(2,128)S(1)}, f32[4,2,512]{2,1,0:T(2,128)}, u32[]{:S(2)}) copy-start(f32[4,2,512]{2,1,0:T(2,128)} %cw.3) | copy-start | bytes 49156
  11.1 3.1 %copy-start = (bf16[512,2048]{1,0:T(8,128)(2,1)S(1)}, bf16[512,2048]{1,0:T(8,128)(2,1)}, u32[]{:S(2)}) copy-start(bf16[512,2048]{1,0:T(8,128)(2,1)} %w.3) | copy-start | bytes 6291460
  14.2 25.3 %collective-permute-start.11 = (bf16[512,2048]{1,0:T(8,128)(2,1)S(1)}, bf16[512,2048]{1,0:T(8,128)(2,1)S(1)}, u32[]{:S(2)}, u32[]{:S(2)}) collective-permute-start(bf16[512,2048]{1,0:T(8,128)(2,1)S(1)} %copy-done), channel_id=1, source_target_pairs={{0,1},{1,0},{2,3},{3,2},{4,5},{5,4},{6,7},{7,6},{8,9},{9,8},{10,11... | collective-permute-start | bytes 6291464 | tf_op jit(solution)/shard_map/ppermute | solution.py:394
  14.5 5.7 %collective-permute-start.6 = (bf16[2,128,256]{2,1,0:T(8,128)(2,1)S(1)}, bf16[2,128,256]{2,1,0:T(8,128)(2,1)S(1)}, u32[]{:S(2)}, u32[]{:S(2)}) collective-permute-start(bf16[2,128,256]{2,1,0:T(8,128)(2,1)S(1)} %get-tuple-element.49), channel_id=1, source_target_pairs={{0,4},{4,0},{8,12},{12,8},{16,20},{20,16},{24,28},{28,24},{1,5},{5... | collective-permute-start | bytes 393224 | tf_op jit(solution)/shard_map/ppermute | solution.py:394
  20.4 5.0 %collective-permute-start.7 = (bf16[2,128,256]{2,1,0:T(8,128)(2,1)S(1)}, bf16[2,128,256]{2,1,0:T(8,128)(2,1)S(1)}, u32[]{:S(2)}, u32[]{:S(2)}) collective-permute-start(bf16[2,128,256]{2,1,0:T(8,128)(2,1)S(1)} %shard_map.68.own), channel_id=1, source_target_pairs={{0,8},{4,12},{8,0},{12,4},{16,24},{20,28},{24,16},{28,20},{1,9},{5... | collective-permute-start | bytes 393224 | tf_op jit(solution)/shard_map/ppermute | solution.py:394
  22.3 1.6 %slice-start.1 = ((bf16[2048,2,768]{2,1,0:T(2,128)(2,1)}), bf16[2048,2,256]{2,1,0:T(2,128)(2,1)S(1)}, s32[]{:S(2)}) async-start(bf16[2048,2,768]{2,1,0:T(2,128)(2,1)} %param.7), calls=%async_computation.1 | async-start | bytes 4194304 | tf_op jit(solution)/shard_map/slice | solution.py:456
  23.9 1.2 %slice-start.2 = ((bf16[2048,2,768]{2,1,0:T(2,128)(2,1)}), bf16[2048,2,128]{2,1,0:T(2,128)(2,1)S(1)}, s32[]{:S(2)}) async-start(bf16[2048,2,768]{2,1,0:T(2,128)(2,1)} %param.7), calls=%async_computation.2 | async-start | bytes 2097152 | tf_op jit(solution)/shard_map/slice | solution.py:455
  24.4 4.1 %copy-start.2 = (f32[128]{0:T(128)S(1)}, f32[128]{0:T(128)}, u32[]{:S(2)}) copy-start(f32[128]{0:T(128)} %param.10) | copy-start | bytes 1540
  25.6 5.2 %collective-permute-start.8 = (bf16[2,128,128]{2,1,0:T(8,128)(2,1)S(1)}, bf16[2,128,128]{2,1,0:T(8,128)(2,1)S(1)}, u32[]{:S(2)}, u32[]{:S(2)}) collective-permute-start(bf16[2,128,128]{2,1,0:T(8,128)(2,1)S(1)} %shard_map.69), channel_id=1, source_target_pairs={{0,16},{4,20},{8,24},{12,28},{16,0},{20,4},{24,8},{28,12},{1,17},{... | collective-permute-start | bytes 196616 | tf_op jit(solution)/shard_map/ppermute | solution.py:394
  31.2 4.3 %collective-permute-start.9 = (bf16[2,128,128]{2,1,0:T(8,128)(2,1)S(1)}, bf16[2,128,128]{2,1,0:T(8,128)(2,1)S(1)}, u32[]{:S(2)}, u32[]{:S(2)}) collective-permute-start(bf16[2,128,128]{2,1,0:T(8,128)(2,1)S(1)} %get-tuple-element.63), channel_id=1, source_target_pairs={{0,4},{4,0},{8,12},{12,8},{16,20},{20,16},{24,28},{28,24},{1,5},{5... | collective-permute-start | bytes 196616 | tf_op jit(solution)/shard_map/ppermute | solution.py:394
  36.3 7.1 %collective-permute-start.12 = (bf16[64,2048]{1,0:T(8,128)(2,1)S(1)}, bf16[64,2048]{1,0:T(8,128)(2,1)S(1)}, u32[]{:S(2)}, u32[]{:S(2)}) collective-permute-start(bf16[64,2048]{1,0:T(8,128)(2,1)S(1)} %shard_map.76), channel_id=1, source_target_pairs={{0,2},{1,3},{2,0},{3,1},{4,6},{5,7},{6,4},{7,5},{8,10},{9,11},{10,... | collective-permute-start | bytes 786440 | tf_op jit(solution)/shard_map/ppermute | solution.py:394
  38.2 1.3 %collective-permute-start.10 = (bf16[128,512]{1,0:T(8,128)(2,1)S(1)}, bf16[128,512]{1,0:T(8,128)(2,1)S(1)}, u32[]{:S(2)}, u32[]{:S(2)}) collective-permute-start(bf16[128,512]{1,0:T(8,128)(2,1)S(1)} %get-tuple-element.66.send), channel_id=1, source_target_pairs={{0,1},{1,0},{2,3},{3,2},{4,5},{5,4},{6,7},{7,6},{8,9},{9,8},{10,11... | collective-permute-start | bytes 393224 | tf_op jit(solution)/shard_map/ppermute | solution.py:394
  40.0 6.4 %collective-permute-start.14 = (bf16[64,2048]{1,0:T(8,128)(2,1)S(1)}, bf16[64,2048]{1,0:T(8,128)(2,1)S(1)}, u32[]{:S(2)}, u32[]{:S(2)}) collective-permute-start(bf16[64,2048]{1,0:T(8,128)(2,1)S(1)} %shard_map.77), channel_id=1, source_target_pairs={{0,8},{1,3},{2,10},{3,1},{4,12},{5,7},{6,14},{7,5},{8,0},{9,11},{1... | collective-permute-start | bytes 786440 | tf_op jit(solution)/shard_map/ppermute | solution.py:549
  43.4 3.0 %collective-permute-start.13 = (bf16[64,2048]{1,0:T(8,128)(2,1)S(1)}, bf16[64,2048]{1,0:T(8,128)(2,1)S(1)}, u32[]{:S(2)}, u32[]{:S(2)}) collective-permute-start(bf16[64,2048]{1,0:T(8,128)(2,1)S(1)} %collective-permute-done.12.refs_1_), channel_id=1, source_target_pairs={{0,1},{1,0},{2,3},{3,2},{4,5},{5,4},{6,7},{7,6},{8,9},{9,8},{10,11... | collective-permute-start | bytes 786440 | tf_op jit(solution)/shard_map/ppermute | solution.py:394
